TPU v7x, 32 devices: a whole 2x2x4 slice. The times are simulated.
32 devices in a mesh: grp: 2 (over y), batch: 8 (over z, x), tensor: 2 (over core).
Axes of the slice: x: 2, y: 2, z: 4, core: 2. Of those that a mesh axis runs over, the one named last changes fastest.
Arguments:
- init_cache: bfloat16 [16, 2, 64, 3072], P(('grp', 'batch'), None, None, 'tensor'), parts along dimension 0, may hold values from -6 to 6
- memory: bfloat16 [16, 2, 64, 3072], P(('grp', 'batch'), None, None, 'tensor'), parts along dimension 0, may hold values from -6 to 6
- queries: bfloat16 [1, 16, 2, 3072], P(None, ('grp', 'batch'), None, 'tensor'), parts along dimension 1, may hold values from -600 to 600
- new_kv: bfloat16 [1, 16, 2, 3072], P(None, ('grp', 'batch'), None, 'tensor'), parts along dimension 1, may hold values from -6 to 6
- residual: bfloat16 [1, 16, 6144], P(None, 'grp', 'batch'), parts along dimension 1, may hold values from -6 to 6
- out_weight: bfloat16 [2, 3072, 6144], P(None, 'tensor', 'batch'), may hold values from -0.078125 to 0.078125
- up_weight: bfloat16 [6144, 24576], P(None, ('batch', 'tensor')), may hold values from -0.078125 to 0.078125
- down_weight: bfloat16 [24576, 6144], P('batch', 'tensor'), may hold values from -0.0390625 to 0.0390625
- parents: int32 [1, 16], P(None, 'grp'), parts along dimension 1, may hold values from 0 to 7
- lengths: int32 [2], P('grp'), parts along dimension 0, may hold values from 1 to 63
Outputs:
- hidden: bfloat16 [1, 16, 6144], P(None, 'grp', 'batch'), parts along dimension 1
- ffn_out: bfloat16 [1, 16, 6144], P(None, ('grp', 'batch'), 'tensor'), parts along dimension 1
- final_cache: bfloat16 [16, 2, 64, 3072], P(('grp', 'batch'), None, None, 'tensor'), parts along dimension 0
There are 2 independent parts, one for each index of `grp`. A program takes and returns all parts, laid end to end along the dimension named above; an argument that names none is the same for every part. Nothing has to cross between parts.
Inputs may be any that keep to these rules, and one draw needn't show every extreme that they name: parents[s, b + r] is the beam of request r whose cache beam b continues at step s.
All inputs are finite; a program needn't handle non-finite values.
Results may differ from a plain program's by a relative error of at most 0.006.
Values may be sent and summed in bfloat16 or wider, within the bound.
No kernel may reach another device: no remote copies, remote signals or barrier semaphores. Data moves between devices by JAX's collectives and lax.ppermute only.
A program may use at most 128 MiB of HBM per device.

v0:
```python
import math

import jax
import jax.numpy as jnp
from jax import lax
from jax.sharding import PartitionSpec as P

HD = 128
BEAMS = 8


def from_behind(value, axis, by):
    devices = lax.axis_size(axis)
    return lax.ppermute(value, axis, [(i, (i + by) % devices) for i in range(devices)])


def attend(query, keys, values, valid):
    highest = lax.Precision.HIGHEST
    scores = jnp.einsum("nhd,chd->nhc", query, keys, precision=highest) / math.sqrt(HD)
    mask = valid[:, None, :]
    masked = jnp.where(mask, scores, -1e30)
    peak = jnp.max(masked, axis=-1)
    weights = jnp.where(mask, jnp.exp(masked - peak[..., None]), 0.0)
    total = jnp.sum(weights, axis=-1)
    weighted = jnp.einsum("nhc,chd->nhd", weights, values, precision=highest)
    return (weighted, peak, total)


def spread(payload, stride):
    items = [payload]
    for offset in range(1, BEAMS):
        items.append(from_behind(payload, "batch", offset * stride))
    return jnp.stack(items)


def take_from(block, source, own_beam, stride):
    wanted = (own_beam - source) % BEAMS
    result = block
    for offset in range(1, BEAMS):
        moved = from_behind(block, "batch", offset * stride)
        result = jnp.where(wanted == offset, moved, result)
    return result


def collect(weighted, peak, total, stride):
    gathered = [(weighted[0], peak[0], total[0])]
    for offset in range(1, BEAMS):
        gathered.append(
            from_behind((weighted[offset], peak[offset], total[offset]), "batch", -offset * stride)
        )
    return gathered


def combine(gathered):
    peaks = jnp.stack([entry[1] for entry in gathered])
    top = jnp.max(peaks, axis=0)
    factors = jnp.exp(peaks - top[None])
    numer = jnp.sum(jnp.stack([entry[0] for entry in gathered]) * factors[..., None], axis=0)
    denom = jnp.sum(jnp.stack([entry[2] for entry in gathered]) * factors, axis=0)
    return numer / denom[..., None]


def body(
    init_cache,
    memory,
    queries,
    new_kv,
    residual,
    out_weight,
    up_weight,
    down_weight,
    parents,
    lengths,
):
    stride = lax.axis_size("batch") // BEAMS
    position = lax.axis_index("batch")
    own_beam = position // stride
    request = position % stride
    width_local = queries.shape[-1]
    local_heads = width_local // HD
    cache_len = init_cache.shape[2]
    steps = queries.shape[0]
    request_ids = jnp.arange(stride, dtype=jnp.int32)
    length = jnp.sum(jnp.where(request_ids == request, lengths, 0))
    grouped = parents.reshape(steps, BEAMS, stride)
    parent_table = jnp.sum(jnp.where(request_ids[None, None, :] == request, grouped, 0), axis=2)
    slots = jnp.arange(cache_len, dtype=jnp.int32)
    beam_ids = jnp.arange(BEAMS, dtype=jnp.int32)
    mem_keys = memory[0, 0].astype(jnp.float32).reshape(-1, local_heads, HD)
    mem_values = memory[0, 1].astype(jnp.float32).reshape(-1, local_heads, HD)
    cross_valid = jnp.ones((BEAMS, mem_keys.shape[0]), dtype=bool)
    init_rows = init_cache[0]
    cache = init_rows
    proj_weight = out_weight.reshape(2 * width_local, out_weight.shape[2])
    own_query = queries[0, 0]
    parent_beam = jnp.sum(jnp.where(beam_ids == own_beam, parent_table[0], 0))
    cache = take_from(cache, parent_beam, own_beam, stride)
    cache = jnp.where((slots == length + 0)[None, :, None], new_kv[0, 0][:, None, :], cache)
    self_query = own_query[0].astype(jnp.float32).reshape(1, local_heads, HD)
    keys = cache[0].astype(jnp.float32).reshape(cache_len, local_heads, HD)
    values = cache[1].astype(jnp.float32).reshape(cache_len, local_heads, HD)
    valid = (slots <= length + 0)[None, :]
    weighted, peak, total = attend(self_query, keys, values, valid)
    self_out = (weighted / total[..., None])[0]
    items = spread(own_query[1], stride)
    cross_query = items.astype(jnp.float32).reshape(BEAMS, local_heads, HD)
    weighted, peak, total = attend(cross_query, mem_keys, mem_values, cross_valid)
    merged = combine(collect(weighted[:, None], peak[:, None], total[:, None], stride))
    cross_out = merged[0]
    attended = jnp.stack([self_out, cross_out]).reshape(1, 2 * width_local).astype(jnp.bfloat16)
    partial_proj = jnp.dot(
        lax.all_gather(attended, "batch", axis=0, tiled=True),
        proj_weight,
        preferred_element_type=jnp.float32,
    )
    projected = lax.psum(partial_proj, "tensor")
    hidden = (residual[0].astype(jnp.float32) + projected).astype(jnp.bfloat16)
    pre_act = jnp.dot(
        lax.all_gather(hidden, "batch", axis=1, tiled=True),
        up_weight,
        preferred_element_type=jnp.float32,
    )
    activation = jax.nn.gelu(pre_act, approximate=False).astype(jnp.bfloat16)
    joined = lax.all_gather(activation, "tensor", axis=1, tiled=True)
    ffn_row = lax.psum_scatter(
        jnp.dot(joined, down_weight, preferred_element_type=jnp.float32),
        "batch",
        scatter_dimension=0,
        tiled=True,
    ).astype(jnp.bfloat16)
    hidden_list = [hidden]
    ffn_list = [ffn_row]
    return (jnp.stack(hidden_list), jnp.stack(ffn_list), cache[None])


def solution(mesh):
    placed = (
        P(("grp", "batch"), None, None, "tensor"),
        P(("grp", "batch"), None, None, "tensor"),
        P(None, ("grp", "batch"), None, "tensor"),
        P(None, ("grp", "batch"), None, "tensor"),
        P(None, "grp", "batch"),
        P(None, "tensor", "batch"),
        P(None, ("batch", "tensor")),
        P("batch", "tensor"),
        P(None, "grp"),
        P("grp"),
    )
    return jax.shard_map(
        body,
        mesh=mesh,
        in_specs=placed,
        out_specs=(
            P(None, "grp", "batch"),
            P(None, ("grp", "batch"), "tensor"),
            P(("grp", "batch"), None, None, "tensor"),
        ),
        check_vma=False,
    )
```

profile of v0, /device:TPU:0, one launch (start us, length us, event | category | flops | bytes accessed | tf_op | source)
XLA Modules:
  0.0 249.9 jit_solution(13383487695798441000)
XLA Ops:
  1.4 3.0 %collective-permute-start.7 = (bf16[1536]{0:T(1024)(128)(2,1)S(1)}, bf16[1536]{0:T(1024)(128)(2,1)S(1)}, u32[]{:S(2)}, u32[]{:S(2)}) collective-permute-start(bf16[1536]{0:T(1024)(128)(2,1)S(1)} %get-tuple-element.42), channel_id=1, source_target_pairs={{0,2},{2,4},{4,6},{6,8},{8,10},{10,12},{12,14},{14,0},{1,3},{3,5},... | collective-permute-start | bytes 9224 | tf_op jit(solution)/shard_map/ppermute | solution.py:14
  4.3 1.6 collective-permute-start.8
  5.9 2.6 %collective-permute-start.9 = (bf16[1536]{0:T(1024)(128)(2,1)S(1)}, bf16[1536]{0:T(1024)(128)(2,1)S(1)}, u32[]{:S(2)}, u32[]{:S(2)}) collective-permute-start(bf16[1536]{0:T(1024)(128)(2,1)S(1)} %get-tuple-element.42), channel_id=1, source_target_pairs={{0,6},{2,8},{4,10},{6,12},{8,14},{10,0},{12,2},{14,4},{1,7},{3,9},... | collective-permute-start | bytes 9224 | tf_op jit(solution)/shard_map/ppermute | solution.py:14
  9.7 2.6 %collective-permute-start.11 = (bf16[1536]{0:T(1024)(128)(2,1)S(1)}, bf16[1536]{0:T(1024)(128)(2,1)S(1)}, u32[]{:S(2)}, u32[]{:S(2)}) collective-permute-start(bf16[1536]{0:T(1024)(128)(2,1)S(1)} %get-tuple-element.42), channel_id=1, source_target_pairs={{0,10},{2,12},{4,14},{6,0},{8,2},{10,4},{12,6},{14,8},{1,11},{3,13... | collective-permute-start | bytes 9224 | tf_op jit(solution)/shard_map/ppermute | solution.py:14
  16.7 1.4 collective-permute-start.13
  21.0 1.4 collective-permute-start.1
  23.0 2.0 collective-permute-start.21
  27.3 9.3 %collective-permute-done.21 = f32[1,12]{0,1:T(8,128)S(1)} collective-permute-done((f32[1,12]{0,1:T(8,128)S(1)}, f32[1,12]{0,1:T(8,128)S(1)}, u32[]{:S(2)}, u32[]{:S(2)}) %collective-permute-start.21) | collective-permute-done | bytes 80 | tf_op jit(solution)/shard_map/ppermute | solution.py:14
  36.6 1.9 collective-permute-start.24
  38.6 3.8 %collective-permute-start.25 = (f32[1,12]{0,1:T(8,128)S(1)}, f32[1,12]{0,1:T(8,128)S(1)}, u32[]{:S(2)}, u32[]{:S(2)}) collective-permute-start(f32[1,12]{0,1:T(8,128)S(1)} %get-tuple-element.35), channel_id=1, source_target_pairs={{0,6},{2,8},{4,10},{6,12},{8,14},{10,0},{12,2},{14,4},{1,7},{3,9},... | collective-permute-start | bytes 152 | tf_op jit(solution)/shard_map/ppermute | solution.py:14
  43.0 1.6 collective-permute-start.27
  44.6 3.1 %collective-permute-start.28 = (f32[1,12]{0,1:T(8,128)S(1)}, f32[1,12]{0,1:T(8,128)S(1)}, u32[]{:S(2)}, u32[]{:S(2)}) collective-permute-start(f32[1,12]{0,1:T(8,128)S(1)} %get-tuple-element.30), channel_id=1, source_target_pairs={{0,14},{2,0},{4,2},{6,4},{8,6},{10,8},{12,10},{14,12},{1,15},{3,1}... | collective-permute-start | bytes 152 | tf_op jit(solution)/shard_map/ppermute | solution.py:14
  49.7 2.1 collective-permute-start.31
  51.9 2.9 %collective-permute-start.32 = (f32[1,12]{0,1:T(8,128)S(1)}, f32[1,12]{0,1:T(8,128)S(1)}, u32[]{:S(2)}, u32[]{:S(2)}) collective-permute-start(f32[1,12]{0,1:T(8,128)S(1)} %get-tuple-element.26), channel_id=1, source_target_pairs={{0,6},{2,8},{4,10},{6,12},{8,14},{10,0},{12,2},{14,4},{1,7},{3,9},... | collective-permute-start | bytes 152 | tf_op jit(solution)/shard_map/ppermute | solution.py:14
  57.6 3.6 %collective-permute-start.14 = (f32[1,12,128]{2,0,1:T(1,128)S(1)}, f32[1,12,128]{2,0,1:T(1,128)S(1)}, u32[]{:S(2)}, u32[]{:S(2)}) collective-permute-start(f32[1,12,128]{2,0,1:T(1,128)S(1)} %get-tuple-element.22), channel_id=1, source_target_pairs={{0,14},{2,0},{4,2},{6,4},{8,6},{10,8},{12,10},{14,12},{1,15},{3,1}... | collective-permute-start | bytes 18440 | tf_op jit(solution)/shard_map/ppermute | solution.py:14
  62.7 2.2 collective-permute-start.17
  65.0 3.3 %collective-permute-start.18 = (f32[1,12,128]{2,0,1:T(1,128)S(1)}, f32[1,12,128]{2,0,1:T(1,128)S(1)}, u32[]{:S(2)}, u32[]{:S(2)}) collective-permute-start(f32[1,12,128]{2,0,1:T(1,128)S(1)} %get-tuple-element.18), channel_id=1, source_target_pairs={{0,6},{2,8},{4,10},{6,12},{8,14},{10,0},{12,2},{14,4},{1,7},{3,9},... | collective-permute-start | bytes 18440 | tf_op jit(solution)/shard_map/ppermute | solution.py:14
  68.3 15.4 %collective-permute-done.17 = f32[1,12,128]{2,0,1:T(1,128)S(1)} collective-permute-done((f32[1,12,128]{2,0,1:T(1,128)S(1)}, f32[1,12,128]{2,0,1:T(1,128)S(1)}, u32[]{:S(2)}, u32[]{:S(2)}) %collective-permute-start.17) | collective-permute-done | bytes 6176 | tf_op jit(solution)/shard_map/ppermute | solution.py:14
  83.7 3.3 %collective-permute-done.18 = f32[1,12,128]{2,0,1:T(1,128)S(1)} collective-permute-done((f32[1,12,128]{2,0,1:T(1,128)S(1)}, f32[1,12,128]{2,0,1:T(1,128)S(1)}, u32[]{:S(2)}, u32[]{:S(2)}) %collective-permute-start.18) | collective-permute-done | bytes 6176 | tf_op jit(solution)/shard_map/ppermute | solution.py:14
  87.0 3.1 %collective-permute-done.20 = f32[1,12,128]{2,0,1:T(1,128)S(1)} collective-permute-done((f32[1,12,128]{2,0,1:T(1,128)S(1)}, f32[1,12,128]{2,0,1:T(1,128)S(1)}, u32[]{:S(2)}, u32[]{:S(2)}) %collective-permute-start.20) | collective-permute-done | bytes 6176 | tf_op jit(solution)/shard_map/ppermute | solution.py:14
  90.1 3.2 %collective-permute-start.6 = (bf16[2,64,1536]{2,1,0:T(8,128)(2,1)}, bf16[2,64,1536]{2,1,0:T(8,128)(2,1)S(1)}, u32[]{:S(2)}, u32[]{:S(2)}) collective-permute-start(bf16[2,64,1536]{2,1,0:T(8,128)(2,1)} %bitcast.121), channel_id=1, source_target_pairs={{0,2},{2,4},{4,6},{6,8},{8,10},{10,12},{12,14},{14,0},{1,3},{3,5},... | collective-permute-start | bytes 1179656 | tf_op jit(solution)/shard_map/ppermute | solution.py:14
  93.7 3.6 %collective-permute-done.2 = bf16[2,64,1536]{2,1,0:T(8,128)(2,1)S(1)} collective-permute-done((bf16[2,64,1536]{2,1,0:T(8,128)(2,1)}, bf16[2,64,1536]{2,1,0:T(8,128)(2,1)S(1)}, u32[]{:S(2)}, u32[]{:S(2)}) %collective-permute-start.2) | collective-permute-done | bytes 393248 | tf_op jit(solution)/shard_map/ppermute | solution.py:14
  97.3 20.1 %collective-permute-done.3 = bf16[2,64,1536]{2,1,0:T(8,128)(2,1)S(1)} collective-permute-done((bf16[2,64,1536]{2,1,0:T(8,128)(2,1)}, bf16[2,64,1536]{2,1,0:T(8,128)(2,1)S(1)}, u32[]{:S(2)}, u32[]{:S(2)}) %collective-permute-start.3) | collective-permute-done | bytes 393248 | tf_op jit(solution)/shard_map/ppermute | solution.py:14
  117.3 7.5 %collective-permute-done.4 = bf16[2,64,1536]{2,1,0:T(8,128)(2,1)S(1)} collective-permute-done((bf16[2,64,1536]{2,1,0:T(8,128)(2,1)}, bf16[2,64,1536]{2,1,0:T(8,128)(2,1)S(1)}, u32[]{:S(2)}, u32[]{:S(2)}) %collective-permute-start.4) | collective-permute-done | bytes 393248 | tf_op jit(solution)/shard_map/ppermute | solution.py:14
  128.0 30.5 %all-gather = bf16[8,1,3072]{2,1,0:T(2,128)(2,1)S(1)} all-gather(bf16[1,1,3072]{2,1,0:T(2,128)(2,1)S(1)} %reshape.802), channel_id=1, replica_groups=mesh['grp'=2,'batch'=8,'tensor'=2] {'batch'}, dimensions={0}, use_global_device_ids=true | all-gather | bytes 55296 | tf_op jit(solution)/shard_map/all_gather | solution.py:112
  158.6 3.1 %fusion.10 = f32[8,768]{1,0:T(8,128)S(1)} fusion(bf16[3072,768]{1,0:T(8,128)(2,1)} %bitcast.113, bf16[8,1,3072]{2,1,0:T(2,128)(2,1)S(1)} %all-gather), kind=kOutput, calls=%fused_computation.14 | convolution fusion | flops 37748736 | bytes 4792320 | tf_op jit(solution)/shard_map/dot_general | solution.py:111
  161.6 3.4 %psum.7 = f32[8,768]{1,0:T(8,128)S(1)} all-reduce(f32[8,768]{1,0:T(8,128)S(1)} %fusion.10), channel_id=1, replica_groups=mesh['grp'=2,'batch'=8,'tensor'=2] {'tensor'}, use_global_device_ids=true, to_apply=%region_7.8 | all-reduce | flops 6144 | bytes 49152 | tf_op jit(solution)/shard_map/psum | solution.py:116
  165.8 30.5 %all_gather.10 = bf16[8,6144]{1,0:T(8,128)(2,1)S(1)} all-gather(bf16[8,768]{1,0:T(8,128)(2,1)S(1)} %fusion.21), channel_id=1, replica_groups=mesh['grp'=2,'batch'=8,'tensor'=2] {'batch'}, dimensions={1}, use_global_device_ids=true | all-gather | bytes 110592 | tf_op jit(solution)/shard_map/all_gather | solution.py:119
  196.3 9.0 %fusion.9 = bf16[8,1536]{1,0:T(8,128)(2,1)S(1)} fusion(bf16[8,6144]{1,0:T(8,128)(2,1)S(1)} %all_gather.10, bf16[6144,1536]{1,0:T(8,128)(2,1)} %param.16), kind=kOutput, calls=%fused_computation.13 | convolution fusion | flops 151793664 | bytes 18997248 | tf_op jit(solution)/shard_map/dot_general | solution.py:118
  205.3 1.8 all_gather.11
  207.1 7.7 %fusion.42 = f32[8,3072]{1,0:T(8,128)S(1)} fusion(bf16[8,3072]{1,0:T(8,128)(2,1)S(1)} %all_gather.11, bf16[3072,3072]{1,0:T(8,128)(2,1)} %param.17), kind=kOutput, calls=%fused_computation.90 | convolution fusion | flops 150994944 | bytes 19021824 | tf_op jit(solution)/shard_map/dot_general | solution.py:126
  214.8 33.8 %all-reduce = bf16[8,3072]{1,0:T(8,128)(2,1)S(1)} all-reduce(f32[8,3072]{1,0:T(8,128)S(1)} %fusion.42), channel_id=2, replica_groups=mesh['grp'=2,'batch'=8,'tensor'=2] {'batch'}, use_global_device_ids=true, to_apply=%region_8.9.clone | all-reduce | flops 24576 | bytes 147456
  (115 shorter events, 23.2 us)
Async XLA Ops:
  1.4 14.0 %collective-permute-start.7 = (bf16[1536]{0:T(1024)(128)(2,1)S(1)}, bf16[1536]{0:T(1024)(128)(2,1)S(1)}, u32[]{:S(2)}, u32[]{:S(2)}) collective-permute-start(bf16[1536]{0:T(1024)(128)(2,1)S(1)} %get-tuple-element.42), channel_id=1, source_target_pairs={{0,2},{2,4},{4,6},{6,8},{8,10},{10,12},{12,14},{14,0},{1,3},{3,5},... | collective-permute-start | bytes 9224 | tf_op jit(solution)/shard_map/ppermute | solution.py:14
  4.3 12.4 %collective-permute-start.8 = (bf16[1536]{0:T(1024)(128)(2,1)S(1)}, bf16[1536]{0:T(1024)(128)(2,1)S(1)}, u32[]{:S(2)}, u32[]{:S(2)}) collective-permute-start(bf16[1536]{0:T(1024)(128)(2,1)S(1)} %get-tuple-element.42), channel_id=1, source_target_pairs={{0,4},{2,6},{4,8},{6,10},{8,12},{10,14},{12,0},{14,2},{1,5},{3,7},... | collective-permute-start | bytes 9224 | tf_op jit(solution)/shard_map/ppermute | solution.py:14
  5.9 14.6 %collective-permute-start.9 = (bf16[1536]{0:T(1024)(128)(2,1)S(1)}, bf16[1536]{0:T(1024)(128)(2,1)S(1)}, u32[]{:S(2)}, u32[]{:S(2)}) collective-permute-start(bf16[1536]{0:T(1024)(128)(2,1)S(1)} %get-tuple-element.42), channel_id=1, source_target_pairs={{0,6},{2,8},{4,10},{6,12},{8,14},{10,0},{12,2},{14,4},{1,7},{3,9},... | collective-permute-start | bytes 9224 | tf_op jit(solution)/shard_map/ppermute | solution.py:14
  8.5 12.6 %collective-permute-start.10 = (bf16[1536]{0:T(1024)(128)(2,1)S(1)}, bf16[1536]{0:T(1024)(128)(2,1)S(1)}, u32[]{:S(2)}, u32[]{:S(2)}) collective-permute-start(bf16[1536]{0:T(1024)(128)(2,1)S(1)} %get-tuple-element.42), channel_id=1, source_target_pairs={{0,8},{2,10},{4,12},{6,14},{8,0},{10,2},{12,4},{14,6},{1,9},{3,11}... | collective-permute-start | bytes 9224 | tf_op jit(solution)/shard_map/ppermute | solution.py:14
  9.7 12.7 %collective-permute-start.11 = (bf16[1536]{0:T(1024)(128)(2,1)S(1)}, bf16[1536]{0:T(1024)(128)(2,1)S(1)}, u32[]{:S(2)}, u32[]{:S(2)}) collective-permute-start(bf16[1536]{0:T(1024)(128)(2,1)S(1)} %get-tuple-element.42), channel_id=1, source_target_pairs={{0,10},{2,12},{4,14},{6,0},{8,2},{10,4},{12,6},{14,8},{1,11},{3,13... | collective-permute-start | bytes 9224 | tf_op jit(solution)/shard_map/ppermute | solution.py:14
  15.3 7.1 %collective-permute-start.12 = (bf16[1536]{0:T(1024)(128)(2,1)S(1)}, bf16[1536]{0:T(1024)(128)(2,1)S(1)}, u32[]{:S(2)}, u32[]{:S(2)}) collective-permute-start(bf16[1536]{0:T(1024)(128)(2,1)S(1)} %get-tuple-element.42), channel_id=1, source_target_pairs={{0,12},{2,14},{4,0},{6,2},{8,4},{10,6},{12,8},{14,10},{1,13},{3,15... | collective-permute-start | bytes 9224 | tf_op jit(solution)/shard_map/ppermute | solution.py:14
  16.7 5.8 %collective-permute-start.13 = (bf16[1536]{0:T(1024)(128)(2,1)S(1)}, bf16[1536]{0:T(1024)(128)(2,1)S(1)}, u32[]{:S(2)}, u32[]{:S(2)}) collective-permute-start(bf16[1536]{0:T(1024)(128)(2,1)S(1)} %get-tuple-element.42), channel_id=1, source_target_pairs={{0,14},{2,0},{4,2},{6,4},{8,6},{10,8},{12,10},{14,12},{1,15},{3,1}... | collective-permute-start | bytes 9224 | tf_op jit(solution)/shard_map/ppermute | solution.py:14
  20.5 69.6 %collective-permute-start = (bf16[2,64,1536]{2,1,0:T(8,128)(2,1)}, bf16[2,64,1536]{2,1,0:T(8,128)(2,1)S(1)}, u32[]{:S(2)}, u32[]{:S(2)}) collective-permute-start(bf16[2,64,1536]{2,1,0:T(8,128)(2,1)} %bitcast.115), channel_id=1, source_target_pairs={{0,14},{2,0},{4,2},{6,4},{8,6},{10,8},{12,10},{14,12},{1,15},{3,1}... | collective-permute-start | bytes 1179656 | tf_op jit(solution)/shard_map/ppermute | solution.py:14
  21.0 69.1 %collective-permute-start.1 = (bf16[2,64,1536]{2,1,0:T(8,128)(2,1)}, bf16[2,64,1536]{2,1,0:T(8,128)(2,1)S(1)}, u32[]{:S(2)}, u32[]{:S(2)}) collective-permute-start(bf16[2,64,1536]{2,1,0:T(8,128)(2,1)} %bitcast.116), channel_id=1, source_target_pairs={{0,12},{2,14},{4,0},{6,2},{8,4},{10,6},{12,8},{14,10},{1,13},{3,15... | collective-permute-start | bytes 1179656 | tf_op jit(solution)/shard_map/ppermute | solution.py:14
  23.0 13.6 %collective-permute-start.21 = (f32[1,12]{0,1:T(8,128)S(1)}, f32[1,12]{0,1:T(8,128)S(1)}, u32[]{:S(2)}, u32[]{:S(2)}) collective-permute-start(f32[1,12]{0,1:T(8,128)S(1)} %get-tuple-element.39), channel_id=1, source_target_pairs={{0,14},{2,0},{4,2},{6,4},{8,6},{10,8},{12,10},{14,12},{1,15},{3,1}... | collective-permute-start | bytes 152 | tf_op jit(solution)/shard_map/ppermute | solution.py:14
  24.9 13.7 %collective-permute-start.22 = (f32[1,12]{0,1:T(8,128)S(1)}, f32[1,12]{0,1:T(8,128)S(1)}, u32[]{:S(2)}, u32[]{:S(2)}) collective-permute-start(f32[1,12]{0,1:T(8,128)S(1)} %get-tuple-element.38), channel_id=1, source_target_pairs={{0,12},{2,14},{4,0},{6,2},{8,4},{10,6},{12,8},{14,10},{1,13},{3,15... | collective-permute-start | bytes 152 | tf_op jit(solution)/shard_map/ppermute | solution.py:14
  26.2 16.2 %collective-permute-start.23 = (f32[1,12]{0,1:T(8,128)S(1)}, f32[1,12]{0,1:T(8,128)S(1)}, u32[]{:S(2)}, u32[]{:S(2)}) collective-permute-start(f32[1,12]{0,1:T(8,128)S(1)} %get-tuple-element.37), channel_id=1, source_target_pairs={{0,10},{2,12},{4,14},{6,0},{8,2},{10,4},{12,6},{14,8},{1,11},{3,13... | collective-permute-start | bytes 152 | tf_op jit(solution)/shard_map/ppermute | solution.py:14
  36.6 6.3 %collective-permute-start.24 = (f32[1,12]{0,1:T(8,128)S(1)}, f32[1,12]{0,1:T(8,128)S(1)}, u32[]{:S(2)}, u32[]{:S(2)}) collective-permute-start(f32[1,12]{0,1:T(8,128)S(1)} %get-tuple-element.36), channel_id=1, source_target_pairs={{0,8},{2,10},{4,12},{6,14},{8,0},{10,2},{12,4},{14,6},{1,9},{3,11}... | collective-permute-start | bytes 152 | tf_op jit(solution)/shard_map/ppermute | solution.py:14
  38.6 5.9 %collective-permute-start.25 = (f32[1,12]{0,1:T(8,128)S(1)}, f32[1,12]{0,1:T(8,128)S(1)}, u32[]{:S(2)}, u32[]{:S(2)}) collective-permute-start(f32[1,12]{0,1:T(8,128)S(1)} %get-tuple-element.35), channel_id=1, source_target_pairs={{0,6},{2,8},{4,10},{6,12},{8,14},{10,0},{12,2},{14,4},{1,7},{3,9},... | collective-permute-start | bytes 152 | tf_op jit(solution)/shard_map/ppermute | solution.py:14
  42.4 5.4 %collective-permute-start.26 = (f32[1,12]{0,1:T(8,128)S(1)}, f32[1,12]{0,1:T(8,128)S(1)}, u32[]{:S(2)}, u32[]{:S(2)}) collective-permute-start(f32[1,12]{0,1:T(8,128)S(1)} %get-tuple-element.34), channel_id=1, source_target_pairs={{0,4},{2,6},{4,8},{6,10},{8,12},{10,14},{12,0},{14,2},{1,5},{3,7},... | collective-permute-start | bytes 152 | tf_op jit(solution)/shard_map/ppermute | solution.py:14
  43.0 6.3 %collective-permute-start.27 = (f32[1,12]{0,1:T(8,128)S(1)}, f32[1,12]{0,1:T(8,128)S(1)}, u32[]{:S(2)}, u32[]{:S(2)}) collective-permute-start(f32[1,12]{0,1:T(8,128)S(1)} %get-tuple-element.33), channel_id=1, source_target_pairs={{0,2},{2,4},{4,6},{6,8},{8,10},{10,12},{12,14},{14,0},{1,3},{3,5},... | collective-permute-start | bytes 152 | tf_op jit(solution)/shard_map/ppermute | solution.py:14
  44.6 5.1 %collective-permute-start.28 = (f32[1,12]{0,1:T(8,128)S(1)}, f32[1,12]{0,1:T(8,128)S(1)}, u32[]{:S(2)}, u32[]{:S(2)}) collective-permute-start(f32[1,12]{0,1:T(8,128)S(1)} %get-tuple-element.30), channel_id=1, source_target_pairs={{0,14},{2,0},{4,2},{6,4},{8,6},{10,8},{12,10},{14,12},{1,15},{3,1}... | collective-permute-start | bytes 152 | tf_op jit(solution)/shard_map/ppermute | solution.py:14
  49.3 5.7 %collective-permute-start.30 = (f32[1,12]{0,1:T(8,128)S(1)}, f32[1,12]{0,1:T(8,128)S(1)}, u32[]{:S(2)}, u32[]{:S(2)}) collective-permute-start(f32[1,12]{0,1:T(8,128)S(1)} %get-tuple-element.28), channel_id=1, source_target_pairs={{0,10},{2,12},{4,14},{6,0},{8,2},{10,4},{12,6},{14,8},{1,11},{3,13... | collective-permute-start | bytes 152 | tf_op jit(solution)/shard_map/ppermute | solution.py:14
  49.7 6.4 %collective-permute-start.31 = (f32[1,12]{0,1:T(8,128)S(1)}, f32[1,12]{0,1:T(8,128)S(1)}, u32[]{:S(2)}, u32[]{:S(2)}) collective-permute-start(f32[1,12]{0,1:T(8,128)S(1)} %get-tuple-element.27), channel_id=1, source_target_pairs={{0,8},{2,10},{4,12},{6,14},{8,0},{10,2},{12,4},{14,6},{1,9},{3,11}... | collective-permute-start | bytes 152 | tf_op jit(solution)/shard_map/ppermute | solution.py:14
  51.9 5.7 %collective-permute-start.32 = (f32[1,12]{0,1:T(8,128)S(1)}, f32[1,12]{0,1:T(8,128)S(1)}, u32[]{:S(2)}, u32[]{:S(2)}) collective-permute-start(f32[1,12]{0,1:T(8,128)S(1)} %get-tuple-element.26), channel_id=1, source_target_pairs={{0,6},{2,8},{4,10},{6,12},{8,14},{10,0},{12,2},{14,4},{1,7},{3,9},... | collective-permute-start | bytes 152 | tf_op jit(solution)/shard_map/ppermute | solution.py:14
  55.0 6.4 %collective-permute-start.33 = (f32[1,12]{0,1:T(8,128)S(1)}, f32[1,12]{0,1:T(8,128)S(1)}, u32[]{:S(2)}, u32[]{:S(2)}) collective-permute-start(f32[1,12]{0,1:T(8,128)S(1)} %get-tuple-element.25), channel_id=1, source_target_pairs={{0,4},{2,6},{4,8},{6,10},{8,12},{10,14},{12,0},{14,2},{1,5},{3,7},... | collective-permute-start | bytes 152 | tf_op jit(solution)/shard_map/ppermute | solution.py:14
  56.1 6.5 %collective-permute-start.34 = (f32[1,12]{0,1:T(8,128)S(1)}, f32[1,12]{0,1:T(8,128)S(1)}, u32[]{:S(2)}, u32[]{:S(2)}) collective-permute-start(f32[1,12]{0,1:T(8,128)S(1)} %get-tuple-element.24), channel_id=1, source_target_pairs={{0,2},{2,4},{4,6},{6,8},{8,10},{10,12},{12,14},{14,0},{1,3},{3,5},... | collective-permute-start | bytes 152 | tf_op jit(solution)/shard_map/ppermute | solution.py:14
  62.6 5.7 %collective-permute-start.16 = (f32[1,12,128]{2,0,1:T(1,128)S(1)}, f32[1,12,128]{2,0,1:T(1,128)S(1)}, u32[]{:S(2)}, u32[]{:S(2)}) collective-permute-start(f32[1,12,128]{2,0,1:T(1,128)S(1)} %get-tuple-element.20), channel_id=1, source_target_pairs={{0,10},{2,12},{4,14},{6,0},{8,2},{10,4},{12,6},{14,8},{1,11},{3,13... | collective-permute-start | bytes 18440 | tf_op jit(solution)/shard_map/ppermute | solution.py:14
  62.7 21.0 %collective-permute-start.17 = (f32[1,12,128]{2,0,1:T(1,128)S(1)}, f32[1,12,128]{2,0,1:T(1,128)S(1)}, u32[]{:S(2)}, u32[]{:S(2)}) collective-permute-start(f32[1,12,128]{2,0,1:T(1,128)S(1)} %get-tuple-element.19), channel_id=1, source_target_pairs={{0,8},{2,10},{4,12},{6,14},{8,0},{10,2},{12,4},{14,6},{1,9},{3,11}... | collective-permute-start | bytes 18440 | tf_op jit(solution)/shard_map/ppermute | solution.py:14
  65.0 22.0 %collective-permute-start.18 = (f32[1,12,128]{2,0,1:T(1,128)S(1)}, f32[1,12,128]{2,0,1:T(1,128)S(1)}, u32[]{:S(2)}, u32[]{:S(2)}) collective-permute-start(f32[1,12,128]{2,0,1:T(1,128)S(1)} %get-tuple-element.18), channel_id=1, source_target_pairs={{0,6},{2,8},{4,10},{6,12},{8,14},{10,0},{12,2},{14,4},{1,7},{3,9},... | collective-permute-start | bytes 18440 | tf_op jit(solution)/shard_map/ppermute | solution.py:14
  68.3 18.7 %collective-permute-start.19 = (f32[1,12,128]{2,0,1:T(1,128)S(1)}, f32[1,12,128]{2,0,1:T(1,128)S(1)}, u32[]{:S(2)}, u32[]{:S(2)}) collective-permute-start(f32[1,12,128]{2,0,1:T(1,128)S(1)} %get-tuple-element.17), channel_id=1, source_target_pairs={{0,4},{2,6},{4,8},{6,10},{8,12},{10,14},{12,0},{14,2},{1,5},{3,7},... | collective-permute-start | bytes 18440 | tf_op jit(solution)/shard_map/ppermute | solution.py:14
  83.7 6.4 %collective-permute-start.20 = (f32[1,12,128]{2,0,1:T(1,128)S(1)}, f32[1,12,128]{2,0,1:T(1,128)S(1)}, u32[]{:S(2)}, u32[]{:S(2)}) collective-permute-start(f32[1,12,128]{2,0,1:T(1,128)S(1)} %get-tuple-element.16), channel_id=1, source_target_pairs={{0,2},{2,4},{4,6},{6,8},{8,10},{10,12},{12,14},{14,0},{1,3},{3,5},... | collective-permute-start | bytes 18440 | tf_op jit(solution)/shard_map/ppermute | solution.py:14
  87.0 10.3 %collective-permute-start.2 = (bf16[2,64,1536]{2,1,0:T(8,128)(2,1)}, bf16[2,64,1536]{2,1,0:T(8,128)(2,1)S(1)}, u32[]{:S(2)}, u32[]{:S(2)}) collective-permute-start(bf16[2,64,1536]{2,1,0:T(8,128)(2,1)} %bitcast.117), channel_id=1, source_target_pairs={{0,10},{2,12},{4,14},{6,0},{8,2},{10,4},{12,6},{14,8},{1,11},{3,13... | collective-permute-start | bytes 1179656 | tf_op jit(solution)/shard_map/ppermute | solution.py:14
  87.0 30.4 %collective-permute-start.3 = (bf16[2,64,1536]{2,1,0:T(8,128)(2,1)}, bf16[2,64,1536]{2,1,0:T(8,128)(2,1)S(1)}, u32[]{:S(2)}, u32[]{:S(2)}) collective-permute-start(bf16[2,64,1536]{2,1,0:T(8,128)(2,1)} %bitcast.118), channel_id=1, source_target_pairs={{0,8},{2,10},{4,12},{6,14},{8,0},{10,2},{12,4},{14,6},{1,9},{3,11}... | collective-permute-start | bytes 1179656 | tf_op jit(solution)/shard_map/ppermute | solution.py:14
  90.1 34.8 %collective-permute-start.4 = (bf16[2,64,1536]{2,1,0:T(8,128)(2,1)}, bf16[2,64,1536]{2,1,0:T(8,128)(2,1)S(1)}, u32[]{:S(2)}, u32[]{:S(2)}) collective-permute-start(bf16[2,64,1536]{2,1,0:T(8,128)(2,1)} %bitcast.119), channel_id=1, source_target_pairs={{0,6},{2,8},{4,10},{6,12},{8,14},{10,0},{12,2},{14,4},{1,7},{3,9},... | collective-permute-start | bytes 1179656 | tf_op jit(solution)/shard_map/ppermute | solution.py:14
  90.1 34.8 %collective-permute-start.5 = (bf16[2,64,1536]{2,1,0:T(8,128)(2,1)}, bf16[2,64,1536]{2,1,0:T(8,128)(2,1)S(1)}, u32[]{:S(2)}, u32[]{:S(2)}) collective-permute-start(bf16[2,64,1536]{2,1,0:T(8,128)(2,1)} %bitcast.120), channel_id=1, source_target_pairs={{0,4},{2,6},{4,8},{6,10},{8,12},{10,14},{12,0},{14,2},{1,5},{3,7},... | collective-permute-start | bytes 1179656 | tf_op jit(solution)/shard_map/ppermute | solution.py:14
  90.1 34.7 %collective-permute-start.6 = (bf16[2,64,1536]{2,1,0:T(8,128)(2,1)}, bf16[2,64,1536]{2,1,0:T(8,128)(2,1)S(1)}, u32[]{:S(2)}, u32[]{:S(2)}) collective-permute-start(bf16[2,64,1536]{2,1,0:T(8,128)(2,1)} %bitcast.121), channel_id=1, source_target_pairs={{0,2},{2,4},{4,6},{6,8},{8,10},{10,12},{12,14},{14,0},{1,3},{3,5},... | collective-permute-start | bytes 1179656 | tf_op jit(solution)/shard_map/ppermute | solution.py:14
  (5 other events, 150.6 us)
where the time goes:
time: 250 us
  blocking collectives  100 us (40%)
  waiting for transfers between devices  62.8 us (25%)
  starting transfers between devices  52.3 us (21%)
  matrix products  21.5 us (9%)
  local copies, waits for them, and re-layouts  5.75 us (2%)
  other arithmetic  5.14 us (2%)
    ppermute x35, waiting for transfers between devices, from_behind(): lax.ppermute(value, axis, [(i, (i + by) % devices) for i in range(devices)])  62.8 us
    ppermute x35, starting transfers between devices, from_behind(): lax.ppermute(value, axis, [(i, (i + by) % devices) for i in range(devices)])  52.3 us
    unnamed x1, blocking collectives  33.8 us
    all_gather x1, blocking collectives, body(): lax.all_gather(attended, 'batch', axis=0, tiled=True)  30.5 us
    all_gather x1, blocking collectives, body(): lax.all_gather(hidden, 'batch', axis=1, tiled=True)  30.5 us
    dot_general x1, matrix products, body(): jnp.dot(lax.all_gather(hidden, 'batch', axis=1, tiled=True), up_weight, p...  8.99 us
    dot_general x1, matrix products, body(): jnp.dot(joined, down_weight, preferred_element_type=jnp.float32)  7.68 us
  transfers between devices with their start and end apart: 35, of which 10 were waited for; matrix products, arithmetic and copies ran while one was open for 3% of the time, Pallas kernels for 0%

commit v1 on v0

v1 whole, which is shorter than its diff:
```python
import math

import jax
import jax.numpy as jnp
from jax import lax
from jax.sharding import PartitionSpec as P

HD = 128
BEAMS = 8
LOW = -1e30


def body(
    init_cache,
    memory,
    queries,
    new_kv,
    residual,
    out_weight,
    up_weight,
    down_weight,
    parents,
    lengths,
):
    devices = lax.axis_size("batch")
    stride = devices // BEAMS
    position = lax.axis_index("batch")
    own_beam = position // stride
    request = position % stride
    width = queries.shape[-1]
    heads = width // HD
    cache_len = init_cache.shape[2]
    rows = parents.shape[1]
    groups = None
    if stride > 1:
        groups = [[b * stride + r for b in range(BEAMS)] for r in range(stride)]

    def swap(value):
        return lax.all_to_all(value, "batch", 0, 0, axis_index_groups=groups, tiled=True)

    def swap_all(value):
        return lax.all_to_all(value, "batch", 0, 0, tiled=True)

    def gather_all(value):
        return swap_all(jnp.broadcast_to(value[None], (devices,) + value.shape))

    request_ids = jnp.arange(stride, dtype=jnp.int32)
    length = jnp.sum(jnp.where(request_ids == request, lengths, 0))
    grouped = parents.reshape(BEAMS, stride)
    parent = jnp.sum(jnp.where(request_ids[None, :] == request, grouped, 0), axis=1)
    slots = jnp.arange(cache_len, dtype=jnp.int32)
    scale = 1.0 / math.sqrt(HD)

    own_query = queries[0, 0]
    query = swap(jnp.broadcast_to(own_query[None], (BEAMS, 2, width)))
    query = query.reshape(BEAMS, 2, heads, HD)

    def partial(q, kv, valid):
        keys = kv[0].reshape(-1, heads, HD)
        values = kv[1].reshape(-1, heads, HD)
        scores = jnp.einsum("nhd,chd->nhc", q, keys, preferred_element_type=jnp.float32) * scale
        if valid is not None:
            scores = jnp.where(valid[:, None, :], scores, LOW)
        peak = jnp.max(scores, axis=-1)
        weights = jnp.exp(scores - peak[..., None])
        if valid is not None:
            weights = jnp.where(valid[:, None, :], weights, 0.0)
        total = jnp.sum(weights, axis=-1)
        high = weights.astype(jnp.bfloat16)
        low = (weights - high.astype(jnp.float32)).astype(jnp.bfloat16)
        both = jnp.einsum(
            "nhc,chd->nhd", jnp.concatenate([high, low]), values, preferred_element_type=jnp.float32
        )
        return both[:BEAMS] + both[BEAMS:], peak, total

    valid = (slots < length)[None, :] & (parent == own_beam)[:, None]
    ws, ps, ts = partial(query[:, 0], init_cache[0], valid)
    wc, pc, tc = partial(query[:, 1], memory[0], None)
    packed = jnp.concatenate(
        [
            ws.reshape(BEAMS, width),
            wc.reshape(BEAMS, width),
            ps,
            pc,
            ts,
            tc,
        ],
        axis=1,
    )
    got = swap(packed)
    both = 2 * heads
    weighted = got[:, : 2 * width].reshape(BEAMS, both, HD)
    peaks = got[:, 2 * width : 2 * width + both]
    totals = got[:, 2 * width + both :]

    new_score = jnp.sum(
        own_query[0].astype(jnp.float32).reshape(heads, HD)
        * new_kv[0, 0, 0].astype(jnp.float32).reshape(heads, HD),
        axis=1,
    ) * scale
    new_peak = jnp.concatenate([new_score, jnp.full((heads,), LOW, jnp.float32)])
    new_total = jnp.concatenate([jnp.ones((heads,), jnp.float32), jnp.zeros((heads,), jnp.float32)])
    new_value = jnp.concatenate(
        [new_kv[0, 0, 1].astype(jnp.float32), jnp.zeros((width,), jnp.float32)]
    ).reshape(both, HD)
    top = jnp.maximum(jnp.max(peaks, axis=0), new_peak)
    factors = jnp.exp(peaks - top[None])
    new_factor = jnp.exp(new_peak - top) * new_total
    denom = jnp.sum(totals * factors, axis=0) + new_factor
    numer = jnp.sum(weighted * factors[..., None], axis=0) + new_value * new_factor[:, None]
    attended = (numer / denom[:, None]).astype(jnp.bfloat16).reshape(2 * width)

    projected = lax.psum(
        jnp.dot(
            gather_all(attended),
            out_weight.reshape(2 * width, -1),
            preferred_element_type=jnp.float32,
        ),
        "tensor",
    )
    hidden = (residual[0].astype(jnp.float32) + projected).astype(jnp.bfloat16)
    wide = jnp.swapaxes(gather_all(hidden), 0, 1).reshape(rows, -1)
    pre_act = jnp.dot(wide, up_weight, preferred_element_type=jnp.float32)
    activation = jax.nn.gelu(pre_act, approximate=False).astype(jnp.bfloat16)
    joined = lax.all_gather(activation, "tensor", axis=1, tiled=True)
    part = jnp.dot(joined, down_weight, preferred_element_type=jnp.float32)
    ffn_row = jnp.sum(swap_all(part), axis=0, keepdims=True).astype(jnp.bfloat16)

    pieces = init_cache.reshape(BEAMS, 2 * cache_len // BEAMS, width)
    mine = swap(pieces)
    chosen = jnp.stack([lax.dynamic_index_in_dim(mine, parent[b], 0, False) for b in range(BEAMS)])
    cache = swap(chosen).reshape(2, cache_len, width)
    cache = jnp.where((slots == length)[None, :, None], new_kv[0, 0][:, None, :], cache)
    return (hidden[None], ffn_row[None], cache[None])


def solution(mesh):
    placed = (
        P(("grp", "batch"), None, None, "tensor"),
        P(("grp", "batch"), None, None, "tensor"),
        P(None, ("grp", "batch"), None, "tensor"),
        P(None, ("grp", "batch"), None, "tensor"),
        P(None, "grp", "batch"),
        P(None, "tensor", "batch"),
        P(None, ("batch", "tensor")),
        P("batch", "tensor"),
        P(None, "grp"),
        P("grp"),
    )
    return jax.shard_map(
        body,
        mesh=mesh,
        in_specs=placed,
        out_specs=(
            P(None, "grp", "batch"),
            P(None, ("grp", "batch"), "tensor"),
            P(("grp", "batch"), None, None, "tensor"),
        ),
        check_vma=False,
    )
```

time: 250 us -> 126 us (0.50)
  blocking collectives: 100 us -> 14.4 us
  waiting for transfers between devices: 62.8 us -> 21.2 us
  starting transfers between devices: 52.3 us -> 31.3 us
  between operations: 2.27 us -> 16.4 us
  local copies, waits for them, and re-layouts: 5.75 us -> 15.2 us
    ppermute x35 -> x0, waiting for transfers between devices: 62.8 us -> none  [from_behind(): lax.ppermute(value, axis, [(i, (i + by) % devices) for i in range(devices)])]
    all_gather x2 -> x0, blocking collectives: 61.1 us -> none  [the longest x1 30.5 us: body(): lax.all_gather(attended, 'batch', axis=0, tiled=True)]
    ppermute x35 -> x0, starting transfers between devices: 52.3 us -> none  [from_behind(): lax.ppermute(value, axis, [(i, (i + by) % devices) for i in range(devices)])]
    unnamed x1 -> x0, blocking collectives: 33.8 us -> none
    all_to_all x0 -> x6, starting transfers between devices: none -> 31.3 us  [the longest x4 22 us: swap(): lax.all_to_all(value, 'batch', 0, 0, axis_index_groups=groups, tiled=True)]
    all_to_all x0 -> x6, waiting for transfers between devices: none -> 21.2 us  [the longest x4 19 us: swap(): lax.all_to_all(value, 'batch', 0, 0, axis_index_groups=groups, tiled=True)]
    all_to_all x0 -> x1, blocking collectives: none -> 9.17 us  [swap_all(): return lax.all_to_all(value, 'batch', 0, 0, tiled=True)]
    unnamed x20 -> x14, local copies, waits for them, and re-layouts: 1.47 us -> 4.45 us
  transfers between devices with their start and end apart: 35 -> 6, of which waited for: 10 -> 4; matrix products, arithmetic and copies ran while one was open for 3% -> 24% of each run, Pallas kernels for 0% -> 0%
where the time goes in v1:
time: 126 us; the launch traced here: 125 us
  starting transfers between devices  31.3 us (25%)
  waiting for transfers between devices  21.2 us (17%)
  matrix products  20.6 us (16%)
  between operations  16.4 us (13%)
  local copies, waits for them, and re-layouts  15.2 us (12%)
  blocking collectives  14.4 us (11%)
  other arithmetic  5.5 us (4%)
    all_to_all x4, starting transfers between devices, swap(): lax.all_to_all(value, 'batch', 0, 0, axis_index_groups=groups, tiled=True)  22 us
    all_to_all x4, waiting for transfers between devices, swap(): lax.all_to_all(value, 'batch', 0, 0, axis_index_groups=groups, tiled=True)  19 us
    all_to_all x2, starting transfers between devices, swap_all(): return lax.all_to_all(value, 'batch', 0, 0, tiled=True)  9.36 us
    all_to_all x1, blocking collectives, swap_all(): return lax.all_to_all(value, 'batch', 0, 0, tiled=True)  9.17 us
    dot_general x1, matrix products, body(): pre_act = jnp.dot(wide, up_weight, preferred_element_type=jnp.float32)  8.99 us
    dot_general x1, matrix products, body(): part = jnp.dot(joined, down_weight, preferred_element_type=jnp.float32)  7.68 us
    unnamed x14, local copies, waits for them, and re-layouts  4.45 us
    psum x1, blocking collectives, body(): lax.psum(jnp.dot(gather_all(attended), out_weight.reshape(2 * width, -1),...  3.41 us
  transfers between devices with their start and end apart: 6, of which 4 were waited for; matrix products, arithmetic and copies ran while one was open for 24% of the time, Pallas kernels for 0%

profile of v1, /device:TPU:0, one launch (start us, length us, event | category | flops | bytes accessed | tf_op | source)
XLA Modules:
  0.0 124.7 jit_solution(10049549526771711962)
XLA Ops:
  0.6 1.3 %broadcast_in_dim.84 = bf16[8,2,1536]{2,1,0:T(2,128)(2,1)} broadcast(bf16[2,1536]{1,0:T(2,128)(2,1)} %bitcast.99), dimensions={1,2} | broadcast | bytes 55296 | tf_op jit(solution)/shard_map/broadcast_in_dim | solution.py:55
  2.0 7.3 %all-to-all-start = ((bf16[8,2,1536]{2,1,0:T(2,128)(2,1)}), bf16[8,2,1536]{2,1,0:T(2,128)(2,1)S(1)}, u32[]{:S(2)}, u32[]{:S(2)}) async-start(bf16[8,2,1536]{2,1,0:T(2,128)(2,1)} %broadcast_in_dim.84), calls=%async_computation | async-start | bytes 98304 | tf_op jit(solution)/shard_map/all_to_all | solution.py:39
  9.2 0.7 multiply_reduce_fusion
  10.0 0.7 slice_reduce_fusion
  10.7 1.0 fusion.40
  12.0 1.1 fusion.41
  14.1 0.7 compare_bitcast_fusion
  14.9 1.1 all-to-all-done
  17.7 0.7 all_to_all.33
  18.5 4.9 %all-to-all-start.1 = ((f32[8,1,3120]{2,1,0:T(1,128)}), f32[8,1,3120]{2,1,0:T(1,128)S(1)}, u32[]{:S(2)}, u32[]{:S(2)}) async-start(f32[8,1,3120]{2,1,0:T(1,128)} %all_to_all.33), calls=%async_computation.1 | async-start | bytes 204800 | tf_op jit(solution)/shard_map/all_to_all | solution.py:39
  23.4 7.1 %all-to-all-done.1 = f32[8,1,3120]{2,1,0:T(1,128)S(1)} async-done(((f32[8,1,3120]{2,1,0:T(1,128)}), f32[8,1,3120]{2,1,0:T(1,128)S(1)}, u32[]{:S(2)}, u32[]{:S(2)}) %all-to-all-start.1) | async-done | bytes 99872 | tf_op jit(solution)/shard_map/all_to_all | solution.py:39
  30.8 0.7 fusion.39
  32.2 0.9 reduce.6
  33.1 9.2 %all_to_all.50 = bf16[8,2,1536]{2,1,0:T(2,128)(2,1)S(1)} all-to-all(bf16[8,2,1536]{2,1,0:T(2,128)(2,1)S(1)} %reshape.198), channel_id=1, replica_groups=mesh['grp'=2,'batch'=8,'tensor'=2] {'batch'}, dimensions={0} | all-to-all | bytes 98304 | tf_op jit(solution)/shard_map/all_to_all | solution.py:42
  42.3 3.1 %fusion.19 = f32[8,768]{1,0:T(8,128)S(1)} fusion(bf16[3072,768]{1,0:T(8,128)(2,1)} %bitcast.88, bf16[8,1,3072]{2,1,0:T(2,128)(2,1)S(1)} %reshape.199), kind=kOutput, calls=%fused_computation.30 | convolution fusion | flops 37748736 | bytes 4792320 | tf_op jit(solution)/shard_map/dot_general | solution.py:114
  45.4 3.4 %psum.7 = f32[8,768]{1,0:T(8,128)S(1)} all-reduce(f32[8,768]{1,0:T(8,128)S(1)} %fusion.19), channel_id=1, replica_groups=mesh['grp'=2,'batch'=8,'tensor'=2] {'tensor'}, use_global_device_ids=true, to_apply=%region_8.9 | all-reduce | flops 6144 | bytes 49152 | tf_op jit(solution)/shard_map/psum | solution.py:113
  48.8 0.7 fusion.33
  49.5 0.7 broadcast_in_dim.89
  50.2 3.4 %all-to-all-start.3 = ((bf16[8,8,768]{2,1,0:T(8,128)(2,1)}), bf16[8,8,768]{2,1,0:T(8,128)(2,1)S(1)}, u32[]{:S(2)}, u32[]{:S(2)}) async-start(bf16[8,8,768]{2,1,0:T(8,128)(2,1)} %broadcast_in_dim.89), calls=%async_computation.3 | async-start | bytes 196608 | tf_op jit(solution)/shard_map/all_to_all | solution.py:42
  53.6 1.6 %fusion.42 = (s32[1,1]{1,0:T(1,128)}, s32[1,1]{1,0:T(1,128)}, s32[1,1]{1,0:T(1,128)}, s32[1,1]{1,0:T(1,128)}, s32[1,1]{1,0:T(1,128)}, /*index=5*/s32[1,1]{1,0:T(1,128)}, s32[1,1]{1,0:T(1,128)}, s32[1,1]{1,0:T(1,128)}) fusion(s32[1,8]{1,0:T(1,128)} %param.18), kind=kLoop, calls=%fused_computation.92 | loop fusion | bytes 64 | tf_op jit(solution)/shard_map/slice | solution.py:131
  70.2 5.9 %all-to-all-start.5 = ((bf16[8,16,1536]{2,1,0:T(8,128)(2,1)}), bf16[8,16,1536]{2,1,0:T(8,128)(2,1)S(1)}, u32[]{:S(2)}, u32[]{:S(2)}) async-start(bf16[8,16,1536]{2,1,0:T(8,128)(2,1)} %bitcast.89), calls=%async_computation.5 | async-start | bytes 786432 | tf_op jit(solution)/shard_map/all_to_all | solution.py:39
  76.1 9.0 %fusion.10 = bf16[8,1536]{1,0:T(8,128)(2,1)S(1)} fusion(bf16[8,6144]{1,0:T(8,128)(2,1)S(1)} %bitcast.91, bf16[6144,1536]{1,0:T(8,128)(2,1)} %param.16), kind=kOutput, calls=%fused_computation.19 | convolution fusion | flops 151793664 | bytes 18997248 | tf_op jit(solution)/shard_map/dot_general | solution.py:123
  85.1 1.8 %all_gather.3 = bf16[8,3072]{1,0:T(8,128)(2,1)S(1)} all-gather(bf16[8,1536]{1,0:T(8,128)(2,1)S(1)} %fusion.10), channel_id=1, replica_groups=mesh['grp'=2,'batch'=8,'tensor'=2] {'tensor'}, dimensions={1}, use_global_device_ids=true | all-gather | bytes 73728 | tf_op jit(solution)/shard_map/all_gather | solution.py:125
  87.0 7.7 %convolution_bitcast_fusion = f32[8,1,3072]{2,0,1:T(8,128)S(1)} fusion(bf16[8,3072]{1,0:T(8,128)(2,1)S(1)} %all_gather.3, bf16[3072,3072]{1,0:T(8,128)(2,1)} %param.17), kind=kOutput, calls=%fused_computation | convolution fusion | flops 150994944 | bytes 19021824 | tf_op jit(solution)/shard_map/dot_general | solution.py:126
  94.7 0.7 copy.50
  95.4 6.0 %all-to-all-start.4 = ((f32[8,1,3072]{2,1,0:T(1,128)}), f32[8,1,3072]{2,1,0:T(1,128)S(1)}, u32[]{:S(2)}, u32[]{:S(2)}) async-start(f32[8,1,3072]{2,1,0:T(1,128)} %copy.50), calls=%async_computation.4 | async-start | bytes 196608 | tf_op jit(solution)/shard_map/all_to_all | solution.py:42
  101.4 0.6 dynamic-slice_dynamic-update-slice_fusion.7
  102.0 0.6 dynamic-slice_dynamic-update-slice_fusion.6
  106.4 2.1 %all-to-all-done.4 = f32[8,1,3072]{2,1,0:T(1,128)S(1)} async-done(((f32[8,1,3072]{2,1,0:T(1,128)}), f32[8,1,3072]{2,1,0:T(1,128)S(1)}, u32[]{:S(2)}, u32[]{:S(2)}) %all-to-all-start.4) | async-done | bytes 98336 | tf_op jit(solution)/shard_map/all_to_all | solution.py:42
  108.5 3.9 %all-to-all-start.6 = ((bf16[8,16,1536]{2,1,0:T(8,128)(2,1)}), bf16[8,16,1536]{2,1,0:T(8,128)(2,1)S(1)}, u32[]{:S(2)}, u32[]{:S(2)}) async-start(bf16[8,16,1536]{2,1,0:T(8,128)(2,1)} %dynamic-slice_dynamic-update-slice_fusion), calls=%async_computation.6 | async-start | bytes 786432 | tf_op jit(solution)/shard_map/all_to_all | solution.py:39
  113.1 10.8 %all-to-all-done.6 = bf16[8,16,1536]{2,1,0:T(8,128)(2,1)S(1)} async-done(((bf16[8,16,1536]{2,1,0:T(8,128)(2,1)}), bf16[8,16,1536]{2,1,0:T(8,128)(2,1)S(1)}, u32[]{:S(2)}, u32[]{:S(2)}) %all-to-all-start.6) | async-done | bytes 393248 | tf_op jit(solution)/shard_map/all_to_all | solution.py:39
  123.9 0.8 broadcast_select_fusion
  (47 shorter events, 8.0 us)
Async XLA Ops:
  2.0 14.0 %all-to-all-start = ((bf16[8,2,1536]{2,1,0:T(2,128)(2,1)}), bf16[8,2,1536]{2,1,0:T(2,128)(2,1)S(1)}, u32[]{:S(2)}, u32[]{:S(2)}) async-start(bf16[8,2,1536]{2,1,0:T(2,128)(2,1)} %broadcast_in_dim.84), calls=%async_computation | async-start | bytes 98304 | tf_op jit(solution)/shard_map/all_to_all | solution.py:39
  18.5 12.1 %all-to-all-start.1 = ((f32[8,1,3120]{2,1,0:T(1,128)}), f32[8,1,3120]{2,1,0:T(1,128)S(1)}, u32[]{:S(2)}, u32[]{:S(2)}) async-start(f32[8,1,3120]{2,1,0:T(1,128)} %all_to_all.33), calls=%async_computation.1 | async-start | bytes 204800 | tf_op jit(solution)/shard_map/all_to_all | solution.py:39
  49.5 45.1 %copy-start.1 = (bf16[8,768]{1,0:T(8,128)(2,1)}, bf16[8,768]{1,0:T(8,128)(2,1)S(1)}, u32[]{:S(2)}) copy-start(bf16[8,768]{1,0:T(8,128)(2,1)S(1)} %fusion.33) | copy-start | bytes 36868
  50.2 20.0 %all-to-all-start.3 = ((bf16[8,8,768]{2,1,0:T(8,128)(2,1)}), bf16[8,8,768]{2,1,0:T(8,128)(2,1)S(1)}, u32[]{:S(2)}, u32[]{:S(2)}) async-start(bf16[8,8,768]{2,1,0:T(8,128)(2,1)} %broadcast_in_dim.89), calls=%async_computation.3 | async-start | bytes 196608 | tf_op jit(solution)/shard_map/all_to_all | solution.py:42
  70.2 25.2 %all-to-all-start.5 = ((bf16[8,16,1536]{2,1,0:T(8,128)(2,1)}), bf16[8,16,1536]{2,1,0:T(8,128)(2,1)S(1)}, u32[]{:S(2)}, u32[]{:S(2)}) async-start(bf16[8,16,1536]{2,1,0:T(8,128)(2,1)} %bitcast.89), calls=%async_computation.5 | async-start | bytes 786432 | tf_op jit(solution)/shard_map/all_to_all | solution.py:39
  85.1 38.8 %copy-start = (bf16[1,1,2,1536]{3,2,1,0:T(2,128)(2,1)S(1)}, bf16[1,1,2,1536]{3,2,1,0:T(2,128)(2,1)}, u32[]{:S(2)}) copy-start(bf16[1,1,2,1536]{3,2,1,0:T(2,128)(2,1)} %param.13) | copy-start | bytes 18436
  95.4 13.1 %all-to-all-start.4 = ((f32[8,1,3072]{2,1,0:T(1,128)}), f32[8,1,3072]{2,1,0:T(1,128)S(1)}, u32[]{:S(2)}, u32[]{:S(2)}) async-start(f32[8,1,3072]{2,1,0:T(1,128)} %copy.50), calls=%async_computation.4 | async-start | bytes 196608 | tf_op jit(solution)/shard_map/all_to_all | solution.py:42
  108.5 15.4 %all-to-all-start.6 = ((bf16[8,16,1536]{2,1,0:T(8,128)(2,1)}), bf16[8,16,1536]{2,1,0:T(8,128)(2,1)S(1)}, u32[]{:S(2)}, u32[]{:S(2)}) async-start(bf16[8,16,1536]{2,1,0:T(8,128)(2,1)} %dynamic-slice_dynamic-update-slice_fusion), calls=%async_computation.6 | async-start | bytes 786432 | tf_op jit(solution)/shard_map/all_to_all | solution.py:39

commit v2 on v1

--- a/solution.py
+++ b/solution.py
@@ -3,11 +3,52 @@
 import jax
 import jax.numpy as jnp
 from jax import lax
+from jax.experimental import pallas as pl
+from jax.experimental.pallas import tpu as pltpu
 from jax.sharding import PartitionSpec as P
 
 HD = 128
 BEAMS = 8
 LOW = -1e30
+
+
+def doubling(value, position, first, last):
+    total = lax.axis_size("batch")
+    buffer = value[None]
+    bit = first
+    while bit < last:
+        pairs = [(i, i ^ bit) for i in range(total)]
+        other = lax.ppermute(buffer, "batch", pairs)
+        upper = (position // bit) % 2 == 1
+        buffer = jnp.concatenate([jnp.where(upper, other, buffer), jnp.where(upper, buffer, other)])
+        bit *= 2
+    return buffer
+
+
+def place_kernel(parent_ref, length_ref, row_ref, new_ref, out_ref):
+    slots = lax.broadcasted_iota(jnp.int32, row_ref.shape[2:], 0)
+    for kind in range(2):
+        old = row_ref[0, kind]
+        new = jnp.broadcast_to(new_ref[kind : kind + 1, :], old.shape)
+        out_ref[kind] = jnp.where(slots == length_ref[0], new, old)
+
+
+def place(gathered, new_kv, parent, length):
+    _, kinds, positions, width = gathered.shape
+    return pl.pallas_call(
+        place_kernel,
+        out_shape=jax.ShapeDtypeStruct((kinds, positions, width), gathered.dtype),
+        grid_spec=pltpu.PrefetchScalarGridSpec(
+            num_scalar_prefetch=2,
+            grid=(1,),
+            in_specs=[
+                pl.BlockSpec((1, kinds, positions, width), lambda i, p, n: (p[0], 0, 0, 0)),
+                pl.BlockSpec((kinds, width), lambda i, p, n: (0, 0)),
+            ],
+            out_specs=pl.BlockSpec((kinds, positions, width), lambda i, p, n: (0, 0, 0)),
+        ),
+        compiler_params=pltpu.CompilerParams(vmem_limit_bytes=8 * 1024 * 1024),
+    )(parent, length, gathered, new_kv)
 
 
 def body(
@@ -42,7 +83,7 @@
         return lax.all_to_all(value, "batch", 0, 0, tiled=True)
 
     def gather_all(value):
-        return swap_all(jnp.broadcast_to(value[None], (devices,) + value.shape))
+        return doubling(value, position, 1, devices)
 
     request_ids = jnp.arange(stride, dtype=jnp.int32)
     length = jnp.sum(jnp.where(request_ids == request, lengths, 0))
@@ -52,7 +93,7 @@
     scale = 1.0 / math.sqrt(HD)
 
     own_query = queries[0, 0]
-    query = swap(jnp.broadcast_to(own_query[None], (BEAMS, 2, width)))
+    query = doubling(own_query, position, stride, devices)
     query = query.reshape(BEAMS, 2, heads, HD)
 
     def partial(q, kv, valid):
@@ -126,11 +167,9 @@
     part = jnp.dot(joined, down_weight, preferred_element_type=jnp.float32)
     ffn_row = jnp.sum(swap_all(part), axis=0, keepdims=True).astype(jnp.bfloat16)
 
-    pieces = init_cache.reshape(BEAMS, 2 * cache_len // BEAMS, width)
-    mine = swap(pieces)
-    chosen = jnp.stack([lax.dynamic_index_in_dim(mine, parent[b], 0, False) for b in range(BEAMS)])
-    cache = swap(chosen).reshape(2, cache_len, width)
-    cache = jnp.where((slots == length)[None, :, None], new_kv[0, 0][:, None, :], cache)
+    gathered = lax.all_gather(init_cache[0], "batch", axis_index_groups=groups)
+    parent_own = jnp.sum(jnp.where(jnp.arange(BEAMS) == own_beam, parent, 0))
+    cache = place(gathered, new_kv[0, 0], parent_own[None], length[None])
     return (hidden[None], ffn_row[None], cache[None])
 
 

time: 126 us -> 117 us (0.929)
  waiting for transfers between devices: 21.2 us -> 41 us
  starting transfers between devices: 31.3 us -> 19.1 us
  blocking collectives: 14.4 us -> 5.25 us
  local copies, waits for them, and re-layouts: 15.2 us -> 7.91 us
  Pallas kernels: 0 us -> 1.41 us
  between operations: 16.4 us -> 15 us
    ppermute x0 -> x9, waiting for transfers between devices: none -> 25.2 us  [doubling(): other = lax.ppermute(buffer, 'batch', pairs)]
    all_to_all x4 -> x1, starting transfers between devices: 22 us -> 5.03 us  [swap(): lax.all_to_all(value, 'batch', 0, 0, axis_index_groups=groups, tiled=True)]
    all_to_all x4 -> x1, waiting for transfers between devices: 19 us -> 7.1 us  [swap(): lax.all_to_all(value, 'batch', 0, 0, axis_index_groups=groups, tiled=True)]
    ppermute x0 -> x9, starting transfers between devices: none -> 9.91 us  [doubling(): other = lax.ppermute(buffer, 'batch', pairs)]
    all_to_all x1 -> x0, blocking collectives: 9.17 us -> none  [swap_all(): return lax.all_to_all(value, 'batch', 0, 0, tiled=True)]
    all_to_all x2 -> x1, waiting for transfers between devices: 2.14 us -> 8.19 us  [swap_all(): return lax.all_to_all(value, 'batch', 0, 0, tiled=True)]
    all_to_all x2 -> x1, starting transfers between devices: 9.36 us -> 4.1 us  [swap_all(): return lax.all_to_all(value, 'batch', 0, 0, tiled=True)]
    broadcast_in_dim x4 -> x0, local copies, waits for them, and re-layouts: 2.56 us -> none  [the longest x1 1.34 us: body(): query = swap(jnp.broadcast_to(own_query[None], (BEAMS, 2, width)))]
  transfers between devices with their start and end apart: 6 -> 12, of which waited for: 4 -> 11; matrix products, arithmetic and copies ran while one was open for 24% -> 24% of each run, Pallas kernels for 0% -> 0%
where the time goes in v2:
time: 117 us; the launch traced here: 116 us
  waiting for transfers between devices  41 us (35%)
  matrix products  20.8 us (18%)
  starting transfers between devices  19.1 us (16%)
  between operations  15 us (13%)
  local copies, waits for them, and re-layouts  7.91 us (7%)
  other arithmetic  5.54 us (5%)
  blocking collectives  5.25 us (4%)
  Pallas kernels  1.41 us (1%)
    ppermute x9, waiting for transfers between devices, doubling(): other = lax.ppermute(buffer, 'batch', pairs)  25.2 us
    ppermute x9, starting transfers between devices, doubling(): other = lax.ppermute(buffer, 'batch', pairs)  9.91 us
    dot_general x1, matrix products, body(): pre_act = jnp.dot(wide, up_weight, preferred_element_type=jnp.float32)  9.1 us
    all_to_all x1, waiting for transfers between devices, swap_all(): return lax.all_to_all(value, 'batch', 0, 0, tiled=True)  8.19 us
    dot_general x1, matrix products, body(): part = jnp.dot(joined, down_weight, preferred_element_type=jnp.float32)  7.75 us
    all_to_all x1, waiting for transfers between devices, swap(): lax.all_to_all(value, 'batch', 0, 0, axis_index_groups=groups, tiled=True)  7.1 us
    all_to_all x1, starting transfers between devices, swap(): lax.all_to_all(value, 'batch', 0, 0, axis_index_groups=groups, tiled=True)  5.03 us
    all_to_all x1, starting transfers between devices, swap_all(): return lax.all_to_all(value, 'batch', 0, 0, tiled=True)  4.1 us
  transfers between devices with their start and end apart: 12, of which 11 were waited for; matrix products, arithmetic and copies ran while one was open for 24% of the time, Pallas kernels for 0%

profile of v2, /device:TPU:0, one launch (start us, length us, event | category | flops | bytes accessed | tf_op | source)
XLA Modules:
  0.0 116.0 jit_solution(17613243689351656034)
XLA Ops:
  7.2 3.0 %collective-permute-start = (bf16[1,2,1536]{2,1,0:T(2,128)(2,1)}, bf16[1,2,1536]{2,1,0:T(2,128)(2,1)S(1)}, u32[]{:S(2)}, u32[]{:S(2)}) collective-permute-start(bf16[1,2,1536]{2,1,0:T(2,128)(2,1)} %bitcast.87), channel_id=1, source_target_pairs={{0,2},{2,0},{4,6},{6,4},{8,10},{10,8},{12,14},{14,12},{1,3},{3,1},... | collective-permute-start | bytes 18440 | tf_op jit(solution)/shard_map/ppermute | solution.py:21
  10.8 1.1 fusion.44
  11.9 1.1 fusion.45
  13.7 0.7 multiply_reduce_fusion
  14.4 0.7 broadcast_select_fusion.17
  15.2 1.6 %collective-permute-start.1 = (bf16[2,2,1536]{2,1,0:T(2,128)(2,1)S(1)}, bf16[2,2,1536]{2,1,0:T(2,128)(2,1)S(1)}, u32[]{:S(2)}, u32[]{:S(2)}) collective-permute-start(bf16[2,2,1536]{2,1,0:T(2,128)(2,1)S(1)} %pad_maximum_fusion.6), channel_id=1, source_target_pairs={{0,4},{2,6},{4,0},{6,2},{8,12},{10,14},{12,8},{14,10},{1,5},{3,7},... | collective-permute-start | bytes 36872 | tf_op jit(solution)/shard_map/ppermute | solution.py:21
  16.8 0.7 slice_reduce_fusion
  17.6 1.4 %collective-permute-done.1 = bf16[2,2,1536]{2,1,0:T(2,128)(2,1)S(1)} collective-permute-done((bf16[2,2,1536]{2,1,0:T(2,128)(2,1)S(1)}, bf16[2,2,1536]{2,1,0:T(2,128)(2,1)S(1)}, u32[]{:S(2)}, u32[]{:S(2)}) %collective-permute-start.1) | collective-permute-done | bytes 12320 | tf_op jit(solution)/shard_map/ppermute | solution.py:21
  19.0 2.7 %collective-permute-start.2 = (bf16[4,2,1536]{2,1,0:T(2,128)(2,1)S(1)}, bf16[4,2,1536]{2,1,0:T(2,128)(2,1)S(1)}, u32[]{:S(2)}, u32[]{:S(2)}) collective-permute-start(bf16[4,2,1536]{2,1,0:T(2,128)(2,1)S(1)} %pad_maximum_fusion.3), channel_id=1, source_target_pairs={{0,8},{2,10},{4,12},{6,14},{8,0},{10,2},{12,4},{14,6},{1,9},{3,11}... | collective-permute-start | bytes 73736 | tf_op jit(solution)/shard_map/ppermute | solution.py:21
  22.4 1.4 %collective-permute-done.2 = bf16[4,2,1536]{2,1,0:T(2,128)(2,1)S(1)} collective-permute-done((bf16[4,2,1536]{2,1,0:T(2,128)(2,1)S(1)}, bf16[4,2,1536]{2,1,0:T(2,128)(2,1)S(1)}, u32[]{:S(2)}, u32[]{:S(2)}) %collective-permute-start.2) | collective-permute-done | bytes 24608 | tf_op jit(solution)/shard_map/ppermute | solution.py:21
  25.7 0.7 all_to_all.14
  26.4 5.0 %all-to-all-start = ((f32[8,1,3120]{2,1,0:T(1,128)}), f32[8,1,3120]{2,1,0:T(1,128)S(1)}, u32[]{:S(2)}, u32[]{:S(2)}) async-start(f32[8,1,3120]{2,1,0:T(1,128)} %all_to_all.14), calls=%async_computation | async-start | bytes 204800 | tf_op jit(solution)/shard_map/all_to_all | solution.py:80
  31.5 7.1 %all-to-all-done = f32[8,1,3120]{2,1,0:T(1,128)S(1)} async-done(((f32[8,1,3120]{2,1,0:T(1,128)}), f32[8,1,3120]{2,1,0:T(1,128)S(1)}, u32[]{:S(2)}, u32[]{:S(2)}) %all-to-all-start) | async-done | bytes 99872 | tf_op jit(solution)/shard_map/all_to_all | solution.py:80
  38.9 0.7 fusion.43
  40.0 3.4 %collective-permute-done.3 = bf16[1,3072]{1,0:T(2,128)(2,1)S(1)} collective-permute-done((bf16[1,3072]{1,0:T(2,128)(2,1)S(1)}, bf16[1,3072]{1,0:T(2,128)(2,1)S(1)}, u32[]{:S(2)}, u32[]{:S(2)}) %collective-permute-start.3) | collective-permute-done | bytes 6176 | tf_op jit(solution)/shard_map/ppermute | solution.py:21
  43.6 3.7 %collective-permute-done.4 = bf16[2,3072]{1,0:T(2,128)(2,1)S(1)} collective-permute-done((bf16[2,3072]{1,0:T(2,128)(2,1)S(1)}, bf16[2,3072]{1,0:T(2,128)(2,1)S(1)}, u32[]{:S(2)}, u32[]{:S(2)}) %collective-permute-start.4) | collective-permute-done | bytes 12320 | tf_op jit(solution)/shard_map/ppermute | solution.py:21
  47.8 4.3 %collective-permute-done.5 = bf16[4,3072]{1,0:T(4,128)(2,1)S(1)} collective-permute-done((bf16[4,3072]{1,0:T(4,128)(2,1)S(1)}, bf16[4,3072]{1,0:T(4,128)(2,1)S(1)}, u32[]{:S(2)}, u32[]{:S(2)}) %collective-permute-start.5) | collective-permute-done | bytes 24608 | tf_op jit(solution)/shard_map/ppermute | solution.py:21
  52.2 3.1 %fusion.19 = f32[8,768]{1,0:T(8,128)S(1)} fusion(bf16[3072,768]{1,0:T(8,128)(2,1)} %bitcast.79, bf16[4,3072]{1,0:T(4,128)(2,1)S(1)} %get-tuple-element.22, bf16[4,3072]{1,0:T(4,128)(2,1)S(1)} %get-tuple-element.21), kind=kOutput, calls=%fused_computation.31 | convolution fusion | flops 37847040 | bytes 4792320 | tf_op jit(solution)/shard_map/dot_general | solution.py:155
  55.2 3.4 %psum.7 = f32[8,768]{1,0:T(8,128)S(1)} all-reduce(f32[8,768]{1,0:T(8,128)S(1)} %fusion.19), channel_id=1, replica_groups=mesh['grp'=2,'batch'=8,'tensor'=2] {'tensor'}, use_global_device_ids=true, to_apply=%region_8.9 | all-reduce | flops 6144 | bytes 49152 | tf_op jit(solution)/shard_map/psum | solution.py:154
  58.7 0.7 fusion.35
  59.8 3.3 %collective-permute-done.6 = bf16[1,8,768]{2,1,0:T(8,128)(2,1)S(1)} collective-permute-done((bf16[1,8,768]{2,1,0:T(8,128)(2,1)S(1)}, bf16[1,8,768]{2,1,0:T(8,128)(2,1)S(1)}, u32[]{:S(2)}, u32[]{:S(2)}) %collective-permute-start.6) | collective-permute-done | bytes 12320 | tf_op jit(solution)/shard_map/ppermute | solution.py:21
  63.3 3.8 %collective-permute-done.7 = bf16[2,8,768]{2,1,0:T(8,128)(2,1)S(1)} collective-permute-done((bf16[2,8,768]{2,1,0:T(8,128)(2,1)S(1)}, bf16[2,8,768]{2,1,0:T(8,128)(2,1)S(1)}, u32[]{:S(2)}, u32[]{:S(2)}) %collective-permute-start.7) | collective-permute-done | bytes 24608 | tf_op jit(solution)/shard_map/ppermute | solution.py:21
  67.1 1.1 collective-permute-start.8
  68.2 4.0 %collective-permute-done.8 = bf16[4,8,768]{2,1,0:T(8,128)(2,1)S(1)} collective-permute-done((bf16[4,8,768]{2,1,0:T(8,128)(2,1)S(1)}, bf16[4,8,768]{2,1,0:T(8,128)(2,1)S(1)}, u32[]{:S(2)}, u32[]{:S(2)}) %collective-permute-start.8) | collective-permute-done | bytes 49184 | tf_op jit(solution)/shard_map/ppermute | solution.py:21
  72.2 9.1 %fusion.10 = bf16[8,1536]{1,0:T(8,128)(2,1)S(1)} fusion(bf16[8,6144]{1,0:T(8,128)(2,1)S(1)} %bitcast.80, bf16[6144,1536]{1,0:T(8,128)(2,1)} %param.16), kind=kOutput, calls=%fused_computation.19 | convolution fusion | flops 151793664 | bytes 18997248 | tf_op jit(solution)/shard_map/dot_general | solution.py:164
  81.4 1.8 %all_gather.6 = bf16[8,3072]{1,0:T(8,128)(2,1)S(1)} all-gather(bf16[8,1536]{1,0:T(8,128)(2,1)S(1)} %fusion.10), channel_id=1, replica_groups=mesh['grp'=2,'batch'=8,'tensor'=2] {'tensor'}, dimensions={1}, use_global_device_ids=true | all-gather | bytes 73728 | tf_op jit(solution)/shard_map/all_gather | solution.py:166
  83.2 7.7 %convolution_bitcast_fusion = f32[8,1,3072]{2,0,1:T(8,128)S(1)} fusion(bf16[8,3072]{1,0:T(8,128)(2,1)S(1)} %all_gather.6, bf16[3072,3072]{1,0:T(8,128)(2,1)} %param.17), kind=kOutput, calls=%fused_computation | convolution fusion | flops 150994944 | bytes 19021824 | tf_op jit(solution)/shard_map/dot_general | solution.py:167
  91.0 0.8 copy.51
  91.7 4.1 %all-to-all-start.1 = ((f32[8,1,3072]{2,1,0:T(1,128)}), f32[8,1,3072]{2,1,0:T(1,128)S(1)}, u32[]{:S(2)}, u32[]{:S(2)}) async-start(f32[8,1,3072]{2,1,0:T(1,128)} %copy.51), calls=%async_computation.1 | async-start | bytes 196608 | tf_op jit(solution)/shard_map/all_to_all | solution.py:83
  96.5 8.2 %all-to-all-done.1 = f32[8,1,3072]{2,1,0:T(1,128)S(1)} async-done(((f32[8,1,3072]{2,1,0:T(1,128)}), f32[8,1,3072]{2,1,0:T(1,128)S(1)}, u32[]{:S(2)}, u32[]{:S(2)}) %all-to-all-start.1) | async-done | bytes 98336 | tf_op jit(solution)/shard_map/all_to_all | solution.py:83
  105.9 1.9 %copy-done = bf16[8,2,64,1536]{3,2,1,0:T(8,128)(2,1)S(1)} copy-done((bf16[8,2,64,1536]{3,2,1,0:T(8,128)(2,1)S(1)}, bf16[8,2,64,1536]{3,2,1,0:T(8,128)(2,1)}, u32[]{:S(2)}) %copy-start) | copy-done | bytes 3145752
  107.7 1.4 %shard_map.121 = bf16[2,64,1536]{2,1,0:T(8,128)(2,1)} custom-call(s32[1]{0:T(128)} %bitcast.22.parent_ref, s32[1]{0:T(128)} %copy.69.length_ref, bf16[8,2,64,1536]{3,2,1,0:T(8,128)(2,1)S(1)} %copy-done, bf16[2,1536]{1,0:T(2,128)(2,1)S(1)} %bitcast.78), custom_call_target="tpu_custom_call" | custom-call | tf_op jit(solution)/shard_map/pallas_call | solution.py:38
  (65 shorter events, 7.5 us)
Async XLA Ops:
  7.2 7.3 %collective-permute-start = (bf16[1,2,1536]{2,1,0:T(2,128)(2,1)}, bf16[1,2,1536]{2,1,0:T(2,128)(2,1)S(1)}, u32[]{:S(2)}, u32[]{:S(2)}) collective-permute-start(bf16[1,2,1536]{2,1,0:T(2,128)(2,1)} %bitcast.87), channel_id=1, source_target_pairs={{0,2},{2,0},{4,6},{6,4},{8,10},{10,8},{12,14},{14,12},{1,3},{3,1},... | collective-permute-start | bytes 18440 | tf_op jit(solution)/shard_map/ppermute | solution.py:21
  15.2 3.8 %collective-permute-start.1 = (bf16[2,2,1536]{2,1,0:T(2,128)(2,1)S(1)}, bf16[2,2,1536]{2,1,0:T(2,128)(2,1)S(1)}, u32[]{:S(2)}, u32[]{:S(2)}) collective-permute-start(bf16[2,2,1536]{2,1,0:T(2,128)(2,1)S(1)} %pad_maximum_fusion.6), channel_id=1, source_target_pairs={{0,4},{2,6},{4,0},{6,2},{8,12},{10,14},{12,8},{14,10},{1,5},{3,7},... | collective-permute-start | bytes 36872 | tf_op jit(solution)/shard_map/ppermute | solution.py:21
  19.0 4.8 %collective-permute-start.2 = (bf16[4,2,1536]{2,1,0:T(2,128)(2,1)S(1)}, bf16[4,2,1536]{2,1,0:T(2,128)(2,1)S(1)}, u32[]{:S(2)}, u32[]{:S(2)}) collective-permute-start(bf16[4,2,1536]{2,1,0:T(2,128)(2,1)S(1)} %pad_maximum_fusion.3), channel_id=1, source_target_pairs={{0,8},{2,10},{4,12},{6,14},{8,0},{10,2},{12,4},{14,6},{1,9},{3,11}... | collective-permute-start | bytes 73736 | tf_op jit(solution)/shard_map/ppermute | solution.py:21
  26.4 12.2 %all-to-all-start = ((f32[8,1,3120]{2,1,0:T(1,128)}), f32[8,1,3120]{2,1,0:T(1,128)S(1)}, u32[]{:S(2)}, u32[]{:S(2)}) async-start(f32[8,1,3120]{2,1,0:T(1,128)} %all_to_all.14), calls=%async_computation | async-start | bytes 204800 | tf_op jit(solution)/shard_map/all_to_all | solution.py:80
  31.4 74.4 %all-gather.2.cloned.1.call-start = ((), (), s32[]{:S(2)}) async-start(), calls=%async_computation.2 | async-start | bytes 3538944 | tf_op jit(solution)/shard_map/all_gather | solution.py:170
  39.7 3.8 %collective-permute-start.3 = (bf16[1,3072]{1,0:T(2,128)(2,1)S(1)}, bf16[1,3072]{1,0:T(2,128)(2,1)S(1)}, u32[]{:S(2)}, u32[]{:S(2)}) collective-permute-start(bf16[1,3072]{1,0:T(2,128)(2,1)S(1)} %convert_element_type.86), channel_id=1, source_target_pairs={{0,2},{2,0},{4,6},{6,4},{8,10},{10,8},{12,14},{14,12},{1,3},{3,1},... | collective-permute-start | bytes 18440 | tf_op jit(solution)/shard_map/ppermute | solution.py:21
  43.5 3.8 %collective-permute-start.4 = (bf16[2,3072]{1,0:T(2,128)(2,1)S(1)}, bf16[2,3072]{1,0:T(2,128)(2,1)S(1)}, u32[]{:S(2)}, u32[]{:S(2)}) collective-permute-start(bf16[2,3072]{1,0:T(2,128)(2,1)S(1)} %pad_maximum_fusion.7), channel_id=1, source_target_pairs={{0,4},{2,6},{4,0},{6,2},{8,12},{10,14},{12,8},{14,10},{1,5},{3,7},... | collective-permute-start | bytes 36872 | tf_op jit(solution)/shard_map/ppermute | solution.py:21
  47.3 4.8 %collective-permute-start.5 = (bf16[4,3072]{1,0:T(4,128)(2,1)S(1)}, bf16[4,3072]{1,0:T(4,128)(2,1)S(1)}, u32[]{:S(2)}, u32[]{:S(2)}) collective-permute-start(bf16[4,3072]{1,0:T(4,128)(2,1)S(1)} %pad_maximum_fusion.4), channel_id=1, source_target_pairs={{0,8},{2,10},{4,12},{6,14},{8,0},{10,2},{12,4},{14,6},{1,9},{3,11}... | collective-permute-start | bytes 73736 | tf_op jit(solution)/shard_map/ppermute | solution.py:21
  59.4 31.6 %copy-start.2 = (bf16[1,8,768]{2,1,0:T(8,128)(2,1)}, bf16[1,8,768]{2,1,0:T(8,128)(2,1)S(1)}, u32[]{:S(2)}) copy-start(bf16[1,8,768]{2,1,0:T(8,128)(2,1)S(1)} %fusion.35) | copy-start | bytes 36868
  59.4 3.7 %collective-permute-start.6 = (bf16[1,8,768]{2,1,0:T(8,128)(2,1)S(1)}, bf16[1,8,768]{2,1,0:T(8,128)(2,1)S(1)}, u32[]{:S(2)}, u32[]{:S(2)}) collective-permute-start(bf16[1,8,768]{2,1,0:T(8,128)(2,1)S(1)} %fusion.35), channel_id=1, source_target_pairs={{0,2},{2,0},{4,6},{6,4},{8,10},{10,8},{12,14},{14,12},{1,3},{3,1},... | collective-permute-start | bytes 36872 | tf_op jit(solution)/shard_map/ppermute | solution.py:21
  63.1 4.0 %collective-permute-start.7 = (bf16[2,8,768]{2,1,0:T(8,128)(2,1)S(1)}, bf16[2,8,768]{2,1,0:T(8,128)(2,1)S(1)}, u32[]{:S(2)}, u32[]{:S(2)}) collective-permute-start(bf16[2,8,768]{2,1,0:T(8,128)(2,1)S(1)} %pad_maximum_fusion.5), channel_id=1, source_target_pairs={{0,4},{2,6},{4,0},{6,2},{8,12},{10,14},{12,8},{14,10},{1,5},{3,7},... | collective-permute-start | bytes 73736 | tf_op jit(solution)/shard_map/ppermute | solution.py:21
  67.1 5.1 %collective-permute-start.8 = (bf16[4,8,768]{2,1,0:T(8,128)(2,1)S(1)}, bf16[4,8,768]{2,1,0:T(8,128)(2,1)S(1)}, u32[]{:S(2)}, u32[]{:S(2)}) collective-permute-start(bf16[4,8,768]{2,1,0:T(8,128)(2,1)S(1)} %pad_maximum_fusion.2), channel_id=1, source_target_pairs={{0,8},{2,10},{4,12},{6,14},{8,0},{10,2},{12,4},{14,6},{1,9},{3,11}... | collective-permute-start | bytes 147464 | tf_op jit(solution)/shard_map/ppermute | solution.py:21
  81.4 14.5 %copy-start.3 = (s32[1,8]{1,0:T(1,128)S(1)}, s32[1,8]{1,0:T(1,128)}, u32[]{:S(2)}) copy-start(s32[1,8]{1,0:T(1,128)} %param.18) | copy-start | bytes 100
  81.4 24.5 %copy-start.1 = (bf16[1,1,2,1536]{3,2,1,0:T(2,128)(2,1)S(1)}, bf16[1,1,2,1536]{3,2,1,0:T(2,128)(2,1)}, u32[]{:S(2)}) copy-start(bf16[1,1,2,1536]{3,2,1,0:T(2,128)(2,1)} %param.13) | copy-start | bytes 18436
  91.7 12.9 %all-to-all-start.1 = ((f32[8,1,3072]{2,1,0:T(1,128)}), f32[8,1,3072]{2,1,0:T(1,128)S(1)}, u32[]{:S(2)}, u32[]{:S(2)}) async-start(f32[8,1,3072]{2,1,0:T(1,128)} %copy.51), calls=%async_computation.1 | async-start | bytes 196608 | tf_op jit(solution)/shard_map/all_to_all | solution.py:83
  105.9 1.9 %copy-start = (bf16[8,2,64,1536]{3,2,1,0:T(8,128)(2,1)S(1)}, bf16[8,2,64,1536]{3,2,1,0:T(8,128)(2,1)}, u32[]{:S(2)}) copy-start(bf16[8,2,64,1536]{3,2,1,0:T(8,128)(2,1)} %all-gather.2.cloned.1.call-done.row_ref) | copy-start | bytes 9437188
Sparse Core Ops, SparseCore 0:
  43.7 62.0 all-gather.1

commit v3 on v2

v3 whole, which is shorter than its diff:
```python
import functools
import math

import jax
import jax.numpy as jnp
from jax import lax
from jax.experimental import pallas as pl
from jax.experimental.pallas import tpu as pltpu
from jax.sharding import PartitionSpec as P

HD = 128
LANES = 128
SLOT = 16
BEAMS = 8
LOW = -1e30
MIB = 1024 * 1024
RESIDENT = True

VM = pl.BlockSpec(memory_space=pltpu.VMEM)
SM = pl.BlockSpec(memory_space=pltpu.SMEM)


def xor_permute(value, axis, bit):
    total = lax.axis_size(axis)
    return lax.ppermute(value, axis, [(i, i ^ bit) for i in range(total)])


def doubling(buffer, first, last):
    bit = first
    while bit < last:
        buffer = jnp.concatenate([buffer, xor_permute(buffer, "batch", bit)])
        bit *= 2
    return buffer


def call(kernel, out, *args, specs=None, vmem=8, flops=0, moved=0):
    return pl.pallas_call(
        kernel,
        out_shape=out,
        in_specs=specs or [VM] * len(args),
        out_specs=jax.tree.map(lambda _: VM, out),
        compiler_params=pltpu.CompilerParams(vmem_limit_bytes=vmem * MIB),
        cost_estimate=pl.CostEstimate(flops=flops, bytes_accessed=moved, transcendentals=0),
    )(*args)


def split3(value):
    high = value.astype(jnp.bfloat16).astype(jnp.float32)
    rest = value - high
    middle = rest.astype(jnp.bfloat16).astype(jnp.float32)
    return high, middle, rest - middle


def export(num_ref, state_ref, pay_ref, peaks, totals):
    heads = num_ref.shape[1] // HD
    inverse = jnp.where(totals > 0.0, 1.0 / jnp.where(totals > 0.0, totals, 1.0), 0.0)
    for h in range(heads):
        cols = slice(h * HD, (h + 1) * HD)
        pay_ref[:, cols] = (num_ref[:, cols] * inverse[:, h : h + 1]).astype(jnp.bfloat16)
    state_ref[:, :LANES] = peaks
    state_ref[:, LANES:] = totals
    group = lax.broadcasted_iota(jnp.int32, peaks.shape, 1) // SLOT
    extra = jnp.zeros_like(peaks)
    for g, part in enumerate(split3(peaks) + split3(totals)):
        extra = jnp.where(group == g, pltpu.roll(part, g * SLOT, 1) if g else part, extra)
    pay_ref[:, heads * HD :] = extra.astype(jnp.bfloat16)


def attend_kernel(stride, query_ref, cache_ref, memory_ref, new_ref, parents_ref, lengths_ref, num_ref, state_ref, pay_ref):
    position = lax.axis_index("batch")
    own, request = position // stride, lax.rem(position, stride)
    length = lengths_ref[request]
    rows, width = query_ref.shape
    heads = width // HD
    past = cache_ref.shape[1]
    span = past + memory_ref.shape[1]

    to = lax.broadcasted_iota(jnp.int32, (rows, rows), 0)
    source = lax.broadcasted_iota(jnp.int32, (rows, rows), 1)
    beam = jnp.bitwise_xor(source // 2, own)
    order = jnp.where(to == (source % 2) * BEAMS + beam, 1.0, 0.0).astype(jnp.bfloat16)

    row = lax.broadcasted_iota(jnp.int32, (rows, span), 0)
    slot = lax.broadcasted_iota(jnp.int32, (rows, span), 1)
    parent = jnp.zeros_like(row)
    for b in range(BEAMS):
        parent = jnp.where(row == b, parents_ref[0, b * stride + request], parent)
    in_past = ((slot < length) & (parent == own)) | ((slot == length) & (row == own))
    valid = jnp.where(row < BEAMS, jnp.where(in_past, 1, 0), jnp.where(slot >= past, 1, 0)) == 1
    fresh = lax.broadcasted_iota(jnp.int32, (past, HD), 0) == length
    lane = lax.broadcasted_iota(jnp.int32, (rows, LANES), 1)
    peaks = jnp.zeros((rows, LANES), jnp.float32)
    totals = jnp.zeros((rows, LANES), jnp.float32)

    def block(kind, cols):
        old = cache_ref[kind, :, cols].astype(jnp.float32)
        new = new_ref[kind : kind + 1, cols].astype(jnp.float32)
        merged = jnp.where(fresh, new, old).astype(jnp.bfloat16)
        return jnp.concatenate([merged, memory_ref[kind, :, cols]])

    for h in range(heads):
        cols = slice(h * HD, (h + 1) * HD)
        query = jnp.dot(order, query_ref[:, cols], preferred_element_type=jnp.float32).astype(jnp.bfloat16)
        scores = lax.dot_general(
            query, block(0, cols), (((1,), (1,)), ((), ())), preferred_element_type=jnp.float32
        ) * (1.0 / math.sqrt(HD))
        scores = jnp.where(valid, scores, LOW)
        peak = jnp.max(scores, axis=1, keepdims=True)
        weights = jnp.where(valid, jnp.exp(scores - peak), 0.0)
        total = jnp.sum(weights, axis=1, keepdims=True)
        high = weights.astype(jnp.bfloat16)
        low = (weights - high.astype(jnp.float32)).astype(jnp.bfloat16)
        values = block(1, cols)
        num_ref[:, cols] = jnp.dot(high, values, preferred_element_type=jnp.float32) + jnp.dot(
            low, values, preferred_element_type=jnp.float32
        )
        peaks = jnp.where(lane == h, peak, peaks)
        totals = jnp.where(lane == h, total, totals)
    export(num_ref, state_ref, pay_ref, peaks, totals)


def combine(num_ref, state_ref, pay_ref, out_ref):
    heads = num_ref.shape[1] // HD
    extra = pay_ref[:, heads * HD :].astype(jnp.float32)
    summed = extra + pltpu.roll(extra, LANES - SLOT, 1) + pltpu.roll(extra, LANES - 2 * SLOT, 1)
    other_total = pltpu.roll(summed, LANES - 3 * SLOT, 1)
    lane = lax.broadcasted_iota(jnp.int32, extra.shape, 1)
    used = lane < SLOT
    other_peak = jnp.where(used, summed, 0.0)
    other_total = jnp.where(used, other_total, 0.0)
    own_peak, own_total = state_ref[:, :LANES], state_ref[:, LANES:]
    peaks = jnp.maximum(own_peak, other_peak)
    own_factor = jnp.exp(own_peak - peaks)
    other_factor = jnp.exp(other_peak - peaks) * other_total
    totals = own_total * own_factor + other_factor
    for h in range(heads):
        cols = slice(h * HD, (h + 1) * HD)
        other = pay_ref[:, cols].astype(jnp.float32)
        out_ref[:, cols] = num_ref[:, cols] * own_factor[:, h : h + 1] + other * other_factor[:, h : h + 1]
    return peaks, totals


def merge_kernel(num_ref, state_ref, pay_ref, num_out, state_out, pay_out):
    peaks, totals = combine(num_ref, state_ref, pay_ref, num_out)
    export(num_out, state_out, pay_out, peaks, totals)


def finish_kernel(num_ref, state_ref, pay_ref, out_ref, num):
    _, totals = combine(num_ref, state_ref, pay_ref, num)
    for h in range(num.shape[1] // HD):
        cols = slice(h * HD, (h + 1) * HD)
        out_ref[:, cols] = (num[:, cols] / totals[:, h : h + 1]).astype(jnp.bfloat16)


def finish(num, state, pay):
    return pl.pallas_call(
        finish_kernel,
        out_shape=jax.ShapeDtypeStruct(num.shape, jnp.bfloat16),
        in_specs=[VM] * 3,
        out_specs=VM,
        scratch_shapes=[pltpu.VMEM(num.shape, jnp.float32)],
        compiler_params=pltpu.CompilerParams(vmem_limit_bytes=8 * MIB),
    )(num, state, pay)


def project_kernel(attended_ref, weight_ref, out_ref):
    rows = out_ref.shape[0]
    first = jnp.dot(attended_ref[...], weight_ref[0], preferred_element_type=jnp.float32)
    second = jnp.dot(attended_ref[...], weight_ref[1], preferred_element_type=jnp.float32)
    out_ref[...] = first[:rows] + second[rows:]


def add_kernel(own_ref, other_ref, residual_ref, out_ref):
    total = residual_ref[...].astype(jnp.float32) + (own_ref[...] + other_ref[...])
    out_ref[...] = total.astype(jnp.bfloat16)


def up_kernel(hidden_ref, weight_ref, out_ref):
    blocks, rows, depth = hidden_ref.shape
    position = lax.axis_index("batch")

    def step(j, total):
        start = pl.multiple_of(jnp.bitwise_xor(position, j) * depth, depth)
        return total + jnp.dot(
            hidden_ref[j], weight_ref[pl.ds(start, depth), :], preferred_element_type=jnp.float32
        )

    total = lax.fori_loop(0, blocks, step, jnp.zeros(out_ref.shape, jnp.float32), unroll=blocks <= 8)
    out_ref[...] = (0.5 * total * (1.0 + lax.erf(total * math.sqrt(0.5)))).astype(jnp.bfloat16)


def reorder(activation):
    rows = activation.shape[0]
    position = lax.axis_index("batch")
    to = lax.broadcasted_iota(jnp.int32, (rows, rows), 0)
    source = lax.broadcasted_iota(jnp.int32, (rows, rows), 1)
    reverse = jnp.zeros_like(to)
    bits = rows.bit_length() - 1
    for k in range(bits):
        reverse = reverse + ((to >> k) % 2) * (1 << (bits - 1 - k))
    order = jnp.where(source == jnp.bitwise_xor(reverse, position), 1.0, 0.0).astype(jnp.bfloat16)
    return jnp.dot(order, activation, preferred_element_type=jnp.float32).astype(jnp.bfloat16)


def down_kernel(mine, act_ref, weight_ref, *rest):
    depth = act_ref.shape[1]
    side = lax.axis_index("tensor")
    start = pl.multiple_of((side if mine else 1 - side) * depth, depth)
    part = jnp.dot(
        reorder(act_ref[...]), weight_ref[pl.ds(start, depth), :], preferred_element_type=jnp.float32
    )
    if mine:
        rest[0][...] = part
        return
    before, keep_ref, send_ref = rest
    total = before[...] + part
    half = total.shape[0] // 2
    keep_ref[...] = total[:half]
    send_ref[...] = total[half:]


def place_kernel(parent_ref, length_ref, row_ref, new_ref, out_ref):
    slots = lax.broadcasted_iota(jnp.int32, row_ref.shape[2:], 0)
    for kind in range(2):
        old = row_ref[0, kind]
        new = jnp.broadcast_to(new_ref[kind : kind + 1, :], old.shape)
        out_ref[kind] = jnp.where(slots == length_ref[0], new, old)


def place(gathered, new_kv, parent, length):
    _, kinds, positions, width = gathered.shape
    return pl.pallas_call(
        place_kernel,
        out_shape=jax.ShapeDtypeStruct((kinds, positions, width), gathered.dtype),
        grid_spec=pltpu.PrefetchScalarGridSpec(
            num_scalar_prefetch=2,
            grid=(1,),
            in_specs=[
                pl.BlockSpec((1, kinds, positions, width), lambda i, p, n: (p[0], 0, 0, 0)),
                pl.BlockSpec((kinds, width), lambda i, p, n: (0, 0)),
            ],
            out_specs=pl.BlockSpec((kinds, positions, width), lambda i, p, n: (0, 0, 0)),
        ),
        compiler_params=pltpu.CompilerParams(vmem_limit_bytes=8 * MIB),
    )(parent, length, gathered, new_kv)


def body(
    init_cache,
    memory,
    queries,
    new_kv,
    residual,
    out_weight,
    up_weight,
    down_weight,
    parents,
    lengths,
):
    devices = lax.axis_size("batch")
    stride = devices // BEAMS
    position = lax.axis_index("batch")
    own_beam = position // stride
    request = position % stride
    width = queries.shape[-1]
    rows = parents.shape[1]
    columns = out_weight.shape[2]
    hidden_units = up_weight.shape[1]
    out_columns = down_weight.shape[1]
    groups = None
    if stride > 1:
        groups = [[b * stride + r for b in range(BEAMS)] for r in range(stride)]
    f32, bf16 = jnp.float32, jnp.bfloat16
    shape = jax.ShapeDtypeStruct

    if RESIDENT:
        out_weight, up_weight, down_weight = (
            pltpu.with_memory_space_constraint(w, pltpu.VMEM) for w in (out_weight, up_weight, down_weight)
        )

    query = doubling(queries[0, 0], stride, devices)
    state_shapes = (
        shape((2 * BEAMS, width), f32),
        shape((2 * BEAMS, 2 * LANES), f32),
        shape((2 * BEAMS, width + LANES), bf16),
    )
    num, state, pay = call(
        functools.partial(attend_kernel, stride),
        state_shapes,
        query,
        init_cache[0],
        memory[0],
        new_kv[0, 0],
        parents,
        lengths,
        specs=[VM] * 4 + [SM] * 2,
    )
    bit = stride
    while 2 * bit < devices:
        num, state, pay = call(merge_kernel, state_shapes, num, state, xor_permute(pay, "batch", bit))
        bit *= 2
    attended = finish(num, state, xor_permute(pay, "batch", bit))
    if stride > 1:
        stacked = doubling(attended[None], 1, stride)
        wanted = jnp.bitwise_xor(jnp.arange(stride, dtype=jnp.int32), request)
        stacked = stacked[wanted].reshape(stride, 2, BEAMS, width)
        attended = stacked.transpose(1, 2, 0, 3).reshape(2 * rows, width)

    partial = call(project_kernel, shape((rows, columns), f32), attended, out_weight)
    other = xor_permute(partial, "tensor", 1)
    hidden = call(add_kernel, shape((rows, columns), bf16), partial, other, residual[0])
    wide = doubling(hidden[None], 1, devices)
    activation = call(up_kernel, shape((rows, hidden_units), bf16), wide, up_weight)
    arrived = xor_permute(activation, "tensor", 1)
    before = call(
        functools.partial(down_kernel, True), shape((rows, out_columns), f32), activation, down_weight
    )
    keep, send = call(
        functools.partial(down_kernel, False),
        (shape((rows // 2, out_columns), f32),) * 2,
        arrived,
        down_weight,
        before,
    )
    bit = 1
    while True:
        total = keep + xor_permute(send, "batch", bit)
        bit *= 2
        if bit == devices:
            break
        half = total.shape[0] // 2
        keep, send = total[:half], total[half:]
    ffn_row = total.astype(bf16)

    gathered = lax.all_gather(init_cache[0], "batch", axis_index_groups=groups)
    grouped = parents.reshape(BEAMS, stride)
    here = (jnp.arange(BEAMS)[:, None] == own_beam) & (jnp.arange(stride)[None] == request)
    parent_own = jnp.sum(jnp.where(here, grouped, 0))
    length = jnp.sum(jnp.where(jnp.arange(stride) == request, lengths, 0))
    cache = place(gathered, new_kv[0, 0], parent_own[None], length[None])
    return (hidden[None], ffn_row[None], cache[None])


def solution(mesh):
    placed = (
        P(("grp", "batch"), None, None, "tensor"),
        P(("grp", "batch"), None, None, "tensor"),
        P(None, ("grp", "batch"), None, "tensor"),
        P(None, ("grp", "batch"), None, "tensor"),
        P(None, "grp", "batch"),
        P(None, "tensor", "batch"),
        P(None, ("batch", "tensor")),
        P("batch", "tensor"),
        P(None, "grp"),
        P("grp"),
    )
    return jax.shard_map(
        body,
        mesh=mesh,
        in_specs=placed,
        out_specs=(
            P(None, "grp", "batch"),
            P(None, ("grp", "batch"), "tensor"),
            P(("grp", "batch"), None, None, "tensor"),
        ),
        check_vma=False,
    )
```

time: 117 us -> 110 us (0.940)
  matrix products: 20.8 us -> 0 us
  Pallas kernels: 1.41 us -> 12.8 us
  starting transfers between devices: 19.1 us -> 29.2 us
  waiting for transfers between devices: 41 us -> 32 us
  local copies, waits for them, and re-layouts: 7.91 us -> 14.7 us
  blocking collectives: 5.25 us -> 0 us
    dot_general x7 -> x0, matrix products: 20.8 us -> none  [the longest x1 9.1 us: body(): pre_act = jnp.dot(wide, up_weight, preferred_element_type=jnp.float32)]
    ppermute x9 -> x14, starting transfers between devices: 9.91 us -> 29.2 us  [xor_permute(): return lax.ppermute(value, axis, [(i, i ^ bit) for i in range(total)])]
    all_to_all x2 -> x0, waiting for transfers between devices: 15.3 us -> none  [the longest x1 8.19 us: swap_all(): return lax.all_to_all(value, 'batch', 0, 0, tiled=True)]
    unnamed x9 -> x22, local copies, waits for them, and re-layouts: 1.91 us -> 14.7 us
    pallas_call x0 -> x9, Pallas kernels: none -> 11.4 us  [the longest x8 11.1 us: call(): pl.pallas_call(kernel, out_shape=out, in_specs=specs or [VM] * len(args),...]
    all_to_all x2 -> x0, starting transfers between devices: 9.12 us -> none  [the longest x1 5.03 us: swap(): lax.all_to_all(value, 'batch', 0, 0, axis_index_groups=groups, tiled=True)]
    ppermute x9 -> x14, waiting for transfers between devices: 25.2 us -> 31.3 us  [xor_permute(): return lax.ppermute(value, axis, [(i, i ^ bit) for i in range(total)])]
    concatenate x8 -> x6, other arithmetic: 0.22 us -> 4.83 us  [doubling(): buffer = jnp.concatenate([buffer, xor_permute(buffer, 'batch', bit)])]
  transfers between devices with their start and end apart: 12 -> 15, of which waited for: 11 -> 13; matrix products, arithmetic and copies ran while one was open for 24% -> 6% of each run, Pallas kernels for 0% -> 10%
where the time goes in v3:
time: 110 us
  waiting for transfers between devices  32 us (29%)
  starting transfers between devices  29.2 us (27%)
  between operations  14.8 us (13%)
  local copies, waits for them, and re-layouts  14.7 us (13%)
  Pallas kernels  12.8 us (12%)
  other arithmetic  6.11 us (6%)
    ppermute x14, waiting for transfers between devices, xor_permute(): return lax.ppermute(value, axis, [(i, i ^ bit) for i in range(total)])  31.3 us
    ppermute x14, starting transfers between devices, xor_permute(): return lax.ppermute(value, axis, [(i, i ^ bit) for i in range(total)])  29.2 us
    unnamed x22, local copies, waits for them, and re-layouts  14.7 us
    pallas_call x8, Pallas kernels, call(): pl.pallas_call(kernel, out_shape=out, in_specs=specs or [VM] * len(args),...  11.1 us
    concatenate x6, other arithmetic, doubling(): buffer = jnp.concatenate([buffer, xor_permute(buffer, 'batch', bit)])  4.83 us
  transfers between devices with their start and end apart: 15, of which 13 were waited for; matrix products, arithmetic and copies ran while one was open for 6% of the time, Pallas kernels for 10%

profile of v3, /device:TPU:0, one launch (start us, length us, event | category | flops | bytes accessed | tf_op | source)
XLA Modules:
  0.0 109.7 jit_solution(15640339766614981036)
XLA Ops:
  7.9 3.0 %collective-permute-start = (bf16[2,1536]{1,0:T(2,128)(2,1)}, bf16[2,1536]{1,0:T(2,128)(2,1)S(1)}, u32[]{:S(2)}, u32[]{:S(2)}) collective-permute-start(bf16[2,1536]{1,0:T(2,128)(2,1)} %bitcast.23), channel_id=1, source_target_pairs={{0,2},{2,0},{4,6},{6,4},{8,10},{10,8},{12,14},{14,12},{1,3},{3,1},... | collective-permute-start | bytes 18440 | tf_op jit(solution)/shard_map/ppermute | solution.py:25
  10.9 1.8 %collective-permute-done = bf16[2,1536]{1,0:T(2,128)(2,1)S(1)} collective-permute-done((bf16[2,1536]{1,0:T(2,128)(2,1)}, bf16[2,1536]{1,0:T(2,128)(2,1)S(1)}, u32[]{:S(2)}, u32[]{:S(2)}) %collective-permute-start) | collective-permute-done | bytes 6176 | tf_op jit(solution)/shard_map/ppermute | solution.py:25
  12.7 1.2 %pad_maximum_fusion.5 = bf16[4,1536]{1,0:T(4,128)(2,1)S(1)} fusion(bf16[2,1536]{1,0:T(2,128)(2,1)S(1)} %collective-permute-done, bf16[2,1536]{1,0:T(2,128)(2,1)} %bitcast.24), kind=kLoop, calls=%fused_computation.9 | loop fusion | flops 24576 | bytes 24576 | tf_op jit(solution)/shard_map/concatenate | solution.py:31
  14.0 2.4 %collective-permute-start.1 = (bf16[4,1536]{1,0:T(4,128)(2,1)S(1)}, bf16[4,1536]{1,0:T(4,128)(2,1)S(1)}, u32[]{:S(2)}, u32[]{:S(2)}) collective-permute-start(bf16[4,1536]{1,0:T(4,128)(2,1)S(1)} %pad_maximum_fusion.5), channel_id=1, source_target_pairs={{0,4},{2,6},{4,0},{6,2},{8,12},{10,14},{12,8},{14,10},{1,5},{3,7},... | collective-permute-start | bytes 36872 | tf_op jit(solution)/shard_map/ppermute | solution.py:25
  16.4 1.7 %collective-permute-done.1 = bf16[4,1536]{1,0:T(4,128)(2,1)S(1)} collective-permute-done((bf16[4,1536]{1,0:T(4,128)(2,1)S(1)}, bf16[4,1536]{1,0:T(4,128)(2,1)S(1)}, u32[]{:S(2)}, u32[]{:S(2)}) %collective-permute-start.1) | collective-permute-done | bytes 12320 | tf_op jit(solution)/shard_map/ppermute | solution.py:25
  18.8 3.1 %collective-permute-start.2 = (bf16[8,1536]{1,0:T(8,128)(2,1)S(1)}, bf16[8,1536]{1,0:T(8,128)(2,1)S(1)}, u32[]{:S(2)}, u32[]{:S(2)}) collective-permute-start(bf16[8,1536]{1,0:T(8,128)(2,1)S(1)} %pad_maximum_fusion.3), channel_id=1, source_target_pairs={{0,8},{2,10},{4,12},{6,14},{8,0},{10,2},{12,4},{14,6},{1,9},{3,11}... | collective-permute-start | bytes 73736 | tf_op jit(solution)/shard_map/ppermute | solution.py:25
  27.7 3.9 %shard_map.121 = (f32[16,1536]{1,0:T(8,128)S(1)}, f32[16,256]{1,0:T(8,128)S(1)}, bf16[16,1664]{1,0:T(8,128)(2,1)S(1)}) custom-call(bf16[16,1536]{1,0:T(8,128)(2,1)S(1)} %pad_maximum_fusion.1.query_ref, bf16[2,64,1536]{2,1,0:T(8,128)(2,1)S(1)} %bitcast.12, bf16[2,64,1536]{2,1,0:T(8,128)(2,1)S(1)} %bitcast.13, bf16[2,1536]{1,0:T(2,128)(2,1)S(1)} %bitcast.14, ...), custom_call_target="tpu_custom_call" | custom-call | tf_op jit(solution)/shard_map/pallas_call | solution.py:37
  31.7 1.9 %collective-permute-start.3 = (bf16[16,1664]{1,0:T(8,128)(2,1)S(1)}, bf16[16,1664]{1,0:T(8,128)(2,1)S(1)}, u32[]{:S(2)}, u32[]{:S(2)}) collective-permute-start(bf16[16,1664]{1,0:T(8,128)(2,1)S(1)} %get-tuple-element.16), channel_id=1, source_target_pairs={{0,2},{2,0},{4,6},{6,4},{8,10},{10,8},{12,14},{14,12},{1,3},{3,1},... | collective-permute-start | bytes 159752 | tf_op jit(solution)/shard_map/ppermute | solution.py:25
  33.6 2.3 %collective-permute-done.3.pay_ref = bf16[16,1664]{1,0:T(8,128)(2,1)S(1)} collective-permute-done((bf16[16,1664]{1,0:T(8,128)(2,1)S(1)}, bf16[16,1664]{1,0:T(8,128)(2,1)S(1)}, u32[]{:S(2)}, u32[]{:S(2)}) %collective-permute-start.3) | collective-permute-done | bytes 53280 | tf_op jit(solution)/shard_map/ppermute | solution.py:25
  36.2 2.0 %collective-permute-start.4 = (bf16[16,1664]{1,0:T(8,128)(2,1)S(1)}, bf16[16,1664]{1,0:T(8,128)(2,1)S(1)}, u32[]{:S(2)}, u32[]{:S(2)}) collective-permute-start(bf16[16,1664]{1,0:T(8,128)(2,1)S(1)} %get-tuple-element.19), channel_id=1, source_target_pairs={{0,4},{2,6},{4,0},{6,2},{8,12},{10,14},{12,8},{14,10},{1,5},{3,7},... | collective-permute-start | bytes 159752 | tf_op jit(solution)/shard_map/ppermute | solution.py:25
  38.1 2.2 %collective-permute-done.4.pay_ref = bf16[16,1664]{1,0:T(8,128)(2,1)S(1)} collective-permute-done((bf16[16,1664]{1,0:T(8,128)(2,1)S(1)}, bf16[16,1664]{1,0:T(8,128)(2,1)S(1)}, u32[]{:S(2)}, u32[]{:S(2)}) %collective-permute-start.4) | collective-permute-done | bytes 53280 | tf_op jit(solution)/shard_map/ppermute | solution.py:25
  40.7 3.3 %collective-permute-start.5 = (bf16[16,1664]{1,0:T(8,128)(2,1)S(1)}, bf16[16,1664]{1,0:T(8,128)(2,1)S(1)}, u32[]{:S(2)}, u32[]{:S(2)}) collective-permute-start(bf16[16,1664]{1,0:T(8,128)(2,1)S(1)} %get-tuple-element.22), channel_id=1, source_target_pairs={{0,8},{2,10},{4,12},{6,14},{8,0},{10,2},{12,4},{14,6},{1,9},{3,11}... | collective-permute-start | bytes 159752 | tf_op jit(solution)/shard_map/ppermute | solution.py:25
  44.0 2.8 %collective-permute-done.5.pay_ref = bf16[16,1664]{1,0:T(8,128)(2,1)S(1)} collective-permute-done((bf16[16,1664]{1,0:T(8,128)(2,1)S(1)}, bf16[16,1664]{1,0:T(8,128)(2,1)S(1)}, u32[]{:S(2)}, u32[]{:S(2)}) %collective-permute-start.5) | collective-permute-done | bytes 53280 | tf_op jit(solution)/shard_map/ppermute | solution.py:25
  47.1 2.3 %copy-done.2 = bf16[2,1536,768]{2,1,0:T(8,128)(2,1)S(1)} copy-done((bf16[2,1536,768]{2,1,0:T(8,128)(2,1)S(1)}, bf16[2,1536,768]{2,1,0:T(8,128)(2,1)}, u32[]{:S(2)}) %copy-start.2) | copy-done | bytes 4718616
  50.1 1.2 %collective-permute-done.6.other_ref = f32[8,768]{1,0:T(8,128)S(1)} collective-permute-done((f32[8,768]{1,0:T(8,128)S(1)}, f32[8,768]{1,0:T(8,128)S(1)}, u32[]{:S(2)}, u32[]{:S(2)}) %collective-permute-start.6) | collective-permute-done | bytes 24608 | tf_op jit(solution)/shard_map/ppermute | solution.py:25
  52.6 3.1 %collective-permute-start.7 = (bf16[1,8,768]{2,1,0:T(8,128)(2,1)}, bf16[1,8,768]{2,1,0:T(8,128)(2,1)S(1)}, u32[]{:S(2)}, u32[]{:S(2)}) collective-permute-start(bf16[1,8,768]{2,1,0:T(8,128)(2,1)} %bitcast.18), channel_id=1, source_target_pairs={{0,2},{2,0},{4,6},{6,4},{8,10},{10,8},{12,14},{14,12},{1,3},{3,1},... | collective-permute-start | bytes 36872 | tf_op jit(solution)/shard_map/ppermute | solution.py:25
  55.8 2.1 %collective-permute-done.7 = bf16[1,8,768]{2,1,0:T(8,128)(2,1)S(1)} collective-permute-done((bf16[1,8,768]{2,1,0:T(8,128)(2,1)}, bf16[1,8,768]{2,1,0:T(8,128)(2,1)S(1)}, u32[]{:S(2)}, u32[]{:S(2)}) %collective-permute-start.7) | collective-permute-done | bytes 12320 | tf_op jit(solution)/shard_map/ppermute | solution.py:25
  58.6 2.7 %collective-permute-start.8 = (bf16[2,8,768]{2,1,0:T(8,128)(2,1)S(1)}, bf16[2,8,768]{2,1,0:T(8,128)(2,1)S(1)}, u32[]{:S(2)}, u32[]{:S(2)}) collective-permute-start(bf16[2,8,768]{2,1,0:T(8,128)(2,1)S(1)} %pad_maximum_fusion.4), channel_id=1, source_target_pairs={{0,4},{2,6},{4,0},{6,2},{8,12},{10,14},{12,8},{14,10},{1,5},{3,7},... | collective-permute-start | bytes 73736 | tf_op jit(solution)/shard_map/ppermute | solution.py:25
  61.3 2.2 %collective-permute-done.8 = bf16[2,8,768]{2,1,0:T(8,128)(2,1)S(1)} collective-permute-done((bf16[2,8,768]{2,1,0:T(8,128)(2,1)S(1)}, bf16[2,8,768]{2,1,0:T(8,128)(2,1)S(1)}, u32[]{:S(2)}, u32[]{:S(2)}) %collective-permute-start.8) | collective-permute-done | bytes 24608 | tf_op jit(solution)/shard_map/ppermute | solution.py:25
  64.2 3.2 %collective-permute-start.9 = (bf16[4,8,768]{2,1,0:T(8,128)(2,1)S(1)}, bf16[4,8,768]{2,1,0:T(8,128)(2,1)S(1)}, u32[]{:S(2)}, u32[]{:S(2)}) collective-permute-start(bf16[4,8,768]{2,1,0:T(8,128)(2,1)S(1)} %pad_maximum_fusion.2), channel_id=1, source_target_pairs={{0,8},{2,10},{4,12},{6,14},{8,0},{10,2},{12,4},{14,6},{1,9},{3,11}... | collective-permute-start | bytes 147464 | tf_op jit(solution)/shard_map/ppermute | solution.py:25
  67.4 5.5 %collective-permute-done.9 = bf16[4,8,768]{2,1,0:T(8,128)(2,1)S(1)} collective-permute-done((bf16[4,8,768]{2,1,0:T(8,128)(2,1)S(1)}, bf16[4,8,768]{2,1,0:T(8,128)(2,1)S(1)}, u32[]{:S(2)}, u32[]{:S(2)}) %collective-permute-start.9) | collective-permute-done | bytes 49184 | tf_op jit(solution)/shard_map/ppermute | solution.py:25
  73.7 6.4 %copy-done.1 = bf16[6144,1536]{1,0:T(8,128)(2,1)S(1)} copy-done((bf16[6144,1536]{1,0:T(8,128)(2,1)S(1)}, bf16[6144,1536]{1,0:T(8,128)(2,1)}, u32[]{:S(2)}) %copy-start.1) | copy-done | bytes 18874392
  80.0 2.5 %shard_map.127.act_ref = bf16[8,1536]{1,0:T(8,128)(2,1)S(1)} custom-call(bf16[8,8,768]{2,1,0:T(8,128)(2,1)S(1)} %pad_maximum_fusion.hidden_ref, bf16[6144,1536]{1,0:T(8,128)(2,1)S(1)} %copy-done.1), custom_call_target="tpu_custom_call" | custom-call | tf_op jit(solution)/shard_map/pallas_call | solution.py:37
  82.7 1.4 %shard_map.128.rest_0_ = f32[8,3072]{1,0:T(8,128)S(1)} custom-call(bf16[8,1536]{1,0:T(8,128)(2,1)S(1)} %shard_map.127.act_ref, bf16[3072,3072]{1,0:T(8,128)(2,1)S(1)} %copy-done), custom_call_target="tpu_custom_call" | custom-call | tf_op jit(solution)/shard_map/pallas_call | solution.py:37
  84.1 1.4 %shard_map.129 = (f32[4,3072]{1,0:T(4,128)S(1)}, f32[4,3072]{1,0:T(4,128)S(1)}) custom-call(bf16[8,1536]{1,0:T(8,128)(2,1)S(1)} %collective-permute-done.10.act_ref, bf16[3072,3072]{1,0:T(8,128)(2,1)S(1)} %copy-done, f32[8,3072]{1,0:T(8,128)S(1)} %shard_map.128.rest_0_), custom_call_target="tpu_custom_call" | custom-call | tf_op jit(solution)/shard_map/pallas_call | solution.py:37
  85.5 2.4 %collective-permute-start.11 = (f32[4,3072]{1,0:T(4,128)S(1)}, f32[4,3072]{1,0:T(4,128)S(1)}, u32[]{:S(2)}, u32[]{:S(2)}) collective-permute-start(f32[4,3072]{1,0:T(4,128)S(1)} %get-tuple-element.24), channel_id=1, source_target_pairs={{0,2},{2,0},{4,6},{6,4},{8,10},{10,8},{12,14},{14,12},{1,3},{3,1},... | collective-permute-start | bytes 147464 | tf_op jit(solution)/shard_map/ppermute | solution.py:25
  87.9 2.4 %collective-permute-done.11 = f32[4,3072]{1,0:T(4,128)S(1)} collective-permute-done((f32[4,3072]{1,0:T(4,128)S(1)}, f32[4,3072]{1,0:T(4,128)S(1)}, u32[]{:S(2)}, u32[]{:S(2)}) %collective-permute-start.11) | collective-permute-done | bytes 49184 | tf_op jit(solution)/shard_map/ppermute | solution.py:25
  90.6 3.7 %collective-permute-done.12 = f32[2,3072]{1,0:T(2,128)S(1)} collective-permute-done((f32[2,3072]{1,0:T(2,128)S(1)}, f32[2,3072]{1,0:T(2,128)S(1)}, u32[]{:S(2)}, u32[]{:S(2)}) %collective-permute-start.12) | collective-permute-done | bytes 24608 | tf_op jit(solution)/shard_map/ppermute | solution.py:25
  94.3 1.7 %collective-permute-start.13 = (f32[1,3072]{1,0:T(1,128)S(1)}, f32[1,3072]{1,0:T(1,128)S(1)}, u32[]{:S(2)}, u32[]{:S(2)}) collective-permute-start(f32[1,3072]{1,0:T(1,128)S(1)} %slice.19), channel_id=1, source_target_pairs={{0,8},{2,10},{4,12},{6,14},{8,0},{10,2},{12,4},{14,6},{1,9},{3,11}... | collective-permute-start | bytes 36872 | tf_op jit(solution)/shard_map/ppermute | solution.py:25
  96.6 2.3 %collective-permute-done.13 = f32[1,3072]{1,0:T(1,128)S(1)} collective-permute-done((f32[1,3072]{1,0:T(1,128)S(1)}, f32[1,3072]{1,0:T(1,128)S(1)}, u32[]{:S(2)}, u32[]{:S(2)}) %collective-permute-start.13) | collective-permute-done | bytes 12320 | tf_op jit(solution)/shard_map/ppermute | solution.py:25
  99.6 1.9 %copy-done.3 = bf16[8,2,64,1536]{3,2,1,0:T(8,128)(2,1)S(1)} copy-done((bf16[8,2,64,1536]{3,2,1,0:T(8,128)(2,1)S(1)}, bf16[8,2,64,1536]{3,2,1,0:T(8,128)(2,1)}, u32[]{:S(2)}) %copy-start.3) | copy-done | bytes 3145752
  101.5 1.4 %shard_map.130 = bf16[2,64,1536]{2,1,0:T(8,128)(2,1)} custom-call(s32[1]{0:T(128)} %bitcast.8.parent_ref, s32[1]{0:T(128)S(6)} %copy.13.lengths_ref.length_ref, bf16[8,2,64,1536]{3,2,1,0:T(8,128)(2,1)S(1)} %copy-done.3, bf16[2,1536]{1,0:T(2,128)(2,1)S(1)} %bitcast.15), custom_call_target="tpu_custom_call" | custom-call | tf_op jit(solution)/shard_map/pallas_call | solution.py:232
  (43 shorter events, 13.3 us)
Async XLA Ops:
  7.2 92.4 %all-gather.2.cloned.1.call-start = ((), (), s32[]{:S(2)}) async-start(), calls=%async_computation | async-start | bytes 3538944 | tf_op jit(solution)/shard_map/all_gather | solution.py:335
  7.9 74.8 %copy-start = (bf16[3072,3072]{1,0:T(8,128)(2,1)S(1)}, bf16[3072,3072]{1,0:T(8,128)(2,1)}, u32[]{:S(2)}) copy-start(bf16[3072,3072]{1,0:T(8,128)(2,1)} %weight_ref.7) | copy-start | bytes 56623108
  7.9 4.8 %collective-permute-start = (bf16[2,1536]{1,0:T(2,128)(2,1)}, bf16[2,1536]{1,0:T(2,128)(2,1)S(1)}, u32[]{:S(2)}, u32[]{:S(2)}) collective-permute-start(bf16[2,1536]{1,0:T(2,128)(2,1)} %bitcast.23), channel_id=1, source_target_pairs={{0,2},{2,0},{4,6},{6,4},{8,10},{10,8},{12,14},{14,12},{1,3},{3,1},... | collective-permute-start | bytes 18440 | tf_op jit(solution)/shard_map/ppermute | solution.py:25
  14.0 4.1 %collective-permute-start.1 = (bf16[4,1536]{1,0:T(4,128)(2,1)S(1)}, bf16[4,1536]{1,0:T(4,128)(2,1)S(1)}, u32[]{:S(2)}, u32[]{:S(2)}) collective-permute-start(bf16[4,1536]{1,0:T(4,128)(2,1)S(1)} %pad_maximum_fusion.5), channel_id=1, source_target_pairs={{0,4},{2,6},{4,0},{6,2},{8,12},{10,14},{12,8},{14,10},{1,5},{3,7},... | collective-permute-start | bytes 36872 | tf_op jit(solution)/shard_map/ppermute | solution.py:25
  18.8 4.9 %collective-permute-start.2 = (bf16[8,1536]{1,0:T(8,128)(2,1)S(1)}, bf16[8,1536]{1,0:T(8,128)(2,1)S(1)}, u32[]{:S(2)}, u32[]{:S(2)}) collective-permute-start(bf16[8,1536]{1,0:T(8,128)(2,1)S(1)} %pad_maximum_fusion.3), channel_id=1, source_target_pairs={{0,8},{2,10},{4,12},{6,14},{8,0},{10,2},{12,4},{14,6},{1,9},{3,11}... | collective-permute-start | bytes 73736 | tf_op jit(solution)/shard_map/ppermute | solution.py:25
  24.4 1.0 copy-start.4
  25.4 1.0 copy-start.5
  26.4 0.7 copy-start.6
  27.1 0.7 copy-start.9
  31.7 4.2 %collective-permute-start.3 = (bf16[16,1664]{1,0:T(8,128)(2,1)S(1)}, bf16[16,1664]{1,0:T(8,128)(2,1)S(1)}, u32[]{:S(2)}, u32[]{:S(2)}) collective-permute-start(bf16[16,1664]{1,0:T(8,128)(2,1)S(1)} %get-tuple-element.16), channel_id=1, source_target_pairs={{0,2},{2,0},{4,6},{6,4},{8,10},{10,8},{12,14},{14,12},{1,3},{3,1},... | collective-permute-start | bytes 159752 | tf_op jit(solution)/shard_map/ppermute | solution.py:25
  36.2 4.2 %collective-permute-start.4 = (bf16[16,1664]{1,0:T(8,128)(2,1)S(1)}, bf16[16,1664]{1,0:T(8,128)(2,1)S(1)}, u32[]{:S(2)}, u32[]{:S(2)}) collective-permute-start(bf16[16,1664]{1,0:T(8,128)(2,1)S(1)} %get-tuple-element.19), channel_id=1, source_target_pairs={{0,4},{2,6},{4,0},{6,2},{8,12},{10,14},{12,8},{14,10},{1,5},{3,7},... | collective-permute-start | bytes 159752 | tf_op jit(solution)/shard_map/ppermute | solution.py:25
  40.7 6.1 %collective-permute-start.5 = (bf16[16,1664]{1,0:T(8,128)(2,1)S(1)}, bf16[16,1664]{1,0:T(8,128)(2,1)S(1)}, u32[]{:S(2)}, u32[]{:S(2)}) collective-permute-start(bf16[16,1664]{1,0:T(8,128)(2,1)S(1)} %get-tuple-element.22), channel_id=1, source_target_pairs={{0,8},{2,10},{4,12},{6,14},{8,0},{10,2},{12,4},{14,6},{1,9},{3,11}... | collective-permute-start | bytes 159752 | tf_op jit(solution)/shard_map/ppermute | solution.py:25
  47.1 2.4 %copy-start.2 = (bf16[2,1536,768]{2,1,0:T(8,128)(2,1)S(1)}, bf16[2,1536,768]{2,1,0:T(8,128)(2,1)}, u32[]{:S(2)}) copy-start(bf16[2,1536,768]{2,1,0:T(8,128)(2,1)} %weight_ref.4) | copy-start | bytes 14155780
  50.1 1.3 %collective-permute-start.6 = (f32[8,768]{1,0:T(8,128)S(1)}, f32[8,768]{1,0:T(8,128)S(1)}, u32[]{:S(2)}, u32[]{:S(2)}) collective-permute-start(f32[8,768]{1,0:T(8,128)S(1)} %shard_map.125.own_ref), channel_id=1, source_target_pairs={{0,1},{1,0},{2,3},{3,2},{4,5},{5,4},{6,7},{7,6},{8,9},{9,8},{10,11... | collective-permute-start | bytes 73736 | tf_op jit(solution)/shard_map/ppermute | solution.py:25
  51.3 0.7 copy-start.8
  52.6 5.2 %collective-permute-start.7 = (bf16[1,8,768]{2,1,0:T(8,128)(2,1)}, bf16[1,8,768]{2,1,0:T(8,128)(2,1)S(1)}, u32[]{:S(2)}, u32[]{:S(2)}) collective-permute-start(bf16[1,8,768]{2,1,0:T(8,128)(2,1)} %bitcast.18), channel_id=1, source_target_pairs={{0,2},{2,0},{4,6},{6,4},{8,10},{10,8},{12,14},{14,12},{1,3},{3,1},... | collective-permute-start | bytes 36872 | tf_op jit(solution)/shard_map/ppermute | solution.py:25
  58.6 4.9 %collective-permute-start.8 = (bf16[2,8,768]{2,1,0:T(8,128)(2,1)S(1)}, bf16[2,8,768]{2,1,0:T(8,128)(2,1)S(1)}, u32[]{:S(2)}, u32[]{:S(2)}) collective-permute-start(bf16[2,8,768]{2,1,0:T(8,128)(2,1)S(1)} %pad_maximum_fusion.4), channel_id=1, source_target_pairs={{0,4},{2,6},{4,0},{6,2},{8,12},{10,14},{12,8},{14,10},{1,5},{3,7},... | collective-permute-start | bytes 73736 | tf_op jit(solution)/shard_map/ppermute | solution.py:25
  64.2 8.7 %collective-permute-start.9 = (bf16[4,8,768]{2,1,0:T(8,128)(2,1)S(1)}, bf16[4,8,768]{2,1,0:T(8,128)(2,1)S(1)}, u32[]{:S(2)}, u32[]{:S(2)}) collective-permute-start(bf16[4,8,768]{2,1,0:T(8,128)(2,1)S(1)} %pad_maximum_fusion.2), channel_id=1, source_target_pairs={{0,8},{2,10},{4,12},{6,14},{8,0},{10,2},{12,4},{14,6},{1,9},{3,11}... | collective-permute-start | bytes 147464 | tf_op jit(solution)/shard_map/ppermute | solution.py:25
  73.6 6.4 %copy-start.1 = (bf16[6144,1536]{1,0:T(8,128)(2,1)S(1)}, bf16[6144,1536]{1,0:T(8,128)(2,1)}, u32[]{:S(2)}) copy-start(bf16[6144,1536]{1,0:T(8,128)(2,1)} %weight_ref.5) | copy-start | bytes 56623108
  82.6 13.5 %copy-start.10 = (s32[1,8]{1,0:T(1,128)S(1)}, s32[1,8]{1,0:T(1,128)}, u32[]{:S(2)}) copy-start(s32[1,8]{1,0:T(1,128)} %parents_ref.1) | copy-start | bytes 100
  82.6 17.0 %copy-start.7 = (bf16[1,1,2,1536]{3,2,1,0:T(2,128)(2,1)S(1)}, bf16[1,1,2,1536]{3,2,1,0:T(2,128)(2,1)}, u32[]{:S(2)}) copy-start(bf16[1,1,2,1536]{3,2,1,0:T(2,128)(2,1)} %param.13) | copy-start | bytes 18436
  82.6 1.5 %collective-permute-start.10 = (bf16[8,1536]{1,0:T(8,128)(2,1)S(1)}, bf16[8,1536]{1,0:T(8,128)(2,1)S(1)}, u32[]{:S(2)}, u32[]{:S(2)}) collective-permute-start(bf16[8,1536]{1,0:T(8,128)(2,1)S(1)} %shard_map.127.act_ref), channel_id=1, source_target_pairs={{0,1},{1,0},{2,3},{3,2},{4,5},{5,4},{6,7},{7,6},{8,9},{9,8},{10,11... | collective-permute-start | bytes 73736 | tf_op jit(solution)/shard_map/ppermute | solution.py:25
  85.5 4.8 %collective-permute-start.11 = (f32[4,3072]{1,0:T(4,128)S(1)}, f32[4,3072]{1,0:T(4,128)S(1)}, u32[]{:S(2)}, u32[]{:S(2)}) collective-permute-start(f32[4,3072]{1,0:T(4,128)S(1)} %get-tuple-element.24), channel_id=1, source_target_pairs={{0,2},{2,0},{4,6},{6,4},{8,10},{10,8},{12,14},{14,12},{1,3},{3,1},... | collective-permute-start | bytes 147464 | tf_op jit(solution)/shard_map/ppermute | solution.py:25
  90.4 3.9 %collective-permute-start.12 = (f32[2,3072]{1,0:T(2,128)S(1)}, f32[2,3072]{1,0:T(2,128)S(1)}, u32[]{:S(2)}, u32[]{:S(2)}) collective-permute-start(f32[2,3072]{1,0:T(2,128)S(1)} %slice.17), channel_id=1, source_target_pairs={{0,4},{2,6},{4,0},{6,2},{8,12},{10,14},{12,8},{14,10},{1,5},{3,7},... | collective-permute-start | bytes 73736 | tf_op jit(solution)/shard_map/ppermute | solution.py:25
  94.3 4.7 %collective-permute-start.13 = (f32[1,3072]{1,0:T(1,128)S(1)}, f32[1,3072]{1,0:T(1,128)S(1)}, u32[]{:S(2)}, u32[]{:S(2)}) collective-permute-start(f32[1,3072]{1,0:T(1,128)S(1)} %slice.19), channel_id=1, source_target_pairs={{0,8},{2,10},{4,12},{6,14},{8,0},{10,2},{12,4},{14,6},{1,9},{3,11}... | collective-permute-start | bytes 36872 | tf_op jit(solution)/shard_map/ppermute | solution.py:25
  99.6 1.9 %copy-start.3 = (bf16[8,2,64,1536]{3,2,1,0:T(8,128)(2,1)S(1)}, bf16[8,2,64,1536]{3,2,1,0:T(8,128)(2,1)}, u32[]{:S(2)}) copy-start(bf16[8,2,64,1536]{3,2,1,0:T(8,128)(2,1)} %all-gather.2.cloned.1.call-done.row_ref) | copy-start | bytes 9437188
Sparse Core Ops, SparseCore 0:
  10.2 66.3 all-gather.1

commit v4 on v3

v4 whole, which is shorter than its diff:
```python
import functools
import math

import jax
import jax.numpy as jnp
from jax import lax
from jax.experimental import pallas as pl
from jax.experimental.pallas import tpu as pltpu
from jax.sharding import PartitionSpec as P

HD = 128
LANES = 128
SLOT = 16
BEAMS = 8
LOW = -1e30
MIB = 1024 * 1024

VM = pl.BlockSpec(memory_space=pltpu.VMEM)
SM = pl.BlockSpec(memory_space=pltpu.SMEM)
ANY = pl.BlockSpec(memory_space=pl.ANY)


def xor_permute(value, axis, bit):
    total = lax.axis_size(axis)
    return lax.ppermute(value, axis, [(i, i ^ bit) for i in range(total)])


def reverse(index, size):
    bits = size.bit_length() - 1
    return sum(((index >> k) & 1) << (bits - 1 - k) for k in range(bits))


def doubling(buffer, first, last, work):
    bit = last
    while True:
        bit //= 2
        other = xor_permute(buffer, "batch", bit)
        work(buffer)
        if bit == first:
            return buffer, other
        buffer = jnp.concatenate([buffer, other])


def call(kernel, out, *args, specs=None, vmem=8, flops=0, moved=0):
    return pl.pallas_call(
        kernel,
        out_shape=out,
        in_specs=specs or [VM] * len(args),
        out_specs=jax.tree.map(lambda _: VM, out),
        compiler_params=pltpu.CompilerParams(vmem_limit_bytes=vmem * MIB),
        cost_estimate=pl.CostEstimate(flops=flops, bytes_accessed=moved, transcendentals=0),
    )(*args)


def start_all(copies):
    for copy in copies:
        copy.start()
    for copy in copies:
        copy.wait()


def fetch_kernel(count, *refs):
    sems = refs[-1]
    outs = refs[-1 - count : -1]
    start_all([pltpu.make_async_copy(refs[i], outs[i], sems.at[i]) for i in range(count)])


def fetch(arrays, after):
    count = len(arrays)
    return pl.pallas_call(
        functools.partial(fetch_kernel, count),
        out_shape=[pltpu.VMEM(x.shape, x.dtype) for x in arrays],
        in_specs=[ANY] * (count + 1),
        out_specs=[VM] * count,
        scratch_shapes=[pltpu.SemaphoreType.DMA((count,))],
        compiler_params=pltpu.CompilerParams(vmem_limit_bytes=2 * MIB),
        cost_estimate=pl.CostEstimate(flops=0, bytes_accessed=2 * MIB, transcendentals=0),
    )(*arrays, after)


def fetch_rows_kernel(first, blocks, total, weight_ref, _, out_ref, sems):
    position = lax.axis_index("batch")
    depth = out_ref.shape[0] // blocks
    copies = []
    for k in range(blocks):
        start = pl.multiple_of(jnp.bitwise_xor(position, reverse(first + k, total)) * depth, depth)
        copies.append(
            pltpu.make_async_copy(
                weight_ref.at[pl.ds(start, depth), :], out_ref.at[pl.ds(k * depth, depth), :], sems.at[k]
            )
        )
    start_all(copies)


def fetch_rows(weight, first, blocks, total, after):
    depth = weight.shape[0] // total * blocks
    return pl.pallas_call(
        functools.partial(fetch_rows_kernel, first, blocks, total),
        out_shape=pltpu.VMEM((depth, weight.shape[1]), weight.dtype),
        in_specs=[ANY] * 2,
        out_specs=VM,
        scratch_shapes=[pltpu.SemaphoreType.DMA((blocks,))],
        compiler_params=pltpu.CompilerParams(vmem_limit_bytes=2 * MIB),
        cost_estimate=pl.CostEstimate(flops=0, bytes_accessed=2 * MIB, transcendentals=0),
    )(weight, after)


def split3(value):
    high = value.astype(jnp.bfloat16).astype(jnp.float32)
    rest = value - high
    middle = rest.astype(jnp.bfloat16).astype(jnp.float32)
    return high, middle, rest - middle


def export(num_ref, state_ref, pay_ref, peaks, totals):
    heads = num_ref.shape[1] // HD
    inverse = jnp.where(totals > 0.0, 1.0 / jnp.where(totals > 0.0, totals, 1.0), 0.0)
    for h in range(heads):
        cols = slice(h * HD, (h + 1) * HD)
        pay_ref[:, cols] = (num_ref[:, cols] * inverse[:, h : h + 1]).astype(jnp.bfloat16)
    state_ref[:, :LANES] = peaks
    state_ref[:, LANES:] = totals
    group = lax.broadcasted_iota(jnp.int32, peaks.shape, 1) // SLOT
    extra = jnp.zeros_like(peaks)
    for g, part in enumerate(split3(peaks) + split3(totals)):
        extra = jnp.where(group == g, pltpu.roll(part, g * SLOT, 1) if g else part, extra)
    pay_ref[:, heads * HD :] = extra.astype(jnp.bfloat16)


def attend_kernel(
    stride, near_ref, far_ref, cache_ref, memory_ref, new_ref, parents_ref, lengths_ref, num_ref, state_ref, pay_ref
):
    position = lax.axis_index("batch")
    own, request = position // stride, lax.rem(position, stride)
    length = lengths_ref[request]
    rows, width = num_ref.shape
    heads = width // HD
    past = cache_ref.shape[1]
    span = past + memory_ref.shape[1]
    f32, bf16 = jnp.float32, jnp.bfloat16

    to = lax.broadcasted_iota(jnp.int32, (rows, BEAMS), 0)
    source = lax.broadcasted_iota(jnp.int32, (rows, BEAMS), 1)

    def place_rows(piece_ref, first):
        beam = jnp.bitwise_xor(reverse(first + source // 2, BEAMS), own)
        order = jnp.where(to == (source % 2) * BEAMS + beam, 1.0, 0.0).astype(bf16)
        return jnp.dot(order, piece_ref[...], preferred_element_type=f32)

    query = (place_rows(near_ref, 0) + place_rows(far_ref, BEAMS // 2)).astype(bf16)

    row = lax.broadcasted_iota(jnp.int32, (rows, span), 0)
    slot = lax.broadcasted_iota(jnp.int32, (rows, span), 1)
    parent = jnp.zeros_like(row)
    for b in range(BEAMS):
        parent = jnp.where(row == b, parents_ref[0, b * stride + request], parent)
    in_past = ((slot < length) & (parent == own)) | ((slot == length) & (row == own))
    valid = jnp.where(row < BEAMS, jnp.where(in_past, 1, 0), jnp.where(slot >= past, 1, 0)) == 1
    fresh = lax.broadcasted_iota(jnp.int32, (past, HD), 0) == length
    lane = lax.broadcasted_iota(jnp.int32, (rows, LANES), 1)
    all_cols = [slice(h * HD, (h + 1) * HD) for h in range(heads)]

    def block(kind, cols):
        old = cache_ref[kind, :, cols].astype(f32)
        new = new_ref[kind : kind + 1, cols].astype(f32)
        merged = jnp.where(fresh, new, old).astype(bf16)
        return jnp.concatenate([merged, memory_ref[kind, :, cols]])

    scores = [
        lax.dot_general(
            query[:, cols], block(0, cols), (((1,), (1,)), ((), ())), preferred_element_type=f32
        )
        for cols in all_cols
    ]
    values = [block(1, cols) for cols in all_cols]
    scores = [jnp.where(valid, s * (1.0 / math.sqrt(HD)), LOW) for s in scores]
    tops = [jnp.max(s, axis=1, keepdims=True) for s in scores]
    weights = [jnp.where(valid, jnp.exp(s - t), 0.0) for s, t in zip(scores, tops)]
    sums = [jnp.sum(w, axis=1, keepdims=True) for w in weights]
    highs = [w.astype(bf16) for w in weights]
    lows = [(w - high.astype(f32)).astype(bf16) for w, high in zip(weights, highs)]
    both = [
        jnp.dot(jnp.concatenate([high, low]), v, preferred_element_type=f32)
        for high, low, v in zip(highs, lows, values)
    ]
    peaks = jnp.zeros((rows, LANES), f32)
    totals = jnp.zeros((rows, LANES), f32)
    for h, cols in enumerate(all_cols):
        num_ref[:, cols] = both[h][:rows] + both[h][rows:]
        peaks = jnp.where(lane == h, tops[h], peaks)
        totals = jnp.where(lane == h, sums[h], totals)
    export(num_ref, state_ref, pay_ref, peaks, totals)


def combine(num_ref, state_ref, pay_ref, out_ref):
    heads = num_ref.shape[1] // HD
    extra = pay_ref[:, heads * HD :].astype(jnp.float32)
    summed = extra + pltpu.roll(extra, LANES - SLOT, 1) + pltpu.roll(extra, LANES - 2 * SLOT, 1)
    other_total = pltpu.roll(summed, LANES - 3 * SLOT, 1)
    lane = lax.broadcasted_iota(jnp.int32, extra.shape, 1)
    used = lane < SLOT
    other_peak = jnp.where(used, summed, 0.0)
    other_total = jnp.where(used, other_total, 0.0)
    own_peak, own_total = state_ref[:, :LANES], state_ref[:, LANES:]
    peaks = jnp.maximum(own_peak, other_peak)
    own_factor = jnp.exp(own_peak - peaks)
    other_factor = jnp.exp(other_peak - peaks) * other_total
    totals = own_total * own_factor + other_factor
    for h in range(heads):
        cols = slice(h * HD, (h + 1) * HD)
        other = pay_ref[:, cols].astype(jnp.float32)
        out_ref[:, cols] = num_ref[:, cols] * own_factor[:, h : h + 1] + other * other_factor[:, h : h + 1]
    return peaks, totals


def merge_kernel(num_ref, state_ref, pay_ref, num_out, state_out, pay_out):
    peaks, totals = combine(num_ref, state_ref, pay_ref, num_out)
    export(num_out, state_out, pay_out, peaks, totals)


def finish_kernel(num_ref, state_ref, pay_ref, out_ref, num):
    _, totals = combine(num_ref, state_ref, pay_ref, num)
    for h in range(num.shape[1] // HD):
        cols = slice(h * HD, (h + 1) * HD)
        out_ref[:, cols] = (num[:, cols] / totals[:, h : h + 1]).astype(jnp.bfloat16)


def finish(num, state, pay):
    return pl.pallas_call(
        finish_kernel,
        out_shape=jax.ShapeDtypeStruct(num.shape, jnp.bfloat16),
        in_specs=[VM] * 3,
        out_specs=VM,
        scratch_shapes=[pltpu.VMEM(num.shape, jnp.float32)],
        compiler_params=pltpu.CompilerParams(vmem_limit_bytes=8 * MIB),
    )(num, state, pay)


def project_kernel(attended_ref, first_ref, second_ref, out_ref):
    rows = out_ref.shape[0]
    first = jnp.dot(attended_ref[...], first_ref[0], preferred_element_type=jnp.float32)
    second = jnp.dot(attended_ref[...], second_ref[0], preferred_element_type=jnp.float32)
    out_ref[...] = first[:rows] + second[rows:]


def add_kernel(own_ref, other_ref, residual_ref, out_ref):
    total = residual_ref[0].astype(jnp.float32) + (own_ref[...] + other_ref[...])
    out_ref[0] = total.astype(jnp.bfloat16)


def up_kernel(near_ref, far_ref, *refs):
    chunks, (hidden_ref, out_ref, sem) = refs[:-3], refs[-3:]
    half, _, depth = near_ref.shape
    per = 2 * half // len(chunks)
    copy = pltpu.make_async_copy(near_ref.at[0], hidden_ref, sem)
    copy.start()
    total = jnp.zeros(out_ref.shape, jnp.float32)
    for j in range(2 * half):
        block = near_ref[j] if j < half else far_ref[j - half]
        weight = chunks[j // per][pl.ds(j % per * depth, depth), :]
        total = total + jnp.dot(block, weight, preferred_element_type=jnp.float32)
    out_ref[...] = (0.5 * total * (1.0 + lax.erf(total * math.sqrt(0.5)))).astype(jnp.bfloat16)
    copy.wait()


def up(near, far, chunks, units):
    _, rows, columns = near.shape
    return pl.pallas_call(
        up_kernel,
        out_shape=(
            jax.ShapeDtypeStruct((rows, columns), jnp.bfloat16),
            jax.ShapeDtypeStruct((rows, units), jnp.bfloat16),
        ),
        in_specs=[VM] * (2 + len(chunks)),
        out_specs=(ANY, VM),
        scratch_shapes=[pltpu.SemaphoreType.DMA],
        compiler_params=pltpu.CompilerParams(vmem_limit_bytes=8 * MIB),
    )(near, far, *chunks)


def reorder(activation):
    rows = activation.shape[0]
    position = lax.axis_index("batch")
    to = lax.broadcasted_iota(jnp.int32, (rows, rows), 0)
    source = lax.broadcasted_iota(jnp.int32, (rows, rows), 1)
    order = jnp.where(source == jnp.bitwise_xor(reverse(to, rows), position), 1.0, 0.0).astype(jnp.bfloat16)
    return jnp.dot(order, activation, preferred_element_type=jnp.float32).astype(jnp.bfloat16)


def down_kernel(mine, act_ref, weight_ref, *rest):
    depth = act_ref.shape[1]
    side = lax.axis_index("tensor")
    start = pl.multiple_of((side if mine else 1 - side) * depth, depth)
    part = jnp.dot(
        reorder(act_ref[...]), weight_ref[pl.ds(start, depth), :], preferred_element_type=jnp.float32
    )
    if mine:
        rest[0][...] = part
        return
    before, keep_ref, send_ref = rest
    total = before[...] + part
    half = total.shape[0] // 2
    keep_ref[...] = total[:half]
    send_ref[...] = total[half:]


def ring(devices):
    if devices > BEAMS:
        return list(range(BEAMS))
    return list(range(0, BEAMS, 2)) + list(range(BEAMS - 1, 0, -2))


def place_kernel(stride, order, gathered_ref, new_ref, parents_ref, lengths_ref, out_ref, row, sem):
    position = lax.axis_index("batch")
    request = lax.rem(position, stride)
    parent = parents_ref[0, position]
    place = jnp.int32(0)
    for k, beam in enumerate(order):
        place = jnp.where(parent == beam, k, place)
    place = jnp.where(lax.axis_index("tensor") == 1, BEAMS - 1 - place, place)
    copy = pltpu.make_async_copy(gathered_ref.at[place], row, sem)
    copy.start()
    slots = lax.broadcasted_iota(jnp.int32, row.shape[1:], 0)
    copy.wait()
    for kind in range(2):
        old = row[kind].astype(jnp.float32)
        new = new_ref[kind : kind + 1, :].astype(jnp.float32)
        out_ref[kind] = jnp.where(slots == lengths_ref[request], new, old).astype(jnp.bfloat16)


def place(stride, order, gathered, new_kv, parents, lengths):
    return pl.pallas_call(
        functools.partial(place_kernel, stride, order),
        out_shape=jax.ShapeDtypeStruct(gathered.shape[1:], gathered.dtype),
        in_specs=[pl.BlockSpec(memory_space=pltpu.HBM), VM, SM, SM],
        out_specs=VM,
        scratch_shapes=[pltpu.VMEM(gathered.shape[1:], gathered.dtype), pltpu.SemaphoreType.DMA],
        compiler_params=pltpu.CompilerParams(vmem_limit_bytes=8 * MIB),
    )(gathered, new_kv, parents, lengths)


def body(
    init_cache,
    memory,
    queries,
    new_kv,
    residual,
    out_weight,
    up_weight,
    down_weight,
    parents,
    lengths,
):
    devices = lax.axis_size("batch")
    stride = devices // BEAMS
    position = lax.axis_index("batch")
    request = position % stride
    width = queries.shape[-1]
    rows = parents.shape[1]
    columns = out_weight.shape[2]
    hidden_units = up_weight.shape[1]
    out_columns = down_weight.shape[1]
    f32, bf16 = jnp.float32, jnp.bfloat16
    shape = jax.ShapeDtypeStruct
    down_weight = pltpu.with_memory_space_constraint(down_weight, pltpu.VMEM)
    pieces = 8
    local = {}
    chunks = []

    def load_operands(after):
        sources = (queries[0, 0], init_cache[0], memory[0], new_kv[0, 0], residual)
        local["all"] = fetch(sources, after)

    def load_out(kind):
        def work(after):
            local[kind] = fetch([out_weight[kind : kind + 1]], after)[0]

        return work

    def load_up(after):
        if len(chunks) < pieces:
            per = devices // pieces
            chunks.append(fetch_rows(up_weight, len(chunks) * per, per, devices, after))

    bit = devices // 2
    other = xor_permute(queries[0, 0], "batch", bit)
    load_operands(queries[0, 0])
    query, cache_row, memory_row, new_row, residual_row = local["all"]
    works = [load_out(0), load_out(1)]
    query = jnp.concatenate([query, other])
    query, far = doubling(query, stride, bit, lambda after: works.pop(0)(after))
    state_shapes = (
        shape((2 * BEAMS, width), f32),
        shape((2 * BEAMS, 2 * LANES), f32),
        shape((2 * BEAMS, width + LANES), bf16),
    )
    num, state, pay = call(
        functools.partial(attend_kernel, stride),
        state_shapes,
        query,
        far,
        cache_row,
        memory_row,
        new_row,
        parents,
        lengths,
        specs=[VM] * 5 + [SM] * 2,
    )
    bit = stride
    while True:
        arrived = xor_permute(pay, "batch", bit)
        load_up(pay)
        load_up(pay)
        bit *= 2
        if bit == devices:
            break
        num, state, pay = call(merge_kernel, state_shapes, num, state, arrived)
    attended = finish(num, state, arrived)
    if stride > 1:
        stacked = jnp.concatenate(doubling(attended[None], 1, stride, lambda after: None))
        wanted = reverse(jnp.bitwise_xor(jnp.arange(stride, dtype=jnp.int32), request), stride)
        stacked = stacked[wanted].reshape(stride, 2, BEAMS, width)
        attended = stacked.transpose(1, 2, 0, 3).reshape(2 * rows, width)

    partial = call(project_kernel, shape((rows, columns), f32), attended, local[0], local[1])
    other = xor_permute(partial, "tensor", 1)
    mine = call(add_kernel, pltpu.VMEM((1, rows, columns), bf16), partial, other, residual_row)
    near, far = doubling(mine, 1, devices, load_up)
    while len(chunks) < pieces:
        load_up(near)
    hidden, activation = up(near, far, chunks, hidden_units)
    arrived = xor_permute(activation, "tensor", 1)
    before = call(
        functools.partial(down_kernel, True), shape((rows, out_columns), f32), activation, down_weight
    )
    keep, send = call(
        functools.partial(down_kernel, False),
        (shape((rows // 2, out_columns), f32),) * 2,
        arrived,
        down_weight,
        before,
    )
    bit = 1
    while True:
        total = keep + xor_permute(send, "batch", bit)
        bit *= 2
        if bit == devices:
            break
        half = total.shape[0] // 2
        keep, send = total[:half], total[half:]
    ffn_row = total.astype(bf16)

    order = ring(devices)
    groups = []
    for r in range(stride):
        groups.append([(beam * stride + r) * 2 for beam in order])
        groups.append([(beam * stride + r) * 2 + 1 for beam in reversed(order)])
    gathered = lax.all_gather(init_cache[0], ("batch", "tensor"), axis_index_groups=groups)
    cache = place(stride, order, gathered, new_row, parents, lengths)
    return (hidden[None], ffn_row[None], cache[None])


def solution(mesh):
    placed = (
        P(("grp", "batch"), None, None, "tensor"),
        P(("grp", "batch"), None, None, "tensor"),
        P(None, ("grp", "batch"), None, "tensor"),
        P(None, ("grp", "batch"), None, "tensor"),
        P(None, "grp", "batch"),
        P(None, "tensor", "batch"),
        P(None, ("batch", "tensor")),
        P("batch", "tensor"),
        P(None, "grp"),
        P("grp"),
    )
    return jax.shard_map(
        body,
        mesh=mesh,
        in_specs=placed,
        out_specs=(
            P(None, "grp", "batch"),
            P(None, ("grp", "batch"), "tensor"),
            P(("grp", "batch"), None, None, "tensor"),
        ),
        check_vma=False,
    )
```

time: 110 us -> 91.8 us (0.83)
  starting transfers between devices: 29.2 us -> 11.6 us
  waiting for transfers between devices: 32 us -> 39.8 us
  other arithmetic: 6.11 us -> 0.7 us
  local copies, waits for them, and re-layouts: 14.7 us -> 12.3 us
    ppermute x14, starting transfers between devices: 29.2 us -> 11.6 us  [xor_permute(): return lax.ppermute(value, axis, [(i, i ^ bit) for i in range(total)])]
    ppermute x14, waiting for transfers between devices: 31.3 us -> 39.2 us  [xor_permute(): return lax.ppermute(value, axis, [(i, i ^ bit) for i in range(total)])]
    pallas_call x8 -> x7, Pallas kernels: 11.1 us -> 5.35 us  [call(): pl.pallas_call(kernel, out_shape=out, in_specs=specs or [VM] * len(args),...]
    unnamed x22 -> x28, local copies, waits for them, and re-layouts: 14.7 us -> 9.41 us
    pallas_call x1 -> x13, Pallas kernels: 1.36 us -> 6.37 us  [the longest x1 2.56 us: up(): pl.pallas_call(up_kernel, out_shape=(jax.ShapeDtypeStruct((rows, columns)...]
    concatenate x6 -> x4, other arithmetic: 4.83 us -> 0.06 us  [the longest x3 0.04 us: doubling(): buffer = jnp.concatenate([buffer, other])]
    slice x0 -> x1, local copies, waits for them, and re-layouts: none -> 2.88 us  [work(): local[kind] = fetch([out_weight[kind:kind + 1]], after)[0]]
  transfers between devices with their start and end apart: 15 -> 15, of which waited for: 13 -> 12; matrix products, arithmetic and copies ran while one was open for 6% -> 4% of each run, Pallas kernels for 10% -> 11%
where the time goes in v4:
time: 91.8 us; the launch traced here: 91.5 us
  waiting for transfers between devices  39.8 us (43%)
  between operations  15 us (16%)
  local copies, waits for them, and re-layouts  12.3 us (13%)
  Pallas kernels  12 us (13%)
  starting transfers between devices  11.6 us (13%)
    ppermute x14, waiting for transfers between devices, xor_permute(): return lax.ppermute(value, axis, [(i, i ^ bit) for i in range(total)])  39.2 us
    ppermute x14, starting transfers between devices, xor_permute(): return lax.ppermute(value, axis, [(i, i ^ bit) for i in range(total)])  11.6 us
    unnamed x28, local copies, waits for them, and re-layouts  9.41 us
    pallas_call x7, Pallas kernels, call(): pl.pallas_call(kernel, out_shape=out, in_specs=specs or [VM] * len(args),...  5.35 us
    slice x1, local copies, waits for them, and re-layouts, work(): local[kind] = fetch([out_weight[kind:kind + 1]], after)[0]  2.88 us
    pallas_call x1, Pallas kernels, up(): pl.pallas_call(up_kernel, out_shape=(jax.ShapeDtypeStruct((rows, columns)...  2.56 us
  transfers between devices with their start and end apart: 15, of which 12 were waited for; matrix products, arithmetic and copies ran while one was open for 4% of the time, Pallas kernels for 11%

profile of v4, /device:TPU:0, one launch (start us, length us, event | category | flops | bytes accessed | tf_op | source)
XLA Modules:
  0.0 91.5 jit_solution(16178498632716063711)
XLA Ops:
  7.2 0.7 all-gather.2.cloned.1.call-update
  7.9 4.1 %collective-permute-start = (bf16[2,1536]{1,0:T(2,128)(2,1)}, bf16[2,1536]{1,0:T(2,128)(2,1)S(1)}, u32[]{:S(2)}, u32[]{:S(2)}) collective-permute-start(bf16[2,1536]{1,0:T(2,128)(2,1)} %bitcast.12), channel_id=1, source_target_pairs={{0,8},{2,10},{4,12},{6,14},{8,0},{10,2},{12,4},{14,6},{1,9},{3,11}... | collective-permute-start | bytes 18440 | tf_op jit(solution)/shard_map/ppermute | solution.py:25
  12.0 1.0 %copy-done.2 = bf16[1,2,64,1536]{3,2,1,0:T(8,128)(2,1)S(1)} copy-done((bf16[1,2,64,1536]{3,2,1,0:T(8,128)(2,1)S(1)}, bf16[1,2,64,1536]{3,2,1,0:T(8,128)(2,1)}, u32[]{:S(2)}) %copy-start.2) | copy-done | bytes 393240
  13.0 1.0 %copy-done.3 = bf16[1,2,64,1536]{3,2,1,0:T(8,128)(2,1)S(1)} copy-done((bf16[1,2,64,1536]{3,2,1,0:T(8,128)(2,1)S(1)}, bf16[1,2,64,1536]{3,2,1,0:T(8,128)(2,1)}, u32[]{:S(2)}) %copy-start.3) | copy-done | bytes 393240
  14.0 0.7 copy-done.4
  14.7 0.7 copy-done.5
  15.4 0.7 copy-done.6
  16.6 1.6 %collective-permute-start.1 = (bf16[4,1536]{1,0:T(4,128)(2,1)S(1)}, bf16[4,1536]{1,0:T(4,128)(2,1)S(1)}, u32[]{:S(2)}, u32[]{:S(2)}) collective-permute-start(bf16[4,1536]{1,0:T(4,128)(2,1)S(1)} %pad_maximum_fusion.3.refs_1_), channel_id=1, source_target_pairs={{0,4},{2,6},{4,0},{6,2},{8,12},{10,14},{12,8},{14,10},{1,5},{3,7},... | collective-permute-start | bytes 36872 | tf_op jit(solution)/shard_map/ppermute | solution.py:25
  18.2 2.2 %collective-permute-done.1 = bf16[4,1536]{1,0:T(4,128)(2,1)S(1)} collective-permute-done((bf16[4,1536]{1,0:T(4,128)(2,1)S(1)}, bf16[4,1536]{1,0:T(4,128)(2,1)S(1)}, u32[]{:S(2)}, u32[]{:S(2)}) %collective-permute-start.1) | collective-permute-done | bytes 12320 | tf_op jit(solution)/shard_map/ppermute | solution.py:25
  20.5 1.6 %collective-permute-start.2 = (bf16[8,1536]{1,0:T(8,128)(2,1)S(1)}, bf16[8,1536]{1,0:T(8,128)(2,1)S(1)}, u32[]{:S(2)}, u32[]{:S(2)}) collective-permute-start(bf16[8,1536]{1,0:T(8,128)(2,1)S(1)} %pad_maximum_fusion.1.near_ref.refs_1_), channel_id=1, source_target_pairs={{0,2},{2,0},{4,6},{6,4},{8,10},{10,8},{12,14},{14,12},{1,3},{3,1},... | collective-permute-start | bytes 73736 | tf_op jit(solution)/shard_map/ppermute | solution.py:25
  22.7 2.2 %collective-permute-done.2.far_ref = bf16[8,1536]{1,0:T(8,128)(2,1)S(1)} collective-permute-done((bf16[8,1536]{1,0:T(8,128)(2,1)S(1)}, bf16[8,1536]{1,0:T(8,128)(2,1)S(1)}, u32[]{:S(2)}, u32[]{:S(2)}) %collective-permute-start.2) | collective-permute-done | bytes 24608 | tf_op jit(solution)/shard_map/ppermute | solution.py:25
  25.5 1.3 %shard_map.122 = (f32[16,1536]{1,0:T(8,128)S(1)}, f32[16,256]{1,0:T(8,128)S(1)}, bf16[16,1664]{1,0:T(8,128)(2,1)S(1)}) custom-call(bf16[8,1536]{1,0:T(8,128)(2,1)S(1)} %pad_maximum_fusion.1.near_ref.refs_1_, bf16[8,1536]{1,0:T(8,128)(2,1)S(1)} %collective-permute-done.2.far_ref, bf16[2,64,1536]{2,1,0:T(8,128)(2,1)S(1)} %get-tuple-element.22.cache_ref, ...), custom_call_target="tpu_custom_call" | custom-call | tf_op jit(solution)/shard_map/pallas_call | solution.py:45
  26.8 1.5 %collective-permute-start.3 = (bf16[16,1664]{1,0:T(8,128)(2,1)S(1)}, bf16[16,1664]{1,0:T(8,128)(2,1)S(1)}, u32[]{:S(2)}, u32[]{:S(2)}) collective-permute-start(bf16[16,1664]{1,0:T(8,128)(2,1)S(1)} %get-tuple-element.27._), channel_id=1, source_target_pairs={{0,2},{2,0},{4,6},{6,4},{8,10},{10,8},{12,14},{14,12},{1,3},{3,1},... | collective-permute-start | bytes 159752 | tf_op jit(solution)/shard_map/ppermute | solution.py:25
  28.3 3.8 %collective-permute-done.3.pay_ref = bf16[16,1664]{1,0:T(8,128)(2,1)S(1)} collective-permute-done((bf16[16,1664]{1,0:T(8,128)(2,1)S(1)}, bf16[16,1664]{1,0:T(8,128)(2,1)S(1)}, u32[]{:S(2)}, u32[]{:S(2)}) %collective-permute-start.3) | collective-permute-done | bytes 53280 | tf_op jit(solution)/shard_map/ppermute | solution.py:25
  32.5 5.4 %collective-permute-done.4.pay_ref = bf16[16,1664]{1,0:T(8,128)(2,1)S(1)} collective-permute-done((bf16[16,1664]{1,0:T(8,128)(2,1)S(1)}, bf16[16,1664]{1,0:T(8,128)(2,1)S(1)}, u32[]{:S(2)}, u32[]{:S(2)}) %collective-permute-start.4) | collective-permute-done | bytes 53280 | tf_op jit(solution)/shard_map/ppermute | solution.py:25
  38.3 2.9 %fusion.2 = (bf16[1,1536,768]{2,1,0:T(8,128)(2,1)S(1)}, bf16[1,1536,768]{2,1,0:T(8,128)(2,1)S(1)}) fusion(bf16[2,1536,768]{2,1,0:T(8,128)(2,1)} %param.15), kind=kLoop, calls=%fused_computation.8 | loop fusion | bytes 9437184 | tf_op jit(solution)/shard_map/slice | solution.py:376
  41.5 2.9 %collective-permute-done.5.pay_ref = bf16[16,1664]{1,0:T(8,128)(2,1)S(1)} collective-permute-done((bf16[16,1664]{1,0:T(8,128)(2,1)S(1)}, bf16[16,1664]{1,0:T(8,128)(2,1)S(1)}, u32[]{:S(2)}, u32[]{:S(2)}) %collective-permute-start.5) | collective-permute-done | bytes 53280 | tf_op jit(solution)/shard_map/ppermute | solution.py:25
  45.4 1.2 %collective-permute-done.6.other_ref = f32[8,768]{1,0:T(8,128)S(1)} collective-permute-done((f32[8,768]{1,0:T(8,128)S(1)}, f32[8,768]{1,0:T(8,128)S(1)}, u32[]{:S(2)}, u32[]{:S(2)}) %collective-permute-start.6) | collective-permute-done | bytes 24608 | tf_op jit(solution)/shard_map/ppermute | solution.py:25
  46.7 4.8 %collective-permute-done.7 = bf16[1,8,768]{2,1,0:T(8,128)(2,1)S(1)} collective-permute-done((bf16[1,8,768]{2,1,0:T(8,128)(2,1)S(1)}, bf16[1,8,768]{2,1,0:T(8,128)(2,1)S(1)}, u32[]{:S(2)}, u32[]{:S(2)}) %collective-permute-start.7) | collective-permute-done | bytes 12320 | tf_op jit(solution)/shard_map/ppermute | solution.py:25
  51.5 3.8 %collective-permute-done.8 = bf16[2,8,768]{2,1,0:T(8,128)(2,1)S(1)} collective-permute-done((bf16[2,8,768]{2,1,0:T(8,128)(2,1)S(1)}, bf16[2,8,768]{2,1,0:T(8,128)(2,1)S(1)}, u32[]{:S(2)}, u32[]{:S(2)}) %collective-permute-start.8) | collective-permute-done | bytes 24608 | tf_op jit(solution)/shard_map/ppermute | solution.py:25
  55.3 1.8 %collective-permute-start.9 = (bf16[4,8,768]{2,1,0:T(8,128)(2,1)S(1)}, bf16[4,8,768]{2,1,0:T(8,128)(2,1)S(1)}, u32[]{:S(2)}, u32[]{:S(2)}) collective-permute-start(bf16[4,8,768]{2,1,0:T(8,128)(2,1)S(1)} %pad_maximum_fusion.near_ref), channel_id=1, source_target_pairs={{0,2},{2,0},{4,6},{6,4},{8,10},{10,8},{12,14},{14,12},{1,3},{3,1},... | collective-permute-start | bytes 147464 | tf_op jit(solution)/shard_map/ppermute | solution.py:25
  58.7 0.8 collective-permute-done.9.far_ref
  59.5 2.6 %shard_map.138 = (bf16[8,768]{1,0:T(8,128)(2,1)}, bf16[8,1536]{1,0:T(8,128)(2,1)S(1)}) custom-call(bf16[4,8,768]{2,1,0:T(8,128)(2,1)S(1)} %pad_maximum_fusion.near_ref, bf16[4,8,768]{2,1,0:T(8,128)(2,1)S(1)} %collective-permute-done.9.far_ref, bf16[768,1536]{1,0:T(8,128)(2,1)S(1)} %shard_map.130.refs_0_, bf16[768,1536]{1,0:T(8,128)(2,1)S(1)} %shard_map.131.refs_1_, ...), custom_call_target="tpu_custom_call" | custom-call | tf_op jit(solution)/shard_map/pallas_call | solution.py:268
  62.5 1.2 %slice-done.3 = s8[4194304]{0:T(1024)(128)(4,1)S(1)} async-done(((s8[18874368]{0:T(1024)(128)(4,1)}), s8[4194304]{0:T(1024)(128)(4,1)S(1)}, s32[]{:S(2)}) %slice-start.3) | async-done | bytes 4194328
  63.7 1.2 %slice-done.4 = s8[4194304]{0:T(1024)(128)(4,1)S(1)} async-done(((s8[18874368]{0:T(1024)(128)(4,1)}), s8[4194304]{0:T(1024)(128)(4,1)S(1)}, s32[]{:S(2)}) %slice-start.4) | async-done | bytes 4194328
  64.9 1.4 %shard_map.139.rest_0_ = f32[8,3072]{1,0:T(8,128)S(1)} custom-call(bf16[8,1536]{1,0:T(8,128)(2,1)S(1)} %get-tuple-element.36.act_ref, bf16[3072,3072]{1,0:T(8,128)(2,1)S(1)} %bitcast.9), custom_call_target="tpu_custom_call" | custom-call | tf_op jit(solution)/shard_map/pallas_call | solution.py:45
  66.3 1.4 %shard_map.140 = (f32[4,3072]{1,0:T(4,128)S(1)}, f32[4,3072]{1,0:T(4,128)S(1)}) custom-call(bf16[8,1536]{1,0:T(8,128)(2,1)S(1)} %collective-permute-done.10.act_ref, bf16[3072,3072]{1,0:T(8,128)(2,1)S(1)} %bitcast.9, f32[8,3072]{1,0:T(8,128)S(1)} %shard_map.139.rest_0_), custom_call_target="tpu_custom_call" | custom-call | tf_op jit(solution)/shard_map/pallas_call | solution.py:45
  68.1 3.8 %collective-permute-done.11 = f32[4,3072]{1,0:T(4,128)S(1)} collective-permute-done((f32[4,3072]{1,0:T(4,128)S(1)}, f32[4,3072]{1,0:T(4,128)S(1)}, u32[]{:S(2)}, u32[]{:S(2)}) %collective-permute-start.11) | collective-permute-done | bytes 49184 | tf_op jit(solution)/shard_map/ppermute | solution.py:25
  72.0 3.8 %collective-permute-done.12 = f32[2,3072]{1,0:T(2,128)S(1)} collective-permute-done((f32[2,3072]{1,0:T(2,128)S(1)}, f32[2,3072]{1,0:T(2,128)S(1)}, u32[]{:S(2)}, u32[]{:S(2)}) %collective-permute-start.12) | collective-permute-done | bytes 24608 | tf_op jit(solution)/shard_map/ppermute | solution.py:25
  76.0 4.5 %collective-permute-done.13 = f32[1,3072]{1,0:T(1,128)S(1)} collective-permute-done((f32[1,3072]{1,0:T(1,128)S(1)}, f32[1,3072]{1,0:T(1,128)S(1)}, u32[]{:S(2)}, u32[]{:S(2)}) %collective-permute-start.13) | collective-permute-done | bytes 12320 | tf_op jit(solution)/shard_map/ppermute | solution.py:25
  81.1 1.9 %copy-done.1 = bf16[8,2,64,1536]{3,2,1,0:T(8,128)(2,1)S(1)} copy-done((bf16[8,2,64,1536]{3,2,1,0:T(8,128)(2,1)S(1)}, bf16[8,2,64,1536]{3,2,1,0:T(8,128)(2,1)}, u32[]{:S(2)}) %copy-start.1) | copy-done | bytes 3145752
  83.0 1.6 %shard_map.141 = bf16[2,64,1536]{2,1,0:T(8,128)(2,1)} custom-call(bf16[8,2,64,1536]{3,2,1,0:T(8,128)(2,1)S(1)} %copy-done.1, bf16[2,1536]{1,0:T(2,128)(2,1)S(1)} %get-tuple-element.24.new_ref, s32[1,8]{1,0:T(1,128)S(1)} %copy-done.8, s32[1]{0:T(128)S(6)} %copy.13.lengths_ref), custom_call_target="tpu_custom_call" | custom-call | tf_op jit(solution)/shard_map/pallas_call | solution.py:332
  (59 shorter events, 6.5 us)
Async XLA Ops:
  7.2 74.0 %all-gather.2.cloned.1.call-start = ((), (), s32[]{:S(2)}) async-start(), calls=%async_computation | async-start | bytes 3538944 | tf_op jit(solution)/shard_map/all_gather | solution.py:458
  7.9 8.6 %collective-permute-start = (bf16[2,1536]{1,0:T(2,128)(2,1)}, bf16[2,1536]{1,0:T(2,128)(2,1)S(1)}, u32[]{:S(2)}, u32[]{:S(2)}) collective-permute-start(bf16[2,1536]{1,0:T(2,128)(2,1)} %bitcast.12), channel_id=1, source_target_pairs={{0,8},{2,10},{4,12},{6,14},{8,0},{10,2},{12,4},{14,6},{1,9},{3,11}... | collective-permute-start | bytes 18440 | tf_op jit(solution)/shard_map/ppermute | solution.py:25
  12.0 1.0 %copy-start.2 = (bf16[1,2,64,1536]{3,2,1,0:T(8,128)(2,1)S(1)}, bf16[1,2,64,1536]{3,2,1,0:T(8,128)(2,1)}, u32[]{:S(2)}) copy-start(bf16[1,2,64,1536]{3,2,1,0:T(8,128)(2,1)} %param.10) | copy-start | bytes 1179652
  13.0 1.0 %copy-start.3 = (bf16[1,2,64,1536]{3,2,1,0:T(8,128)(2,1)S(1)}, bf16[1,2,64,1536]{3,2,1,0:T(8,128)(2,1)}, u32[]{:S(2)}) copy-start(bf16[1,2,64,1536]{3,2,1,0:T(8,128)(2,1)} %param.11) | copy-start | bytes 1179652
  14.0 0.7 copy-start.4
  14.7 0.7 copy-start.5
  15.4 0.7 copy-start.6
  16.6 3.9 %collective-permute-start.1 = (bf16[4,1536]{1,0:T(4,128)(2,1)S(1)}, bf16[4,1536]{1,0:T(4,128)(2,1)S(1)}, u32[]{:S(2)}, u32[]{:S(2)}) collective-permute-start(bf16[4,1536]{1,0:T(4,128)(2,1)S(1)} %pad_maximum_fusion.3.refs_1_), channel_id=1, source_target_pairs={{0,4},{2,6},{4,0},{6,2},{8,12},{10,14},{12,8},{14,10},{1,5},{3,7},... | collective-permute-start | bytes 36872 | tf_op jit(solution)/shard_map/ppermute | solution.py:25
  20.5 4.4 %collective-permute-start.2 = (bf16[8,1536]{1,0:T(8,128)(2,1)S(1)}, bf16[8,1536]{1,0:T(8,128)(2,1)S(1)}, u32[]{:S(2)}, u32[]{:S(2)}) collective-permute-start(bf16[8,1536]{1,0:T(8,128)(2,1)S(1)} %pad_maximum_fusion.1.near_ref.refs_1_), channel_id=1, source_target_pairs={{0,2},{2,0},{4,6},{6,4},{8,10},{10,8},{12,14},{14,12},{1,3},{3,1},... | collective-permute-start | bytes 73736 | tf_op jit(solution)/shard_map/ppermute | solution.py:25
  24.9 0.7 copy-start.7
  26.8 5.3 %collective-permute-start.3 = (bf16[16,1664]{1,0:T(8,128)(2,1)S(1)}, bf16[16,1664]{1,0:T(8,128)(2,1)S(1)}, u32[]{:S(2)}, u32[]{:S(2)}) collective-permute-start(bf16[16,1664]{1,0:T(8,128)(2,1)S(1)} %get-tuple-element.27._), channel_id=1, source_target_pairs={{0,2},{2,0},{4,6},{6,4},{8,10},{10,8},{12,14},{14,12},{1,3},{3,1},... | collective-permute-start | bytes 159752 | tf_op jit(solution)/shard_map/ppermute | solution.py:25
  32.4 5.5 %collective-permute-start.4 = (bf16[16,1664]{1,0:T(8,128)(2,1)S(1)}, bf16[16,1664]{1,0:T(8,128)(2,1)S(1)}, u32[]{:S(2)}, u32[]{:S(2)}) collective-permute-start(bf16[16,1664]{1,0:T(8,128)(2,1)S(1)} %get-tuple-element.30._), channel_id=1, source_target_pairs={{0,4},{2,6},{4,0},{6,2},{8,12},{10,14},{12,8},{14,10},{1,5},{3,7},... | collective-permute-start | bytes 159752 | tf_op jit(solution)/shard_map/ppermute | solution.py:25
  38.2 6.2 %collective-permute-start.5 = (bf16[16,1664]{1,0:T(8,128)(2,1)S(1)}, bf16[16,1664]{1,0:T(8,128)(2,1)S(1)}, u32[]{:S(2)}, u32[]{:S(2)}) collective-permute-start(bf16[16,1664]{1,0:T(8,128)(2,1)S(1)} %get-tuple-element.33._), channel_id=1, source_target_pairs={{0,8},{2,10},{4,12},{6,14},{8,0},{10,2},{12,4},{14,6},{1,9},{3,11}... | collective-permute-start | bytes 159752 | tf_op jit(solution)/shard_map/ppermute | solution.py:25
  38.3 18.8 %copy-start = (bf16[6144,1536]{1,0:T(8,128)(2,1)S(1)}, bf16[6144,1536]{1,0:T(8,128)(2,1)}, u32[]{:S(2)}) copy-start(bf16[6144,1536]{1,0:T(8,128)(2,1)} %weight_ref.17) | copy-start | bytes 56623108
  45.3 1.3 %collective-permute-start.6 = (f32[8,768]{1,0:T(8,128)S(1)}, f32[8,768]{1,0:T(8,128)S(1)}, u32[]{:S(2)}, u32[]{:S(2)}) collective-permute-start(f32[8,768]{1,0:T(8,128)S(1)} %shard_map.128.own_ref), channel_id=1, source_target_pairs={{0,1},{1,0},{2,3},{3,2},{4,5},{5,4},{6,7},{7,6},{8,9},{9,8},{10,11... | collective-permute-start | bytes 73736 | tf_op jit(solution)/shard_map/ppermute | solution.py:25
  46.6 4.9 %collective-permute-start.7 = (bf16[1,8,768]{2,1,0:T(8,128)(2,1)S(1)}, bf16[1,8,768]{2,1,0:T(8,128)(2,1)S(1)}, u32[]{:S(2)}, u32[]{:S(2)}) collective-permute-start(bf16[1,8,768]{2,1,0:T(8,128)(2,1)S(1)} %shard_map.129._), channel_id=1, source_target_pairs={{0,8},{2,10},{4,12},{6,14},{8,0},{10,2},{12,4},{14,6},{1,9},{3,11}... | collective-permute-start | bytes 36872 | tf_op jit(solution)/shard_map/ppermute | solution.py:25
  51.5 3.8 %collective-permute-start.8 = (bf16[2,8,768]{2,1,0:T(8,128)(2,1)S(1)}, bf16[2,8,768]{2,1,0:T(8,128)(2,1)S(1)}, u32[]{:S(2)}, u32[]{:S(2)}) collective-permute-start(bf16[2,8,768]{2,1,0:T(8,128)(2,1)S(1)} %pad_maximum_fusion.2._), channel_id=1, source_target_pairs={{0,4},{2,6},{4,0},{6,2},{8,12},{10,14},{12,8},{14,10},{1,5},{3,7},... | collective-permute-start | bytes 73736 | tf_op jit(solution)/shard_map/ppermute | solution.py:25
  55.3 4.2 %collective-permute-start.9 = (bf16[4,8,768]{2,1,0:T(8,128)(2,1)S(1)}, bf16[4,8,768]{2,1,0:T(8,128)(2,1)S(1)}, u32[]{:S(2)}, u32[]{:S(2)}) collective-permute-start(bf16[4,8,768]{2,1,0:T(8,128)(2,1)S(1)} %pad_maximum_fusion.near_ref), channel_id=1, source_target_pairs={{0,2},{2,0},{4,6},{6,4},{8,10},{10,8},{12,14},{14,12},{1,3},{3,1},... | collective-permute-start | bytes 147464 | tf_op jit(solution)/shard_map/ppermute | solution.py:25
  58.4 3.7 %slice-start = ((s8[18874368]{0:T(1024)(128)(4,1)}), s8[2097152]{0:T(1024)(128)(4,1)S(1)}, s32[]{:S(2)}) async-start(s8[18874368]{0:T(1024)(128)(4,1)} %bitcast.8), calls=%async_computation.1 | async-start | bytes 4194304
  58.4 3.7 %slice-start.1 = ((s8[18874368]{0:T(1024)(128)(4,1)}), s8[4194304]{0:T(1024)(128)(4,1)S(1)}, s32[]{:S(2)}) async-start(s8[18874368]{0:T(1024)(128)(4,1)} %bitcast.8), calls=%async_computation.2 | async-start | bytes 8388608
  58.4 4.0 %slice-start.2 = ((s8[18874368]{0:T(1024)(128)(4,1)}), s8[4194304]{0:T(1024)(128)(4,1)S(1)}, s32[]{:S(2)}) async-start(s8[18874368]{0:T(1024)(128)(4,1)} %bitcast.8), calls=%async_computation.3 | async-start | bytes 8388608
  58.7 5.1 %slice-start.3 = ((s8[18874368]{0:T(1024)(128)(4,1)}), s8[4194304]{0:T(1024)(128)(4,1)S(1)}, s32[]{:S(2)}) async-start(s8[18874368]{0:T(1024)(128)(4,1)} %bitcast.8), calls=%async_computation.4 | async-start | bytes 8388608
  58.7 6.3 %slice-start.4 = ((s8[18874368]{0:T(1024)(128)(4,1)}), s8[4194304]{0:T(1024)(128)(4,1)S(1)}, s32[]{:S(2)}) async-start(s8[18874368]{0:T(1024)(128)(4,1)} %bitcast.8), calls=%async_computation.5 | async-start | bytes 8388608
  62.1 4.3 %collective-permute-start.10 = (bf16[8,1536]{1,0:T(8,128)(2,1)S(1)}, bf16[8,1536]{1,0:T(8,128)(2,1)S(1)}, u32[]{:S(2)}, u32[]{:S(2)}) collective-permute-start(bf16[8,1536]{1,0:T(8,128)(2,1)S(1)} %get-tuple-element.36.act_ref), channel_id=1, source_target_pairs={{0,1},{1,0},{2,3},{3,2},{4,5},{5,4},{6,7},{7,6},{8,9},{9,8},{10,11... | collective-permute-start | bytes 73736 | tf_op jit(solution)/shard_map/ppermute | solution.py:25
  66.3 14.8 %copy-start.8 = (s32[1,8]{1,0:T(1,128)S(1)}, s32[1,8]{1,0:T(1,128)}, u32[]{:S(2)}) copy-start(s32[1,8]{1,0:T(1,128)} %parents_ref.3) | copy-start | bytes 100
  67.8 4.1 %collective-permute-start.11 = (f32[4,3072]{1,0:T(4,128)S(1)}, f32[4,3072]{1,0:T(4,128)S(1)}, u32[]{:S(2)}, u32[]{:S(2)}) collective-permute-start(f32[4,3072]{1,0:T(4,128)S(1)} %get-tuple-element.38), channel_id=1, source_target_pairs={{0,2},{2,0},{4,6},{6,4},{8,10},{10,8},{12,14},{14,12},{1,3},{3,1},... | collective-permute-start | bytes 147464 | tf_op jit(solution)/shard_map/ppermute | solution.py:25
  71.9 3.9 %collective-permute-start.12 = (f32[2,3072]{1,0:T(2,128)S(1)}, f32[2,3072]{1,0:T(2,128)S(1)}, u32[]{:S(2)}, u32[]{:S(2)}) collective-permute-start(f32[2,3072]{1,0:T(2,128)S(1)} %slice.25), channel_id=1, source_target_pairs={{0,4},{2,6},{4,0},{6,2},{8,12},{10,14},{12,8},{14,10},{1,5},{3,7},... | collective-permute-start | bytes 73736 | tf_op jit(solution)/shard_map/ppermute | solution.py:25
  75.9 4.7 %collective-permute-start.13 = (f32[1,3072]{1,0:T(1,128)S(1)}, f32[1,3072]{1,0:T(1,128)S(1)}, u32[]{:S(2)}, u32[]{:S(2)}) collective-permute-start(f32[1,3072]{1,0:T(1,128)S(1)} %slice.27), channel_id=1, source_target_pairs={{0,8},{2,10},{4,12},{6,14},{8,0},{10,2},{12,4},{14,6},{1,9},{3,11}... | collective-permute-start | bytes 36872 | tf_op jit(solution)/shard_map/ppermute | solution.py:25
  81.1 1.9 %copy-start.1 = (bf16[8,2,64,1536]{3,2,1,0:T(8,128)(2,1)S(1)}, bf16[8,2,64,1536]{3,2,1,0:T(8,128)(2,1)}, u32[]{:S(2)}) copy-start(bf16[8,2,64,1536]{3,2,1,0:T(8,128)(2,1)} %all-gather.2.cloned.1.call-done.gathered_ref) | copy-start | bytes 9437188
Sparse Core Ops, SparseCore 0:
  9.5 44.7 all-gather.1

commit v5 on v4

--- a/solution.py
+++ b/solution.py
@@ -14,6 +14,7 @@
 BEAMS = 8
 LOW = -1e30
 MIB = 1024 * 1024
+PIECES = 8
 
 VM = pl.BlockSpec(memory_space=pltpu.VMEM)
 SM = pl.BlockSpec(memory_space=pltpu.SMEM)
@@ -25,17 +26,31 @@
     return lax.ppermute(value, axis, [(i, i ^ bit) for i in range(total)])
 
 
+def lead_permute(value, bit):
+    pairs = [(2 * i + 1, 2 * (i ^ bit) + 1) for i in range(lax.axis_size("batch"))]
+    return lax.ppermute(value, ("batch", "tensor"), pairs)
+
+
+def hand(value, to):
+    pairs = [(2 * i + 1 - to, 2 * i + to) for i in range(lax.axis_size("batch"))]
+    return lax.ppermute(value, ("batch", "tensor"), pairs)
+
+
 def reverse(index, size):
     bits = size.bit_length() - 1
     return sum(((index >> k) & 1) << (bits - 1 - k) for k in range(bits))
 
 
-def doubling(buffer, first, last, work):
+def pin(value, loaded):
+    return lax.optimization_barrier((value, loaded))
+
+
+def doubling(buffer, first, last, work, permute=lead_permute):
     bit = last
     while True:
         bit //= 2
-        other = xor_permute(buffer, "batch", bit)
-        work(buffer)
+        other = permute(buffer, bit)
+        other = work(buffer, other)
         if bit == first:
             return buffer, other
         buffer = jnp.concatenate([buffer, other])
@@ -50,6 +65,10 @@
         compiler_params=pltpu.CompilerParams(vmem_limit_bytes=vmem * MIB),
         cost_estimate=pl.CostEstimate(flops=flops, bytes_accessed=moved, transcendentals=0),
     )(*args)
+
+
+def in_hbm(value):
+    return pltpu.with_memory_space_constraint(value, pltpu.HBM)
 
 
 def start_all(copies):
@@ -127,8 +146,36 @@
     pay_ref[:, heads * HD :] = extra.astype(jnp.bfloat16)
 
 
-def attend_kernel(
-    stride, near_ref, far_ref, cache_ref, memory_ref, new_ref, parents_ref, lengths_ref, num_ref, state_ref, pay_ref
+def attend_kernel(stride, near_ref, far_ref, *refs):
+    sides, (parents_ref, lengths_ref, num_ref, state_ref, pay_ref) = refs[:-5], refs[-5:]
+    for side in range(2):
+        attend_side(
+            stride,
+            side,
+            near_ref,
+            far_ref,
+            *sides[3 * side : 3 * side + 3],
+            parents_ref,
+            lengths_ref,
+            num_ref.at[side],
+            state_ref.at[side],
+            pay_ref.at[side],
+        )
+
+
+def attend_side(
+    stride,
+    side,
+    near_ref,
+    far_ref,
+    cache_ref,
+    memory_ref,
+    new_ref,
+    parents_ref,
+    lengths_ref,
+    num_ref,
+    state_ref,
+    pay_ref,
 ):
     position = lax.axis_index("batch")
     own, request = position // stride, lax.rem(position, stride)
@@ -139,12 +186,13 @@
     span = past + memory_ref.shape[1]
     f32, bf16 = jnp.float32, jnp.bfloat16
 
-    to = lax.broadcasted_iota(jnp.int32, (rows, BEAMS), 0)
-    source = lax.broadcasted_iota(jnp.int32, (rows, BEAMS), 1)
+    to = lax.broadcasted_iota(jnp.int32, (rows, near_ref.shape[0]), 0)
+    source = lax.broadcasted_iota(jnp.int32, (rows, near_ref.shape[0]), 1)
 
     def place_rows(piece_ref, first):
-        beam = jnp.bitwise_xor(reverse(first + source // 2, BEAMS), own)
-        order = jnp.where(to == (source % 2) * BEAMS + beam, 1.0, 0.0).astype(bf16)
+        beam = jnp.bitwise_xor(reverse(first + source // 4, BEAMS), own)
+        wanted = jnp.where((source // 2) % 2 == side, (source % 2) * BEAMS + beam, -1)
+        order = jnp.where(to == wanted, 1.0, 0.0).astype(bf16)
         return jnp.dot(order, piece_ref[...], preferred_element_type=f32)
 
     query = (place_rows(near_ref, 0) + place_rows(far_ref, BEAMS // 2)).astype(bf16)
@@ -214,15 +262,17 @@
 
 
 def merge_kernel(num_ref, state_ref, pay_ref, num_out, state_out, pay_out):
-    peaks, totals = combine(num_ref, state_ref, pay_ref, num_out)
-    export(num_out, state_out, pay_out, peaks, totals)
+    for side in range(2):
+        peaks, totals = combine(num_ref.at[side], state_ref.at[side], pay_ref.at[side], num_out.at[side])
+        export(num_out.at[side], state_out.at[side], pay_out.at[side], peaks, totals)
 
 
 def finish_kernel(num_ref, state_ref, pay_ref, out_ref, num):
-    _, totals = combine(num_ref, state_ref, pay_ref, num)
-    for h in range(num.shape[1] // HD):
-        cols = slice(h * HD, (h + 1) * HD)
-        out_ref[:, cols] = (num[:, cols] / totals[:, h : h + 1]).astype(jnp.bfloat16)
+    for side in range(2):
+        _, totals = combine(num_ref.at[side], state_ref.at[side], pay_ref.at[side], num.at[side])
+        for h in range(num.shape[2] // HD):
+            cols = slice(h * HD, (h + 1) * HD)
+            out_ref[side, :, cols] = (num[side, :, cols] / totals[:, h : h + 1]).astype(jnp.bfloat16)
 
 
 def finish(num, state, pay):
@@ -236,46 +286,47 @@
     )(num, state, pay)
 
 
-def project_kernel(attended_ref, first_ref, second_ref, out_ref):
-    rows = out_ref.shape[0]
-    first = jnp.dot(attended_ref[...], first_ref[0], preferred_element_type=jnp.float32)
-    second = jnp.dot(attended_ref[...], second_ref[0], preferred_element_type=jnp.float32)
-    out_ref[...] = first[:rows] + second[rows:]
-
-
-def add_kernel(own_ref, other_ref, residual_ref, out_ref):
-    total = residual_ref[0].astype(jnp.float32) + (own_ref[...] + other_ref[...])
+def project_kernel(attended_ref, own_ref, other_ref, residual_ref, out_ref):
+    rows = out_ref.shape[1]
+    total = residual_ref[0].astype(jnp.float32)
+    for side, weight_ref in enumerate((own_ref, other_ref)):
+        for kind in range(2):
+            part = jnp.dot(attended_ref[side], weight_ref[kind], preferred_element_type=jnp.float32)
+            total = total + part[kind * rows : (kind + 1) * rows]
     out_ref[0] = total.astype(jnp.bfloat16)
 
 
-def up_kernel(near_ref, far_ref, *refs):
-    chunks, (hidden_ref, out_ref, sem) = refs[:-3], refs[-3:]
+def up_kernel(near_ref, far_ref, near_given_ref, far_given_ref, *refs):
+    chunks, (hidden_ref, out_ref, kept, sem) = refs[:-4], refs[-4:]
+    lead = lax.axis_index("tensor") == 1
     half, _, depth = near_ref.shape
     per = 2 * half // len(chunks)
-    copy = pltpu.make_async_copy(near_ref.at[0], hidden_ref, sem)
+    for j in range(half):
+        kept[j] = jnp.where(lead, near_ref[j], near_given_ref[j])
+        kept[half + j] = jnp.where(lead, far_ref[j], far_given_ref[j])
+    copy = pltpu.make_async_copy(kept.at[0], hidden_ref, sem)
     copy.start()
     total = jnp.zeros(out_ref.shape, jnp.float32)
     for j in range(2 * half):
-        block = near_ref[j] if j < half else far_ref[j - half]
         weight = chunks[j // per][pl.ds(j % per * depth, depth), :]
-        total = total + jnp.dot(block, weight, preferred_element_type=jnp.float32)
+        total = total + jnp.dot(kept[j], weight, preferred_element_type=jnp.float32)
     out_ref[...] = (0.5 * total * (1.0 + lax.erf(total * math.sqrt(0.5)))).astype(jnp.bfloat16)
     copy.wait()
 
 
-def up(near, far, chunks, units):
-    _, rows, columns = near.shape
+def up(near, far, near_given, far_given, chunks, units):
+    half, rows, columns = near.shape
     return pl.pallas_call(
         up_kernel,
         out_shape=(
             jax.ShapeDtypeStruct((rows, columns), jnp.bfloat16),
             jax.ShapeDtypeStruct((rows, units), jnp.bfloat16),
         ),
-        in_specs=[VM] * (2 + len(chunks)),
+        in_specs=[VM] * (4 + len(chunks)),
         out_specs=(ANY, VM),
-        scratch_shapes=[pltpu.SemaphoreType.DMA],
+        scratch_shapes=[pltpu.VMEM((2 * half, rows, columns), jnp.bfloat16), pltpu.SemaphoreType.DMA],
         compiler_params=pltpu.CompilerParams(vmem_limit_bytes=8 * MIB),
-    )(near, far, *chunks)
+    )(near, far, near_given, far_given, *chunks)
 
 
 def reorder(activation):
@@ -332,11 +383,11 @@
     return pl.pallas_call(
         functools.partial(place_kernel, stride, order),
         out_shape=jax.ShapeDtypeStruct(gathered.shape[1:], gathered.dtype),
-        in_specs=[pl.BlockSpec(memory_space=pltpu.HBM), VM, SM, SM],
+        in_specs=[ANY, VM, SM, SM],
         out_specs=VM,
         scratch_shapes=[pltpu.VMEM(gathered.shape[1:], gathered.dtype), pltpu.SemaphoreType.DMA],
         compiler_params=pltpu.CompilerParams(vmem_limit_bytes=8 * MIB),
-    )(gathered, new_kv, parents, lengths)
+    )(in_hbm(gathered), new_kv, parents, lengths)
 
 
 def body(
@@ -363,72 +414,85 @@
     f32, bf16 = jnp.float32, jnp.bfloat16
     shape = jax.ShapeDtypeStruct
     down_weight = pltpu.with_memory_space_constraint(down_weight, pltpu.VMEM)
-    pieces = 8
+    per = devices // PIECES
+    chunks = []
+
+    def load_up(count):
+        def work(buffer, other):
+            loaded = []
+            for _ in range(count):
+                first = (len(chunks) + len(loaded)) * per
+                loaded.append(fetch_rows(in_hbm(up_weight), first, per, devices, buffer))
+            other, loaded = pin(other, loaded)
+            chunks.extend(loaded)
+            return other
+
+        return work
+
+    def load_out(buffer, other):
+        other, local["out"] = pin(other, fetch([in_hbm(out_weight)], buffer)[0])
+        return other
+
     local = {}
-    chunks = []
-
-    def load_operands(after):
-        sources = (queries[0, 0], init_cache[0], memory[0], new_kv[0, 0], residual)
-        local["all"] = fetch(sources, after)
-
-    def load_out(kind):
-        def work(after):
-            local[kind] = fetch([out_weight[kind : kind + 1]], after)[0]
-
-        return work
-
-    def load_up(after):
-        if len(chunks) < pieces:
-            per = devices // pieces
-            chunks.append(fetch_rows(up_weight, len(chunks) * per, per, devices, after))
-
-    bit = devices // 2
-    other = xor_permute(queries[0, 0], "batch", bit)
-    load_operands(queries[0, 0])
-    query, cache_row, memory_row, new_row, residual_row = local["all"]
-    works = [load_out(0), load_out(1)]
-    query = jnp.concatenate([query, other])
-    query, far = doubling(query, stride, bit, lambda after: works.pop(0)(after))
+    plan = [load_out, load_up(1), load_up(1), load_up(2), load_up(1), load_up(2), load_up(1)]
+
+    def work(buffer, other):
+        return plan.pop(0)(buffer, other) if plan else other
+
+    query_other = hand(queries[0, 0], 1)
+    sources = (queries[0, 0], init_cache[0], memory[0], new_kv[0, 0], residual)
+    loaded = fetch([in_hbm(x) for x in sources], queries[0, 0])
+    cache_other, memory_other, new_other = (hand(x, 1) for x in (init_cache[0], memory[0], new_kv[0, 0]))
+    out_other = hand(out_weight, 1)
+    query_other, loaded = pin(query_other, loaded)
+    query, cache_row, memory_row, new_row, residual_row = loaded
+    near, far = doubling(jnp.concatenate([query, query_other]), stride, devices, work)
     state_shapes = (
-        shape((2 * BEAMS, width), f32),
-        shape((2 * BEAMS, 2 * LANES), f32),
-        shape((2 * BEAMS, width + LANES), bf16),
+        shape((2, 2 * BEAMS, width), f32),
+        shape((2, 2 * BEAMS, 2 * LANES), f32),
+        shape((2, 2 * BEAMS, width + LANES), bf16),
     )
     num, state, pay = call(
         functools.partial(attend_kernel, stride),
         state_shapes,
-        query,
+        near,
         far,
         cache_row,
         memory_row,
         new_row,
+        cache_other,
+        memory_other,
+        new_other,
         parents,
         lengths,
-        specs=[VM] * 5 + [SM] * 2,
+        specs=[VM] * 8 + [SM] * 2,
     )
     bit = stride
     while True:
-        arrived = xor_permute(pay, "batch", bit)
-        load_up(pay)
-        load_up(pay)
+        arrived = work(pay, lead_permute(pay, bit))
         bit *= 2
         if bit == devices:
             break
         num, state, pay = call(merge_kernel, state_shapes, num, state, arrived)
     attended = finish(num, state, arrived)
     if stride > 1:
-        stacked = jnp.concatenate(doubling(attended[None], 1, stride, lambda after: None))
+        pair = doubling(attended[None], 1, stride, lambda buffer, other: other)
         wanted = reverse(jnp.bitwise_xor(jnp.arange(stride, dtype=jnp.int32), request), stride)
-        stacked = stacked[wanted].reshape(stride, 2, BEAMS, width)
-        attended = stacked.transpose(1, 2, 0, 3).reshape(2 * rows, width)
-
-    partial = call(project_kernel, shape((rows, columns), f32), attended, local[0], local[1])
-    other = xor_permute(partial, "tensor", 1)
-    mine = call(add_kernel, pltpu.VMEM((1, rows, columns), bf16), partial, other, residual_row)
-    near, far = doubling(mine, 1, devices, load_up)
-    while len(chunks) < pieces:
-        load_up(near)
-    hidden, activation = up(near, far, chunks, hidden_units)
+        stacked = jnp.concatenate(pair)[wanted].reshape(stride, 2, 2, BEAMS, width)
+        attended = stacked.transpose(1, 2, 3, 0, 4).reshape(2, 2 * rows, width)
+
+    mine = call(
+        project_kernel,
+        pltpu.VMEM((1, rows, columns), bf16),
+        attended,
+        local["out"],
+        out_other,
+        residual_row,
+    )
+    near, far = doubling(mine, 1, devices, work)
+    while len(chunks) < PIECES:
+        near = load_up(1)(near, near)
+    hidden, activation = up(near, far, hand(near, 0), hand(far, 0), chunks, hidden_units)
     arrived = xor_permute(activation, "tensor", 1)
     before = call(
         functools.partial(down_kernel, True), shape((rows, out_columns), f32), activation, down_weight

time: 91.8 us -> 114 us (1.24)
  starting transfers between devices: 11.6 us -> 32.4 us
  Pallas kernels: 12 us -> 32 us
  local copies, waits for them, and re-layouts: 12.3 us -> 0.07 us
  waiting for transfers between devices: 39.8 us -> 32.9 us
    ppermute x0 -> x16, starting transfers between devices: none -> 29.8 us  [the longest x7 23.5 us: hand(): return lax.ppermute(value, ('batch', 'tensor'), pairs)]
    ppermute x14 -> x4, waiting for transfers between devices: 39.2 us -> 10.3 us  [xor_permute(): return lax.ppermute(value, axis, [(i, i ^ bit) for i in range(total)])]
    ppermute x0 -> x16, waiting for transfers between devices: none -> 22.6 us  [the longest x7 22.6 us: hand(): return lax.ppermute(value, ('batch', 'tensor'), pairs)]
    pallas_call x8, Pallas kernels: 1.45 us -> 13.7 us  [fetch_rows(): pl.pallas_call(functools.partial(fetch_rows_kernel, first, blocks, total)...]
    unnamed x28 -> x14, local copies, waits for them, and re-layouts: 9.41 us -> 0.04 us
    ppermute x14 -> x4, starting transfers between devices: 11.6 us -> 2.58 us  [xor_permute(): return lax.ppermute(value, axis, [(i, i ^ bit) for i in range(total)])]
    pallas_call x7 -> x6, Pallas kernels: 5.35 us -> 9.15 us  [call(): pl.pallas_call(kernel, out_shape=out, in_specs=specs or [VM] * len(args),...]
    slice x1 -> x0, local copies, waits for them, and re-layouts: 2.88 us -> none  [work(): local[kind] = fetch([out_weight[kind:kind + 1]], after)[0]]
  transfers between devices with their start and end apart: 15 -> 21, of which waited for: 12 -> 6; matrix products, arithmetic and copies ran while one was open for 4% -> 1% of each run, Pallas kernels for 11% -> 26%
where the time goes in v5:
time: 114 us; the launch traced here: 113 us
  waiting for transfers between devices  32.9 us (29%)
  starting transfers between devices  32.4 us (28%)
  Pallas kernels  32 us (28%)
  between operations  15.2 us (13%)
    ppermute x7, starting transfers between devices, hand(): return lax.ppermute(value, ('batch', 'tensor'), pairs)  23.5 us
    ppermute x7, waiting for transfers between devices, hand(): return lax.ppermute(value, ('batch', 'tensor'), pairs)  22.6 us
    pallas_call x8, Pallas kernels, fetch_rows(): pl.pallas_call(functools.partial(fetch_rows_kernel, first, blocks, total)...  13.7 us
    ppermute x4, waiting for transfers between devices, xor_permute(): return lax.ppermute(value, axis, [(i, i ^ bit) for i in range(total)])  10.3 us
    pallas_call x6, Pallas kernels, call(): pl.pallas_call(kernel, out_shape=out, in_specs=specs or [VM] * len(args),...  9.15 us
    ppermute x9, starting transfers between devices, lead_permute(): return lax.ppermute(value, ('batch', 'tensor'), pairs)  6.34 us
    pallas_call x2, Pallas kernels, fetch(): pl.pallas_call(functools.partial(fetch_kernel, count), out_shape=[pltpu.V...  3.58 us
    pallas_call x1, Pallas kernels, up(): pl.pallas_call(up_kernel, out_shape=(jax.ShapeDtypeStruct((rows, columns)...  2.74 us
  transfers between devices with their start and end apart: 21, of which 6 were waited for; matrix products, arithmetic and copies ran while one was open for 1% of the time, Pallas kernels for 26%

profile of v5, /device:TPU:0, one launch (start us, length us, event | category | flops | bytes accessed | tf_op | source)
XLA Modules:
  0.0 113.4 jit_solution(13971589471072254549)
XLA Ops:
  7.2 4.5 %collective-permute-start.10 = (bf16[2,1536,768]{2,1,0:T(8,128)(2,1)}, bf16[2,1536,768]{2,1,0:T(8,128)(2,1)}, u32[]{:S(2)}, u32[]{:S(2)}) collective-permute-start(bf16[2,1536,768]{2,1,0:T(8,128)(2,1)} %refs_0_.1), channel_id=1, source_target_pairs={{0,1},{2,3},{4,5},{6,7},{8,9},{10,11},{12,13},{14,15},{16,17},{18,... | collective-permute-start | bytes 14155784 | tf_op jit(solution)/shard_map/ppermute | solution.py:36
  11.7 1.3 %collective-permute-start = (bf16[2,1536]{1,0:T(2,128)(2,1)}, bf16[2,1536]{1,0:T(2,128)(2,1)S(1)}, u32[]{:S(2)}, u32[]{:S(2)}) collective-permute-start(bf16[2,1536]{1,0:T(2,128)(2,1)} %bitcast.15), channel_id=1, source_target_pairs={{0,1},{2,3},{4,5},{6,7},{8,9},{10,11},{12,13},{14,15},{16,17},{18,... | collective-permute-start | bytes 18440 | tf_op jit(solution)/shard_map/ppermute | solution.py:36
  13.0 1.2 %shard_map.121 = (bf16[2,1536]{1,0:T(2,128)(2,1)S(1)}, bf16[2,64,1536]{2,1,0:T(8,128)(2,1)S(1)}, bf16[2,64,1536]{2,1,0:T(8,128)(2,1)S(1)}, bf16[2,1536]{1,0:T(2,128)(2,1)S(1)}, bf16[1,8,768]{2,1,0:T(8,128)(2,1)S(1)}) custom-call(bf16[2,1536]{1,0:T(2,128)(2,1)} %bitcast.16, bf16[2,64,1536]{2,1,0:T(8,128)(2,1)} %bitcast.10, bf16[2,64,1536]{2,1,0:T(8,128)(2,1)} %bitcast.12, ...), custom_call_target="tpu_custom_call" | custom-call | bytes 2097152 | tf_op jit(solution)/shard_map/pallas_call | solution.py:89
  14.2 3.1 %collective-permute-done = bf16[2,1536]{1,0:T(2,128)(2,1)S(1)} collective-permute-done((bf16[2,1536]{1,0:T(2,128)(2,1)}, bf16[2,1536]{1,0:T(2,128)(2,1)S(1)}, u32[]{:S(2)}, u32[]{:S(2)}) %collective-permute-start) | collective-permute-done | bytes 6176 | tf_op jit(solution)/shard_map/ppermute | solution.py:36
  18.0 6.7 %collective-permute-start.4 = (bf16[2,64,1536]{2,1,0:T(8,128)(2,1)}, bf16[2,64,1536]{2,1,0:T(8,128)(2,1)S(1)}, u32[]{:S(2)}, u32[]{:S(2)}) collective-permute-start(bf16[2,64,1536]{2,1,0:T(8,128)(2,1)} %bitcast.11), channel_id=1, source_target_pairs={{0,1},{2,3},{4,5},{6,7},{8,9},{10,11},{12,13},{14,15},{16,17},{18,... | collective-permute-start | bytes 1179656 | tf_op jit(solution)/shard_map/ppermute | solution.py:36
  24.7 1.3 %collective-permute-start.5 = (bf16[2,64,1536]{2,1,0:T(8,128)(2,1)}, bf16[2,64,1536]{2,1,0:T(8,128)(2,1)S(1)}, u32[]{:S(2)}, u32[]{:S(2)}) collective-permute-start(bf16[2,64,1536]{2,1,0:T(8,128)(2,1)} %bitcast.13), channel_id=1, source_target_pairs={{0,1},{2,3},{4,5},{6,7},{8,9},{10,11},{12,13},{14,15},{16,17},{18,... | collective-permute-start | bytes 1179656 | tf_op jit(solution)/shard_map/ppermute | solution.py:36
  26.0 2.4 %shard_map.122.own_ref = bf16[2,1536,768]{2,1,0:T(8,128)(2,1)S(1)} custom-call(bf16[2,1536,768]{2,1,0:T(8,128)(2,1)} %refs_0_.1, bf16[4,1536]{1,0:T(4,128)(2,1)S(1)} %pad_maximum_fusion.4.refs_1_), custom_call_target="tpu_custom_call" | custom-call | bytes 2097152 | tf_op jit(solution)/shard_map/pallas_call | solution.py:89
  29.2 1.7 %shard_map.123.refs_0_ = bf16[768,1536]{1,0:T(8,128)(2,1)S(1)} custom-call(bf16[6144,1536]{1,0:T(8,128)(2,1)} %weight_ref.17, bf16[8,1536]{1,0:T(8,128)(2,1)S(1)} %pad_maximum_fusion.2._), custom_call_target="tpu_custom_call" | custom-call | bytes 2097152 | tf_op jit(solution)/shard_map/pallas_call | solution.py:116
  31.6 6.6 %collective-permute-start.6 = (bf16[2,1536]{1,0:T(2,128)(2,1)S(1)}, bf16[2,1536]{1,0:T(2,128)(2,1)S(1)}, u32[]{:S(2)}, u32[]{:S(2)}) collective-permute-start(bf16[2,1536]{1,0:T(2,128)(2,1)S(1)} %bitcast.19), channel_id=1, source_target_pairs={{0,1},{2,3},{4,5},{6,7},{8,9},{10,11},{12,13},{14,15},{16,17},{18,... | collective-permute-start | bytes 18440 | tf_op jit(solution)/shard_map/ppermute | solution.py:36
  38.9 1.7 %shard_map.124.refs_1_ = bf16[768,1536]{1,0:T(8,128)(2,1)S(1)} custom-call(bf16[6144,1536]{1,0:T(8,128)(2,1)} %weight_ref.17, bf16[16,1536]{1,0:T(8,128)(2,1)S(1)} %pad_maximum_fusion._.near_ref), custom_call_target="tpu_custom_call" | custom-call | bytes 2097152 | tf_op jit(solution)/shard_map/pallas_call | solution.py:116
  40.6 1.9 %shard_map.125 = (f32[2,16,1536]{2,1,0:T(8,128)S(1)}, f32[2,16,256]{2,1,0:T(8,128)S(1)}, bf16[2,16,1664]{2,1,0:T(8,128)(2,1)S(1)}) custom-call(bf16[16,1536]{1,0:T(8,128)(2,1)S(1)} %pad_maximum_fusion._.near_ref, bf16[16,1536]{1,0:T(8,128)(2,1)S(1)} %collective-permute-done.3.far_ref, bf16[2,64,1536]{2,1,0:T(8,128)(2,1)S(1)} %get-tuple-element.53.refs_0_, ...), custom_call_target="tpu_custom_call" | custom-call | tf_op jit(solution)/shard_map/pallas_call | solution.py:60
  43.2 1.7 %shard_map.126.refs_2_ = bf16[768,1536]{1,0:T(8,128)(2,1)S(1)} custom-call(bf16[6144,1536]{1,0:T(8,128)(2,1)} %weight_ref.17, bf16[2,16,1664]{2,1,0:T(8,128)(2,1)S(1)} %get-tuple-element.58._), custom_call_target="tpu_custom_call" | custom-call | bytes 2097152 | tf_op jit(solution)/shard_map/pallas_call | solution.py:116
  44.9 1.7 %shard_map.127.refs_3_ = bf16[768,1536]{1,0:T(8,128)(2,1)S(1)} custom-call(bf16[6144,1536]{1,0:T(8,128)(2,1)} %weight_ref.17, bf16[2,16,1664]{2,1,0:T(8,128)(2,1)S(1)} %get-tuple-element.58._), custom_call_target="tpu_custom_call" | custom-call | bytes 2097152 | tf_op jit(solution)/shard_map/pallas_call | solution.py:116
  47.7 1.7 %shard_map.129.refs_4_ = bf16[768,1536]{1,0:T(8,128)(2,1)S(1)} custom-call(bf16[6144,1536]{1,0:T(8,128)(2,1)} %weight_ref.17, bf16[2,16,1664]{2,1,0:T(8,128)(2,1)S(1)} %get-tuple-element.62._), custom_call_target="tpu_custom_call" | custom-call | bytes 2097152 | tf_op jit(solution)/shard_map/pallas_call | solution.py:116
  50.5 1.7 %shard_map.131.refs_5_ = bf16[768,1536]{1,0:T(8,128)(2,1)S(1)} custom-call(bf16[6144,1536]{1,0:T(8,128)(2,1)} %weight_ref.17, bf16[2,16,1664]{2,1,0:T(8,128)(2,1)S(1)} %get-tuple-element.66._), custom_call_target="tpu_custom_call" | custom-call | bytes 2097152 | tf_op jit(solution)/shard_map/pallas_call | solution.py:116
  52.2 1.7 %shard_map.132.refs_6_ = bf16[768,1536]{1,0:T(8,128)(2,1)S(1)} custom-call(bf16[6144,1536]{1,0:T(8,128)(2,1)} %weight_ref.17, bf16[2,16,1664]{2,1,0:T(8,128)(2,1)S(1)} %get-tuple-element.66._), custom_call_target="tpu_custom_call" | custom-call | bytes 2097152 | tf_op jit(solution)/shard_map/pallas_call | solution.py:116
  54.3 3.6 %shard_map.134._ = bf16[1,8,768]{2,1,0:T(8,128)(2,1)S(1)} custom-call(bf16[2,16,1536]{2,1,0:T(8,128)(2,1)S(1)} %shard_map.133.attended_ref, bf16[2,1536,768]{2,1,0:T(8,128)(2,1)S(1)} %shard_map.122.own_ref, bf16[2,1536,768]{2,1,0:T(8,128)(2,1)} %collective-permute-done.10.other_ref, bf16[1,8,768]{2,1,0:T(8,128)(2,1)S(1)} %get-tuple-element.69.residual_ref), custom_call_target="tpu_custom_call" | custom-call | tf_op jit(solution)/shard_map/pallas_call | solution.py:60
  58.7 1.8 %shard_map.135.refs_7_ = bf16[768,1536]{1,0:T(8,128)(2,1)S(1)} custom-call(bf16[6144,1536]{1,0:T(8,128)(2,1)} %weight_ref.17, bf16[1,8,768]{2,1,0:T(8,128)(2,1)S(1)} %shard_map.134._), custom_call_target="tpu_custom_call" | custom-call | bytes 2097152 | tf_op jit(solution)/shard_map/pallas_call | solution.py:116
  60.6 0.8 collective-permute-start.12
  61.4 0.8 collective-permute-start.13
  62.2 1.6 %collective-permute-start.14 = (bf16[4,8,768]{2,1,0:T(8,128)(2,1)S(1)}, bf16[4,8,768]{2,1,0:T(8,128)(2,1)S(1)}, u32[]{:S(2)}, u32[]{:S(2)}) collective-permute-start(bf16[4,8,768]{2,1,0:T(8,128)(2,1)S(1)} %pad_maximum_fusion.1.near_ref), channel_id=1, source_target_pairs={{1,0},{3,2},{5,4},{7,6},{9,8},{11,10},{13,12},{15,14},{17,16},{19,... | collective-permute-start | bytes 147464 | tf_op jit(solution)/shard_map/ppermute | solution.py:36
  63.8 1.6 %collective-permute-start.15 = (bf16[4,8,768]{2,1,0:T(8,128)(2,1)S(1)}, bf16[4,8,768]{2,1,0:T(8,128)(2,1)S(1)}, u32[]{:S(2)}, u32[]{:S(2)}) collective-permute-start(bf16[4,8,768]{2,1,0:T(8,128)(2,1)S(1)} %collective-permute-done.13.far_ref), channel_id=1, source_target_pairs={{1,0},{3,2},{5,4},{7,6},{9,8},{11,10},{13,12},{15,14},{17,16},{19,... | collective-permute-start | bytes 147464 | tf_op jit(solution)/shard_map/ppermute | solution.py:36
  65.4 17.0 %collective-permute-done.14.near_given_ref = bf16[4,8,768]{2,1,0:T(8,128)(2,1)S(1)} collective-permute-done((bf16[4,8,768]{2,1,0:T(8,128)(2,1)S(1)}, bf16[4,8,768]{2,1,0:T(8,128)(2,1)S(1)}, u32[]{:S(2)}, u32[]{:S(2)}) %collective-permute-start.14) | collective-permute-done | bytes 49184 | tf_op jit(solution)/shard_map/ppermute | solution.py:36
  82.4 2.5 %collective-permute-done.15.far_given_ref = bf16[4,8,768]{2,1,0:T(8,128)(2,1)S(1)} collective-permute-done((bf16[4,8,768]{2,1,0:T(8,128)(2,1)S(1)}, bf16[4,8,768]{2,1,0:T(8,128)(2,1)S(1)}, u32[]{:S(2)}, u32[]{:S(2)}) %collective-permute-start.15) | collective-permute-done | bytes 49184 | tf_op jit(solution)/shard_map/ppermute | solution.py:36
  84.9 2.7 %shard_map.136 = (bf16[8,768]{1,0:T(8,128)(2,1)}, bf16[8,1536]{1,0:T(8,128)(2,1)S(1)}) custom-call(bf16[4,8,768]{2,1,0:T(8,128)(2,1)S(1)} %pad_maximum_fusion.1.near_ref, bf16[4,8,768]{2,1,0:T(8,128)(2,1)S(1)} %collective-permute-done.13.far_ref, bf16[4,8,768]{2,1,0:T(8,128)(2,1)S(1)} %collective-permute-done.14.near_given_ref, ...), custom_call_target="tpu_custom_call" | custom-call | tf_op jit(solution)/shard_map/pallas_call | solution.py:319
  87.9 1.4 %shard_map.137.rest_0_ = f32[8,3072]{1,0:T(8,128)S(1)} custom-call(bf16[8,1536]{1,0:T(8,128)(2,1)S(1)} %get-tuple-element.80.act_ref, bf16[3072,3072]{1,0:T(8,128)(2,1)S(1)} %bitcast.9), custom_call_target="tpu_custom_call" | custom-call | tf_op jit(solution)/shard_map/pallas_call | solution.py:60
  89.3 1.4 %shard_map.138 = (f32[4,3072]{1,0:T(4,128)S(1)}, f32[4,3072]{1,0:T(4,128)S(1)}) custom-call(bf16[8,1536]{1,0:T(8,128)(2,1)S(1)} %collective-permute-done.16.act_ref, bf16[3072,3072]{1,0:T(8,128)(2,1)S(1)} %bitcast.9, f32[8,3072]{1,0:T(8,128)S(1)} %shard_map.137.rest_0_), custom_call_target="tpu_custom_call" | custom-call | tf_op jit(solution)/shard_map/pallas_call | solution.py:60
  91.4 3.4 %collective-permute-done.17 = f32[4,3072]{1,0:T(4,128)S(1)} collective-permute-done((f32[4,3072]{1,0:T(4,128)S(1)}, f32[4,3072]{1,0:T(4,128)S(1)}, u32[]{:S(2)}, u32[]{:S(2)}) %collective-permute-start.17) | collective-permute-done | bytes 49184 | tf_op jit(solution)/shard_map/ppermute | solution.py:26
  95.4 3.4 %collective-permute-done.18 = f32[2,3072]{1,0:T(2,128)S(1)} collective-permute-done((f32[2,3072]{1,0:T(2,128)S(1)}, f32[2,3072]{1,0:T(2,128)S(1)}, u32[]{:S(2)}, u32[]{:S(2)}) %collective-permute-start.18) | collective-permute-done | bytes 24608 | tf_op jit(solution)/shard_map/ppermute | solution.py:26
  98.8 1.2 %collective-permute-start.19 = (f32[1,3072]{1,0:T(1,128)S(1)}, f32[1,3072]{1,0:T(1,128)S(1)}, u32[]{:S(2)}, u32[]{:S(2)}) collective-permute-start(f32[1,3072]{1,0:T(1,128)S(1)} %slice.19), channel_id=1, source_target_pairs={{0,8},{2,10},{4,12},{6,14},{8,0},{10,2},{12,4},{14,6},{1,9},{3,11}... | collective-permute-start | bytes 36872 | tf_op jit(solution)/shard_map/ppermute | solution.py:26
  100.0 3.5 %collective-permute-done.19 = f32[1,3072]{1,0:T(1,128)S(1)} collective-permute-done((f32[1,3072]{1,0:T(1,128)S(1)}, f32[1,3072]{1,0:T(1,128)S(1)}, u32[]{:S(2)}, u32[]{:S(2)}) %collective-permute-start.19) | collective-permute-done | bytes 12320 | tf_op jit(solution)/shard_map/ppermute | solution.py:26
  104.1 2.4 %shard_map.139 = bf16[2,64,1536]{2,1,0:T(8,128)(2,1)} custom-call(bf16[8,2,64,1536]{3,2,1,0:T(8,128)(2,1)} %all-gather.2.cloned.1.call-done.gathered_ref, bf16[2,1536]{1,0:T(2,128)(2,1)S(1)} %get-tuple-element.55.refs_2_.new_ref, s32[1,8]{1,0:T(1,128)S(1)} %copy-done, s32[1]{0:T(128)S(6)} %copy.13.refs_7_.lengths_ref), custom_call_target="tpu_custom_call" | custom-call | tf_op jit(solution)/shard_map/pallas_call | solution.py:383
  (55 shorter events, 8.2 us)
Async XLA Ops:
  7.2 97.0 %all-gather.2.cloned.1.call-start = ((), (), s32[]{:S(2)}) async-start(), calls=%async_computation | async-start | bytes 3538944 | tf_op jit(solution)/shard_map/all_gather | solution.py:522
  7.2 47.1 %collective-permute-start.10 = (bf16[2,1536,768]{2,1,0:T(8,128)(2,1)}, bf16[2,1536,768]{2,1,0:T(8,128)(2,1)}, u32[]{:S(2)}, u32[]{:S(2)}) collective-permute-start(bf16[2,1536,768]{2,1,0:T(8,128)(2,1)} %refs_0_.1), channel_id=1, source_target_pairs={{0,1},{2,3},{4,5},{6,7},{8,9},{10,11},{12,13},{14,15},{16,17},{18,... | collective-permute-start | bytes 14155784 | tf_op jit(solution)/shard_map/ppermute | solution.py:36
  11.7 5.6 %collective-permute-start = (bf16[2,1536]{1,0:T(2,128)(2,1)}, bf16[2,1536]{1,0:T(2,128)(2,1)S(1)}, u32[]{:S(2)}, u32[]{:S(2)}) collective-permute-start(bf16[2,1536]{1,0:T(2,128)(2,1)} %bitcast.15), channel_id=1, source_target_pairs={{0,1},{2,3},{4,5},{6,7},{8,9},{10,11},{12,13},{14,15},{16,17},{18,... | collective-permute-start | bytes 18440 | tf_op jit(solution)/shard_map/ppermute | solution.py:36
  17.3 11.1 %collective-permute-start.1 = (bf16[4,1536]{1,0:T(4,128)(2,1)S(1)}, bf16[4,1536]{1,0:T(4,128)(2,1)S(1)}, u32[]{:S(2)}, u32[]{:S(2)}) collective-permute-start(bf16[4,1536]{1,0:T(4,128)(2,1)S(1)} %pad_maximum_fusion.4.refs_1_), channel_id=1, source_target_pairs={{1,9},{3,11},{5,13},{7,15},{9,1},{11,3},{13,5},{15,7},{17,25},{19,... | collective-permute-start | bytes 36872 | tf_op jit(solution)/shard_map/ppermute | solution.py:31
  18.0 22.6 %collective-permute-start.4 = (bf16[2,64,1536]{2,1,0:T(8,128)(2,1)}, bf16[2,64,1536]{2,1,0:T(8,128)(2,1)S(1)}, u32[]{:S(2)}, u32[]{:S(2)}) collective-permute-start(bf16[2,64,1536]{2,1,0:T(8,128)(2,1)} %bitcast.11), channel_id=1, source_target_pairs={{0,1},{2,3},{4,5},{6,7},{8,9},{10,11},{12,13},{14,15},{16,17},{18,... | collective-permute-start | bytes 1179656 | tf_op jit(solution)/shard_map/ppermute | solution.py:36
  24.7 15.9 %collective-permute-start.5 = (bf16[2,64,1536]{2,1,0:T(8,128)(2,1)}, bf16[2,64,1536]{2,1,0:T(8,128)(2,1)S(1)}, u32[]{:S(2)}, u32[]{:S(2)}) collective-permute-start(bf16[2,64,1536]{2,1,0:T(8,128)(2,1)} %bitcast.13), channel_id=1, source_target_pairs={{0,1},{2,3},{4,5},{6,7},{8,9},{10,11},{12,13},{14,15},{16,17},{18,... | collective-permute-start | bytes 1179656 | tf_op jit(solution)/shard_map/ppermute | solution.py:36
  28.5 3.1 %copy-start.1 = (bf16[1,1,2,1536]{3,2,1,0:T(2,128)(2,1)S(1)}, bf16[1,1,2,1536]{3,2,1,0:T(2,128)(2,1)}, u32[]{:S(2)}) copy-start(bf16[1,1,2,1536]{3,2,1,0:T(2,128)(2,1)} %param.13) | copy-start | bytes 18436
  28.5 2.4 %collective-permute-start.2 = (bf16[8,1536]{1,0:T(8,128)(2,1)S(1)}, bf16[8,1536]{1,0:T(8,128)(2,1)S(1)}, u32[]{:S(2)}, u32[]{:S(2)}) collective-permute-start(bf16[8,1536]{1,0:T(8,128)(2,1)S(1)} %pad_maximum_fusion.2._), channel_id=1, source_target_pairs={{1,5},{3,7},{5,1},{7,3},{9,13},{11,15},{13,9},{15,11},{17,21},{19,... | collective-permute-start | bytes 73736 | tf_op jit(solution)/shard_map/ppermute | solution.py:31
  30.9 9.6 %collective-permute-start.3 = (bf16[16,1536]{1,0:T(8,128)(2,1)S(1)}, bf16[16,1536]{1,0:T(8,128)(2,1)S(1)}, u32[]{:S(2)}, u32[]{:S(2)}) collective-permute-start(bf16[16,1536]{1,0:T(8,128)(2,1)S(1)} %pad_maximum_fusion._.near_ref), channel_id=1, source_target_pairs={{1,3},{3,1},{5,7},{7,5},{9,11},{11,9},{13,15},{15,13},{17,19},{19,... | collective-permute-start | bytes 147464 | tf_op jit(solution)/shard_map/ppermute | solution.py:31
  31.6 9.0 %collective-permute-start.6 = (bf16[2,1536]{1,0:T(2,128)(2,1)S(1)}, bf16[2,1536]{1,0:T(2,128)(2,1)S(1)}, u32[]{:S(2)}, u32[]{:S(2)}) collective-permute-start(bf16[2,1536]{1,0:T(2,128)(2,1)S(1)} %bitcast.19), channel_id=1, source_target_pairs={{0,1},{2,3},{4,5},{6,7},{8,9},{10,11},{12,13},{14,15},{16,17},{18,... | collective-permute-start | bytes 18440 | tf_op jit(solution)/shard_map/ppermute | solution.py:36
  38.9 1.8 %copy-start = (s32[1,8]{1,0:T(1,128)S(1)}, s32[1,8]{1,0:T(1,128)}, u32[]{:S(2)}) copy-start(s32[1,8]{1,0:T(1,128)} %parents_ref.1) | copy-start | bytes 100
  42.6 4.1 %collective-permute-start.7 = (bf16[2,16,1664]{2,1,0:T(8,128)(2,1)S(1)}, bf16[2,16,1664]{2,1,0:T(8,128)(2,1)S(1)}, u32[]{:S(2)}, u32[]{:S(2)}) collective-permute-start(bf16[2,16,1664]{2,1,0:T(8,128)(2,1)S(1)} %get-tuple-element.58._), channel_id=1, source_target_pairs={{1,3},{3,1},{5,7},{7,5},{9,11},{11,9},{13,15},{15,13},{17,19},{19,... | collective-permute-start | bytes 319496 | tf_op jit(solution)/shard_map/ppermute | solution.py:31
  47.1 2.4 %collective-permute-start.8 = (bf16[2,16,1664]{2,1,0:T(8,128)(2,1)S(1)}, bf16[2,16,1664]{2,1,0:T(8,128)(2,1)S(1)}, u32[]{:S(2)}, u32[]{:S(2)}) collective-permute-start(bf16[2,16,1664]{2,1,0:T(8,128)(2,1)S(1)} %get-tuple-element.62._), channel_id=1, source_target_pairs={{1,5},{3,7},{5,1},{7,3},{9,13},{11,15},{13,9},{15,11},{17,21},{19,... | collective-permute-start | bytes 319496 | tf_op jit(solution)/shard_map/ppermute | solution.py:31
  49.9 4.1 %collective-permute-start.9 = (bf16[2,16,1664]{2,1,0:T(8,128)(2,1)S(1)}, bf16[2,16,1664]{2,1,0:T(8,128)(2,1)S(1)}, u32[]{:S(2)}, u32[]{:S(2)}) collective-permute-start(bf16[2,16,1664]{2,1,0:T(8,128)(2,1)S(1)} %get-tuple-element.66._), channel_id=1, source_target_pairs={{1,9},{3,11},{5,13},{7,15},{9,1},{11,3},{13,5},{15,7},{17,25},{19,... | collective-permute-start | bytes 319496 | tf_op jit(solution)/shard_map/ppermute | solution.py:31
  57.9 2.7 %collective-permute-start.11 = (bf16[1,8,768]{2,1,0:T(8,128)(2,1)S(1)}, bf16[1,8,768]{2,1,0:T(8,128)(2,1)S(1)}, u32[]{:S(2)}, u32[]{:S(2)}) collective-permute-start(bf16[1,8,768]{2,1,0:T(8,128)(2,1)S(1)} %shard_map.134._), channel_id=1, source_target_pairs={{1,9},{3,11},{5,13},{7,15},{9,1},{11,3},{13,5},{15,7},{17,25},{19,... | collective-permute-start | bytes 36872 | tf_op jit(solution)/shard_map/ppermute | solution.py:31
  58.7 29.2 %slice-start = ((s8[18874368]{0:T(1024)(128)(4,1)}), s8[4194304]{0:T(1024)(128)(4,1)S(1)}, s32[]{:S(2)}) async-start(s8[18874368]{0:T(1024)(128)(4,1)} %bitcast.8), calls=%async_computation.1 | async-start | bytes 8388608
  58.7 29.2 %slice-start.1 = ((s8[18874368]{0:T(1024)(128)(4,1)}), s8[4194304]{0:T(1024)(128)(4,1)S(1)}, s32[]{:S(2)}) async-start(s8[18874368]{0:T(1024)(128)(4,1)} %bitcast.8), calls=%async_computation.2 | async-start | bytes 8388608
  58.7 29.2 %slice-start.2 = ((s8[18874368]{0:T(1024)(128)(4,1)}), s8[4194304]{0:T(1024)(128)(4,1)S(1)}, s32[]{:S(2)}) async-start(s8[18874368]{0:T(1024)(128)(4,1)} %bitcast.8), calls=%async_computation.3 | async-start | bytes 8388608
  60.6 0.8 collective-permute-start.12
  61.4 26.5 %slice-start.3 = ((s8[18874368]{0:T(1024)(128)(4,1)}), s8[4194304]{0:T(1024)(128)(4,1)S(1)}, s32[]{:S(2)}) async-start(s8[18874368]{0:T(1024)(128)(4,1)} %bitcast.8), calls=%async_computation.4 | async-start | bytes 8388608
  61.4 26.4 %slice-start.4 = ((s8[18874368]{0:T(1024)(128)(4,1)}), s8[2097152]{0:T(1024)(128)(4,1)S(1)}, s32[]{:S(2)}) async-start(s8[18874368]{0:T(1024)(128)(4,1)} %bitcast.8), calls=%async_computation.5 | async-start | bytes 4194304
  61.4 2.4 %collective-permute-start.13 = (bf16[4,8,768]{2,1,0:T(8,128)(2,1)S(1)}, bf16[4,8,768]{2,1,0:T(8,128)(2,1)S(1)}, u32[]{:S(2)}, u32[]{:S(2)}) collective-permute-start(bf16[4,8,768]{2,1,0:T(8,128)(2,1)S(1)} %pad_maximum_fusion.1.near_ref), channel_id=1, source_target_pairs={{1,3},{3,1},{5,7},{7,5},{9,11},{11,9},{13,15},{15,13},{17,19},{19,... | collective-permute-start | bytes 147464 | tf_op jit(solution)/shard_map/ppermute | solution.py:31
  62.2 20.1 %collective-permute-start.14 = (bf16[4,8,768]{2,1,0:T(8,128)(2,1)S(1)}, bf16[4,8,768]{2,1,0:T(8,128)(2,1)S(1)}, u32[]{:S(2)}, u32[]{:S(2)}) collective-permute-start(bf16[4,8,768]{2,1,0:T(8,128)(2,1)S(1)} %pad_maximum_fusion.1.near_ref), channel_id=1, source_target_pairs={{1,0},{3,2},{5,4},{7,6},{9,8},{11,10},{13,12},{15,14},{17,16},{19,... | collective-permute-start | bytes 147464 | tf_op jit(solution)/shard_map/ppermute | solution.py:36
  63.8 21.1 %collective-permute-start.15 = (bf16[4,8,768]{2,1,0:T(8,128)(2,1)S(1)}, bf16[4,8,768]{2,1,0:T(8,128)(2,1)S(1)}, u32[]{:S(2)}, u32[]{:S(2)}) collective-permute-start(bf16[4,8,768]{2,1,0:T(8,128)(2,1)S(1)} %collective-permute-done.13.far_ref), channel_id=1, source_target_pairs={{1,0},{3,2},{5,4},{7,6},{9,8},{11,10},{13,12},{15,14},{17,16},{19,... | collective-permute-start | bytes 147464 | tf_op jit(solution)/shard_map/ppermute | solution.py:36
  87.6 1.7 %collective-permute-start.16 = (bf16[8,1536]{1,0:T(8,128)(2,1)S(1)}, bf16[8,1536]{1,0:T(8,128)(2,1)S(1)}, u32[]{:S(2)}, u32[]{:S(2)}) collective-permute-start(bf16[8,1536]{1,0:T(8,128)(2,1)S(1)} %get-tuple-element.80.act_ref), channel_id=1, source_target_pairs={{0,1},{1,0},{2,3},{3,2},{4,5},{5,4},{6,7},{7,6},{8,9},{9,8},{10,11... | collective-permute-start | bytes 73736 | tf_op jit(solution)/shard_map/ppermute | solution.py:26
  90.8 4.1 %collective-permute-start.17 = (f32[4,3072]{1,0:T(4,128)S(1)}, f32[4,3072]{1,0:T(4,128)S(1)}, u32[]{:S(2)}, u32[]{:S(2)}) collective-permute-start(f32[4,3072]{1,0:T(4,128)S(1)} %get-tuple-element.82), channel_id=1, source_target_pairs={{0,2},{2,0},{4,6},{6,4},{8,10},{10,8},{12,14},{14,12},{1,3},{3,1},... | collective-permute-start | bytes 147464 | tf_op jit(solution)/shard_map/ppermute | solution.py:26
  94.9 3.9 %collective-permute-start.18 = (f32[2,3072]{1,0:T(2,128)S(1)}, f32[2,3072]{1,0:T(2,128)S(1)}, u32[]{:S(2)}, u32[]{:S(2)}) collective-permute-start(f32[2,3072]{1,0:T(2,128)S(1)} %slice.17), channel_id=1, source_target_pairs={{0,4},{2,6},{4,0},{6,2},{8,12},{10,14},{12,8},{14,10},{1,5},{3,7},... | collective-permute-start | bytes 73736 | tf_op jit(solution)/shard_map/ppermute | solution.py:26
  98.8 4.7 %collective-permute-start.19 = (f32[1,3072]{1,0:T(1,128)S(1)}, f32[1,3072]{1,0:T(1,128)S(1)}, u32[]{:S(2)}, u32[]{:S(2)}) collective-permute-start(f32[1,3072]{1,0:T(1,128)S(1)} %slice.19), channel_id=1, source_target_pairs={{0,8},{2,10},{4,12},{6,14},{8,0},{10,2},{12,4},{14,6},{1,9},{3,11}... | collective-permute-start | bytes 36872 | tf_op jit(solution)/shard_map/ppermute | solution.py:26
Sparse Core Ops, SparseCore 0:
  11.9 41.9 all-gather.1

commit v6 on v4

--- a/solution.py
+++ b/solution.py
@@ -14,6 +14,8 @@
 BEAMS = 8
 LOW = -1e30
 MIB = 1024 * 1024
+BUFFERS = 3
+STEP_BYTES = 16 * MIB
 
 VM = pl.BlockSpec(memory_space=pltpu.VMEM)
 SM = pl.BlockSpec(memory_space=pltpu.SMEM)
@@ -30,18 +32,17 @@
     return sum(((index >> k) & 1) << (bits - 1 - k) for k in range(bits))
 
 
-def doubling(buffer, first, last, work):
+def doubling(buffer, first, last):
     bit = last
     while True:
         bit //= 2
         other = xor_permute(buffer, "batch", bit)
-        work(buffer)
         if bit == first:
             return buffer, other
         buffer = jnp.concatenate([buffer, other])
 
 
-def call(kernel, out, *args, specs=None, vmem=8, flops=0, moved=0):
+def call(kernel, out, *args, specs=None, vmem=8, flops=0, moved=STEP_BYTES):
     return pl.pallas_call(
         kernel,
         out_shape=out,
@@ -52,6 +53,14 @@
     )(*args)
 
 
+def in_hbm(value):
+    return pltpu.with_memory_space_constraint(value, pltpu.HBM)
+
+
+def pin(value, loaded):
+    return lax.optimization_barrier((value, loaded))
+
+
 def start_all(copies):
     for copy in copies:
         copy.start()
@@ -62,7 +71,13 @@
 def fetch_kernel(count, *refs):
     sems = refs[-1]
     outs = refs[-1 - count : -1]
-    start_all([pltpu.make_async_copy(refs[i], outs[i], sems.at[i]) for i in range(count)])
+    copies = []
+    for i in range(count):
+        parts = refs[i].shape[0] if len(refs[i].shape) > 2 else 1
+        for k in range(parts):
+            source, target = (refs[i].at[k], outs[i].at[k]) if parts > 1 else (refs[i], outs[i])
+            copies.append(pltpu.make_async_copy(source, target, sems.at[i, k]))
+    start_all(copies)
 
 
 def fetch(arrays, after):
@@ -72,37 +87,41 @@
         out_shape=[pltpu.VMEM(x.shape, x.dtype) for x in arrays],
         in_specs=[ANY] * (count + 1),
         out_specs=[VM] * count,
-        scratch_shapes=[pltpu.SemaphoreType.DMA((count,))],
+        scratch_shapes=[pltpu.SemaphoreType.DMA((count, 2))],
         compiler_params=pltpu.CompilerParams(vmem_limit_bytes=2 * MIB),
         cost_estimate=pl.CostEstimate(flops=0, bytes_accessed=2 * MIB, transcendentals=0),
     )(*arrays, after)
 
 
-def fetch_rows_kernel(first, blocks, total, weight_ref, _, out_ref, sems):
-    position = lax.axis_index("batch")
-    depth = out_ref.shape[0] // blocks
-    copies = []
-    for k in range(blocks):
-        start = pl.multiple_of(jnp.bitwise_xor(position, reverse(first + k, total)) * depth, depth)
-        copies.append(
-            pltpu.make_async_copy(
-                weight_ref.at[pl.ds(start, depth), :], out_ref.at[pl.ds(k * depth, depth), :], sems.at[k]
-            )
-        )
-    start_all(copies)
-
-
-def fetch_rows(weight, first, blocks, total, after):
-    depth = weight.shape[0] // total * blocks
+class Stream:
+    def __init__(self, pieces, buffers, sems):
+        self.pieces, self.buffers, self.sems = pieces, buffers, sems
+        for k in range(min(BUFFERS, len(pieces))):
+            self.copy(k).start()
+
+    def copy(self, k):
+        slot = k % BUFFERS
+        return pltpu.make_async_copy(self.pieces[k], self.buffers.at[slot], self.sems.at[slot])
+
+    def take(self, k, use):
+        self.copy(k).wait()
+        result = use(self.buffers[k % BUFFERS])
+        if k + BUFFERS < len(self.pieces):
+            self.copy(k + BUFFERS).start()
+        return result
+
+
+def stream_call(kernel, out, *args, weight, piece, extra=()):
+    specs = [VM] * len(args) + [ANY] * (1 + len(extra))
     return pl.pallas_call(
-        functools.partial(fetch_rows_kernel, first, blocks, total),
-        out_shape=pltpu.VMEM((depth, weight.shape[1]), weight.dtype),
-        in_specs=[ANY] * 2,
-        out_specs=VM,
-        scratch_shapes=[pltpu.SemaphoreType.DMA((blocks,))],
-        compiler_params=pltpu.CompilerParams(vmem_limit_bytes=2 * MIB),
-        cost_estimate=pl.CostEstimate(flops=0, bytes_accessed=2 * MIB, transcendentals=0),
-    )(weight, after)
+        kernel,
+        out_shape=out,
+        in_specs=specs,
+        out_specs=jax.tree.map(lambda _: VM, out),
+        scratch_shapes=[pltpu.VMEM((BUFFERS, *piece), weight.dtype), pltpu.SemaphoreType.DMA((BUFFERS,))],
+        compiler_params=pltpu.CompilerParams(vmem_limit_bytes=12 * MIB),
+        cost_estimate=pl.CostEstimate(flops=0, bytes_accessed=weight.size * 2, transcendentals=0),
+    )(*args, weight, *extra)
 
 
 def split3(value):
@@ -233,13 +252,14 @@
         out_specs=VM,
         scratch_shapes=[pltpu.VMEM(num.shape, jnp.float32)],
         compiler_params=pltpu.CompilerParams(vmem_limit_bytes=8 * MIB),
+        cost_estimate=pl.CostEstimate(flops=0, bytes_accessed=STEP_BYTES, transcendentals=0),
     )(num, state, pay)
 
 
-def project_kernel(attended_ref, first_ref, second_ref, out_ref):
+def project_kernel(attended_ref, weight_ref, out_ref):
     rows = out_ref.shape[0]
-    first = jnp.dot(attended_ref[...], first_ref[0], preferred_element_type=jnp.float32)
-    second = jnp.dot(attended_ref[...], second_ref[0], preferred_element_type=jnp.float32)
+    first = jnp.dot(attended_ref[...], weight_ref[0], preferred_element_type=jnp.float32)
+    second = jnp.dot(attended_ref[...], weight_ref[1], preferred_element_type=jnp.float32)
     out_ref[...] = first[:rows] + second[rows:]
 
 
@@ -248,34 +268,28 @@
     out_ref[0] = total.astype(jnp.bfloat16)
 
 
-def up_kernel(near_ref, far_ref, *refs):
-    chunks, (hidden_ref, out_ref, sem) = refs[:-3], refs[-3:]
-    half, _, depth = near_ref.shape
-    per = 2 * half // len(chunks)
-    copy = pltpu.make_async_copy(near_ref.at[0], hidden_ref, sem)
-    copy.start()
-    total = jnp.zeros(out_ref.shape, jnp.float32)
-    for j in range(2 * half):
-        block = near_ref[j] if j < half else far_ref[j - half]
-        weight = chunks[j // per][pl.ds(j % per * depth, depth), :]
-        total = total + jnp.dot(block, weight, preferred_element_type=jnp.float32)
-    out_ref[...] = (0.5 * total * (1.0 + lax.erf(total * math.sqrt(0.5)))).astype(jnp.bfloat16)
-    copy.wait()
-
-
-def up(near, far, chunks, units):
-    _, rows, columns = near.shape
-    return pl.pallas_call(
-        up_kernel,
-        out_shape=(
-            jax.ShapeDtypeStruct((rows, columns), jnp.bfloat16),
-            jax.ShapeDtypeStruct((rows, units), jnp.bfloat16),
-        ),
-        in_specs=[VM] * (2 + len(chunks)),
-        out_specs=(ANY, VM),
-        scratch_shapes=[pltpu.SemaphoreType.DMA],
-        compiler_params=pltpu.CompilerParams(vmem_limit_bytes=8 * MIB),
-    )(near, far, *chunks)
+def up_kernel(last, hidden_ref, *refs):
+    half, _, depth = hidden_ref.shape
+    if last:
+        before_ref, weight_ref, _, out_ref, buffers, sems = refs
+    else:
+        weight_ref, own_ref, out_ref, buffers, sems = refs
+        own_ref[...] = hidden_ref[0]
+    position = lax.axis_index("batch")
+    pieces = []
+    for j in range(half):
+        index = reverse(j + half if last else j, 2 * half)
+        start = pl.multiple_of(jnp.bitwise_xor(position, index) * depth, depth)
+        pieces.append(weight_ref.at[pl.ds(start, depth), :])
+    stream = Stream(pieces, buffers, sems)
+    total = before_ref[...] if last else jnp.zeros(out_ref.shape, jnp.float32)
+    for j in range(half):
+        total = total + stream.take(
+            j, lambda weight: jnp.dot(hidden_ref[j], weight, preferred_element_type=jnp.float32)
+        )
+    if last:
+        total = (0.5 * total * (1.0 + lax.erf(total * math.sqrt(0.5)))).astype(jnp.bfloat16)
+    out_ref[...] = total
 
 
 def reorder(activation):
@@ -287,18 +301,28 @@
     return jnp.dot(order, activation, preferred_element_type=jnp.float32).astype(jnp.bfloat16)
 
 
-def down_kernel(mine, act_ref, weight_ref, *rest):
+def down_kernel(mine, act_ref, *refs):
+    if mine:
+        weight_ref, out_ref, buffers, sems = refs
+    else:
+        before_ref, weight_ref, keep_ref, send_ref, buffers, sems = refs
     depth = act_ref.shape[1]
+    count = depth // buffers.shape[1]
+    step = buffers.shape[1]
     side = lax.axis_index("tensor")
-    start = pl.multiple_of((side if mine else 1 - side) * depth, depth)
-    part = jnp.dot(
-        reorder(act_ref[...]), weight_ref[pl.ds(start, depth), :], preferred_element_type=jnp.float32
-    )
+    base = (side if mine else 1 - side) * depth
+    stream = Stream(
+        [weight_ref.at[pl.ds(pl.multiple_of(base + k * step, step), step), :] for k in range(count)], buffers, sems
+    )
+    activation = reorder(act_ref[...])
+    total = None if mine else before_ref[...]
+    for k in range(count):
+        block = activation[:, k * step : (k + 1) * step]
+        part = stream.take(k, lambda weight: jnp.dot(block, weight, preferred_element_type=jnp.float32))
+        total = part if total is None else total + part
     if mine:
-        rest[0][...] = part
+        out_ref[...] = total
         return
-    before, keep_ref, send_ref = rest
-    total = before[...] + part
     half = total.shape[0] // 2
     keep_ref[...] = total[:half]
     send_ref[...] = total[half:]
@@ -332,11 +356,11 @@
     return pl.pallas_call(
         functools.partial(place_kernel, stride, order),
         out_shape=jax.ShapeDtypeStruct(gathered.shape[1:], gathered.dtype),
-        in_specs=[pl.BlockSpec(memory_space=pltpu.HBM), VM, SM, SM],
+        in_specs=[ANY, VM, SM, SM],
         out_specs=VM,
         scratch_shapes=[pltpu.VMEM(gathered.shape[1:], gathered.dtype), pltpu.SemaphoreType.DMA],
         compiler_params=pltpu.CompilerParams(vmem_limit_bytes=8 * MIB),
-    )(gathered, new_kv, parents, lengths)
+    )(in_hbm(gathered), new_kv, parents, lengths)
 
 
 def body(
@@ -362,33 +386,13 @@
     out_columns = down_weight.shape[1]
     f32, bf16 = jnp.float32, jnp.bfloat16
     shape = jax.ShapeDtypeStruct
-    down_weight = pltpu.with_memory_space_constraint(down_weight, pltpu.VMEM)
-    pieces = 8
-    local = {}
-    chunks = []
-
-    def load_operands(after):
-        sources = (queries[0, 0], init_cache[0], memory[0], new_kv[0, 0], residual)
-        local["all"] = fetch(sources, after)
-
-    def load_out(kind):
-        def work(after):
-            local[kind] = fetch([out_weight[kind : kind + 1]], after)[0]
-
-        return work
-
-    def load_up(after):
-        if len(chunks) < pieces:
-            per = devices // pieces
-            chunks.append(fetch_rows(up_weight, len(chunks) * per, per, devices, after))
-
+    up_weight = in_hbm(up_weight)
+    sources = (queries[0, 0], init_cache[0], memory[0], new_kv[0, 0], residual)
     bit = devices // 2
     other = xor_permute(queries[0, 0], "batch", bit)
-    load_operands(queries[0, 0])
-    query, cache_row, memory_row, new_row, residual_row = local["all"]
-    works = [load_out(0), load_out(1)]
-    query = jnp.concatenate([query, other])
-    query, far = doubling(query, stride, bit, lambda after: works.pop(0)(after))
+    loaded = fetch([in_hbm(x) for x in sources], queries[0, 0])
+    other, (query, cache_row, memory_row, new_row, residual_row) = pin(other, loaded)
+    query, far = doubling(jnp.concatenate([query, other]), stride, bit)
     state_shapes = (
         shape((2 * BEAMS, width), f32),
         shape((2 * BEAMS, 2 * LANES), f32),
@@ -409,36 +413,57 @@
     bit = stride
     while True:
         arrived = xor_permute(pay, "batch", bit)
-        load_up(pay)
-        load_up(pay)
+        if bit == stride:
+            arrived, (out_row,) = pin(arrived, fetch([in_hbm(out_weight)], pay))
         bit *= 2
         if bit == devices:
             break
         num, state, pay = call(merge_kernel, state_shapes, num, state, arrived)
     attended = finish(num, state, arrived)
     if stride > 1:
-        stacked = jnp.concatenate(doubling(attended[None], 1, stride, lambda after: None))
+        stacked = jnp.concatenate(doubling(attended[None], 1, stride))
         wanted = reverse(jnp.bitwise_xor(jnp.arange(stride, dtype=jnp.int32), request), stride)
         stacked = stacked[wanted].reshape(stride, 2, BEAMS, width)
         attended = stacked.transpose(1, 2, 0, 3).reshape(2 * rows, width)
 
-    partial = call(project_kernel, shape((rows, columns), f32), attended, local[0], local[1])
+    partial = call(project_kernel, shape((rows, columns), f32), attended, out_row)
     other = xor_permute(partial, "tensor", 1)
     mine = call(add_kernel, pltpu.VMEM((1, rows, columns), bf16), partial, other, residual_row)
-    near, far = doubling(mine, 1, devices, load_up)
-    while len(chunks) < pieces:
-        load_up(near)
-    hidden, activation = up(near, far, chunks, hidden_units)
+    near, far = doubling(mine, 1, devices)
+    piece = (columns, hidden_units)
+    hidden, first_half = stream_call(
+        functools.partial(up_kernel, False),
+        (shape((rows, columns), bf16), shape((rows, hidden_units), f32)),
+        near,
+        weight=up_weight,
+        piece=piece,
+    )
+    far, first_half = pin(far, first_half)
+    activation = stream_call(
+        functools.partial(up_kernel, True),
+        shape((rows, hidden_units), bf16),
+        far,
+        first_half,
+        weight=up_weight,
+        piece=piece,
+        extra=(down_weight,),
+    )
     arrived = xor_permute(activation, "tensor", 1)
-    before = call(
-        functools.partial(down_kernel, True), shape((rows, out_columns), f32), activation, down_weight
-    )
-    keep, send = call(
+    piece = (hidden_units // min(4, hidden_units // LANES or 1), out_columns)
+    before = stream_call(
+        functools.partial(down_kernel, True),
+        shape((rows, out_columns), f32),
+        activation,
+        weight=down_weight,
+        piece=piece,
+    )
+    keep, send = stream_call(
         functools.partial(down_kernel, False),
         (shape((rows // 2, out_columns), f32),) * 2,
         arrived,
-        down_weight,
         before,
+        weight=down_weight,
+        piece=piece,
     )
     bit = 1
     while True:

time: 91.8 us -> 91.6 us (level)
  starting transfers between devices: 11.6 us -> 24.6 us
  waiting for transfers between devices: 39.8 us -> 27.9 us
  local copies, waits for them, and re-layouts: 12.3 us -> 0.72 us
  Pallas kernels: 12 us -> 22.6 us
    ppermute x14, starting transfers between devices: 11.6 us -> 24.5 us  [xor_permute(): return lax.ppermute(value, axis, [(i, i ^ bit) for i in range(total)])]
    ppermute x14, waiting for transfers between devices: 39.2 us -> 27.2 us  [xor_permute(): return lax.ppermute(value, axis, [(i, i ^ bit) for i in range(total)])]
    pallas_call x9 -> x4, Pallas kernels: 4.01 us -> 13.5 us  [stream_call(): pl.pallas_call(kernel, out_shape=out, in_specs=specs, out_specs=jax.tree....]
    unnamed x28 -> x14, local copies, waits for them, and re-layouts: 9.41 us -> 0.69 us
    pallas_call x3 -> x2, Pallas kernels: 0.78 us -> 3.92 us  [fetch(): pl.pallas_call(functools.partial(fetch_kernel, count), out_shape=[pltpu.V...]
    slice x1 -> x0, local copies, waits for them, and re-layouts: 2.88 us -> none  [work(): local[kind] = fetch([out_weight[kind:kind + 1]], after)[0]]
    pallas_call x7 -> x5, Pallas kernels: 5.35 us -> 2.49 us  [call(): pl.pallas_call(kernel, out_shape=out, in_specs=specs or [VM] * len(args),...]
  transfers between devices with their start and end apart: 15 -> 15, of which waited for: 12 -> 12; matrix products, arithmetic and copies ran while one was open for 4% -> 1% of each run, Pallas kernels for 11% -> 22%
where the time goes in v6:
time: 91.6 us; the launch traced here: 91.4 us
  waiting for transfers between devices  27.9 us (30%)
  starting transfers between devices  24.6 us (27%)
  Pallas kernels  22.6 us (25%)
  between operations  14.9 us (16%)
    ppermute x14, waiting for transfers between devices, xor_permute(): return lax.ppermute(value, axis, [(i, i ^ bit) for i in range(total)])  27.2 us
    ppermute x14, starting transfers between devices, xor_permute(): return lax.ppermute(value, axis, [(i, i ^ bit) for i in range(total)])  24.5 us
    pallas_call x4, Pallas kernels, stream_call(): pl.pallas_call(kernel, out_shape=out, in_specs=specs, out_specs=jax.tree....  13.5 us
    pallas_call x2, Pallas kernels, fetch(): pl.pallas_call(functools.partial(fetch_kernel, count), out_shape=[pltpu.V...  3.92 us
    pallas_call x5, Pallas kernels, call(): pl.pallas_call(kernel, out_shape=out, in_specs=specs or [VM] * len(args),...  2.49 us
    pallas_call x1, Pallas kernels, place(): pl.pallas_call(functools.partial(place_kernel, stride, order), out_shape=...  2.38 us
  transfers between devices with their start and end apart: 15, of which 12 were waited for; matrix products, arithmetic and copies ran while one was open for 1% of the time, Pallas kernels for 22%

profile of v6, /device:TPU:0, one launch (start us, length us, event | category | flops | bytes accessed | tf_op | source)
XLA Modules:
  0.0 91.4 jit_solution(3987963108967662762)
XLA Ops:
  7.2 0.7 all-gather.2.cloned.1.call-update
  7.9 4.1 %collective-permute-start = (bf16[2,1536]{1,0:T(2,128)(2,1)}, bf16[2,1536]{1,0:T(2,128)(2,1)S(1)}, u32[]{:S(2)}, u32[]{:S(2)}) collective-permute-start(bf16[2,1536]{1,0:T(2,128)(2,1)} %bitcast.13), channel_id=1, source_target_pairs={{0,8},{2,10},{4,12},{6,14},{8,0},{10,2},{12,4},{14,6},{1,9},{3,11}... | collective-permute-start | bytes 18440 | tf_op jit(solution)/shard_map/ppermute | solution.py:27
  12.0 1.3 %shard_map.121 = (bf16[2,1536]{1,0:T(2,128)(2,1)S(1)}, bf16[2,64,1536]{2,1,0:T(8,128)(2,1)S(1)}, bf16[2,64,1536]{2,1,0:T(8,128)(2,1)S(1)}, bf16[2,1536]{1,0:T(2,128)(2,1)S(1)}, bf16[1,8,768]{2,1,0:T(8,128)(2,1)S(1)}) custom-call(bf16[2,1536]{1,0:T(2,128)(2,1)} %bitcast.14, bf16[2,64,1536]{2,1,0:T(8,128)(2,1)} %bitcast.10, bf16[2,64,1536]{2,1,0:T(8,128)(2,1)} %bitcast.11, ...), custom_call_target="tpu_custom_call" | custom-call | bytes 2097152 | tf_op jit(solution)/shard_map/pallas_call | solution.py:85
  13.8 2.0 %collective-permute-start.1 = (bf16[4,1536]{1,0:T(4,128)(2,1)S(1)}, bf16[4,1536]{1,0:T(4,128)(2,1)S(1)}, u32[]{:S(2)}, u32[]{:S(2)}) collective-permute-start(bf16[4,1536]{1,0:T(4,128)(2,1)S(1)} %pad_maximum_fusion.3), channel_id=1, source_target_pairs={{0,4},{2,6},{4,0},{6,2},{8,12},{10,14},{12,8},{14,10},{1,5},{3,7},... | collective-permute-start | bytes 36872 | tf_op jit(solution)/shard_map/ppermute | solution.py:27
  15.8 1.8 %collective-permute-done.1 = bf16[4,1536]{1,0:T(4,128)(2,1)S(1)} collective-permute-done((bf16[4,1536]{1,0:T(4,128)(2,1)S(1)}, bf16[4,1536]{1,0:T(4,128)(2,1)S(1)}, u32[]{:S(2)}, u32[]{:S(2)}) %collective-permute-start.1) | collective-permute-done | bytes 12320 | tf_op jit(solution)/shard_map/ppermute | solution.py:27
  17.6 1.9 %collective-permute-start.2 = (bf16[8,1536]{1,0:T(8,128)(2,1)S(1)}, bf16[8,1536]{1,0:T(8,128)(2,1)S(1)}, u32[]{:S(2)}, u32[]{:S(2)}) collective-permute-start(bf16[8,1536]{1,0:T(8,128)(2,1)S(1)} %pad_maximum_fusion.1.near_ref), channel_id=1, source_target_pairs={{0,2},{2,0},{4,6},{6,4},{8,10},{10,8},{12,14},{14,12},{1,3},{3,1},... | collective-permute-start | bytes 73736 | tf_op jit(solution)/shard_map/ppermute | solution.py:27
  20.2 1.6 %collective-permute-done.2.far_ref = bf16[8,1536]{1,0:T(8,128)(2,1)S(1)} collective-permute-done((bf16[8,1536]{1,0:T(8,128)(2,1)S(1)}, bf16[8,1536]{1,0:T(8,128)(2,1)S(1)}, u32[]{:S(2)}, u32[]{:S(2)}) %collective-permute-start.2) | collective-permute-done | bytes 24608 | tf_op jit(solution)/shard_map/ppermute | solution.py:27
  21.8 0.7 copy-done
  22.4 1.3 %shard_map.122 = (f32[16,1536]{1,0:T(8,128)S(1)}, f32[16,256]{1,0:T(8,128)S(1)}, bf16[16,1664]{1,0:T(8,128)(2,1)S(1)}) custom-call(bf16[8,1536]{1,0:T(8,128)(2,1)S(1)} %pad_maximum_fusion.1.near_ref, bf16[8,1536]{1,0:T(8,128)(2,1)S(1)} %collective-permute-done.2.far_ref, bf16[2,64,1536]{2,1,0:T(8,128)(2,1)S(1)} %get-tuple-element.38.cache_ref, ...), custom_call_target="tpu_custom_call" | custom-call | bytes 16777216 | tf_op jit(solution)/shard_map/pallas_call | solution.py:46
  23.7 2.2 %collective-permute-start.3 = (bf16[16,1664]{1,0:T(8,128)(2,1)S(1)}, bf16[16,1664]{1,0:T(8,128)(2,1)S(1)}, u32[]{:S(2)}, u32[]{:S(2)}) collective-permute-start(bf16[16,1664]{1,0:T(8,128)(2,1)S(1)} %get-tuple-element.43.refs_1_), channel_id=1, source_target_pairs={{0,2},{2,0},{4,6},{6,4},{8,10},{10,8},{12,14},{14,12},{1,3},{3,1},... | collective-permute-start | bytes 159752 | tf_op jit(solution)/shard_map/ppermute | solution.py:27
  25.9 2.6 %shard_map.123.weight_ref = bf16[2,1536,768]{2,1,0:T(8,128)(2,1)S(1)} custom-call(bf16[2,1536,768]{2,1,0:T(8,128)(2,1)} %refs_0_.3, bf16[16,1664]{1,0:T(8,128)(2,1)S(1)} %get-tuple-element.43.refs_1_), custom_call_target="tpu_custom_call" | custom-call | bytes 2097152 | tf_op jit(solution)/shard_map/pallas_call | solution.py:85
  29.9 5.2 %collective-permute-done.4.pay_ref = bf16[16,1664]{1,0:T(8,128)(2,1)S(1)} collective-permute-done((bf16[16,1664]{1,0:T(8,128)(2,1)S(1)}, bf16[16,1664]{1,0:T(8,128)(2,1)S(1)}, u32[]{:S(2)}, u32[]{:S(2)}) %collective-permute-start.4) | collective-permute-done | bytes 53280 | tf_op jit(solution)/shard_map/ppermute | solution.py:27
  35.4 2.3 %collective-permute-start.5 = (bf16[16,1664]{1,0:T(8,128)(2,1)S(1)}, bf16[16,1664]{1,0:T(8,128)(2,1)S(1)}, u32[]{:S(2)}, u32[]{:S(2)}) collective-permute-start(bf16[16,1664]{1,0:T(8,128)(2,1)S(1)} %get-tuple-element.50), channel_id=1, source_target_pairs={{0,8},{2,10},{4,12},{6,14},{8,0},{10,2},{12,4},{14,6},{1,9},{3,11}... | collective-permute-start | bytes 159752 | tf_op jit(solution)/shard_map/ppermute | solution.py:27
  37.7 3.8 %collective-permute-done.5.pay_ref = bf16[16,1664]{1,0:T(8,128)(2,1)S(1)} collective-permute-done((bf16[16,1664]{1,0:T(8,128)(2,1)S(1)}, bf16[16,1664]{1,0:T(8,128)(2,1)S(1)}, u32[]{:S(2)}, u32[]{:S(2)}) %collective-permute-start.5) | collective-permute-done | bytes 53280 | tf_op jit(solution)/shard_map/ppermute | solution.py:27
  42.5 1.2 %collective-permute-done.6.other_ref = f32[8,768]{1,0:T(8,128)S(1)} collective-permute-done((f32[8,768]{1,0:T(8,128)S(1)}, f32[8,768]{1,0:T(8,128)S(1)}, u32[]{:S(2)}, u32[]{:S(2)}) %collective-permute-start.6) | collective-permute-done | bytes 24608 | tf_op jit(solution)/shard_map/ppermute | solution.py:27
  43.7 2.4 %collective-permute-start.7 = (bf16[1,8,768]{2,1,0:T(8,128)(2,1)S(1)}, bf16[1,8,768]{2,1,0:T(8,128)(2,1)S(1)}, u32[]{:S(2)}, u32[]{:S(2)}) collective-permute-start(bf16[1,8,768]{2,1,0:T(8,128)(2,1)S(1)} %shard_map.128), channel_id=1, source_target_pairs={{0,8},{2,10},{4,12},{6,14},{8,0},{10,2},{12,4},{14,6},{1,9},{3,11}... | collective-permute-start | bytes 36872 | tf_op jit(solution)/shard_map/ppermute | solution.py:27
  46.1 2.5 %collective-permute-done.7 = bf16[1,8,768]{2,1,0:T(8,128)(2,1)S(1)} collective-permute-done((bf16[1,8,768]{2,1,0:T(8,128)(2,1)S(1)}, bf16[1,8,768]{2,1,0:T(8,128)(2,1)S(1)}, u32[]{:S(2)}, u32[]{:S(2)}) %collective-permute-start.7) | collective-permute-done | bytes 12320 | tf_op jit(solution)/shard_map/ppermute | solution.py:27
  48.6 1.9 %collective-permute-start.8 = (bf16[2,8,768]{2,1,0:T(8,128)(2,1)S(1)}, bf16[2,8,768]{2,1,0:T(8,128)(2,1)S(1)}, u32[]{:S(2)}, u32[]{:S(2)}) collective-permute-start(bf16[2,8,768]{2,1,0:T(8,128)(2,1)S(1)} %pad_maximum_fusion.2), channel_id=1, source_target_pairs={{0,4},{2,6},{4,0},{6,2},{8,12},{10,14},{12,8},{14,10},{1,5},{3,7},... | collective-permute-start | bytes 73736 | tf_op jit(solution)/shard_map/ppermute | solution.py:27
  50.5 2.1 %collective-permute-done.8 = bf16[2,8,768]{2,1,0:T(8,128)(2,1)S(1)} collective-permute-done((bf16[2,8,768]{2,1,0:T(8,128)(2,1)S(1)}, bf16[2,8,768]{2,1,0:T(8,128)(2,1)S(1)}, u32[]{:S(2)}, u32[]{:S(2)}) %collective-permute-start.8) | collective-permute-done | bytes 24608 | tf_op jit(solution)/shard_map/ppermute | solution.py:27
  52.7 2.3 %collective-permute-start.9 = (bf16[4,8,768]{2,1,0:T(8,128)(2,1)S(1)}, bf16[4,8,768]{2,1,0:T(8,128)(2,1)S(1)}, u32[]{:S(2)}, u32[]{:S(2)}) collective-permute-start(bf16[4,8,768]{2,1,0:T(8,128)(2,1)S(1)} %pad_maximum_fusion.hidden_ref), channel_id=1, source_target_pairs={{0,2},{2,0},{4,6},{6,4},{8,10},{10,8},{12,14},{14,12},{1,3},{3,1},... | collective-permute-start | bytes 147464 | tf_op jit(solution)/shard_map/ppermute | solution.py:27
  55.0 4.6 %shard_map.129 = (bf16[8,768]{1,0:T(8,128)(2,1)}, f32[8,1536]{1,0:T(8,128)S(1)}) custom-call(bf16[4,8,768]{2,1,0:T(8,128)(2,1)S(1)} %pad_maximum_fusion.hidden_ref, bf16[6144,1536]{1,0:T(8,128)(2,1)} %refs_1_.2), custom_call_target="tpu_custom_call" | custom-call | bytes 18874368 | tf_op jit(solution)/shard_map/pallas_call | solution.py:116
  59.7 4.5 %shard_map.130.act_ref = bf16[8,1536]{1,0:T(8,128)(2,1)S(1)} custom-call(bf16[4,8,768]{2,1,0:T(8,128)(2,1)S(1)} %collective-permute-done.9.hidden_ref, f32[8,1536]{1,0:T(8,128)S(1)} %get-tuple-element.56.refs_0_, bf16[6144,1536]{1,0:T(8,128)(2,1)} %refs_1_.2, bf16[3072,3072]{1,0:T(8,128)(2,1)S(1)} %bitcast.9), custom_call_target="tpu_custom_call" | custom-call | bytes 18874368 | tf_op jit(solution)/shard_map/pallas_call | solution.py:116
  64.2 2.3 %shard_map.131.refs_0_ = f32[8,3072]{1,0:T(8,128)S(1)} custom-call(bf16[8,1536]{1,0:T(8,128)(2,1)S(1)} %shard_map.130.act_ref, bf16[3072,3072]{1,0:T(8,128)(2,1)S(1)} %bitcast.9), custom_call_target="tpu_custom_call" | custom-call | bytes 18874368 | tf_op jit(solution)/shard_map/pallas_call | solution.py:116
  66.5 2.2 %shard_map.132 = (f32[4,3072]{1,0:T(4,128)S(1)}, f32[4,3072]{1,0:T(4,128)S(1)}) custom-call(bf16[8,1536]{1,0:T(8,128)(2,1)S(1)} %collective-permute-done.10.act_ref, f32[8,3072]{1,0:T(8,128)S(1)} %shard_map.131.refs_0_, bf16[3072,3072]{1,0:T(8,128)(2,1)S(1)} %bitcast.9), custom_call_target="tpu_custom_call" | custom-call | bytes 18874368 | tf_op jit(solution)/shard_map/pallas_call | solution.py:116
  68.7 0.9 collective-permute-start.11
  69.6 3.3 %collective-permute-done.11 = f32[4,3072]{1,0:T(4,128)S(1)} collective-permute-done((f32[4,3072]{1,0:T(4,128)S(1)}, f32[4,3072]{1,0:T(4,128)S(1)}, u32[]{:S(2)}, u32[]{:S(2)}) %collective-permute-start.11) | collective-permute-done | bytes 49184 | tf_op jit(solution)/shard_map/ppermute | solution.py:27
  72.9 1.3 %collective-permute-start.12 = (f32[2,3072]{1,0:T(2,128)S(1)}, f32[2,3072]{1,0:T(2,128)S(1)}, u32[]{:S(2)}, u32[]{:S(2)}) collective-permute-start(f32[2,3072]{1,0:T(2,128)S(1)} %slice.17), channel_id=1, source_target_pairs={{0,4},{2,6},{4,0},{6,2},{8,12},{10,14},{12,8},{14,10},{1,5},{3,7},... | collective-permute-start | bytes 73736 | tf_op jit(solution)/shard_map/ppermute | solution.py:27
  74.3 2.6 %collective-permute-done.12 = f32[2,3072]{1,0:T(2,128)S(1)} collective-permute-done((f32[2,3072]{1,0:T(2,128)S(1)}, f32[2,3072]{1,0:T(2,128)S(1)}, u32[]{:S(2)}, u32[]{:S(2)}) %collective-permute-start.12) | collective-permute-done | bytes 24608 | tf_op jit(solution)/shard_map/ppermute | solution.py:27
  76.9 2.6 %collective-permute-start.13 = (f32[1,3072]{1,0:T(1,128)S(1)}, f32[1,3072]{1,0:T(1,128)S(1)}, u32[]{:S(2)}, u32[]{:S(2)}) collective-permute-start(f32[1,3072]{1,0:T(1,128)S(1)} %slice.19), channel_id=1, source_target_pairs={{0,8},{2,10},{4,12},{6,14},{8,0},{10,2},{12,4},{14,6},{1,9},{3,11}... | collective-permute-start | bytes 36872 | tf_op jit(solution)/shard_map/ppermute | solution.py:27
  79.4 2.1 %collective-permute-done.13 = f32[1,3072]{1,0:T(1,128)S(1)} collective-permute-done((f32[1,3072]{1,0:T(1,128)S(1)}, f32[1,3072]{1,0:T(1,128)S(1)}, u32[]{:S(2)}, u32[]{:S(2)}) %collective-permute-start.13) | collective-permute-done | bytes 12320 | tf_op jit(solution)/shard_map/ppermute | solution.py:27
  81.5 0.6 fusion.1
  82.1 2.4 %shard_map.133 = bf16[2,64,1536]{2,1,0:T(8,128)(2,1)} custom-call(bf16[8,2,64,1536]{3,2,1,0:T(8,128)(2,1)} %all-gather.2.cloned.1.call-done.gathered_ref, bf16[2,1536]{1,0:T(2,128)(2,1)S(1)} %get-tuple-element.40.new_ref, s32[1,8]{1,0:T(1,128)S(1)} %copy-done.1, s32[1]{0:T(128)S(6)} %copy.13.lengths_ref), custom_call_target="tpu_custom_call" | custom-call | tf_op jit(solution)/shard_map/pallas_call | solution.py:356
  (36 shorter events, 3.5 us)
Async XLA Ops:
  7.2 75.0 %all-gather.2.cloned.1.call-start = ((), (), s32[]{:S(2)}) async-start(), calls=%async_computation | async-start | bytes 3538944 | tf_op jit(solution)/shard_map/all_gather | solution.py:483
  7.9 5.9 %collective-permute-start = (bf16[2,1536]{1,0:T(2,128)(2,1)}, bf16[2,1536]{1,0:T(2,128)(2,1)S(1)}, u32[]{:S(2)}, u32[]{:S(2)}) collective-permute-start(bf16[2,1536]{1,0:T(2,128)(2,1)} %bitcast.13), channel_id=1, source_target_pairs={{0,8},{2,10},{4,12},{6,14},{8,0},{10,2},{12,4},{14,6},{1,9},{3,11}... | collective-permute-start | bytes 18440 | tf_op jit(solution)/shard_map/ppermute | solution.py:27
  13.8 3.8 %collective-permute-start.1 = (bf16[4,1536]{1,0:T(4,128)(2,1)S(1)}, bf16[4,1536]{1,0:T(4,128)(2,1)S(1)}, u32[]{:S(2)}, u32[]{:S(2)}) collective-permute-start(bf16[4,1536]{1,0:T(4,128)(2,1)S(1)} %pad_maximum_fusion.3), channel_id=1, source_target_pairs={{0,4},{2,6},{4,0},{6,2},{8,12},{10,14},{12,8},{14,10},{1,5},{3,7},... | collective-permute-start | bytes 36872 | tf_op jit(solution)/shard_map/ppermute | solution.py:27
  17.6 4.1 %collective-permute-start.2 = (bf16[8,1536]{1,0:T(8,128)(2,1)S(1)}, bf16[8,1536]{1,0:T(8,128)(2,1)S(1)}, u32[]{:S(2)}, u32[]{:S(2)}) collective-permute-start(bf16[8,1536]{1,0:T(8,128)(2,1)S(1)} %pad_maximum_fusion.1.near_ref), channel_id=1, source_target_pairs={{0,2},{2,0},{4,6},{6,4},{8,10},{10,8},{12,14},{14,12},{1,3},{3,1},... | collective-permute-start | bytes 73736 | tf_op jit(solution)/shard_map/ppermute | solution.py:27
  21.7 0.7 copy-start
  23.7 5.4 %collective-permute-start.3 = (bf16[16,1664]{1,0:T(8,128)(2,1)S(1)}, bf16[16,1664]{1,0:T(8,128)(2,1)S(1)}, u32[]{:S(2)}, u32[]{:S(2)}) collective-permute-start(bf16[16,1664]{1,0:T(8,128)(2,1)S(1)} %get-tuple-element.43.refs_1_), channel_id=1, source_target_pairs={{0,2},{2,0},{4,6},{6,4},{8,10},{10,8},{12,14},{14,12},{1,3},{3,1},... | collective-permute-start | bytes 159752 | tf_op jit(solution)/shard_map/ppermute | solution.py:27
  25.8 33.8 %slice-start = ((s8[18874368]{0:T(1024)(128)(4,1)}), s8[4194304]{0:T(1024)(128)(4,1)S(1)}, s32[]{:S(2)}) async-start(s8[18874368]{0:T(1024)(128)(4,1)} %bitcast.8), calls=%async_computation.1 | async-start | bytes 8388608
  25.9 33.8 %slice-start.1 = ((s8[18874368]{0:T(1024)(128)(4,1)}), s8[4194304]{0:T(1024)(128)(4,1)S(1)}, s32[]{:S(2)}) async-start(s8[18874368]{0:T(1024)(128)(4,1)} %bitcast.8), calls=%async_computation.2 | async-start | bytes 8388608
  29.4 5.7 %collective-permute-start.4 = (bf16[16,1664]{1,0:T(8,128)(2,1)S(1)}, bf16[16,1664]{1,0:T(8,128)(2,1)S(1)}, u32[]{:S(2)}, u32[]{:S(2)}) collective-permute-start(bf16[16,1664]{1,0:T(8,128)(2,1)S(1)} %get-tuple-element.47), channel_id=1, source_target_pairs={{0,4},{2,6},{4,0},{6,2},{8,12},{10,14},{12,8},{14,10},{1,5},{3,7},... | collective-permute-start | bytes 159752 | tf_op jit(solution)/shard_map/ppermute | solution.py:27
  35.4 6.1 %collective-permute-start.5 = (bf16[16,1664]{1,0:T(8,128)(2,1)S(1)}, bf16[16,1664]{1,0:T(8,128)(2,1)S(1)}, u32[]{:S(2)}, u32[]{:S(2)}) collective-permute-start(bf16[16,1664]{1,0:T(8,128)(2,1)S(1)} %get-tuple-element.50), channel_id=1, source_target_pairs={{0,8},{2,10},{4,12},{6,14},{8,0},{10,2},{12,4},{14,6},{1,9},{3,11}... | collective-permute-start | bytes 159752 | tf_op jit(solution)/shard_map/ppermute | solution.py:27
  41.8 17.9 %slice-start.2 = ((s8[18874368]{0:T(1024)(128)(4,1)}), s8[4194304]{0:T(1024)(128)(4,1)S(1)}, s32[]{:S(2)}) async-start(s8[18874368]{0:T(1024)(128)(4,1)} %bitcast.8), calls=%async_computation.3 | async-start | bytes 8388608
  42.4 1.3 %collective-permute-start.6 = (f32[8,768]{1,0:T(8,128)S(1)}, f32[8,768]{1,0:T(8,128)S(1)}, u32[]{:S(2)}, u32[]{:S(2)}) collective-permute-start(f32[8,768]{1,0:T(8,128)S(1)} %shard_map.127.own_ref), channel_id=1, source_target_pairs={{0,1},{1,0},{2,3},{3,2},{4,5},{5,4},{6,7},{7,6},{8,9},{9,8},{10,11... | collective-permute-start | bytes 73736 | tf_op jit(solution)/shard_map/ppermute | solution.py:27
  43.7 4.9 %collective-permute-start.7 = (bf16[1,8,768]{2,1,0:T(8,128)(2,1)S(1)}, bf16[1,8,768]{2,1,0:T(8,128)(2,1)S(1)}, u32[]{:S(2)}, u32[]{:S(2)}) collective-permute-start(bf16[1,8,768]{2,1,0:T(8,128)(2,1)S(1)} %shard_map.128), channel_id=1, source_target_pairs={{0,8},{2,10},{4,12},{6,14},{8,0},{10,2},{12,4},{14,6},{1,9},{3,11}... | collective-permute-start | bytes 36872 | tf_op jit(solution)/shard_map/ppermute | solution.py:27
  48.6 4.1 %collective-permute-start.8 = (bf16[2,8,768]{2,1,0:T(8,128)(2,1)S(1)}, bf16[2,8,768]{2,1,0:T(8,128)(2,1)S(1)}, u32[]{:S(2)}, u32[]{:S(2)}) collective-permute-start(bf16[2,8,768]{2,1,0:T(8,128)(2,1)S(1)} %pad_maximum_fusion.2), channel_id=1, source_target_pairs={{0,4},{2,6},{4,0},{6,2},{8,12},{10,14},{12,8},{14,10},{1,5},{3,7},... | collective-permute-start | bytes 73736 | tf_op jit(solution)/shard_map/ppermute | solution.py:27
  52.6 7.0 %slice-start.3 = ((s8[18874368]{0:T(1024)(128)(4,1)}), s8[4194304]{0:T(1024)(128)(4,1)S(1)}, s32[]{:S(2)}) async-start(s8[18874368]{0:T(1024)(128)(4,1)} %bitcast.8), calls=%async_computation.4 | async-start | bytes 8388608
  52.6 7.0 %slice-start.4 = ((s8[18874368]{0:T(1024)(128)(4,1)}), s8[2097152]{0:T(1024)(128)(4,1)S(1)}, s32[]{:S(2)}) async-start(s8[18874368]{0:T(1024)(128)(4,1)} %bitcast.8), calls=%async_computation.5 | async-start | bytes 4194304
  52.7 6.9 %collective-permute-start.9 = (bf16[4,8,768]{2,1,0:T(8,128)(2,1)S(1)}, bf16[4,8,768]{2,1,0:T(8,128)(2,1)S(1)}, u32[]{:S(2)}, u32[]{:S(2)}) collective-permute-start(bf16[4,8,768]{2,1,0:T(8,128)(2,1)S(1)} %pad_maximum_fusion.hidden_ref), channel_id=1, source_target_pairs={{0,2},{2,0},{4,6},{6,4},{8,10},{10,8},{12,14},{14,12},{1,3},{3,1},... | collective-permute-start | bytes 147464 | tf_op jit(solution)/shard_map/ppermute | solution.py:27
  64.1 2.4 %collective-permute-start.10 = (bf16[8,1536]{1,0:T(8,128)(2,1)S(1)}, bf16[8,1536]{1,0:T(8,128)(2,1)S(1)}, u32[]{:S(2)}, u32[]{:S(2)}) collective-permute-start(bf16[8,1536]{1,0:T(8,128)(2,1)S(1)} %shard_map.130.act_ref), channel_id=1, source_target_pairs={{0,1},{1,0},{2,3},{3,2},{4,5},{5,4},{6,7},{7,6},{8,9},{9,8},{10,11... | collective-permute-start | bytes 73736 | tf_op jit(solution)/shard_map/ppermute | solution.py:27
  66.5 15.6 %copy-start.1 = (s32[1,8]{1,0:T(1,128)S(1)}, s32[1,8]{1,0:T(1,128)}, u32[]{:S(2)}) copy-start(s32[1,8]{1,0:T(1,128)} %parents_ref.3) | copy-start | bytes 100
  68.7 4.2 %collective-permute-start.11 = (f32[4,3072]{1,0:T(4,128)S(1)}, f32[4,3072]{1,0:T(4,128)S(1)}, u32[]{:S(2)}, u32[]{:S(2)}) collective-permute-start(f32[4,3072]{1,0:T(4,128)S(1)} %get-tuple-element.58), channel_id=1, source_target_pairs={{0,2},{2,0},{4,6},{6,4},{8,10},{10,8},{12,14},{14,12},{1,3},{3,1},... | collective-permute-start | bytes 147464 | tf_op jit(solution)/shard_map/ppermute | solution.py:27
  72.9 3.9 %collective-permute-start.12 = (f32[2,3072]{1,0:T(2,128)S(1)}, f32[2,3072]{1,0:T(2,128)S(1)}, u32[]{:S(2)}, u32[]{:S(2)}) collective-permute-start(f32[2,3072]{1,0:T(2,128)S(1)} %slice.17), channel_id=1, source_target_pairs={{0,4},{2,6},{4,0},{6,2},{8,12},{10,14},{12,8},{14,10},{1,5},{3,7},... | collective-permute-start | bytes 73736 | tf_op jit(solution)/shard_map/ppermute | solution.py:27
  76.9 4.7 %collective-permute-start.13 = (f32[1,3072]{1,0:T(1,128)S(1)}, f32[1,3072]{1,0:T(1,128)S(1)}, u32[]{:S(2)}, u32[]{:S(2)}) collective-permute-start(f32[1,3072]{1,0:T(1,128)S(1)} %slice.19), channel_id=1, source_target_pairs={{0,8},{2,10},{4,12},{6,14},{8,0},{10,2},{12,4},{14,6},{1,9},{3,11}... | collective-permute-start | bytes 36872 | tf_op jit(solution)/shard_map/ppermute | solution.py:27
Sparse Core Ops, SparseCore 0:
  9.5 44.7 all-gather.1

commit v7 on v6

--- a/solution.py
+++ b/solution.py
@@ -14,7 +14,7 @@
 BEAMS = 8
 LOW = -1e30
 MIB = 1024 * 1024
-BUFFERS = 3
+SPLIT = 2
 STEP_BYTES = 16 * MIB
 
 VM = pl.BlockSpec(memory_space=pltpu.VMEM)
@@ -95,31 +95,27 @@
 
 class Stream:
     def __init__(self, pieces, buffers, sems):
-        self.pieces, self.buffers, self.sems = pieces, buffers, sems
-        for k in range(min(BUFFERS, len(pieces))):
-            self.copy(k).start()
-
-    def copy(self, k):
-        slot = k % BUFFERS
-        return pltpu.make_async_copy(self.pieces[k], self.buffers.at[slot], self.sems.at[slot])
-
-    def take(self, k, use):
-        self.copy(k).wait()
-        result = use(self.buffers[k % BUFFERS])
-        if k + BUFFERS < len(self.pieces):
-            self.copy(k + BUFFERS).start()
-        return result
-
-
-def stream_call(kernel, out, *args, weight, piece, extra=()):
+        self.buffers = buffers
+        self.copies = [
+            pltpu.make_async_copy(piece, buffers.at[k], sems.at[k]) for k, piece in enumerate(pieces)
+        ]
+        for copy in self.copies:
+            copy.start()
+
+    def take(self, k):
+        self.copies[k].wait()
+        return self.buffers[k]
+
+
+def stream_call(kernel, out, *args, weight, count, piece, extra=()):
     specs = [VM] * len(args) + [ANY] * (1 + len(extra))
     return pl.pallas_call(
         kernel,
         out_shape=out,
         in_specs=specs,
         out_specs=jax.tree.map(lambda _: VM, out),
-        scratch_shapes=[pltpu.VMEM((BUFFERS, *piece), weight.dtype), pltpu.SemaphoreType.DMA((BUFFERS,))],
-        compiler_params=pltpu.CompilerParams(vmem_limit_bytes=12 * MIB),
+        scratch_shapes=[pltpu.VMEM((count, *piece), weight.dtype), pltpu.SemaphoreType.DMA((count,))],
+        compiler_params=pltpu.CompilerParams(vmem_limit_bytes=14 * MIB),
         cost_estimate=pl.CostEstimate(flops=0, bytes_accessed=weight.size * 2, transcendentals=0),
     )(*args, weight, *extra)
 
@@ -276,17 +272,20 @@
         weight_ref, own_ref, out_ref, buffers, sems = refs
         own_ref[...] = hidden_ref[0]
     position = lax.axis_index("batch")
+    split = buffers.shape[0] // half
+    step = depth // split
     pieces = []
     for j in range(half):
         index = reverse(j + half if last else j, 2 * half)
-        start = pl.multiple_of(jnp.bitwise_xor(position, index) * depth, depth)
-        pieces.append(weight_ref.at[pl.ds(start, depth), :])
+        start = jnp.bitwise_xor(position, index) * depth
+        for k in range(split):
+            pieces.append(weight_ref.at[pl.ds(pl.multiple_of(start + k * step, step), step), :])
     stream = Stream(pieces, buffers, sems)
     total = before_ref[...] if last else jnp.zeros(out_ref.shape, jnp.float32)
     for j in range(half):
-        total = total + stream.take(
-            j, lambda weight: jnp.dot(hidden_ref[j], weight, preferred_element_type=jnp.float32)
-        )
+        for k in range(split):
+            block = hidden_ref[j][:, k * step : (k + 1) * step]
+            total = total + jnp.dot(block, stream.take(j * split + k), preferred_element_type=jnp.float32)
     if last:
         total = (0.5 * total * (1.0 + lax.erf(total * math.sqrt(0.5)))).astype(jnp.bfloat16)
     out_ref[...] = total
@@ -301,28 +300,18 @@
     return jnp.dot(order, activation, preferred_element_type=jnp.float32).astype(jnp.bfloat16)
 
 
-def down_kernel(mine, act_ref, *refs):
+def down_kernel(mine, act_ref, weight_ref, *rest):
+    depth = act_ref.shape[1]
+    side = lax.axis_index("tensor")
+    start = pl.multiple_of((side if mine else 1 - side) * depth, depth)
+    part = jnp.dot(
+        reorder(act_ref[...]), weight_ref[pl.ds(start, depth), :], preferred_element_type=jnp.float32
+    )
     if mine:
-        weight_ref, out_ref, buffers, sems = refs
-    else:
-        before_ref, weight_ref, keep_ref, send_ref, buffers, sems = refs
-    depth = act_ref.shape[1]
-    count = depth // buffers.shape[1]
-    step = buffers.shape[1]
-    side = lax.axis_index("tensor")
-    base = (side if mine else 1 - side) * depth
-    stream = Stream(
-        [weight_ref.at[pl.ds(pl.multiple_of(base + k * step, step), step), :] for k in range(count)], buffers, sems
-    )
-    activation = reorder(act_ref[...])
-    total = None if mine else before_ref[...]
-    for k in range(count):
-        block = activation[:, k * step : (k + 1) * step]
-        part = stream.take(k, lambda weight: jnp.dot(block, weight, preferred_element_type=jnp.float32))
-        total = part if total is None else total + part
-    if mine:
-        out_ref[...] = total
+        rest[0][...] = part
         return
+    before, keep_ref, send_ref = rest
+    total = before[...] + part
     half = total.shape[0] // 2
     keep_ref[...] = total[:half]
     send_ref[...] = total[half:]
@@ -387,6 +376,7 @@
     f32, bf16 = jnp.float32, jnp.bfloat16
     shape = jax.ShapeDtypeStruct
     up_weight = in_hbm(up_weight)
+    down_weight = pltpu.with_memory_space_constraint(down_weight, pltpu.VMEM)
     sources = (queries[0, 0], init_cache[0], memory[0], new_kv[0, 0], residual)
     bit = devices // 2
     other = xor_permute(queries[0, 0], "batch", bit)
@@ -430,12 +420,14 @@
     other = xor_permute(partial, "tensor", 1)
     mine = call(add_kernel, pltpu.VMEM((1, rows, columns), bf16), partial, other, residual_row)
     near, far = doubling(mine, 1, devices)
-    piece = (columns, hidden_units)
+    split = SPLIT if columns % (SPLIT * LANES) == 0 else 1
+    count, piece = devices // 2 * split, (columns // split, hidden_units)
     hidden, first_half = stream_call(
         functools.partial(up_kernel, False),
         (shape((rows, columns), bf16), shape((rows, hidden_units), f32)),
         near,
         weight=up_weight,
+        count=count,
         piece=piece,
     )
     far, first_half = pin(far, first_half)
@@ -445,43 +437,39 @@
         far,
         first_half,
         weight=up_weight,
+        count=count,
         piece=piece,
         extra=(down_weight,),
     )
     arrived = xor_permute(activation, "tensor", 1)
-    piece = (hidden_units // min(4, hidden_units // LANES or 1), out_columns)
-    before = stream_call(
-        functools.partial(down_kernel, True),
-        shape((rows, out_columns), f32),
-        activation,
-        weight=down_weight,
-        piece=piece,
-    )
-    keep, send = stream_call(
+    before = call(
+        functools.partial(down_kernel, True), shape((rows, out_columns), f32), activation, down_weight
+    )
+    keep, send = call(
         functools.partial(down_kernel, False),
         (shape((rows // 2, out_columns), f32),) * 2,
         arrived,
+        down_weight,
         before,
-        weight=down_weight,
-        piece=piece,
-    )
-    bit = 1
-    while True:
-        total = keep + xor_permute(send, "batch", bit)
-        bit *= 2
-        if bit == devices:
-            break
-        half = total.shape[0] // 2
-        keep, send = total[:half], total[half:]
-    ffn_row = total.astype(bf16)
-
+    )
     order = ring(devices)
     groups = []
     for r in range(stride):
         groups.append([(beam * stride + r) * 2 for beam in order])
         groups.append([(beam * stride + r) * 2 + 1 for beam in reversed(order)])
     gathered = lax.all_gather(init_cache[0], ("batch", "tensor"), axis_index_groups=groups)
+    bit = 1
+    while True:
+        arrived = xor_permute(send, "batch", bit)
+        bit *= 2
+        if bit == devices:
+            break
+        total = keep + arrived
+        half = total.shape[0] // 2
+        keep, send = total[:half], total[half:]
     cache = place(stride, order, gathered, new_row, parents, lengths)
+    arrived, cache = pin(arrived, cache)
+    ffn_row = (keep + arrived).astype(bf16)
     return (hidden[None], ffn_row[None], cache[None])
 
 

time: 91.6 us -> 87.1 us (0.951)
  waiting for transfers between devices: 27.9 us -> 25.5 us
  Pallas kernels: 22.6 us -> 20.4 us
    pallas_call x4 -> x2, Pallas kernels: 13.5 us -> 8.47 us  [stream_call(): pl.pallas_call(kernel, out_shape=out, in_specs=specs, out_specs=jax.tree....]
    pallas_call x5 -> x7, Pallas kernels: 2.49 us -> 5.35 us  [call(): pl.pallas_call(kernel, out_shape=out, in_specs=specs or [VM] * len(args),...]
    ppermute x14, waiting for transfers between devices: 27.2 us -> 24.8 us  [xor_permute(): return lax.ppermute(value, axis, [(i, i ^ bit) for i in range(total)])]
  transfers between devices with their start and end apart: 15 -> 15, of which waited for: 12 -> 11; matrix products, arithmetic and copies ran while one was open for 1% -> 0% of each run, Pallas kernels for 22% -> 24%
where the time goes in v7:
time: 87.1 us; the launch traced here: 86.9 us
  waiting for transfers between devices  25.5 us (29%)
  starting transfers between devices  24.6 us (28%)
  Pallas kernels  20.4 us (23%)
  between operations  14.9 us (17%)
    ppermute x14, waiting for transfers between devices, xor_permute(): return lax.ppermute(value, axis, [(i, i ^ bit) for i in range(total)])  24.8 us
    ppermute x14, starting transfers between devices, xor_permute(): return lax.ppermute(value, axis, [(i, i ^ bit) for i in range(total)])  24.6 us
    pallas_call x2, Pallas kernels, stream_call(): pl.pallas_call(kernel, out_shape=out, in_specs=specs, out_specs=jax.tree....  8.47 us
    pallas_call x7, Pallas kernels, call(): pl.pallas_call(kernel, out_shape=out, in_specs=specs or [VM] * len(args),...  5.35 us
    pallas_call x2, Pallas kernels, fetch(): pl.pallas_call(functools.partial(fetch_kernel, count), out_shape=[pltpu.V...  3.92 us
    pallas_call x1, Pallas kernels, place(): pl.pallas_call(functools.partial(place_kernel, stride, order), out_shape=...  2.38 us
  transfers between devices with their start and end apart: 15, of which 11 were waited for; matrix products, arithmetic and copies ran while one was open for 0% of the time, Pallas kernels for 24%

profile of v7, /device:TPU:0, one launch (start us, length us, event | category | flops | bytes accessed | tf_op | source)
XLA Modules:
  0.0 86.9 jit_solution(2395515209837746718)
XLA Ops:
  7.2 0.7 all-gather.2.cloned.1.call-update
  7.9 4.1 %collective-permute-start = (bf16[2,1536]{1,0:T(2,128)(2,1)}, bf16[2,1536]{1,0:T(2,128)(2,1)S(1)}, u32[]{:S(2)}, u32[]{:S(2)}) collective-permute-start(bf16[2,1536]{1,0:T(2,128)(2,1)} %bitcast.13), channel_id=1, source_target_pairs={{0,8},{2,10},{4,12},{6,14},{8,0},{10,2},{12,4},{14,6},{1,9},{3,11}... | collective-permute-start | bytes 18440 | tf_op jit(solution)/shard_map/ppermute | solution.py:27
  12.0 1.3 %shard_map.121 = (bf16[2,1536]{1,0:T(2,128)(2,1)S(1)}, bf16[2,64,1536]{2,1,0:T(8,128)(2,1)S(1)}, bf16[2,64,1536]{2,1,0:T(8,128)(2,1)S(1)}, bf16[2,1536]{1,0:T(2,128)(2,1)S(1)}, bf16[1,8,768]{2,1,0:T(8,128)(2,1)S(1)}) custom-call(bf16[2,1536]{1,0:T(2,128)(2,1)} %bitcast.14, bf16[2,64,1536]{2,1,0:T(8,128)(2,1)} %bitcast.10, bf16[2,64,1536]{2,1,0:T(8,128)(2,1)} %bitcast.11, ...), custom_call_target="tpu_custom_call" | custom-call | bytes 2097152 | tf_op jit(solution)/shard_map/pallas_call | solution.py:85
  13.8 2.0 %collective-permute-start.1 = (bf16[4,1536]{1,0:T(4,128)(2,1)S(1)}, bf16[4,1536]{1,0:T(4,128)(2,1)S(1)}, u32[]{:S(2)}, u32[]{:S(2)}) collective-permute-start(bf16[4,1536]{1,0:T(4,128)(2,1)S(1)} %pad_maximum_fusion.3), channel_id=1, source_target_pairs={{0,4},{2,6},{4,0},{6,2},{8,12},{10,14},{12,8},{14,10},{1,5},{3,7},... | collective-permute-start | bytes 36872 | tf_op jit(solution)/shard_map/ppermute | solution.py:27
  15.8 1.8 %collective-permute-done.1 = bf16[4,1536]{1,0:T(4,128)(2,1)S(1)} collective-permute-done((bf16[4,1536]{1,0:T(4,128)(2,1)S(1)}, bf16[4,1536]{1,0:T(4,128)(2,1)S(1)}, u32[]{:S(2)}, u32[]{:S(2)}) %collective-permute-start.1) | collective-permute-done | bytes 12320 | tf_op jit(solution)/shard_map/ppermute | solution.py:27
  17.6 1.9 %collective-permute-start.2 = (bf16[8,1536]{1,0:T(8,128)(2,1)S(1)}, bf16[8,1536]{1,0:T(8,128)(2,1)S(1)}, u32[]{:S(2)}, u32[]{:S(2)}) collective-permute-start(bf16[8,1536]{1,0:T(8,128)(2,1)S(1)} %pad_maximum_fusion.1.near_ref), channel_id=1, source_target_pairs={{0,2},{2,0},{4,6},{6,4},{8,10},{10,8},{12,14},{14,12},{1,3},{3,1},... | collective-permute-start | bytes 73736 | tf_op jit(solution)/shard_map/ppermute | solution.py:27
  20.2 1.6 %collective-permute-done.2.far_ref = bf16[8,1536]{1,0:T(8,128)(2,1)S(1)} collective-permute-done((bf16[8,1536]{1,0:T(8,128)(2,1)S(1)}, bf16[8,1536]{1,0:T(8,128)(2,1)S(1)}, u32[]{:S(2)}, u32[]{:S(2)}) %collective-permute-start.2) | collective-permute-done | bytes 24608 | tf_op jit(solution)/shard_map/ppermute | solution.py:27
  21.8 0.7 copy-done
  22.4 1.3 %shard_map.122 = (f32[16,1536]{1,0:T(8,128)S(1)}, f32[16,256]{1,0:T(8,128)S(1)}, bf16[16,1664]{1,0:T(8,128)(2,1)S(1)}) custom-call(bf16[8,1536]{1,0:T(8,128)(2,1)S(1)} %pad_maximum_fusion.1.near_ref, bf16[8,1536]{1,0:T(8,128)(2,1)S(1)} %collective-permute-done.2.far_ref, bf16[2,64,1536]{2,1,0:T(8,128)(2,1)S(1)} %get-tuple-element.40.cache_ref, ...), custom_call_target="tpu_custom_call" | custom-call | bytes 16777216 | tf_op jit(solution)/shard_map/pallas_call | solution.py:46
  23.7 2.2 %collective-permute-start.3 = (bf16[16,1664]{1,0:T(8,128)(2,1)S(1)}, bf16[16,1664]{1,0:T(8,128)(2,1)S(1)}, u32[]{:S(2)}, u32[]{:S(2)}) collective-permute-start(bf16[16,1664]{1,0:T(8,128)(2,1)S(1)} %get-tuple-element.45.refs_1_), channel_id=1, source_target_pairs={{0,2},{2,0},{4,6},{6,4},{8,10},{10,8},{12,14},{14,12},{1,3},{3,1},... | collective-permute-start | bytes 159752 | tf_op jit(solution)/shard_map/ppermute | solution.py:27
  25.9 2.6 %shard_map.123.weight_ref = bf16[2,1536,768]{2,1,0:T(8,128)(2,1)S(1)} custom-call(bf16[2,1536,768]{2,1,0:T(8,128)(2,1)} %refs_0_.2, bf16[16,1664]{1,0:T(8,128)(2,1)S(1)} %get-tuple-element.45.refs_1_), custom_call_target="tpu_custom_call" | custom-call | bytes 2097152 | tf_op jit(solution)/shard_map/pallas_call | solution.py:85
  29.9 5.2 %collective-permute-done.4.pay_ref = bf16[16,1664]{1,0:T(8,128)(2,1)S(1)} collective-permute-done((bf16[16,1664]{1,0:T(8,128)(2,1)S(1)}, bf16[16,1664]{1,0:T(8,128)(2,1)S(1)}, u32[]{:S(2)}, u32[]{:S(2)}) %collective-permute-start.4) | collective-permute-done | bytes 53280 | tf_op jit(solution)/shard_map/ppermute | solution.py:27
  35.4 2.3 %collective-permute-start.5 = (bf16[16,1664]{1,0:T(8,128)(2,1)S(1)}, bf16[16,1664]{1,0:T(8,128)(2,1)S(1)}, u32[]{:S(2)}, u32[]{:S(2)}) collective-permute-start(bf16[16,1664]{1,0:T(8,128)(2,1)S(1)} %get-tuple-element.52), channel_id=1, source_target_pairs={{0,8},{2,10},{4,12},{6,14},{8,0},{10,2},{12,4},{14,6},{1,9},{3,11}... | collective-permute-start | bytes 159752 | tf_op jit(solution)/shard_map/ppermute | solution.py:27
  37.7 3.8 %collective-permute-done.5.pay_ref = bf16[16,1664]{1,0:T(8,128)(2,1)S(1)} collective-permute-done((bf16[16,1664]{1,0:T(8,128)(2,1)S(1)}, bf16[16,1664]{1,0:T(8,128)(2,1)S(1)}, u32[]{:S(2)}, u32[]{:S(2)}) %collective-permute-start.5) | collective-permute-done | bytes 53280 | tf_op jit(solution)/shard_map/ppermute | solution.py:27
  41.8 0.6 shard_map.127.own_ref
  42.5 1.2 %collective-permute-done.6.other_ref = f32[8,768]{1,0:T(8,128)S(1)} collective-permute-done((f32[8,768]{1,0:T(8,128)S(1)}, f32[8,768]{1,0:T(8,128)S(1)}, u32[]{:S(2)}, u32[]{:S(2)}) %collective-permute-start.6) | collective-permute-done | bytes 24608 | tf_op jit(solution)/shard_map/ppermute | solution.py:27
  43.7 2.4 %collective-permute-start.7 = (bf16[1,8,768]{2,1,0:T(8,128)(2,1)S(1)}, bf16[1,8,768]{2,1,0:T(8,128)(2,1)S(1)}, u32[]{:S(2)}, u32[]{:S(2)}) collective-permute-start(bf16[1,8,768]{2,1,0:T(8,128)(2,1)S(1)} %shard_map.128), channel_id=1, source_target_pairs={{0,8},{2,10},{4,12},{6,14},{8,0},{10,2},{12,4},{14,6},{1,9},{3,11}... | collective-permute-start | bytes 36872 | tf_op jit(solution)/shard_map/ppermute | solution.py:27
  46.1 2.5 %collective-permute-done.7 = bf16[1,8,768]{2,1,0:T(8,128)(2,1)S(1)} collective-permute-done((bf16[1,8,768]{2,1,0:T(8,128)(2,1)S(1)}, bf16[1,8,768]{2,1,0:T(8,128)(2,1)S(1)}, u32[]{:S(2)}, u32[]{:S(2)}) %collective-permute-start.7) | collective-permute-done | bytes 12320 | tf_op jit(solution)/shard_map/ppermute | solution.py:27
  48.6 1.9 %collective-permute-start.8 = (bf16[2,8,768]{2,1,0:T(8,128)(2,1)S(1)}, bf16[2,8,768]{2,1,0:T(8,128)(2,1)S(1)}, u32[]{:S(2)}, u32[]{:S(2)}) collective-permute-start(bf16[2,8,768]{2,1,0:T(8,128)(2,1)S(1)} %pad_maximum_fusion.2), channel_id=1, source_target_pairs={{0,4},{2,6},{4,0},{6,2},{8,12},{10,14},{12,8},{14,10},{1,5},{3,7},... | collective-permute-start | bytes 73736 | tf_op jit(solution)/shard_map/ppermute | solution.py:27
  50.5 2.1 %collective-permute-done.8 = bf16[2,8,768]{2,1,0:T(8,128)(2,1)S(1)} collective-permute-done((bf16[2,8,768]{2,1,0:T(8,128)(2,1)S(1)}, bf16[2,8,768]{2,1,0:T(8,128)(2,1)S(1)}, u32[]{:S(2)}, u32[]{:S(2)}) %collective-permute-start.8) | collective-permute-done | bytes 24608 | tf_op jit(solution)/shard_map/ppermute | solution.py:27
  52.7 2.3 %collective-permute-start.9 = (bf16[4,8,768]{2,1,0:T(8,128)(2,1)S(1)}, bf16[4,8,768]{2,1,0:T(8,128)(2,1)S(1)}, u32[]{:S(2)}, u32[]{:S(2)}) collective-permute-start(bf16[4,8,768]{2,1,0:T(8,128)(2,1)S(1)} %pad_maximum_fusion.hidden_ref), channel_id=1, source_target_pairs={{0,2},{2,0},{4,6},{6,4},{8,10},{10,8},{12,14},{14,12},{1,3},{3,1},... | collective-permute-start | bytes 147464 | tf_op jit(solution)/shard_map/ppermute | solution.py:27
  55.0 4.4 %shard_map.129 = (bf16[8,768]{1,0:T(8,128)(2,1)}, f32[8,1536]{1,0:T(8,128)S(1)}) custom-call(bf16[4,8,768]{2,1,0:T(8,128)(2,1)S(1)} %pad_maximum_fusion.hidden_ref, bf16[6144,1536]{1,0:T(8,128)(2,1)} %refs_1_.1), custom_call_target="tpu_custom_call" | custom-call | bytes 18874368 | tf_op jit(solution)/shard_map/pallas_call | solution.py:112
  59.4 4.1 %shard_map.130.act_ref = bf16[8,1536]{1,0:T(8,128)(2,1)S(1)} custom-call(bf16[4,8,768]{2,1,0:T(8,128)(2,1)S(1)} %collective-permute-done.9.hidden_ref, f32[8,1536]{1,0:T(8,128)S(1)} %get-tuple-element.58.refs_0_, bf16[6144,1536]{1,0:T(8,128)(2,1)} %refs_1_.1, bf16[3072,3072]{1,0:T(8,128)(2,1)S(1)} %bitcast.9), custom_call_target="tpu_custom_call" | custom-call | bytes 18874368 | tf_op jit(solution)/shard_map/pallas_call | solution.py:112
  63.6 1.4 %shard_map.131.rest_0_ = f32[8,3072]{1,0:T(8,128)S(1)} custom-call(bf16[8,1536]{1,0:T(8,128)(2,1)S(1)} %shard_map.130.act_ref, bf16[3072,3072]{1,0:T(8,128)(2,1)S(1)} %bitcast.9), custom_call_target="tpu_custom_call" | custom-call | bytes 16777216 | tf_op jit(solution)/shard_map/pallas_call | solution.py:46
  65.0 1.4 %shard_map.132 = (f32[4,3072]{1,0:T(4,128)S(1)}, f32[4,3072]{1,0:T(4,128)S(1)}) custom-call(bf16[8,1536]{1,0:T(8,128)(2,1)S(1)} %collective-permute-done.10.act_ref, bf16[3072,3072]{1,0:T(8,128)(2,1)S(1)} %bitcast.9, f32[8,3072]{1,0:T(8,128)S(1)} %shard_map.131.rest_0_), custom_call_target="tpu_custom_call" | custom-call | bytes 16777216 | tf_op jit(solution)/shard_map/pallas_call | solution.py:46
  66.5 1.1 %collective-permute-start.11 = (f32[4,3072]{1,0:T(4,128)S(1)}, f32[4,3072]{1,0:T(4,128)S(1)}, u32[]{:S(2)}, u32[]{:S(2)}) collective-permute-start(f32[4,3072]{1,0:T(4,128)S(1)} %get-tuple-element.60), channel_id=1, source_target_pairs={{0,2},{2,0},{4,6},{6,4},{8,10},{10,8},{12,14},{14,12},{1,3},{3,1},... | collective-permute-start | bytes 147464 | tf_op jit(solution)/shard_map/ppermute | solution.py:27
  67.5 3.1 %collective-permute-done.11 = f32[4,3072]{1,0:T(4,128)S(1)} collective-permute-done((f32[4,3072]{1,0:T(4,128)S(1)}, f32[4,3072]{1,0:T(4,128)S(1)}, u32[]{:S(2)}, u32[]{:S(2)}) %collective-permute-start.11) | collective-permute-done | bytes 49184 | tf_op jit(solution)/shard_map/ppermute | solution.py:27
  70.7 1.3 %collective-permute-start.12 = (f32[2,3072]{1,0:T(2,128)S(1)}, f32[2,3072]{1,0:T(2,128)S(1)}, u32[]{:S(2)}, u32[]{:S(2)}) collective-permute-start(f32[2,3072]{1,0:T(2,128)S(1)} %slice.17), channel_id=1, source_target_pairs={{0,4},{2,6},{4,0},{6,2},{8,12},{10,14},{12,8},{14,10},{1,5},{3,7},... | collective-permute-start | bytes 73736 | tf_op jit(solution)/shard_map/ppermute | solution.py:27
  72.0 2.6 %collective-permute-done.12 = f32[2,3072]{1,0:T(2,128)S(1)} collective-permute-done((f32[2,3072]{1,0:T(2,128)S(1)}, f32[2,3072]{1,0:T(2,128)S(1)}, u32[]{:S(2)}, u32[]{:S(2)}) %collective-permute-start.12) | collective-permute-done | bytes 24608 | tf_op jit(solution)/shard_map/ppermute | solution.py:27
  74.6 2.4 %collective-permute-start.13 = (f32[1,3072]{1,0:T(1,128)S(1)}, f32[1,3072]{1,0:T(1,128)S(1)}, u32[]{:S(2)}, u32[]{:S(2)}) collective-permute-start(f32[1,3072]{1,0:T(1,128)S(1)} %slice.19), channel_id=1, source_target_pairs={{0,8},{2,10},{4,12},{6,14},{8,0},{10,2},{12,4},{14,6},{1,9},{3,11}... | collective-permute-start | bytes 36872 | tf_op jit(solution)/shard_map/ppermute | solution.py:27
  77.0 2.4 %shard_map.133 = bf16[2,64,1536]{2,1,0:T(8,128)(2,1)} custom-call(bf16[8,2,64,1536]{3,2,1,0:T(8,128)(2,1)} %all-gather.2.cloned.1.call-done.gathered_ref, bf16[2,1536]{1,0:T(2,128)(2,1)S(1)} %get-tuple-element.42.new_ref, s32[1,8]{1,0:T(1,128)S(1)} %copy-done.1, s32[1]{0:T(128)S(6)} %copy.13.lengths_ref), custom_call_target="tpu_custom_call" | custom-call | tf_op jit(solution)/shard_map/pallas_call | solution.py:345
  79.4 0.6 fusion.1
  (36 shorter events, 2.9 us)
Async XLA Ops:
  7.2 69.9 %all-gather.2.cloned.1.call-start = ((), (), s32[]{:S(2)}) async-start(), calls=%async_computation | async-start | bytes 3538944 | tf_op jit(solution)/shard_map/all_gather | solution.py:460
  7.9 5.9 %collective-permute-start = (bf16[2,1536]{1,0:T(2,128)(2,1)}, bf16[2,1536]{1,0:T(2,128)(2,1)S(1)}, u32[]{:S(2)}, u32[]{:S(2)}) collective-permute-start(bf16[2,1536]{1,0:T(2,128)(2,1)} %bitcast.13), channel_id=1, source_target_pairs={{0,8},{2,10},{4,12},{6,14},{8,0},{10,2},{12,4},{14,6},{1,9},{3,11}... | collective-permute-start | bytes 18440 | tf_op jit(solution)/shard_map/ppermute | solution.py:27
  13.8 3.8 %collective-permute-start.1 = (bf16[4,1536]{1,0:T(4,128)(2,1)S(1)}, bf16[4,1536]{1,0:T(4,128)(2,1)S(1)}, u32[]{:S(2)}, u32[]{:S(2)}) collective-permute-start(bf16[4,1536]{1,0:T(4,128)(2,1)S(1)} %pad_maximum_fusion.3), channel_id=1, source_target_pairs={{0,4},{2,6},{4,0},{6,2},{8,12},{10,14},{12,8},{14,10},{1,5},{3,7},... | collective-permute-start | bytes 36872 | tf_op jit(solution)/shard_map/ppermute | solution.py:27
  17.6 4.1 %collective-permute-start.2 = (bf16[8,1536]{1,0:T(8,128)(2,1)S(1)}, bf16[8,1536]{1,0:T(8,128)(2,1)S(1)}, u32[]{:S(2)}, u32[]{:S(2)}) collective-permute-start(bf16[8,1536]{1,0:T(8,128)(2,1)S(1)} %pad_maximum_fusion.1.near_ref), channel_id=1, source_target_pairs={{0,2},{2,0},{4,6},{6,4},{8,10},{10,8},{12,14},{14,12},{1,3},{3,1},... | collective-permute-start | bytes 73736 | tf_op jit(solution)/shard_map/ppermute | solution.py:27
  21.7 0.7 copy-start
  23.7 5.4 %collective-permute-start.3 = (bf16[16,1664]{1,0:T(8,128)(2,1)S(1)}, bf16[16,1664]{1,0:T(8,128)(2,1)S(1)}, u32[]{:S(2)}, u32[]{:S(2)}) collective-permute-start(bf16[16,1664]{1,0:T(8,128)(2,1)S(1)} %get-tuple-element.45.refs_1_), channel_id=1, source_target_pairs={{0,2},{2,0},{4,6},{6,4},{8,10},{10,8},{12,14},{14,12},{1,3},{3,1},... | collective-permute-start | bytes 159752 | tf_op jit(solution)/shard_map/ppermute | solution.py:27
  25.8 33.5 %slice-start = ((s8[18874368]{0:T(1024)(128)(4,1)}), s8[4194304]{0:T(1024)(128)(4,1)S(1)}, s32[]{:S(2)}) async-start(s8[18874368]{0:T(1024)(128)(4,1)} %bitcast.8), calls=%async_computation.1 | async-start | bytes 8388608
  25.9 33.5 %slice-start.1 = ((s8[18874368]{0:T(1024)(128)(4,1)}), s8[4194304]{0:T(1024)(128)(4,1)S(1)}, s32[]{:S(2)}) async-start(s8[18874368]{0:T(1024)(128)(4,1)} %bitcast.8), calls=%async_computation.2 | async-start | bytes 8388608
  29.4 5.7 %collective-permute-start.4 = (bf16[16,1664]{1,0:T(8,128)(2,1)S(1)}, bf16[16,1664]{1,0:T(8,128)(2,1)S(1)}, u32[]{:S(2)}, u32[]{:S(2)}) collective-permute-start(bf16[16,1664]{1,0:T(8,128)(2,1)S(1)} %get-tuple-element.49), channel_id=1, source_target_pairs={{0,4},{2,6},{4,0},{6,2},{8,12},{10,14},{12,8},{14,10},{1,5},{3,7},... | collective-permute-start | bytes 159752 | tf_op jit(solution)/shard_map/ppermute | solution.py:27
  35.4 6.1 %collective-permute-start.5 = (bf16[16,1664]{1,0:T(8,128)(2,1)S(1)}, bf16[16,1664]{1,0:T(8,128)(2,1)S(1)}, u32[]{:S(2)}, u32[]{:S(2)}) collective-permute-start(bf16[16,1664]{1,0:T(8,128)(2,1)S(1)} %get-tuple-element.52), channel_id=1, source_target_pairs={{0,8},{2,10},{4,12},{6,14},{8,0},{10,2},{12,4},{14,6},{1,9},{3,11}... | collective-permute-start | bytes 159752 | tf_op jit(solution)/shard_map/ppermute | solution.py:27
  41.8 17.6 %slice-start.2 = ((s8[18874368]{0:T(1024)(128)(4,1)}), s8[4194304]{0:T(1024)(128)(4,1)S(1)}, s32[]{:S(2)}) async-start(s8[18874368]{0:T(1024)(128)(4,1)} %bitcast.8), calls=%async_computation.3 | async-start | bytes 8388608
  42.4 1.3 %collective-permute-start.6 = (f32[8,768]{1,0:T(8,128)S(1)}, f32[8,768]{1,0:T(8,128)S(1)}, u32[]{:S(2)}, u32[]{:S(2)}) collective-permute-start(f32[8,768]{1,0:T(8,128)S(1)} %shard_map.127.own_ref), channel_id=1, source_target_pairs={{0,1},{1,0},{2,3},{3,2},{4,5},{5,4},{6,7},{7,6},{8,9},{9,8},{10,11... | collective-permute-start | bytes 73736 | tf_op jit(solution)/shard_map/ppermute | solution.py:27
  43.7 4.9 %collective-permute-start.7 = (bf16[1,8,768]{2,1,0:T(8,128)(2,1)S(1)}, bf16[1,8,768]{2,1,0:T(8,128)(2,1)S(1)}, u32[]{:S(2)}, u32[]{:S(2)}) collective-permute-start(bf16[1,8,768]{2,1,0:T(8,128)(2,1)S(1)} %shard_map.128), channel_id=1, source_target_pairs={{0,8},{2,10},{4,12},{6,14},{8,0},{10,2},{12,4},{14,6},{1,9},{3,11}... | collective-permute-start | bytes 36872 | tf_op jit(solution)/shard_map/ppermute | solution.py:27
  48.6 4.1 %collective-permute-start.8 = (bf16[2,8,768]{2,1,0:T(8,128)(2,1)S(1)}, bf16[2,8,768]{2,1,0:T(8,128)(2,1)S(1)}, u32[]{:S(2)}, u32[]{:S(2)}) collective-permute-start(bf16[2,8,768]{2,1,0:T(8,128)(2,1)S(1)} %pad_maximum_fusion.2), channel_id=1, source_target_pairs={{0,4},{2,6},{4,0},{6,2},{8,12},{10,14},{12,8},{14,10},{1,5},{3,7},... | collective-permute-start | bytes 73736 | tf_op jit(solution)/shard_map/ppermute | solution.py:27
  52.6 6.8 %slice-start.3 = ((s8[18874368]{0:T(1024)(128)(4,1)}), s8[4194304]{0:T(1024)(128)(4,1)S(1)}, s32[]{:S(2)}) async-start(s8[18874368]{0:T(1024)(128)(4,1)} %bitcast.8), calls=%async_computation.4 | async-start | bytes 8388608
  52.6 6.8 %slice-start.4 = ((s8[18874368]{0:T(1024)(128)(4,1)}), s8[2097152]{0:T(1024)(128)(4,1)S(1)}, s32[]{:S(2)}) async-start(s8[18874368]{0:T(1024)(128)(4,1)} %bitcast.8), calls=%async_computation.5 | async-start | bytes 4194304
  52.7 6.7 %collective-permute-start.9 = (bf16[4,8,768]{2,1,0:T(8,128)(2,1)S(1)}, bf16[4,8,768]{2,1,0:T(8,128)(2,1)S(1)}, u32[]{:S(2)}, u32[]{:S(2)}) collective-permute-start(bf16[4,8,768]{2,1,0:T(8,128)(2,1)S(1)} %pad_maximum_fusion.hidden_ref), channel_id=1, source_target_pairs={{0,2},{2,0},{4,6},{6,4},{8,10},{10,8},{12,14},{14,12},{1,3},{3,1},... | collective-permute-start | bytes 147464 | tf_op jit(solution)/shard_map/ppermute | solution.py:27
  63.5 1.5 %collective-permute-start.10 = (bf16[8,1536]{1,0:T(8,128)(2,1)S(1)}, bf16[8,1536]{1,0:T(8,128)(2,1)S(1)}, u32[]{:S(2)}, u32[]{:S(2)}) collective-permute-start(bf16[8,1536]{1,0:T(8,128)(2,1)S(1)} %shard_map.130.act_ref), channel_id=1, source_target_pairs={{0,1},{1,0},{2,3},{3,2},{4,5},{5,4},{6,7},{7,6},{8,9},{9,8},{10,11... | collective-permute-start | bytes 73736 | tf_op jit(solution)/shard_map/ppermute | solution.py:27
  65.0 12.0 %copy-start.1 = (s32[1,8]{1,0:T(1,128)S(1)}, s32[1,8]{1,0:T(1,128)}, u32[]{:S(2)}) copy-start(s32[1,8]{1,0:T(1,128)} %parents_ref.3) | copy-start | bytes 100
  66.5 4.2 %collective-permute-start.11 = (f32[4,3072]{1,0:T(4,128)S(1)}, f32[4,3072]{1,0:T(4,128)S(1)}, u32[]{:S(2)}, u32[]{:S(2)}) collective-permute-start(f32[4,3072]{1,0:T(4,128)S(1)} %get-tuple-element.60), channel_id=1, source_target_pairs={{0,2},{2,0},{4,6},{6,4},{8,10},{10,8},{12,14},{14,12},{1,3},{3,1},... | collective-permute-start | bytes 147464 | tf_op jit(solution)/shard_map/ppermute | solution.py:27
  70.7 3.9 %collective-permute-start.12 = (f32[2,3072]{1,0:T(2,128)S(1)}, f32[2,3072]{1,0:T(2,128)S(1)}, u32[]{:S(2)}, u32[]{:S(2)}) collective-permute-start(f32[2,3072]{1,0:T(2,128)S(1)} %slice.17), channel_id=1, source_target_pairs={{0,4},{2,6},{4,0},{6,2},{8,12},{10,14},{12,8},{14,10},{1,5},{3,7},... | collective-permute-start | bytes 73736 | tf_op jit(solution)/shard_map/ppermute | solution.py:27
  74.6 4.8 %collective-permute-start.13 = (f32[1,3072]{1,0:T(1,128)S(1)}, f32[1,3072]{1,0:T(1,128)S(1)}, u32[]{:S(2)}, u32[]{:S(2)}) collective-permute-start(f32[1,3072]{1,0:T(1,128)S(1)} %slice.19), channel_id=1, source_target_pairs={{0,8},{2,10},{4,12},{6,14},{8,0},{10,2},{12,4},{14,6},{1,9},{3,11}... | collective-permute-start | bytes 36872 | tf_op jit(solution)/shard_map/ppermute | solution.py:27
Sparse Core Ops, SparseCore 0:
  9.5 44.7 all-gather.1

commit v8 on v7

--- a/solution.py
+++ b/solution.py
@@ -14,8 +14,7 @@
 BEAMS = 8
 LOW = -1e30
 MIB = 1024 * 1024
-SPLIT = 2
-STEP_BYTES = 16 * MIB
+STEP_FLOPS = 1_000_000_000
 
 VM = pl.BlockSpec(memory_space=pltpu.VMEM)
 SM = pl.BlockSpec(memory_space=pltpu.SMEM)
@@ -27,30 +26,40 @@
     return lax.ppermute(value, axis, [(i, i ^ bit) for i in range(total)])
 
 
+def cross_permute(value, bit):
+    pairs = [(2 * i + t, 2 * (i ^ bit) + 1 - t) for i in range(lax.axis_size("batch")) for t in range(2)]
+    return lax.ppermute(value, ("batch", "tensor"), pairs)
+
+
 def reverse(index, size):
     bits = size.bit_length() - 1
     return sum(((index >> k) & 1) << (bits - 1 - k) for k in range(bits))
 
 
-def doubling(buffer, first, last):
+def doubling(buffer, first, last, cross=False):
     bit = last
     while True:
         bit //= 2
-        other = xor_permute(buffer, "batch", bit)
+        other = cross_permute(buffer, bit) if cross else xor_permute(buffer, "batch", bit)
         if bit == first:
             return buffer, other
         buffer = jnp.concatenate([buffer, other])
 
 
-def call(kernel, out, *args, specs=None, vmem=8, flops=0, moved=STEP_BYTES):
+def drop(kernel, first, count, *refs):
+    kernel(*refs[:first], *refs[first + count :])
+
+
+def call(kernel, out, *args, specs=None, hold=(), vmem=8, flops=STEP_FLOPS, moved=0):
+    first = len(args)
     return pl.pallas_call(
-        kernel,
+        functools.partial(drop, kernel, first, len(hold)),
         out_shape=out,
-        in_specs=specs or [VM] * len(args),
+        in_specs=(specs or [VM] * first) + [ANY] * len(hold),
         out_specs=jax.tree.map(lambda _: VM, out),
         compiler_params=pltpu.CompilerParams(vmem_limit_bytes=vmem * MIB),
         cost_estimate=pl.CostEstimate(flops=flops, bytes_accessed=moved, transcendentals=0),
-    )(*args)
+    )(*args, *hold)
 
 
 def in_hbm(value):
@@ -91,33 +100,6 @@
         compiler_params=pltpu.CompilerParams(vmem_limit_bytes=2 * MIB),
         cost_estimate=pl.CostEstimate(flops=0, bytes_accessed=2 * MIB, transcendentals=0),
     )(*arrays, after)
-
-
-class Stream:
-    def __init__(self, pieces, buffers, sems):
-        self.buffers = buffers
-        self.copies = [
-            pltpu.make_async_copy(piece, buffers.at[k], sems.at[k]) for k, piece in enumerate(pieces)
-        ]
-        for copy in self.copies:
-            copy.start()
-
-    def take(self, k):
-        self.copies[k].wait()
-        return self.buffers[k]
-
-
-def stream_call(kernel, out, *args, weight, count, piece, extra=()):
-    specs = [VM] * len(args) + [ANY] * (1 + len(extra))
-    return pl.pallas_call(
-        kernel,
-        out_shape=out,
-        in_specs=specs,
-        out_specs=jax.tree.map(lambda _: VM, out),
-        scratch_shapes=[pltpu.VMEM((count, *piece), weight.dtype), pltpu.SemaphoreType.DMA((count,))],
-        compiler_params=pltpu.CompilerParams(vmem_limit_bytes=14 * MIB),
-        cost_estimate=pl.CostEstimate(flops=0, bytes_accessed=weight.size * 2, transcendentals=0),
-    )(*args, weight, *extra)
 
 
 def split3(value):
@@ -248,7 +230,7 @@
         out_specs=VM,
         scratch_shapes=[pltpu.VMEM(num.shape, jnp.float32)],
         compiler_params=pltpu.CompilerParams(vmem_limit_bytes=8 * MIB),
-        cost_estimate=pl.CostEstimate(flops=0, bytes_accessed=STEP_BYTES, transcendentals=0),
+        cost_estimate=pl.CostEstimate(flops=STEP_FLOPS, bytes_accessed=0, transcendentals=0),
     )(num, state, pay)
 
 
@@ -264,31 +246,16 @@
     out_ref[0] = total.astype(jnp.bfloat16)
 
 
-def up_kernel(last, hidden_ref, *refs):
-    half, _, depth = hidden_ref.shape
-    if last:
-        before_ref, weight_ref, _, out_ref, buffers, sems = refs
-    else:
-        weight_ref, own_ref, out_ref, buffers, sems = refs
-        own_ref[...] = hidden_ref[0]
+def up_kernel(near_ref, far_ref, weight_ref, hidden_ref, out_ref):
+    half, _, depth = near_ref.shape
     position = lax.axis_index("batch")
-    split = buffers.shape[0] // half
-    step = depth // split
-    pieces = []
-    for j in range(half):
-        index = reverse(j + half if last else j, 2 * half)
-        start = jnp.bitwise_xor(position, index) * depth
-        for k in range(split):
-            pieces.append(weight_ref.at[pl.ds(pl.multiple_of(start + k * step, step), step), :])
-    stream = Stream(pieces, buffers, sems)
-    total = before_ref[...] if last else jnp.zeros(out_ref.shape, jnp.float32)
-    for j in range(half):
-        for k in range(split):
-            block = hidden_ref[j][:, k * step : (k + 1) * step]
-            total = total + jnp.dot(block, stream.take(j * split + k), preferred_element_type=jnp.float32)
-    if last:
-        total = (0.5 * total * (1.0 + lax.erf(total * math.sqrt(0.5)))).astype(jnp.bfloat16)
-    out_ref[...] = total
+    hidden_ref[...] = near_ref[0]
+    total = jnp.zeros(out_ref.shape, jnp.float32)
+    for j in range(2 * half):
+        block = near_ref[j] if j < half else far_ref[j - half]
+        start = pl.multiple_of(jnp.bitwise_xor(position, reverse(j, 2 * half)) * depth, depth)
+        total = total + jnp.dot(block, weight_ref[pl.ds(start, depth), :], preferred_element_type=jnp.float32)
+    out_ref[...] = (0.5 * total * (1.0 + lax.erf(total * math.sqrt(0.5)))).astype(jnp.bfloat16)
 
 
 def reorder(activation):
@@ -375,14 +342,15 @@
     out_columns = down_weight.shape[1]
     f32, bf16 = jnp.float32, jnp.bfloat16
     shape = jax.ShapeDtypeStruct
-    up_weight = in_hbm(up_weight)
     down_weight = pltpu.with_memory_space_constraint(down_weight, pltpu.VMEM)
+    up_weight = pltpu.with_memory_space_constraint(up_weight, pltpu.VMEM)
     sources = (queries[0, 0], init_cache[0], memory[0], new_kv[0, 0], residual)
     bit = devices // 2
     other = xor_permute(queries[0, 0], "batch", bit)
     loaded = fetch([in_hbm(x) for x in sources], queries[0, 0])
     other, (query, cache_row, memory_row, new_row, residual_row) = pin(other, loaded)
     query, far = doubling(jnp.concatenate([query, other]), stride, bit)
+    far, (out_row,) = pin(far, fetch([in_hbm(out_weight)], query))
     state_shapes = (
         shape((2 * BEAMS, width), f32),
         shape((2 * BEAMS, 2 * LANES), f32),
@@ -399,16 +367,15 @@
         parents,
         lengths,
         specs=[VM] * 5 + [SM] * 2,
+        hold=(),
     )
     bit = stride
     while True:
         arrived = xor_permute(pay, "batch", bit)
-        if bit == stride:
-            arrived, (out_row,) = pin(arrived, fetch([in_hbm(out_weight)], pay))
         bit *= 2
         if bit == devices:
             break
-        num, state, pay = call(merge_kernel, state_shapes, num, state, arrived)
+        num, state, pay = call(merge_kernel, state_shapes, num, state, arrived, hold=())
     attended = finish(num, state, arrived)
     if stride > 1:
         stacked = jnp.concatenate(doubling(attended[None], 1, stride))
@@ -416,34 +383,21 @@
         stacked = stacked[wanted].reshape(stride, 2, BEAMS, width)
         attended = stacked.transpose(1, 2, 0, 3).reshape(2 * rows, width)
 
-    partial = call(project_kernel, shape((rows, columns), f32), attended, out_row)
+    partial = call(project_kernel, shape((rows, columns), f32), attended, out_row, hold=())
     other = xor_permute(partial, "tensor", 1)
-    mine = call(add_kernel, pltpu.VMEM((1, rows, columns), bf16), partial, other, residual_row)
-    near, far = doubling(mine, 1, devices)
-    split = SPLIT if columns % (SPLIT * LANES) == 0 else 1
-    count, piece = devices // 2 * split, (columns // split, hidden_units)
-    hidden, first_half = stream_call(
-        functools.partial(up_kernel, False),
-        (shape((rows, columns), bf16), shape((rows, hidden_units), f32)),
+    mine = call(add_kernel, pltpu.VMEM((1, rows, columns), bf16), partial, other, residual_row, hold=())
+    near, far = doubling(mine, 1, devices, cross=True)
+    hidden, activation = call(
+        up_kernel,
+        (shape((rows, columns), bf16), shape((rows, hidden_units), bf16)),
         near,
-        weight=up_weight,
-        count=count,
-        piece=piece,
-    )
-    far, first_half = pin(far, first_half)
-    activation = stream_call(
-        functools.partial(up_kernel, True),
-        shape((rows, hidden_units), bf16),
         far,
-        first_half,
-        weight=up_weight,
-        count=count,
-        piece=piece,
-        extra=(down_weight,),
+        up_weight,
+        hold=(),
     )
     arrived = xor_permute(activation, "tensor", 1)
     before = call(
-        functools.partial(down_kernel, True), shape((rows, out_columns), f32), activation, down_weight
+        functools.partial(down_kernel, True), shape((rows, out_columns), f32), activation, down_weight, hold=()
     )
     keep, send = call(
         functools.partial(down_kernel, False),

time: 87.1 us -> 82.6 us (0.948)
  waiting for transfers between devices: 25.5 us -> 32.2 us
  Pallas kernels: 20.4 us -> 14.8 us
  starting transfers between devices: 24.6 us -> 19.8 us
    ppermute x0 -> x3, waiting for transfers between devices: none -> 8.68 us  [cross_permute(): return lax.ppermute(value, ('batch', 'tensor'), pairs)]
    ppermute x14 -> x11, starting transfers between devices: 24.6 us -> 16.8 us  [xor_permute(): return lax.ppermute(value, axis, [(i, i ^ bit) for i in range(total)])]
    pallas_call x9 -> x8, Pallas kernels: 13.8 us -> 8.37 us  [call(): pl.pallas_call(functools.partial(drop, kernel, first, len(hold)), out_sha...]
    ppermute x0 -> x3, starting transfers between devices: none -> 2.98 us  [cross_permute(): return lax.ppermute(value, ('batch', 'tensor'), pairs)]
    ppermute x14 -> x11, waiting for transfers between devices: 24.8 us -> 22.8 us  [xor_permute(): return lax.ppermute(value, axis, [(i, i ^ bit) for i in range(total)])]
  transfers between devices with their start and end apart: 15 -> 15, of which waited for: 11 -> 11; matrix products, arithmetic and copies ran while one was open for 0% -> 0% of each run, Pallas kernels for 24% -> 18%
where the time goes in v8:
time: 82.6 us; the launch traced here: 82.4 us
  waiting for transfers between devices  32.2 us (39%)
  starting transfers between devices  19.8 us (24%)
  between operations  14.9 us (18%)
  Pallas kernels  14.8 us (18%)
    ppermute x11, waiting for transfers between devices, xor_permute(): return lax.ppermute(value, axis, [(i, i ^ bit) for i in range(total)])  22.8 us
    ppermute x11, starting transfers between devices, xor_permute(): return lax.ppermute(value, axis, [(i, i ^ bit) for i in range(total)])  16.8 us
    ppermute x3, waiting for transfers between devices, cross_permute(): return lax.ppermute(value, ('batch', 'tensor'), pairs)  8.68 us
    pallas_call x8, Pallas kernels, call(): pl.pallas_call(functools.partial(drop, kernel, first, len(hold)), out_sha...  8.37 us
    pallas_call x2, Pallas kernels, fetch(): pl.pallas_call(functools.partial(fetch_kernel, count), out_shape=[pltpu.V...  3.72 us
    ppermute x3, starting transfers between devices, cross_permute(): return lax.ppermute(value, ('batch', 'tensor'), pairs)  2.98 us
    pallas_call x1, Pallas kernels, place(): pl.pallas_call(functools.partial(place_kernel, stride, order), out_shape=...  2.38 us
  transfers between devices with their start and end apart: 15, of which 11 were waited for; matrix products, arithmetic and copies ran while one was open for 0% of the time, Pallas kernels for 18%

profile of v8, /device:TPU:0, one launch (start us, length us, event | category | flops | bytes accessed | tf_op | source)
XLA Modules:
  0.0 82.4 jit_solution(1051426954035641572)
XLA Ops:
  7.2 0.7 all-gather.2.cloned.1.call-update
  7.9 4.1 %collective-permute-start = (bf16[2,1536]{1,0:T(2,128)(2,1)}, bf16[2,1536]{1,0:T(2,128)(2,1)S(1)}, u32[]{:S(2)}, u32[]{:S(2)}) collective-permute-start(bf16[2,1536]{1,0:T(2,128)(2,1)} %bitcast.13), channel_id=1, source_target_pairs={{0,8},{2,10},{4,12},{6,14},{8,0},{10,2},{12,4},{14,6},{1,9},{3,11}... | collective-permute-start | bytes 18440 | tf_op jit(solution)/shard_map/ppermute | solution.py:26
  12.0 1.3 %shard_map.121 = (bf16[2,1536]{1,0:T(2,128)(2,1)S(1)}, bf16[2,64,1536]{2,1,0:T(8,128)(2,1)S(1)}, bf16[2,64,1536]{2,1,0:T(8,128)(2,1)S(1)}, bf16[2,1536]{1,0:T(2,128)(2,1)S(1)}, bf16[1,8,768]{2,1,0:T(8,128)(2,1)S(1)}) custom-call(bf16[2,1536]{1,0:T(2,128)(2,1)} %bitcast.14, bf16[2,64,1536]{2,1,0:T(8,128)(2,1)} %bitcast.10, bf16[2,64,1536]{2,1,0:T(8,128)(2,1)} %bitcast.11, ...), custom_call_target="tpu_custom_call" | custom-call | bytes 2097152 | tf_op jit(solution)/shard_map/pallas_call | solution.py:94
  13.8 2.0 %collective-permute-start.1 = (bf16[4,1536]{1,0:T(4,128)(2,1)S(1)}, bf16[4,1536]{1,0:T(4,128)(2,1)S(1)}, u32[]{:S(2)}, u32[]{:S(2)}) collective-permute-start(bf16[4,1536]{1,0:T(4,128)(2,1)S(1)} %pad_maximum_fusion.3), channel_id=1, source_target_pairs={{0,4},{2,6},{4,0},{6,2},{8,12},{10,14},{12,8},{14,10},{1,5},{3,7},... | collective-permute-start | bytes 36872 | tf_op jit(solution)/shard_map/ppermute | solution.py:26
  15.8 1.8 %collective-permute-done.1 = bf16[4,1536]{1,0:T(4,128)(2,1)S(1)} collective-permute-done((bf16[4,1536]{1,0:T(4,128)(2,1)S(1)}, bf16[4,1536]{1,0:T(4,128)(2,1)S(1)}, u32[]{:S(2)}, u32[]{:S(2)}) %collective-permute-start.1) | collective-permute-done | bytes 12320 | tf_op jit(solution)/shard_map/ppermute | solution.py:26
  17.6 1.9 %collective-permute-start.2 = (bf16[8,1536]{1,0:T(8,128)(2,1)S(1)}, bf16[8,1536]{1,0:T(8,128)(2,1)S(1)}, u32[]{:S(2)}, u32[]{:S(2)}) collective-permute-start(bf16[8,1536]{1,0:T(8,128)(2,1)S(1)} %pad_maximum_fusion.1.refs_1_.refs_0_), channel_id=1, source_target_pairs={{0,2},{2,0},{4,6},{6,4},{8,10},{10,8},{12,14},{14,12},{1,3},{3,1},... | collective-permute-start | bytes 73736 | tf_op jit(solution)/shard_map/ppermute | solution.py:26
  20.2 2.4 %shard_map.122.refs_1_ = bf16[2,1536,768]{2,1,0:T(8,128)(2,1)S(1)} custom-call(bf16[2,1536,768]{2,1,0:T(8,128)(2,1)} %refs_0_.1, bf16[8,1536]{1,0:T(8,128)(2,1)S(1)} %pad_maximum_fusion.1.refs_1_.refs_0_), custom_call_target="tpu_custom_call" | custom-call | bytes 2097152 | tf_op jit(solution)/shard_map/pallas_call | solution.py:94
  22.6 1.3 %shard_map.123 = (f32[16,1536]{1,0:T(8,128)S(1)}, f32[16,256]{1,0:T(8,128)S(1)}, bf16[16,1664]{1,0:T(8,128)(2,1)S(1)}) custom-call(bf16[8,1536]{1,0:T(8,128)(2,1)S(1)} %pad_maximum_fusion.1.refs_1_.refs_0_, bf16[8,1536]{1,0:T(8,128)(2,1)S(1)} %collective-permute-done.2.refs_1_, bf16[2,64,1536]{2,1,0:T(8,128)(2,1)S(1)} %get-tuple-element.39.refs_2_, ...), custom_call_target="tpu_custom_call" | custom-call | flops 1000000000 | tf_op jit(solution)/shard_map/pallas_call | solution.py:55
  23.9 1.3 %collective-permute-start.3 = (bf16[16,1664]{1,0:T(8,128)(2,1)S(1)}, bf16[16,1664]{1,0:T(8,128)(2,1)S(1)}, u32[]{:S(2)}, u32[]{:S(2)}) collective-permute-start(bf16[16,1664]{1,0:T(8,128)(2,1)S(1)} %get-tuple-element.44), channel_id=1, source_target_pairs={{0,2},{2,0},{4,6},{6,4},{8,10},{10,8},{12,14},{14,12},{1,3},{3,1},... | collective-permute-start | bytes 159752 | tf_op jit(solution)/shard_map/ppermute | solution.py:26
  25.2 4.0 %collective-permute-done.3.refs_2_ = bf16[16,1664]{1,0:T(8,128)(2,1)S(1)} collective-permute-done((bf16[16,1664]{1,0:T(8,128)(2,1)S(1)}, bf16[16,1664]{1,0:T(8,128)(2,1)S(1)}, u32[]{:S(2)}, u32[]{:S(2)}) %collective-permute-start.3) | collective-permute-done | bytes 53280 | tf_op jit(solution)/shard_map/ppermute | solution.py:26
  29.5 0.5 collective-permute-start.4
  30.1 5.1 %collective-permute-done.4.refs_2_ = bf16[16,1664]{1,0:T(8,128)(2,1)S(1)} collective-permute-done((bf16[16,1664]{1,0:T(8,128)(2,1)S(1)}, bf16[16,1664]{1,0:T(8,128)(2,1)S(1)}, u32[]{:S(2)}, u32[]{:S(2)}) %collective-permute-start.4) | collective-permute-done | bytes 53280 | tf_op jit(solution)/shard_map/ppermute | solution.py:26
  35.4 1.8 %collective-permute-start.5 = (bf16[16,1664]{1,0:T(8,128)(2,1)S(1)}, bf16[16,1664]{1,0:T(8,128)(2,1)S(1)}, u32[]{:S(2)}, u32[]{:S(2)}) collective-permute-start(bf16[16,1664]{1,0:T(8,128)(2,1)S(1)} %get-tuple-element.50), channel_id=1, source_target_pairs={{0,8},{2,10},{4,12},{6,14},{8,0},{10,2},{12,4},{14,6},{1,9},{3,11}... | collective-permute-start | bytes 159752 | tf_op jit(solution)/shard_map/ppermute | solution.py:26
  37.3 4.9 %collective-permute-done.5.pay_ref = bf16[16,1664]{1,0:T(8,128)(2,1)S(1)} collective-permute-done((bf16[16,1664]{1,0:T(8,128)(2,1)S(1)}, bf16[16,1664]{1,0:T(8,128)(2,1)S(1)}, u32[]{:S(2)}, u32[]{:S(2)}) %collective-permute-start.5) | collective-permute-done | bytes 53280 | tf_op jit(solution)/shard_map/ppermute | solution.py:26
  42.5 0.6 shard_map.127.refs_0_
  43.2 1.2 %collective-permute-done.6.refs_1_ = f32[8,768]{1,0:T(8,128)S(1)} collective-permute-done((f32[8,768]{1,0:T(8,128)S(1)}, f32[8,768]{1,0:T(8,128)S(1)}, u32[]{:S(2)}, u32[]{:S(2)}) %collective-permute-start.6) | collective-permute-done | bytes 24608 | tf_op jit(solution)/shard_map/ppermute | solution.py:26
  44.4 1.0 %collective-permute-start.7 = (bf16[1,8,768]{2,1,0:T(8,128)(2,1)S(1)}, bf16[1,8,768]{2,1,0:T(8,128)(2,1)S(1)}, u32[]{:S(2)}, u32[]{:S(2)}) collective-permute-start(bf16[1,8,768]{2,1,0:T(8,128)(2,1)S(1)} %shard_map.128), channel_id=1, source_target_pairs={{0,9},{1,8},{2,11},{3,10},{4,13},{5,12},{6,15},{7,14},{8,1},{9,0},... | collective-permute-start | bytes 36872 | tf_op jit(solution)/shard_map/ppermute | solution.py:31
  45.4 3.5 %collective-permute-done.7 = bf16[1,8,768]{2,1,0:T(8,128)(2,1)S(1)} collective-permute-done((bf16[1,8,768]{2,1,0:T(8,128)(2,1)S(1)}, bf16[1,8,768]{2,1,0:T(8,128)(2,1)S(1)}, u32[]{:S(2)}, u32[]{:S(2)}) %collective-permute-start.7) | collective-permute-done | bytes 12320 | tf_op jit(solution)/shard_map/ppermute | solution.py:31
  48.8 0.7 collective-permute-start.8
  49.5 2.7 %collective-permute-done.8 = bf16[2,8,768]{2,1,0:T(8,128)(2,1)S(1)} collective-permute-done((bf16[2,8,768]{2,1,0:T(8,128)(2,1)S(1)}, bf16[2,8,768]{2,1,0:T(8,128)(2,1)S(1)}, u32[]{:S(2)}, u32[]{:S(2)}) %collective-permute-start.8) | collective-permute-done | bytes 24608 | tf_op jit(solution)/shard_map/ppermute | solution.py:31
  52.3 1.3 %collective-permute-start.9 = (bf16[4,8,768]{2,1,0:T(8,128)(2,1)S(1)}, bf16[4,8,768]{2,1,0:T(8,128)(2,1)S(1)}, u32[]{:S(2)}, u32[]{:S(2)}) collective-permute-start(bf16[4,8,768]{2,1,0:T(8,128)(2,1)S(1)} %pad_maximum_fusion.refs_0_), channel_id=1, source_target_pairs={{0,3},{1,2},{2,1},{3,0},{4,7},{5,6},{6,5},{7,4},{8,11},{9,10},{10,... | collective-permute-start | bytes 147464 | tf_op jit(solution)/shard_map/ppermute | solution.py:31
  53.6 2.5 %collective-permute-done.9.refs_1_ = bf16[4,8,768]{2,1,0:T(8,128)(2,1)S(1)} collective-permute-done((bf16[4,8,768]{2,1,0:T(8,128)(2,1)S(1)}, bf16[4,8,768]{2,1,0:T(8,128)(2,1)S(1)}, u32[]{:S(2)}, u32[]{:S(2)}) %collective-permute-start.9) | collective-permute-done | bytes 49184 | tf_op jit(solution)/shard_map/ppermute | solution.py:31
  56.1 3.0 %shard_map.129 = (bf16[8,768]{1,0:T(8,128)(2,1)}, bf16[8,1536]{1,0:T(8,128)(2,1)S(1)}) custom-call(bf16[4,8,768]{2,1,0:T(8,128)(2,1)S(1)} %pad_maximum_fusion.refs_0_, bf16[4,8,768]{2,1,0:T(8,128)(2,1)S(1)} %collective-permute-done.9.refs_1_, bf16[6144,1536]{1,0:T(8,128)(2,1)S(1)} %copy-done), custom_call_target="tpu_custom_call" | custom-call | flops 1000000000 | tf_op jit(solution)/shard_map/pallas_call | solution.py:55
  59.2 1.4 %shard_map.130.refs_2_ = f32[8,3072]{1,0:T(8,128)S(1)} custom-call(bf16[8,1536]{1,0:T(8,128)(2,1)S(1)} %get-tuple-element.54.refs_0_, bf16[3072,3072]{1,0:T(8,128)(2,1)S(1)} %bitcast.9), custom_call_target="tpu_custom_call" | custom-call | flops 1000000000 | tf_op jit(solution)/shard_map/pallas_call | solution.py:55
  60.7 1.4 %shard_map.131 = (f32[4,3072]{1,0:T(4,128)S(1)}, f32[4,3072]{1,0:T(4,128)S(1)}) custom-call(bf16[8,1536]{1,0:T(8,128)(2,1)S(1)} %collective-permute-done.10.refs_0_, bf16[3072,3072]{1,0:T(8,128)(2,1)S(1)} %bitcast.9, f32[8,3072]{1,0:T(8,128)S(1)} %shard_map.130.refs_2_), custom_call_target="tpu_custom_call" | custom-call | flops 1000000000 | tf_op jit(solution)/shard_map/pallas_call | solution.py:55
  62.1 1.3 %collective-permute-start.11 = (f32[4,3072]{1,0:T(4,128)S(1)}, f32[4,3072]{1,0:T(4,128)S(1)}, u32[]{:S(2)}, u32[]{:S(2)}) collective-permute-start(f32[4,3072]{1,0:T(4,128)S(1)} %get-tuple-element.56), channel_id=1, source_target_pairs={{0,2},{2,0},{4,6},{6,4},{8,10},{10,8},{12,14},{14,12},{1,3},{3,1},... | collective-permute-start | bytes 147464 | tf_op jit(solution)/shard_map/ppermute | solution.py:26
  63.4 2.9 %collective-permute-done.11 = f32[4,3072]{1,0:T(4,128)S(1)} collective-permute-done((f32[4,3072]{1,0:T(4,128)S(1)}, f32[4,3072]{1,0:T(4,128)S(1)}, u32[]{:S(2)}, u32[]{:S(2)}) %collective-permute-start.11) | collective-permute-done | bytes 49184 | tf_op jit(solution)/shard_map/ppermute | solution.py:26
  66.3 1.4 %collective-permute-start.12 = (f32[2,3072]{1,0:T(2,128)S(1)}, f32[2,3072]{1,0:T(2,128)S(1)}, u32[]{:S(2)}, u32[]{:S(2)}) collective-permute-start(f32[2,3072]{1,0:T(2,128)S(1)} %slice.17), channel_id=1, source_target_pairs={{0,4},{2,6},{4,0},{6,2},{8,12},{10,14},{12,8},{14,10},{1,5},{3,7},... | collective-permute-start | bytes 73736 | tf_op jit(solution)/shard_map/ppermute | solution.py:26
  67.7 2.5 %collective-permute-done.12 = f32[2,3072]{1,0:T(2,128)S(1)} collective-permute-done((f32[2,3072]{1,0:T(2,128)S(1)}, f32[2,3072]{1,0:T(2,128)S(1)}, u32[]{:S(2)}, u32[]{:S(2)}) %collective-permute-start.12) | collective-permute-done | bytes 24608 | tf_op jit(solution)/shard_map/ppermute | solution.py:26
  70.2 2.3 %collective-permute-start.13 = (f32[1,3072]{1,0:T(1,128)S(1)}, f32[1,3072]{1,0:T(1,128)S(1)}, u32[]{:S(2)}, u32[]{:S(2)}) collective-permute-start(f32[1,3072]{1,0:T(1,128)S(1)} %slice.19), channel_id=1, source_target_pairs={{0,8},{2,10},{4,12},{6,14},{8,0},{10,2},{12,4},{14,6},{1,9},{3,11}... | collective-permute-start | bytes 36872 | tf_op jit(solution)/shard_map/ppermute | solution.py:26
  72.5 2.4 %shard_map.132 = bf16[2,64,1536]{2,1,0:T(8,128)(2,1)} custom-call(bf16[8,2,64,1536]{3,2,1,0:T(8,128)(2,1)} %all-gather.2.cloned.1.call-done.gathered_ref, bf16[2,1536]{1,0:T(2,128)(2,1)S(1)} %get-tuple-element.41.refs_4_.new_ref, s32[1,8]{1,0:T(1,128)S(1)} %copy-done.1, s32[1]{0:T(128)S(6)} %copy.13.refs_6_.lengths_ref), custom_call_target="tpu_custom_call" | custom-call | tf_op jit(solution)/shard_map/pallas_call | solution.py:312
  74.9 0.6 fusion.1
  (35 shorter events, 1.8 us)
Async XLA Ops:
  7.2 65.4 %all-gather.2.cloned.1.call-start = ((), (), s32[]{:S(2)}) async-start(), calls=%async_computation | async-start | bytes 3538944 | tf_op jit(solution)/shard_map/all_gather | solution.py:414
  7.9 5.9 %collective-permute-start = (bf16[2,1536]{1,0:T(2,128)(2,1)}, bf16[2,1536]{1,0:T(2,128)(2,1)S(1)}, u32[]{:S(2)}, u32[]{:S(2)}) collective-permute-start(bf16[2,1536]{1,0:T(2,128)(2,1)} %bitcast.13), channel_id=1, source_target_pairs={{0,8},{2,10},{4,12},{6,14},{8,0},{10,2},{12,4},{14,6},{1,9},{3,11}... | collective-permute-start | bytes 18440 | tf_op jit(solution)/shard_map/ppermute | solution.py:26
  13.8 3.8 %collective-permute-start.1 = (bf16[4,1536]{1,0:T(4,128)(2,1)S(1)}, bf16[4,1536]{1,0:T(4,128)(2,1)S(1)}, u32[]{:S(2)}, u32[]{:S(2)}) collective-permute-start(bf16[4,1536]{1,0:T(4,128)(2,1)S(1)} %pad_maximum_fusion.3), channel_id=1, source_target_pairs={{0,4},{2,6},{4,0},{6,2},{8,12},{10,14},{12,8},{14,10},{1,5},{3,7},... | collective-permute-start | bytes 36872 | tf_op jit(solution)/shard_map/ppermute | solution.py:26
  17.6 5.0 %collective-permute-start.2 = (bf16[8,1536]{1,0:T(8,128)(2,1)S(1)}, bf16[8,1536]{1,0:T(8,128)(2,1)S(1)}, u32[]{:S(2)}, u32[]{:S(2)}) collective-permute-start(bf16[8,1536]{1,0:T(8,128)(2,1)S(1)} %pad_maximum_fusion.1.refs_1_.refs_0_), channel_id=1, source_target_pairs={{0,2},{2,0},{4,6},{6,4},{8,10},{10,8},{12,14},{14,12},{1,3},{3,1},... | collective-permute-start | bytes 73736 | tf_op jit(solution)/shard_map/ppermute | solution.py:26
  20.2 2.4 %copy-start.1 = (s32[1,8]{1,0:T(1,128)S(1)}, s32[1,8]{1,0:T(1,128)}, u32[]{:S(2)}) copy-start(s32[1,8]{1,0:T(1,128)} %parents_ref.1) | copy-start | bytes 100
  23.9 5.3 %collective-permute-start.3 = (bf16[16,1664]{1,0:T(8,128)(2,1)S(1)}, bf16[16,1664]{1,0:T(8,128)(2,1)S(1)}, u32[]{:S(2)}, u32[]{:S(2)}) collective-permute-start(bf16[16,1664]{1,0:T(8,128)(2,1)S(1)} %get-tuple-element.44), channel_id=1, source_target_pairs={{0,2},{2,0},{4,6},{6,4},{8,10},{10,8},{12,14},{14,12},{1,3},{3,1},... | collective-permute-start | bytes 159752 | tf_op jit(solution)/shard_map/ppermute | solution.py:26
  29.2 26.9 %copy-start = (bf16[6144,1536]{1,0:T(8,128)(2,1)S(1)}, bf16[6144,1536]{1,0:T(8,128)(2,1)}, u32[]{:S(2)}) copy-start(bf16[6144,1536]{1,0:T(8,128)(2,1)} %refs_2_.1) | copy-start | bytes 56623108
  29.5 5.6 %collective-permute-start.4 = (bf16[16,1664]{1,0:T(8,128)(2,1)S(1)}, bf16[16,1664]{1,0:T(8,128)(2,1)S(1)}, u32[]{:S(2)}, u32[]{:S(2)}) collective-permute-start(bf16[16,1664]{1,0:T(8,128)(2,1)S(1)} %get-tuple-element.47), channel_id=1, source_target_pairs={{0,4},{2,6},{4,0},{6,2},{8,12},{10,14},{12,8},{14,10},{1,5},{3,7},... | collective-permute-start | bytes 159752 | tf_op jit(solution)/shard_map/ppermute | solution.py:26
  35.1 24.1 %slice-start = ((s8[18874368]{0:T(1024)(128)(4,1)}), s8[4194304]{0:T(1024)(128)(4,1)S(1)}, s32[]{:S(2)}) async-start(s8[18874368]{0:T(1024)(128)(4,1)} %bitcast.8), calls=%async_computation.1 | async-start | bytes 8388608
  35.4 6.8 %collective-permute-start.5 = (bf16[16,1664]{1,0:T(8,128)(2,1)S(1)}, bf16[16,1664]{1,0:T(8,128)(2,1)S(1)}, u32[]{:S(2)}, u32[]{:S(2)}) collective-permute-start(bf16[16,1664]{1,0:T(8,128)(2,1)S(1)} %get-tuple-element.50), channel_id=1, source_target_pairs={{0,8},{2,10},{4,12},{6,14},{8,0},{10,2},{12,4},{14,6},{1,9},{3,11}... | collective-permute-start | bytes 159752 | tf_op jit(solution)/shard_map/ppermute | solution.py:26
  42.2 17.1 %slice-start.1 = ((s8[18874368]{0:T(1024)(128)(4,1)}), s8[4194304]{0:T(1024)(128)(4,1)S(1)}, s32[]{:S(2)}) async-start(s8[18874368]{0:T(1024)(128)(4,1)} %bitcast.8), calls=%async_computation.2 | async-start | bytes 8388608
  43.1 16.1 %slice-start.2 = ((s8[18874368]{0:T(1024)(128)(4,1)}), s8[4194304]{0:T(1024)(128)(4,1)S(1)}, s32[]{:S(2)}) async-start(s8[18874368]{0:T(1024)(128)(4,1)} %bitcast.8), calls=%async_computation.3 | async-start | bytes 8388608
  43.1 1.3 %collective-permute-start.6 = (f32[8,768]{1,0:T(8,128)S(1)}, f32[8,768]{1,0:T(8,128)S(1)}, u32[]{:S(2)}, u32[]{:S(2)}) collective-permute-start(f32[8,768]{1,0:T(8,128)S(1)} %shard_map.127.refs_0_), channel_id=1, source_target_pairs={{0,1},{1,0},{2,3},{3,2},{4,5},{5,4},{6,7},{7,6},{8,9},{9,8},{10,11... | collective-permute-start | bytes 73736 | tf_op jit(solution)/shard_map/ppermute | solution.py:26
  44.4 4.5 %collective-permute-start.7 = (bf16[1,8,768]{2,1,0:T(8,128)(2,1)S(1)}, bf16[1,8,768]{2,1,0:T(8,128)(2,1)S(1)}, u32[]{:S(2)}, u32[]{:S(2)}) collective-permute-start(bf16[1,8,768]{2,1,0:T(8,128)(2,1)S(1)} %shard_map.128), channel_id=1, source_target_pairs={{0,9},{1,8},{2,11},{3,10},{4,13},{5,12},{6,15},{7,14},{8,1},{9,0},... | collective-permute-start | bytes 36872 | tf_op jit(solution)/shard_map/ppermute | solution.py:31
  48.8 3.4 %collective-permute-start.8 = (bf16[2,8,768]{2,1,0:T(8,128)(2,1)S(1)}, bf16[2,8,768]{2,1,0:T(8,128)(2,1)S(1)}, u32[]{:S(2)}, u32[]{:S(2)}) collective-permute-start(bf16[2,8,768]{2,1,0:T(8,128)(2,1)S(1)} %pad_maximum_fusion.2), channel_id=1, source_target_pairs={{0,5},{1,4},{2,7},{3,6},{4,1},{5,0},{6,3},{7,2},{8,13},{9,12},{10,... | collective-permute-start | bytes 73736 | tf_op jit(solution)/shard_map/ppermute | solution.py:31
  52.2 7.0 %slice-start.3 = ((s8[18874368]{0:T(1024)(128)(4,1)}), s8[4194304]{0:T(1024)(128)(4,1)S(1)}, s32[]{:S(2)}) async-start(s8[18874368]{0:T(1024)(128)(4,1)} %bitcast.8), calls=%async_computation.4 | async-start | bytes 8388608
  52.3 7.0 %slice-start.4 = ((s8[18874368]{0:T(1024)(128)(4,1)}), s8[2097152]{0:T(1024)(128)(4,1)S(1)}, s32[]{:S(2)}) async-start(s8[18874368]{0:T(1024)(128)(4,1)} %bitcast.8), calls=%async_computation.5 | async-start | bytes 4194304
  52.3 3.8 %collective-permute-start.9 = (bf16[4,8,768]{2,1,0:T(8,128)(2,1)S(1)}, bf16[4,8,768]{2,1,0:T(8,128)(2,1)S(1)}, u32[]{:S(2)}, u32[]{:S(2)}) collective-permute-start(bf16[4,8,768]{2,1,0:T(8,128)(2,1)S(1)} %pad_maximum_fusion.refs_0_), channel_id=1, source_target_pairs={{0,3},{1,2},{2,1},{3,0},{4,7},{5,6},{6,5},{7,4},{8,11},{9,10},{10,... | collective-permute-start | bytes 147464 | tf_op jit(solution)/shard_map/ppermute | solution.py:31
  59.1 1.6 %collective-permute-start.10 = (bf16[8,1536]{1,0:T(8,128)(2,1)S(1)}, bf16[8,1536]{1,0:T(8,128)(2,1)S(1)}, u32[]{:S(2)}, u32[]{:S(2)}) collective-permute-start(bf16[8,1536]{1,0:T(8,128)(2,1)S(1)} %get-tuple-element.54.refs_0_), channel_id=1, source_target_pairs={{0,1},{1,0},{2,3},{3,2},{4,5},{5,4},{6,7},{7,6},{8,9},{9,8},{10,11... | collective-permute-start | bytes 73736 | tf_op jit(solution)/shard_map/ppermute | solution.py:26
  62.1 4.1 %collective-permute-start.11 = (f32[4,3072]{1,0:T(4,128)S(1)}, f32[4,3072]{1,0:T(4,128)S(1)}, u32[]{:S(2)}, u32[]{:S(2)}) collective-permute-start(f32[4,3072]{1,0:T(4,128)S(1)} %get-tuple-element.56), channel_id=1, source_target_pairs={{0,2},{2,0},{4,6},{6,4},{8,10},{10,8},{12,14},{14,12},{1,3},{3,1},... | collective-permute-start | bytes 147464 | tf_op jit(solution)/shard_map/ppermute | solution.py:26
  66.3 3.9 %collective-permute-start.12 = (f32[2,3072]{1,0:T(2,128)S(1)}, f32[2,3072]{1,0:T(2,128)S(1)}, u32[]{:S(2)}, u32[]{:S(2)}) collective-permute-start(f32[2,3072]{1,0:T(2,128)S(1)} %slice.17), channel_id=1, source_target_pairs={{0,4},{2,6},{4,0},{6,2},{8,12},{10,14},{12,8},{14,10},{1,5},{3,7},... | collective-permute-start | bytes 73736 | tf_op jit(solution)/shard_map/ppermute | solution.py:26
  70.2 4.7 %collective-permute-start.13 = (f32[1,3072]{1,0:T(1,128)S(1)}, f32[1,3072]{1,0:T(1,128)S(1)}, u32[]{:S(2)}, u32[]{:S(2)}) collective-permute-start(f32[1,3072]{1,0:T(1,128)S(1)} %slice.19), channel_id=1, source_target_pairs={{0,8},{2,10},{4,12},{6,14},{8,0},{10,2},{12,4},{14,6},{1,9},{3,11}... | collective-permute-start | bytes 36872 | tf_op jit(solution)/shard_map/ppermute | solution.py:26
Sparse Core Ops, SparseCore 0:
  9.5 45.0 all-gather.1

commit v9 on v8

--- a/solution.py
+++ b/solution.py
@@ -290,33 +290,37 @@
     return list(range(0, BEAMS, 2)) + list(range(BEAMS - 1, 0, -2))
 
 
-def place_kernel(stride, order, gathered_ref, new_ref, parents_ref, lengths_ref, out_ref, row, sem):
+def place_kernel(stride, order, keys_ref, values_ref, new_ref, parents_ref, lengths_ref, out_ref, row, sems):
     position = lax.axis_index("batch")
     request = lax.rem(position, stride)
     parent = parents_ref[0, position]
-    place = jnp.int32(0)
+    forward = jnp.int32(0)
     for k, beam in enumerate(order):
-        place = jnp.where(parent == beam, k, place)
-    place = jnp.where(lax.axis_index("tensor") == 1, BEAMS - 1 - place, place)
-    copy = pltpu.make_async_copy(gathered_ref.at[place], row, sem)
-    copy.start()
+        forward = jnp.where(parent == beam, k, forward)
+    backward = BEAMS - 1 - forward
+    first = lax.axis_index("tensor") == 0
+    copies = [
+        pltpu.make_async_copy(keys_ref.at[jnp.where(first, forward, backward)], row.at[0], sems.at[0]),
+        pltpu.make_async_copy(values_ref.at[jnp.where(first, backward, forward)], row.at[1], sems.at[1]),
+    ]
+    start_all(copies)
     slots = lax.broadcasted_iota(jnp.int32, row.shape[1:], 0)
-    copy.wait()
     for kind in range(2):
         old = row[kind].astype(jnp.float32)
         new = new_ref[kind : kind + 1, :].astype(jnp.float32)
         out_ref[kind] = jnp.where(slots == lengths_ref[request], new, old).astype(jnp.bfloat16)
 
 
-def place(stride, order, gathered, new_kv, parents, lengths):
+def place(stride, order, keys, values, new_kv, parents, lengths):
+    shape = (2, *keys.shape[1:])
     return pl.pallas_call(
         functools.partial(place_kernel, stride, order),
-        out_shape=jax.ShapeDtypeStruct(gathered.shape[1:], gathered.dtype),
-        in_specs=[ANY, VM, SM, SM],
+        out_shape=jax.ShapeDtypeStruct(shape, keys.dtype),
+        in_specs=[ANY, ANY, VM, SM, SM],
         out_specs=VM,
-        scratch_shapes=[pltpu.VMEM(gathered.shape[1:], gathered.dtype), pltpu.SemaphoreType.DMA],
+        scratch_shapes=[pltpu.VMEM(shape, keys.dtype), pltpu.SemaphoreType.DMA((2,))],
         compiler_params=pltpu.CompilerParams(vmem_limit_bytes=8 * MIB),
-    )(in_hbm(gathered), new_kv, parents, lengths)
+    )(in_hbm(keys), in_hbm(values), new_kv, parents, lengths)
 
 
 def body(
@@ -411,7 +415,9 @@
     for r in range(stride):
         groups.append([(beam * stride + r) * 2 for beam in order])
         groups.append([(beam * stride + r) * 2 + 1 for beam in reversed(order)])
-    gathered = lax.all_gather(init_cache[0], ("batch", "tensor"), axis_index_groups=groups)
+    opposite = [group[::-1] for group in groups]
+    keys = lax.all_gather(init_cache[0, 0], ("batch", "tensor"), axis_index_groups=groups)
+    values = lax.all_gather(init_cache[0, 1], ("batch", "tensor"), axis_index_groups=opposite)
     bit = 1
     while True:
         arrived = xor_permute(send, "batch", bit)
@@ -421,7 +427,7 @@
         total = keep + arrived
         half = total.shape[0] // 2
         keep, send = total[:half], total[half:]
-    cache = place(stride, order, gathered, new_row, parents, lengths)
+    cache = place(stride, order, keys, values, new_row, parents, lengths)
     arrived, cache = pin(arrived, cache)
     ffn_row = (keep + arrived).astype(bf16)
     return (hidden[None], ffn_row[None], cache[None])

time: 82.6 us -> 89.9 us (1.088)
  waiting for transfers between devices: 32.2 us -> 39.8 us
  starting transfers between devices: 19.8 us -> 17.6 us
  local copies, waits for them, and re-layouts: 0.07 us -> 1.87 us
    all_gather x1 -> x2, waiting for transfers between devices: 0.01 us -> 5.37 us  [the longest x1 5.36 us: body(): lax.all_gather(init_cache[0, 1], ('batch', 'tensor'), axis_index_groups=o...]
    ppermute x11, starting transfers between devices: 16.8 us -> 14.8 us  [xor_permute(): return lax.ppermute(value, axis, [(i, i ^ bit) for i in range(total)])]
    slice x0 -> x1, local copies, waits for them, and re-layouts: none -> 1.8 us  [body(): init_cache[0, 1]]
    ppermute x11, waiting for transfers between devices: 22.8 us -> 24.2 us  [xor_permute(): return lax.ppermute(value, axis, [(i, i ^ bit) for i in range(total)])]
  transfers between devices with their start and end apart: 15 -> 16, of which waited for: 11 -> 12; matrix products, arithmetic and copies ran while one was open for 0% -> 0% of each run, Pallas kernels for 18% -> 17%
where the time goes in v9:
time: 89.9 us; the launch traced here: 89.7 us
  waiting for transfers between devices  39.8 us (44%)
  starting transfers between devices  17.6 us (20%)
  between operations  14.9 us (17%)
  Pallas kernels  14.8 us (16%)
  local copies, waits for them, and re-layouts  1.87 us (2%)
    ppermute x11, waiting for transfers between devices, xor_permute(): return lax.ppermute(value, axis, [(i, i ^ bit) for i in range(total)])  24.2 us
    ppermute x11, starting transfers between devices, xor_permute(): return lax.ppermute(value, axis, [(i, i ^ bit) for i in range(total)])  14.8 us
    ppermute x3, waiting for transfers between devices, cross_permute(): return lax.ppermute(value, ('batch', 'tensor'), pairs)  9.5 us
    pallas_call x8, Pallas kernels, call(): pl.pallas_call(functools.partial(drop, kernel, first, len(hold)), out_sha...  8.37 us
    all_gather x1, waiting for transfers between devices, body(): lax.all_gather(init_cache[0, 1], ('batch', 'tensor'), axis_index_groups=o...  5.36 us
    pallas_call x2, Pallas kernels, fetch(): pl.pallas_call(functools.partial(fetch_kernel, count), out_shape=[pltpu.V...  3.76 us
    ppermute x3, starting transfers between devices, cross_permute(): return lax.ppermute(value, ('batch', 'tensor'), pairs)  2.73 us
    pallas_call x1, Pallas kernels, place(): pl.pallas_call(functools.partial(place_kernel, stride, order), out_shape=...  2.42 us
  transfers between devices with their start and end apart: 16, of which 12 were waited for; matrix products, arithmetic and copies ran while one was open for 0% of the time, Pallas kernels for 17%

profile of v9, /device:TPU:0, one launch (start us, length us, event | category | flops | bytes accessed | tf_op | source)
XLA Modules:
  0.0 89.7 jit_solution(15299533745612193453)
XLA Ops:
  7.2 1.8 %fusion.2 = (bf16[1,1,64,1536]{3,2,1,0:T(8,128)(2,1)}, bf16[1,1,64,1536]{3,2,1,0:T(8,128)(2,1)}) fusion(bf16[1,2,64,1536]{3,2,1,0:T(8,128)(2,1)} %param.10), kind=kLoop, calls=%fused_computation.8 | loop fusion | bytes 786432 | tf_op jit(solution)/shard_map/slice | solution.py:420
  9.1 0.7 all-gather.7.cloned.1.call-update
  9.8 4.1 %collective-permute-start = (bf16[2,1536]{1,0:T(2,128)(2,1)}, bf16[2,1536]{1,0:T(2,128)(2,1)S(1)}, u32[]{:S(2)}, u32[]{:S(2)}) collective-permute-start(bf16[2,1536]{1,0:T(2,128)(2,1)} %bitcast.17), channel_id=1, source_target_pairs={{0,8},{2,10},{4,12},{6,14},{8,0},{10,2},{12,4},{14,6},{1,9},{3,11}... | collective-permute-start | bytes 18440 | tf_op jit(solution)/shard_map/ppermute | solution.py:26
  13.9 1.3 %shard_map.121 = (bf16[2,1536]{1,0:T(2,128)(2,1)S(1)}, bf16[2,64,1536]{2,1,0:T(8,128)(2,1)S(1)}, bf16[2,64,1536]{2,1,0:T(8,128)(2,1)S(1)}, bf16[2,1536]{1,0:T(2,128)(2,1)S(1)}, bf16[1,8,768]{2,1,0:T(8,128)(2,1)S(1)}) custom-call(bf16[2,1536]{1,0:T(2,128)(2,1)} %bitcast.18, bf16[2,64,1536]{2,1,0:T(8,128)(2,1)} %bitcast.14, bf16[2,64,1536]{2,1,0:T(8,128)(2,1)} %bitcast.15, ...), custom_call_target="tpu_custom_call" | custom-call | bytes 2097152 | tf_op jit(solution)/shard_map/pallas_call | solution.py:94
  15.2 0.5 collective-permute-done
  15.7 2.0 %collective-permute-start.1 = (bf16[4,1536]{1,0:T(4,128)(2,1)S(1)}, bf16[4,1536]{1,0:T(4,128)(2,1)S(1)}, u32[]{:S(2)}, u32[]{:S(2)}) collective-permute-start(bf16[4,1536]{1,0:T(4,128)(2,1)S(1)} %pad_maximum_fusion.3), channel_id=1, source_target_pairs={{0,4},{2,6},{4,0},{6,2},{8,12},{10,14},{12,8},{14,10},{1,5},{3,7},... | collective-permute-start | bytes 36872 | tf_op jit(solution)/shard_map/ppermute | solution.py:26
  17.7 1.8 %collective-permute-done.1 = bf16[4,1536]{1,0:T(4,128)(2,1)S(1)} collective-permute-done((bf16[4,1536]{1,0:T(4,128)(2,1)S(1)}, bf16[4,1536]{1,0:T(4,128)(2,1)S(1)}, u32[]{:S(2)}, u32[]{:S(2)}) %collective-permute-start.1) | collective-permute-done | bytes 12320 | tf_op jit(solution)/shard_map/ppermute | solution.py:26
  19.5 1.9 %collective-permute-start.2 = (bf16[8,1536]{1,0:T(8,128)(2,1)S(1)}, bf16[8,1536]{1,0:T(8,128)(2,1)S(1)}, u32[]{:S(2)}, u32[]{:S(2)}) collective-permute-start(bf16[8,1536]{1,0:T(8,128)(2,1)S(1)} %pad_maximum_fusion.1.refs_1_.refs_0_), channel_id=1, source_target_pairs={{0,2},{2,0},{4,6},{6,4},{8,10},{10,8},{12,14},{14,12},{1,3},{3,1},... | collective-permute-start | bytes 73736 | tf_op jit(solution)/shard_map/ppermute | solution.py:26
  22.1 2.4 %shard_map.122.refs_1_ = bf16[2,1536,768]{2,1,0:T(8,128)(2,1)S(1)} custom-call(bf16[2,1536,768]{2,1,0:T(8,128)(2,1)} %refs_0_.1, bf16[8,1536]{1,0:T(8,128)(2,1)S(1)} %pad_maximum_fusion.1.refs_1_.refs_0_), custom_call_target="tpu_custom_call" | custom-call | bytes 2097152 | tf_op jit(solution)/shard_map/pallas_call | solution.py:94
  24.5 1.3 %shard_map.123 = (f32[16,1536]{1,0:T(8,128)S(1)}, f32[16,256]{1,0:T(8,128)S(1)}, bf16[16,1664]{1,0:T(8,128)(2,1)S(1)}) custom-call(bf16[8,1536]{1,0:T(8,128)(2,1)S(1)} %pad_maximum_fusion.1.refs_1_.refs_0_, bf16[8,1536]{1,0:T(8,128)(2,1)S(1)} %collective-permute-done.2.refs_1_, bf16[2,64,1536]{2,1,0:T(8,128)(2,1)S(1)} %get-tuple-element.39.refs_2_, ...), custom_call_target="tpu_custom_call" | custom-call | flops 1000000000 | tf_op jit(solution)/shard_map/pallas_call | solution.py:55
  25.8 1.2 %collective-permute-start.3 = (bf16[16,1664]{1,0:T(8,128)(2,1)S(1)}, bf16[16,1664]{1,0:T(8,128)(2,1)S(1)}, u32[]{:S(2)}, u32[]{:S(2)}) collective-permute-start(bf16[16,1664]{1,0:T(8,128)(2,1)S(1)} %get-tuple-element.44), channel_id=1, source_target_pairs={{0,2},{2,0},{4,6},{6,4},{8,10},{10,8},{12,14},{14,12},{1,3},{3,1},... | collective-permute-start | bytes 159752 | tf_op jit(solution)/shard_map/ppermute | solution.py:26
  27.0 3.6 %collective-permute-done.3.refs_2_ = bf16[16,1664]{1,0:T(8,128)(2,1)S(1)} collective-permute-done((bf16[16,1664]{1,0:T(8,128)(2,1)S(1)}, bf16[16,1664]{1,0:T(8,128)(2,1)S(1)}, u32[]{:S(2)}, u32[]{:S(2)}) %collective-permute-start.3) | collective-permute-done | bytes 53280 | tf_op jit(solution)/shard_map/ppermute | solution.py:26
  30.9 1.1 %collective-permute-start.4 = (bf16[16,1664]{1,0:T(8,128)(2,1)S(1)}, bf16[16,1664]{1,0:T(8,128)(2,1)S(1)}, u32[]{:S(2)}, u32[]{:S(2)}) collective-permute-start(bf16[16,1664]{1,0:T(8,128)(2,1)S(1)} %get-tuple-element.47), channel_id=1, source_target_pairs={{0,4},{2,6},{4,0},{6,2},{8,12},{10,14},{12,8},{14,10},{1,5},{3,7},... | collective-permute-start | bytes 159752 | tf_op jit(solution)/shard_map/ppermute | solution.py:26
  32.0 4.8 %collective-permute-done.4.refs_2_ = bf16[16,1664]{1,0:T(8,128)(2,1)S(1)} collective-permute-done((bf16[16,1664]{1,0:T(8,128)(2,1)S(1)}, bf16[16,1664]{1,0:T(8,128)(2,1)S(1)}, u32[]{:S(2)}, u32[]{:S(2)}) %collective-permute-start.4) | collective-permute-done | bytes 53280 | tf_op jit(solution)/shard_map/ppermute | solution.py:26
  37.1 1.6 %collective-permute-start.5 = (bf16[16,1664]{1,0:T(8,128)(2,1)S(1)}, bf16[16,1664]{1,0:T(8,128)(2,1)S(1)}, u32[]{:S(2)}, u32[]{:S(2)}) collective-permute-start(bf16[16,1664]{1,0:T(8,128)(2,1)S(1)} %get-tuple-element.50), channel_id=1, source_target_pairs={{0,8},{2,10},{4,12},{6,14},{8,0},{10,2},{12,4},{14,6},{1,9},{3,11}... | collective-permute-start | bytes 159752 | tf_op jit(solution)/shard_map/ppermute | solution.py:26
  38.7 3.5 %collective-permute-done.5.pay_ref = bf16[16,1664]{1,0:T(8,128)(2,1)S(1)} collective-permute-done((bf16[16,1664]{1,0:T(8,128)(2,1)S(1)}, bf16[16,1664]{1,0:T(8,128)(2,1)S(1)}, u32[]{:S(2)}, u32[]{:S(2)}) %collective-permute-start.5) | collective-permute-done | bytes 53280 | tf_op jit(solution)/shard_map/ppermute | solution.py:26
  42.5 0.6 shard_map.127.refs_0_
  43.2 1.2 %collective-permute-done.6.refs_1_ = f32[8,768]{1,0:T(8,128)S(1)} collective-permute-done((f32[8,768]{1,0:T(8,128)S(1)}, f32[8,768]{1,0:T(8,128)S(1)}, u32[]{:S(2)}, u32[]{:S(2)}) %collective-permute-start.6) | collective-permute-done | bytes 24608 | tf_op jit(solution)/shard_map/ppermute | solution.py:26
  44.4 1.3 %collective-permute-start.7 = (bf16[1,8,768]{2,1,0:T(8,128)(2,1)S(1)}, bf16[1,8,768]{2,1,0:T(8,128)(2,1)S(1)}, u32[]{:S(2)}, u32[]{:S(2)}) collective-permute-start(bf16[1,8,768]{2,1,0:T(8,128)(2,1)S(1)} %shard_map.128), channel_id=1, source_target_pairs={{0,9},{1,8},{2,11},{3,10},{4,13},{5,12},{6,15},{7,14},{8,1},{9,0},... | collective-permute-start | bytes 36872 | tf_op jit(solution)/shard_map/ppermute | solution.py:31
  45.7 2.8 %collective-permute-done.7 = bf16[1,8,768]{2,1,0:T(8,128)(2,1)S(1)} collective-permute-done((bf16[1,8,768]{2,1,0:T(8,128)(2,1)S(1)}, bf16[1,8,768]{2,1,0:T(8,128)(2,1)S(1)}, u32[]{:S(2)}, u32[]{:S(2)}) %collective-permute-start.7) | collective-permute-done | bytes 12320 | tf_op jit(solution)/shard_map/ppermute | solution.py:31
  48.5 1.4 %collective-permute-start.8 = (bf16[2,8,768]{2,1,0:T(8,128)(2,1)S(1)}, bf16[2,8,768]{2,1,0:T(8,128)(2,1)S(1)}, u32[]{:S(2)}, u32[]{:S(2)}) collective-permute-start(bf16[2,8,768]{2,1,0:T(8,128)(2,1)S(1)} %pad_maximum_fusion.2), channel_id=1, source_target_pairs={{0,5},{1,4},{2,7},{3,6},{4,1},{5,0},{6,3},{7,2},{8,13},{9,12},{10,... | collective-permute-start | bytes 73736 | tf_op jit(solution)/shard_map/ppermute | solution.py:31
  49.8 1.9 %collective-permute-done.8 = bf16[2,8,768]{2,1,0:T(8,128)(2,1)S(1)} collective-permute-done((bf16[2,8,768]{2,1,0:T(8,128)(2,1)S(1)}, bf16[2,8,768]{2,1,0:T(8,128)(2,1)S(1)}, u32[]{:S(2)}, u32[]{:S(2)}) %collective-permute-start.8) | collective-permute-done | bytes 24608 | tf_op jit(solution)/shard_map/ppermute | solution.py:31
  51.8 4.8 %collective-permute-done.9.refs_1_ = bf16[4,8,768]{2,1,0:T(8,128)(2,1)S(1)} collective-permute-done((bf16[4,8,768]{2,1,0:T(8,128)(2,1)S(1)}, bf16[4,8,768]{2,1,0:T(8,128)(2,1)S(1)}, u32[]{:S(2)}, u32[]{:S(2)}) %collective-permute-start.9) | collective-permute-done | bytes 49184 | tf_op jit(solution)/shard_map/ppermute | solution.py:31
  56.7 3.0 %shard_map.129 = (bf16[8,768]{1,0:T(8,128)(2,1)}, bf16[8,1536]{1,0:T(8,128)(2,1)S(1)}) custom-call(bf16[4,8,768]{2,1,0:T(8,128)(2,1)S(1)} %pad_maximum_fusion.refs_0_, bf16[4,8,768]{2,1,0:T(8,128)(2,1)S(1)} %collective-permute-done.9.refs_1_, bf16[6144,1536]{1,0:T(8,128)(2,1)S(1)} %copy-done), custom_call_target="tpu_custom_call" | custom-call | flops 1000000000 | tf_op jit(solution)/shard_map/pallas_call | solution.py:55
  59.9 1.4 %shard_map.130.refs_2_ = f32[8,3072]{1,0:T(8,128)S(1)} custom-call(bf16[8,1536]{1,0:T(8,128)(2,1)S(1)} %get-tuple-element.54.refs_0_, bf16[3072,3072]{1,0:T(8,128)(2,1)S(1)} %bitcast.11), custom_call_target="tpu_custom_call" | custom-call | flops 1000000000 | tf_op jit(solution)/shard_map/pallas_call | solution.py:55
  61.4 1.4 %shard_map.131 = (f32[4,3072]{1,0:T(4,128)S(1)}, f32[4,3072]{1,0:T(4,128)S(1)}) custom-call(bf16[8,1536]{1,0:T(8,128)(2,1)S(1)} %collective-permute-done.10.refs_0_, bf16[3072,3072]{1,0:T(8,128)(2,1)S(1)} %bitcast.11, f32[8,3072]{1,0:T(8,128)S(1)} %shard_map.130.refs_2_), custom_call_target="tpu_custom_call" | custom-call | flops 1000000000 | tf_op jit(solution)/shard_map/pallas_call | solution.py:55
  63.1 4.8 %collective-permute-done.11 = f32[4,3072]{1,0:T(4,128)S(1)} collective-permute-done((f32[4,3072]{1,0:T(4,128)S(1)}, f32[4,3072]{1,0:T(4,128)S(1)}, u32[]{:S(2)}, u32[]{:S(2)}) %collective-permute-start.11) | collective-permute-done | bytes 49184 | tf_op jit(solution)/shard_map/ppermute | solution.py:26
  68.0 4.1 %collective-permute-done.12 = f32[2,3072]{1,0:T(2,128)S(1)} collective-permute-done((f32[2,3072]{1,0:T(2,128)S(1)}, f32[2,3072]{1,0:T(2,128)S(1)}, u32[]{:S(2)}, u32[]{:S(2)}) %collective-permute-start.12) | collective-permute-done | bytes 24608 | tf_op jit(solution)/shard_map/ppermute | solution.py:26
  72.1 2.3 %collective-permute-start.13 = (f32[1,3072]{1,0:T(1,128)S(1)}, f32[1,3072]{1,0:T(1,128)S(1)}, u32[]{:S(2)}, u32[]{:S(2)}) collective-permute-start(f32[1,3072]{1,0:T(1,128)S(1)} %slice.27), channel_id=1, source_target_pairs={{0,8},{2,10},{4,12},{6,14},{8,0},{10,2},{12,4},{14,6},{1,9},{3,11}... | collective-permute-start | bytes 36872 | tf_op jit(solution)/shard_map/ppermute | solution.py:26
  74.5 5.4 %all-gather.7.cloned.1.call-done = bf16[8,1,64,1536]{3,2,1,0:T(8,128)(2,1)} async-done(((bf16[1,1,64,1536]{3,2,1,0:T(8,128)(2,1)}), bf16[8,1,64,1536]{3,2,1,0:T(8,128)(2,1)}) %all-gather.7.cloned.1.call-update) | async-done | bytes 1572880 | tf_op jit(solution)/shard_map/all_gather | solution.py:420
  79.9 2.4 %shard_map.132 = bf16[2,64,1536]{2,1,0:T(8,128)(2,1)} custom-call(bf16[8,64,1536]{2,1,0:T(8,128)(2,1)} %bitcast.12, bf16[8,64,1536]{2,1,0:T(8,128)(2,1)} %bitcast.13, bf16[2,1536]{1,0:T(2,128)(2,1)S(1)} %get-tuple-element.41.refs_4_.new_ref, s32[1,8]{1,0:T(1,128)S(1)} %copy-done.1, s32[1]{0:T(128)S(6)} %copy.15.refs_6_.lengths_ref), custom_call_target="tpu_custom_call" | custom-call | tf_op jit(solution)/shard_map/pallas_call | solution.py:316
  82.3 0.6 fusion.1
  (39 shorter events, 1.9 us)
Async XLA Ops:
  7.2 67.3 %all-gather.5.cloned.1.call-start = ((), (), s32[]{:S(2)}) async-start(), calls=%async_computation | async-start | bytes 1769472 | tf_op jit(solution)/shard_map/all_gather | solution.py:419
  9.0 70.8 %all-gather.7.cloned.1.call-start = ((), (), s32[]{:S(2)}) async-start(), calls=%async_computation.1 | async-start | bytes 1769472 | tf_op jit(solution)/shard_map/all_gather | solution.py:420
  9.8 5.9 %collective-permute-start = (bf16[2,1536]{1,0:T(2,128)(2,1)}, bf16[2,1536]{1,0:T(2,128)(2,1)S(1)}, u32[]{:S(2)}, u32[]{:S(2)}) collective-permute-start(bf16[2,1536]{1,0:T(2,128)(2,1)} %bitcast.17), channel_id=1, source_target_pairs={{0,8},{2,10},{4,12},{6,14},{8,0},{10,2},{12,4},{14,6},{1,9},{3,11}... | collective-permute-start | bytes 18440 | tf_op jit(solution)/shard_map/ppermute | solution.py:26
  15.7 3.8 %collective-permute-start.1 = (bf16[4,1536]{1,0:T(4,128)(2,1)S(1)}, bf16[4,1536]{1,0:T(4,128)(2,1)S(1)}, u32[]{:S(2)}, u32[]{:S(2)}) collective-permute-start(bf16[4,1536]{1,0:T(4,128)(2,1)S(1)} %pad_maximum_fusion.3), channel_id=1, source_target_pairs={{0,4},{2,6},{4,0},{6,2},{8,12},{10,14},{12,8},{14,10},{1,5},{3,7},... | collective-permute-start | bytes 36872 | tf_op jit(solution)/shard_map/ppermute | solution.py:26
  19.5 5.0 %collective-permute-start.2 = (bf16[8,1536]{1,0:T(8,128)(2,1)S(1)}, bf16[8,1536]{1,0:T(8,128)(2,1)S(1)}, u32[]{:S(2)}, u32[]{:S(2)}) collective-permute-start(bf16[8,1536]{1,0:T(8,128)(2,1)S(1)} %pad_maximum_fusion.1.refs_1_.refs_0_), channel_id=1, source_target_pairs={{0,2},{2,0},{4,6},{6,4},{8,10},{10,8},{12,14},{14,12},{1,3},{3,1},... | collective-permute-start | bytes 73736 | tf_op jit(solution)/shard_map/ppermute | solution.py:26
  22.1 2.5 %copy-start.1 = (s32[1,8]{1,0:T(1,128)S(1)}, s32[1,8]{1,0:T(1,128)}, u32[]{:S(2)}) copy-start(s32[1,8]{1,0:T(1,128)} %parents_ref.1) | copy-start | bytes 100
  25.8 4.8 %collective-permute-start.3 = (bf16[16,1664]{1,0:T(8,128)(2,1)S(1)}, bf16[16,1664]{1,0:T(8,128)(2,1)S(1)}, u32[]{:S(2)}, u32[]{:S(2)}) collective-permute-start(bf16[16,1664]{1,0:T(8,128)(2,1)S(1)} %get-tuple-element.44), channel_id=1, source_target_pairs={{0,2},{2,0},{4,6},{6,4},{8,10},{10,8},{12,14},{14,12},{1,3},{3,1},... | collective-permute-start | bytes 159752 | tf_op jit(solution)/shard_map/ppermute | solution.py:26
  30.6 26.1 %copy-start = (bf16[6144,1536]{1,0:T(8,128)(2,1)S(1)}, bf16[6144,1536]{1,0:T(8,128)(2,1)}, u32[]{:S(2)}) copy-start(bf16[6144,1536]{1,0:T(8,128)(2,1)} %refs_2_.1) | copy-start | bytes 56623108
  30.9 5.9 %collective-permute-start.4 = (bf16[16,1664]{1,0:T(8,128)(2,1)S(1)}, bf16[16,1664]{1,0:T(8,128)(2,1)S(1)}, u32[]{:S(2)}, u32[]{:S(2)}) collective-permute-start(bf16[16,1664]{1,0:T(8,128)(2,1)S(1)} %get-tuple-element.47), channel_id=1, source_target_pairs={{0,4},{2,6},{4,0},{6,2},{8,12},{10,14},{12,8},{14,10},{1,5},{3,7},... | collective-permute-start | bytes 159752 | tf_op jit(solution)/shard_map/ppermute | solution.py:26
  36.8 23.1 %slice-start = ((s8[18874368]{0:T(1024)(128)(4,1)}), s8[4194304]{0:T(1024)(128)(4,1)S(1)}, s32[]{:S(2)}) async-start(s8[18874368]{0:T(1024)(128)(4,1)} %bitcast.10), calls=%async_computation.2 | async-start | bytes 8388608
  37.1 5.1 %collective-permute-start.5 = (bf16[16,1664]{1,0:T(8,128)(2,1)S(1)}, bf16[16,1664]{1,0:T(8,128)(2,1)S(1)}, u32[]{:S(2)}, u32[]{:S(2)}) collective-permute-start(bf16[16,1664]{1,0:T(8,128)(2,1)S(1)} %get-tuple-element.50), channel_id=1, source_target_pairs={{0,8},{2,10},{4,12},{6,14},{8,0},{10,2},{12,4},{14,6},{1,9},{3,11}... | collective-permute-start | bytes 159752 | tf_op jit(solution)/shard_map/ppermute | solution.py:26
  42.2 17.7 %slice-start.1 = ((s8[18874368]{0:T(1024)(128)(4,1)}), s8[4194304]{0:T(1024)(128)(4,1)S(1)}, s32[]{:S(2)}) async-start(s8[18874368]{0:T(1024)(128)(4,1)} %bitcast.10), calls=%async_computation.3 | async-start | bytes 8388608
  43.1 16.8 %slice-start.2 = ((s8[18874368]{0:T(1024)(128)(4,1)}), s8[4194304]{0:T(1024)(128)(4,1)S(1)}, s32[]{:S(2)}) async-start(s8[18874368]{0:T(1024)(128)(4,1)} %bitcast.10), calls=%async_computation.4 | async-start | bytes 8388608
  43.1 1.3 %collective-permute-start.6 = (f32[8,768]{1,0:T(8,128)S(1)}, f32[8,768]{1,0:T(8,128)S(1)}, u32[]{:S(2)}, u32[]{:S(2)}) collective-permute-start(f32[8,768]{1,0:T(8,128)S(1)} %shard_map.127.refs_0_), channel_id=1, source_target_pairs={{0,1},{1,0},{2,3},{3,2},{4,5},{5,4},{6,7},{7,6},{8,9},{9,8},{10,11... | collective-permute-start | bytes 73736 | tf_op jit(solution)/shard_map/ppermute | solution.py:26
  44.4 4.1 %collective-permute-start.7 = (bf16[1,8,768]{2,1,0:T(8,128)(2,1)S(1)}, bf16[1,8,768]{2,1,0:T(8,128)(2,1)S(1)}, u32[]{:S(2)}, u32[]{:S(2)}) collective-permute-start(bf16[1,8,768]{2,1,0:T(8,128)(2,1)S(1)} %shard_map.128), channel_id=1, source_target_pairs={{0,9},{1,8},{2,11},{3,10},{4,13},{5,12},{6,15},{7,14},{8,1},{9,0},... | collective-permute-start | bytes 36872 | tf_op jit(solution)/shard_map/ppermute | solution.py:31
  48.5 3.3 %collective-permute-start.8 = (bf16[2,8,768]{2,1,0:T(8,128)(2,1)S(1)}, bf16[2,8,768]{2,1,0:T(8,128)(2,1)S(1)}, u32[]{:S(2)}, u32[]{:S(2)}) collective-permute-start(bf16[2,8,768]{2,1,0:T(8,128)(2,1)S(1)} %pad_maximum_fusion.2), channel_id=1, source_target_pairs={{0,5},{1,4},{2,7},{3,6},{4,1},{5,0},{6,3},{7,2},{8,13},{9,12},{10,... | collective-permute-start | bytes 73736 | tf_op jit(solution)/shard_map/ppermute | solution.py:31
  51.7 8.2 %slice-start.3 = ((s8[18874368]{0:T(1024)(128)(4,1)}), s8[4194304]{0:T(1024)(128)(4,1)S(1)}, s32[]{:S(2)}) async-start(s8[18874368]{0:T(1024)(128)(4,1)} %bitcast.10), calls=%async_computation.5 | async-start | bytes 8388608
  51.8 8.2 %slice-start.4 = ((s8[18874368]{0:T(1024)(128)(4,1)}), s8[2097152]{0:T(1024)(128)(4,1)S(1)}, s32[]{:S(2)}) async-start(s8[18874368]{0:T(1024)(128)(4,1)} %bitcast.10), calls=%async_computation.6 | async-start | bytes 4194304
  51.8 4.9 %collective-permute-start.9 = (bf16[4,8,768]{2,1,0:T(8,128)(2,1)S(1)}, bf16[4,8,768]{2,1,0:T(8,128)(2,1)S(1)}, u32[]{:S(2)}, u32[]{:S(2)}) collective-permute-start(bf16[4,8,768]{2,1,0:T(8,128)(2,1)S(1)} %pad_maximum_fusion.refs_0_), channel_id=1, source_target_pairs={{0,3},{1,2},{2,1},{3,0},{4,7},{5,6},{6,5},{7,4},{8,11},{9,10},{10,... | collective-permute-start | bytes 147464 | tf_op jit(solution)/shard_map/ppermute | solution.py:31
  59.7 1.7 %collective-permute-start.10 = (bf16[8,1536]{1,0:T(8,128)(2,1)S(1)}, bf16[8,1536]{1,0:T(8,128)(2,1)S(1)}, u32[]{:S(2)}, u32[]{:S(2)}) collective-permute-start(bf16[8,1536]{1,0:T(8,128)(2,1)S(1)} %get-tuple-element.54.refs_0_), channel_id=1, source_target_pairs={{0,1},{1,0},{2,3},{3,2},{4,5},{5,4},{6,7},{7,6},{8,9},{9,8},{10,11... | collective-permute-start | bytes 73736 | tf_op jit(solution)/shard_map/ppermute | solution.py:26
  62.8 5.1 %collective-permute-start.11 = (f32[4,3072]{1,0:T(4,128)S(1)}, f32[4,3072]{1,0:T(4,128)S(1)}, u32[]{:S(2)}, u32[]{:S(2)}) collective-permute-start(f32[4,3072]{1,0:T(4,128)S(1)} %get-tuple-element.56), channel_id=1, source_target_pairs={{0,2},{2,0},{4,6},{6,4},{8,10},{10,8},{12,14},{14,12},{1,3},{3,1},... | collective-permute-start | bytes 147464 | tf_op jit(solution)/shard_map/ppermute | solution.py:26
  68.0 4.2 %collective-permute-start.12 = (f32[2,3072]{1,0:T(2,128)S(1)}, f32[2,3072]{1,0:T(2,128)S(1)}, u32[]{:S(2)}, u32[]{:S(2)}) collective-permute-start(f32[2,3072]{1,0:T(2,128)S(1)} %slice.25), channel_id=1, source_target_pairs={{0,4},{2,6},{4,0},{6,2},{8,12},{10,14},{12,8},{14,10},{1,5},{3,7},... | collective-permute-start | bytes 73736 | tf_op jit(solution)/shard_map/ppermute | solution.py:26
  72.1 10.1 %collective-permute-start.13 = (f32[1,3072]{1,0:T(1,128)S(1)}, f32[1,3072]{1,0:T(1,128)S(1)}, u32[]{:S(2)}, u32[]{:S(2)}) collective-permute-start(f32[1,3072]{1,0:T(1,128)S(1)} %slice.27), channel_id=1, source_target_pairs={{0,8},{2,10},{4,12},{6,14},{8,0},{10,2},{12,4},{14,6},{1,9},{3,11}... | collective-permute-start | bytes 36872 | tf_op jit(solution)/shard_map/ppermute | solution.py:26
Sparse Core Ops, SparseCore 0:
  9.5 35.8 all-gather.4
  47.5 32.3 all-gather.6

commit v10 on v8

--- a/solution.py
+++ b/solution.py
@@ -239,6 +239,24 @@
     first = jnp.dot(attended_ref[...], weight_ref[0], preferred_element_type=jnp.float32)
     second = jnp.dot(attended_ref[...], weight_ref[1], preferred_element_type=jnp.float32)
     out_ref[...] = first[:rows] + second[rows:]
+
+
+def finish_project_kernel(num_ref, state_ref, pay_ref, weight_ref, out_ref, num, attended):
+    finish_kernel(num_ref, state_ref, pay_ref, attended, num)
+    project_kernel(attended, weight_ref, out_ref)
+
+
+def finish_project(num, state, pay, weight):
+    rows, columns = num.shape[0] // 2, weight.shape[2]
+    return pl.pallas_call(
+        finish_project_kernel,
+        out_shape=jax.ShapeDtypeStruct((rows, columns), jnp.float32),
+        in_specs=[VM] * 4,
+        out_specs=VM,
+        scratch_shapes=[pltpu.VMEM(num.shape, jnp.float32), pltpu.VMEM(num.shape, jnp.bfloat16)],
+        compiler_params=pltpu.CompilerParams(vmem_limit_bytes=8 * MIB),
+        cost_estimate=pl.CostEstimate(flops=2 * STEP_FLOPS, bytes_accessed=0, transcendentals=0),
+    )(num, state, pay, weight)
 
 
 def add_kernel(own_ref, other_ref, residual_ref, out_ref):
@@ -376,14 +394,15 @@
         if bit == devices:
             break
         num, state, pay = call(merge_kernel, state_shapes, num, state, arrived, hold=())
-    attended = finish(num, state, arrived)
-    if stride > 1:
+    if stride == 1:
+        partial = finish_project(num, state, arrived, out_row)
+    else:
+        attended = finish(num, state, arrived)
         stacked = jnp.concatenate(doubling(attended[None], 1, stride))
         wanted = reverse(jnp.bitwise_xor(jnp.arange(stride, dtype=jnp.int32), request), stride)
         stacked = stacked[wanted].reshape(stride, 2, BEAMS, width)
         attended = stacked.transpose(1, 2, 0, 3).reshape(2 * rows, width)
-
-    partial = call(project_kernel, shape((rows, columns), f32), attended, out_row, hold=())
+        partial = call(project_kernel, shape((rows, columns), f32), attended, out_row)
     other = xor_permute(partial, "tensor", 1)
     mine = call(add_kernel, pltpu.VMEM((1, rows, columns), bf16), partial, other, residual_row, hold=())
     near, far = doubling(mine, 1, devices, cross=True)
@@ -416,14 +435,15 @@
     while True:
         arrived = xor_permute(send, "batch", bit)
         bit *= 2
+        if 2 * bit == devices:
+            cache = place(stride, order, gathered, new_row, parents, lengths)
+            arrived, cache = pin(arrived, cache)
+        total = keep + arrived
         if bit == devices:
             break
-        total = keep + arrived
         half = total.shape[0] // 2
         keep, send = total[:half], total[half:]
-    cache = place(stride, order, gathered, new_row, parents, lengths)
-    arrived, cache = pin(arrived, cache)
-    ffn_row = (keep + arrived).astype(bf16)
+    ffn_row = total.astype(bf16)
     return (hidden[None], ffn_row[None], cache[None])
 
 

time: 82.6 us -> 82.7 us (level)
    pallas_call x8 -> x7, Pallas kernels: 8.37 us -> 7.75 us  [call(): pl.pallas_call(functools.partial(drop, kernel, first, len(hold)), out_sha...]
  transfers between devices with their start and end apart: 15 -> 15, of which waited for: 11 -> 12; matrix products, arithmetic and copies ran while one was open for 0% -> 0% of each run, Pallas kernels for 18% -> 18%
where the time goes in v10:
time: 82.7 us; the launch traced here: 82.5 us
  waiting for transfers between devices  32.8 us (40%)
  starting transfers between devices  19.4 us (23%)
  between operations  14.9 us (18%)
  Pallas kernels  14.7 us (18%)
    ppermute x11, waiting for transfers between devices, xor_permute(): return lax.ppermute(value, axis, [(i, i ^ bit) for i in range(total)])  23.4 us
    ppermute x11, starting transfers between devices, xor_permute(): return lax.ppermute(value, axis, [(i, i ^ bit) for i in range(total)])  16.4 us
    ppermute x3, waiting for transfers between devices, cross_permute(): return lax.ppermute(value, ('batch', 'tensor'), pairs)  8.67 us
    pallas_call x7, Pallas kernels, call(): pl.pallas_call(functools.partial(drop, kernel, first, len(hold)), out_sha...  7.75 us
    pallas_call x2, Pallas kernels, fetch(): pl.pallas_call(functools.partial(fetch_kernel, count), out_shape=[pltpu.V...  3.72 us
    ppermute x3, starting transfers between devices, cross_permute(): return lax.ppermute(value, ('batch', 'tensor'), pairs)  2.97 us
    pallas_call x1, Pallas kernels, place(): pl.pallas_call(functools.partial(place_kernel, stride, order), out_shape=...  2.38 us
  transfers between devices with their start and end apart: 15, of which 12 were waited for; matrix products, arithmetic and copies ran while one was open for 0% of the time, Pallas kernels for 18%

profile of v10, /device:TPU:0, one launch (start us, length us, event | category | flops | bytes accessed | tf_op | source)
XLA Modules:
  0.0 82.5 jit_solution(8472271504976487613)
XLA Ops:
  7.2 0.7 all-gather.2.cloned.1.call-update
  7.9 4.1 %collective-permute-start = (bf16[2,1536]{1,0:T(2,128)(2,1)}, bf16[2,1536]{1,0:T(2,128)(2,1)S(1)}, u32[]{:S(2)}, u32[]{:S(2)}) collective-permute-start(bf16[2,1536]{1,0:T(2,128)(2,1)} %bitcast.13), channel_id=1, source_target_pairs={{0,8},{2,10},{4,12},{6,14},{8,0},{10,2},{12,4},{14,6},{1,9},{3,11}... | collective-permute-start | bytes 18440 | tf_op jit(solution)/shard_map/ppermute | solution.py:26
  12.0 1.3 %shard_map.121 = (bf16[2,1536]{1,0:T(2,128)(2,1)S(1)}, bf16[2,64,1536]{2,1,0:T(8,128)(2,1)S(1)}, bf16[2,64,1536]{2,1,0:T(8,128)(2,1)S(1)}, bf16[2,1536]{1,0:T(2,128)(2,1)S(1)}, bf16[1,8,768]{2,1,0:T(8,128)(2,1)S(1)}) custom-call(bf16[2,1536]{1,0:T(2,128)(2,1)} %bitcast.14, bf16[2,64,1536]{2,1,0:T(8,128)(2,1)} %bitcast.10, bf16[2,64,1536]{2,1,0:T(8,128)(2,1)} %bitcast.11, ...), custom_call_target="tpu_custom_call" | custom-call | bytes 2097152 | tf_op jit(solution)/shard_map/pallas_call | solution.py:94
  13.8 2.0 %collective-permute-start.1 = (bf16[4,1536]{1,0:T(4,128)(2,1)S(1)}, bf16[4,1536]{1,0:T(4,128)(2,1)S(1)}, u32[]{:S(2)}, u32[]{:S(2)}) collective-permute-start(bf16[4,1536]{1,0:T(4,128)(2,1)S(1)} %pad_maximum_fusion.3), channel_id=1, source_target_pairs={{0,4},{2,6},{4,0},{6,2},{8,12},{10,14},{12,8},{14,10},{1,5},{3,7},... | collective-permute-start | bytes 36872 | tf_op jit(solution)/shard_map/ppermute | solution.py:26
  15.8 1.8 %collective-permute-done.1 = bf16[4,1536]{1,0:T(4,128)(2,1)S(1)} collective-permute-done((bf16[4,1536]{1,0:T(4,128)(2,1)S(1)}, bf16[4,1536]{1,0:T(4,128)(2,1)S(1)}, u32[]{:S(2)}, u32[]{:S(2)}) %collective-permute-start.1) | collective-permute-done | bytes 12320 | tf_op jit(solution)/shard_map/ppermute | solution.py:26
  17.6 1.9 %collective-permute-start.2 = (bf16[8,1536]{1,0:T(8,128)(2,1)S(1)}, bf16[8,1536]{1,0:T(8,128)(2,1)S(1)}, u32[]{:S(2)}, u32[]{:S(2)}) collective-permute-start(bf16[8,1536]{1,0:T(8,128)(2,1)S(1)} %pad_maximum_fusion.1.refs_1_.refs_0_), channel_id=1, source_target_pairs={{0,2},{2,0},{4,6},{6,4},{8,10},{10,8},{12,14},{14,12},{1,3},{3,1},... | collective-permute-start | bytes 73736 | tf_op jit(solution)/shard_map/ppermute | solution.py:26
  20.2 2.4 %shard_map.122.weight_ref = bf16[2,1536,768]{2,1,0:T(8,128)(2,1)S(1)} custom-call(bf16[2,1536,768]{2,1,0:T(8,128)(2,1)} %refs_0_.1, bf16[8,1536]{1,0:T(8,128)(2,1)S(1)} %pad_maximum_fusion.1.refs_1_.refs_0_), custom_call_target="tpu_custom_call" | custom-call | bytes 2097152 | tf_op jit(solution)/shard_map/pallas_call | solution.py:94
  22.6 1.3 %shard_map.123 = (f32[16,1536]{1,0:T(8,128)S(1)}, f32[16,256]{1,0:T(8,128)S(1)}, bf16[16,1664]{1,0:T(8,128)(2,1)S(1)}) custom-call(bf16[8,1536]{1,0:T(8,128)(2,1)S(1)} %pad_maximum_fusion.1.refs_1_.refs_0_, bf16[8,1536]{1,0:T(8,128)(2,1)S(1)} %collective-permute-done.2.refs_1_, bf16[2,64,1536]{2,1,0:T(8,128)(2,1)S(1)} %get-tuple-element.39.refs_2_, ...), custom_call_target="tpu_custom_call" | custom-call | flops 1000000000 | tf_op jit(solution)/shard_map/pallas_call | solution.py:55
  23.9 1.3 %collective-permute-start.3 = (bf16[16,1664]{1,0:T(8,128)(2,1)S(1)}, bf16[16,1664]{1,0:T(8,128)(2,1)S(1)}, u32[]{:S(2)}, u32[]{:S(2)}) collective-permute-start(bf16[16,1664]{1,0:T(8,128)(2,1)S(1)} %get-tuple-element.44), channel_id=1, source_target_pairs={{0,2},{2,0},{4,6},{6,4},{8,10},{10,8},{12,14},{14,12},{1,3},{3,1},... | collective-permute-start | bytes 159752 | tf_op jit(solution)/shard_map/ppermute | solution.py:26
  25.2 4.0 %collective-permute-done.3.refs_2_ = bf16[16,1664]{1,0:T(8,128)(2,1)S(1)} collective-permute-done((bf16[16,1664]{1,0:T(8,128)(2,1)S(1)}, bf16[16,1664]{1,0:T(8,128)(2,1)S(1)}, u32[]{:S(2)}, u32[]{:S(2)}) %collective-permute-start.3) | collective-permute-done | bytes 53280 | tf_op jit(solution)/shard_map/ppermute | solution.py:26
  29.5 0.5 collective-permute-start.4
  30.1 5.1 %collective-permute-done.4.refs_2_ = bf16[16,1664]{1,0:T(8,128)(2,1)S(1)} collective-permute-done((bf16[16,1664]{1,0:T(8,128)(2,1)S(1)}, bf16[16,1664]{1,0:T(8,128)(2,1)S(1)}, u32[]{:S(2)}, u32[]{:S(2)}) %collective-permute-start.4) | collective-permute-done | bytes 53280 | tf_op jit(solution)/shard_map/ppermute | solution.py:26
  35.4 1.8 %collective-permute-start.5 = (bf16[16,1664]{1,0:T(8,128)(2,1)S(1)}, bf16[16,1664]{1,0:T(8,128)(2,1)S(1)}, u32[]{:S(2)}, u32[]{:S(2)}) collective-permute-start(bf16[16,1664]{1,0:T(8,128)(2,1)S(1)} %get-tuple-element.50), channel_id=1, source_target_pairs={{0,8},{2,10},{4,12},{6,14},{8,0},{10,2},{12,4},{14,6},{1,9},{3,11}... | collective-permute-start | bytes 159752 | tf_op jit(solution)/shard_map/ppermute | solution.py:26
  37.2 4.8 %collective-permute-done.5.pay_ref = bf16[16,1664]{1,0:T(8,128)(2,1)S(1)} collective-permute-done((bf16[16,1664]{1,0:T(8,128)(2,1)S(1)}, bf16[16,1664]{1,0:T(8,128)(2,1)S(1)}, u32[]{:S(2)}, u32[]{:S(2)}) %collective-permute-start.5) | collective-permute-done | bytes 53280 | tf_op jit(solution)/shard_map/ppermute | solution.py:26
  42.1 0.8 shard_map.126.refs_0_
  43.0 1.2 %collective-permute-done.6.refs_1_ = f32[8,768]{1,0:T(8,128)S(1)} collective-permute-done((f32[8,768]{1,0:T(8,128)S(1)}, f32[8,768]{1,0:T(8,128)S(1)}, u32[]{:S(2)}, u32[]{:S(2)}) %collective-permute-start.6) | collective-permute-done | bytes 24608 | tf_op jit(solution)/shard_map/ppermute | solution.py:26
  44.2 1.1 %collective-permute-start.7 = (bf16[1,8,768]{2,1,0:T(8,128)(2,1)S(1)}, bf16[1,8,768]{2,1,0:T(8,128)(2,1)S(1)}, u32[]{:S(2)}, u32[]{:S(2)}) collective-permute-start(bf16[1,8,768]{2,1,0:T(8,128)(2,1)S(1)} %shard_map.127), channel_id=1, source_target_pairs={{0,9},{1,8},{2,11},{3,10},{4,13},{5,12},{6,15},{7,14},{8,1},{9,0},... | collective-permute-start | bytes 36872 | tf_op jit(solution)/shard_map/ppermute | solution.py:31
  45.3 3.4 %collective-permute-done.7 = bf16[1,8,768]{2,1,0:T(8,128)(2,1)S(1)} collective-permute-done((bf16[1,8,768]{2,1,0:T(8,128)(2,1)S(1)}, bf16[1,8,768]{2,1,0:T(8,128)(2,1)S(1)}, u32[]{:S(2)}, u32[]{:S(2)}) %collective-permute-start.7) | collective-permute-done | bytes 12320 | tf_op jit(solution)/shard_map/ppermute | solution.py:31
  48.7 0.6 collective-permute-start.8
  49.3 3.0 %collective-permute-done.8 = bf16[2,8,768]{2,1,0:T(8,128)(2,1)S(1)} collective-permute-done((bf16[2,8,768]{2,1,0:T(8,128)(2,1)S(1)}, bf16[2,8,768]{2,1,0:T(8,128)(2,1)S(1)}, u32[]{:S(2)}, u32[]{:S(2)}) %collective-permute-start.8) | collective-permute-done | bytes 24608 | tf_op jit(solution)/shard_map/ppermute | solution.py:31
  52.3 1.3 %collective-permute-start.9 = (bf16[4,8,768]{2,1,0:T(8,128)(2,1)S(1)}, bf16[4,8,768]{2,1,0:T(8,128)(2,1)S(1)}, u32[]{:S(2)}, u32[]{:S(2)}) collective-permute-start(bf16[4,8,768]{2,1,0:T(8,128)(2,1)S(1)} %pad_maximum_fusion.refs_0_), channel_id=1, source_target_pairs={{0,3},{1,2},{2,1},{3,0},{4,7},{5,6},{6,5},{7,4},{8,11},{9,10},{10,... | collective-permute-start | bytes 147464 | tf_op jit(solution)/shard_map/ppermute | solution.py:31
  53.6 2.3 %collective-permute-done.9.refs_1_ = bf16[4,8,768]{2,1,0:T(8,128)(2,1)S(1)} collective-permute-done((bf16[4,8,768]{2,1,0:T(8,128)(2,1)S(1)}, bf16[4,8,768]{2,1,0:T(8,128)(2,1)S(1)}, u32[]{:S(2)}, u32[]{:S(2)}) %collective-permute-start.9) | collective-permute-done | bytes 49184 | tf_op jit(solution)/shard_map/ppermute | solution.py:31
  55.9 3.0 %shard_map.128 = (bf16[8,768]{1,0:T(8,128)(2,1)}, bf16[8,1536]{1,0:T(8,128)(2,1)S(1)}) custom-call(bf16[4,8,768]{2,1,0:T(8,128)(2,1)S(1)} %pad_maximum_fusion.refs_0_, bf16[4,8,768]{2,1,0:T(8,128)(2,1)S(1)} %collective-permute-done.9.refs_1_, bf16[6144,1536]{1,0:T(8,128)(2,1)S(1)} %copy-done), custom_call_target="tpu_custom_call" | custom-call | flops 1000000000 | tf_op jit(solution)/shard_map/pallas_call | solution.py:55
  59.4 1.4 %shard_map.129.refs_2_ = f32[8,3072]{1,0:T(8,128)S(1)} custom-call(bf16[8,1536]{1,0:T(8,128)(2,1)S(1)} %get-tuple-element.54.refs_0_, bf16[3072,3072]{1,0:T(8,128)(2,1)S(1)} %bitcast.9), custom_call_target="tpu_custom_call" | custom-call | flops 1000000000 | tf_op jit(solution)/shard_map/pallas_call | solution.py:55
  60.9 1.4 %shard_map.130 = (f32[4,3072]{1,0:T(4,128)S(1)}, f32[4,3072]{1,0:T(4,128)S(1)}) custom-call(bf16[8,1536]{1,0:T(8,128)(2,1)S(1)} %collective-permute-done.10.refs_0_, bf16[3072,3072]{1,0:T(8,128)(2,1)S(1)} %bitcast.9, f32[8,3072]{1,0:T(8,128)S(1)} %shard_map.129.refs_2_), custom_call_target="tpu_custom_call" | custom-call | flops 1000000000 | tf_op jit(solution)/shard_map/pallas_call | solution.py:55
  62.3 1.1 %collective-permute-start.11 = (f32[4,3072]{1,0:T(4,128)S(1)}, f32[4,3072]{1,0:T(4,128)S(1)}, u32[]{:S(2)}, u32[]{:S(2)}) collective-permute-start(f32[4,3072]{1,0:T(4,128)S(1)} %get-tuple-element.56), channel_id=1, source_target_pairs={{0,2},{2,0},{4,6},{6,4},{8,10},{10,8},{12,14},{14,12},{1,3},{3,1},... | collective-permute-start | bytes 147464 | tf_op jit(solution)/shard_map/ppermute | solution.py:26
  63.4 3.0 %collective-permute-done.11 = f32[4,3072]{1,0:T(4,128)S(1)} collective-permute-done((f32[4,3072]{1,0:T(4,128)S(1)}, f32[4,3072]{1,0:T(4,128)S(1)}, u32[]{:S(2)}, u32[]{:S(2)}) %collective-permute-start.11) | collective-permute-done | bytes 49184 | tf_op jit(solution)/shard_map/ppermute | solution.py:26
  66.5 1.1 %collective-permute-start.12 = (f32[2,3072]{1,0:T(2,128)S(1)}, f32[2,3072]{1,0:T(2,128)S(1)}, u32[]{:S(2)}, u32[]{:S(2)}) collective-permute-start(f32[2,3072]{1,0:T(2,128)S(1)} %slice.17), channel_id=1, source_target_pairs={{0,4},{2,6},{4,0},{6,2},{8,12},{10,14},{12,8},{14,10},{1,5},{3,7},... | collective-permute-start | bytes 73736 | tf_op jit(solution)/shard_map/ppermute | solution.py:26
  67.6 2.4 %shard_map.131 = bf16[2,64,1536]{2,1,0:T(8,128)(2,1)} custom-call(bf16[8,2,64,1536]{3,2,1,0:T(8,128)(2,1)} %all-gather.2.cloned.1.call-done.gathered_ref, bf16[2,1536]{1,0:T(2,128)(2,1)S(1)} %get-tuple-element.41.refs_4_.new_ref, s32[1,8]{1,0:T(1,128)S(1)} %copy-done.1, s32[1]{0:T(128)S(6)} %copy.13.refs_6_.lengths_ref), custom_call_target="tpu_custom_call" | custom-call | tf_op jit(solution)/shard_map/pallas_call | solution.py:330
  70.4 2.0 %collective-permute-start.13 = (f32[1,3072]{1,0:T(1,128)S(1)}, f32[1,3072]{1,0:T(1,128)S(1)}, u32[]{:S(2)}, u32[]{:S(2)}) collective-permute-start(f32[1,3072]{1,0:T(1,128)S(1)} %slice.19), channel_id=1, source_target_pairs={{0,8},{2,10},{4,12},{6,14},{8,0},{10,2},{12,4},{14,6},{1,9},{3,11}... | collective-permute-start | bytes 36872 | tf_op jit(solution)/shard_map/ppermute | solution.py:26
  72.4 2.7 %collective-permute-done.13 = f32[1,3072]{1,0:T(1,128)S(1)} collective-permute-done((f32[1,3072]{1,0:T(1,128)S(1)}, f32[1,3072]{1,0:T(1,128)S(1)}, u32[]{:S(2)}, u32[]{:S(2)}) %collective-permute-start.13) | collective-permute-done | bytes 12320 | tf_op jit(solution)/shard_map/ppermute | solution.py:26
  75.0 0.6 fusion.1
  (34 shorter events, 2.3 us)
Async XLA Ops:
  7.2 60.4 %all-gather.2.cloned.1.call-start = ((), (), s32[]{:S(2)}) async-start(), calls=%async_computation | async-start | bytes 3538944 | tf_op jit(solution)/shard_map/all_gather | solution.py:433
  7.9 5.9 %collective-permute-start = (bf16[2,1536]{1,0:T(2,128)(2,1)}, bf16[2,1536]{1,0:T(2,128)(2,1)S(1)}, u32[]{:S(2)}, u32[]{:S(2)}) collective-permute-start(bf16[2,1536]{1,0:T(2,128)(2,1)} %bitcast.13), channel_id=1, source_target_pairs={{0,8},{2,10},{4,12},{6,14},{8,0},{10,2},{12,4},{14,6},{1,9},{3,11}... | collective-permute-start | bytes 18440 | tf_op jit(solution)/shard_map/ppermute | solution.py:26
  13.8 3.8 %collective-permute-start.1 = (bf16[4,1536]{1,0:T(4,128)(2,1)S(1)}, bf16[4,1536]{1,0:T(4,128)(2,1)S(1)}, u32[]{:S(2)}, u32[]{:S(2)}) collective-permute-start(bf16[4,1536]{1,0:T(4,128)(2,1)S(1)} %pad_maximum_fusion.3), channel_id=1, source_target_pairs={{0,4},{2,6},{4,0},{6,2},{8,12},{10,14},{12,8},{14,10},{1,5},{3,7},... | collective-permute-start | bytes 36872 | tf_op jit(solution)/shard_map/ppermute | solution.py:26
  17.6 5.0 %collective-permute-start.2 = (bf16[8,1536]{1,0:T(8,128)(2,1)S(1)}, bf16[8,1536]{1,0:T(8,128)(2,1)S(1)}, u32[]{:S(2)}, u32[]{:S(2)}) collective-permute-start(bf16[8,1536]{1,0:T(8,128)(2,1)S(1)} %pad_maximum_fusion.1.refs_1_.refs_0_), channel_id=1, source_target_pairs={{0,2},{2,0},{4,6},{6,4},{8,10},{10,8},{12,14},{14,12},{1,3},{3,1},... | collective-permute-start | bytes 73736 | tf_op jit(solution)/shard_map/ppermute | solution.py:26
  20.2 2.4 %copy-start.1 = (s32[1,8]{1,0:T(1,128)S(1)}, s32[1,8]{1,0:T(1,128)}, u32[]{:S(2)}) copy-start(s32[1,8]{1,0:T(1,128)} %parents_ref.1) | copy-start | bytes 100
  22.6 33.3 %copy-start = (bf16[6144,1536]{1,0:T(8,128)(2,1)S(1)}, bf16[6144,1536]{1,0:T(8,128)(2,1)}, u32[]{:S(2)}) copy-start(bf16[6144,1536]{1,0:T(8,128)(2,1)} %refs_2_.1) | copy-start | bytes 56623108
  23.9 5.3 %collective-permute-start.3 = (bf16[16,1664]{1,0:T(8,128)(2,1)S(1)}, bf16[16,1664]{1,0:T(8,128)(2,1)S(1)}, u32[]{:S(2)}, u32[]{:S(2)}) collective-permute-start(bf16[16,1664]{1,0:T(8,128)(2,1)S(1)} %get-tuple-element.44), channel_id=1, source_target_pairs={{0,2},{2,0},{4,6},{6,4},{8,10},{10,8},{12,14},{14,12},{1,3},{3,1},... | collective-permute-start | bytes 159752 | tf_op jit(solution)/shard_map/ppermute | solution.py:26
  29.2 30.2 %slice-start = ((s8[18874368]{0:T(1024)(128)(4,1)}), s8[4194304]{0:T(1024)(128)(4,1)S(1)}, s32[]{:S(2)}) async-start(s8[18874368]{0:T(1024)(128)(4,1)} %bitcast.8), calls=%async_computation.1 | async-start | bytes 8388608
  29.5 5.6 %collective-permute-start.4 = (bf16[16,1664]{1,0:T(8,128)(2,1)S(1)}, bf16[16,1664]{1,0:T(8,128)(2,1)S(1)}, u32[]{:S(2)}, u32[]{:S(2)}) collective-permute-start(bf16[16,1664]{1,0:T(8,128)(2,1)S(1)} %get-tuple-element.47), channel_id=1, source_target_pairs={{0,4},{2,6},{4,0},{6,2},{8,12},{10,14},{12,8},{14,10},{1,5},{3,7},... | collective-permute-start | bytes 159752 | tf_op jit(solution)/shard_map/ppermute | solution.py:26
  35.4 6.7 %collective-permute-start.5 = (bf16[16,1664]{1,0:T(8,128)(2,1)S(1)}, bf16[16,1664]{1,0:T(8,128)(2,1)S(1)}, u32[]{:S(2)}, u32[]{:S(2)}) collective-permute-start(bf16[16,1664]{1,0:T(8,128)(2,1)S(1)} %get-tuple-element.50), channel_id=1, source_target_pairs={{0,8},{2,10},{4,12},{6,14},{8,0},{10,2},{12,4},{14,6},{1,9},{3,11}... | collective-permute-start | bytes 159752 | tf_op jit(solution)/shard_map/ppermute | solution.py:26
  42.1 17.3 %slice-start.1 = ((s8[18874368]{0:T(1024)(128)(4,1)}), s8[4194304]{0:T(1024)(128)(4,1)S(1)}, s32[]{:S(2)}) async-start(s8[18874368]{0:T(1024)(128)(4,1)} %bitcast.8), calls=%async_computation.2 | async-start | bytes 8388608
  42.9 16.5 %slice-start.2 = ((s8[18874368]{0:T(1024)(128)(4,1)}), s8[4194304]{0:T(1024)(128)(4,1)S(1)}, s32[]{:S(2)}) async-start(s8[18874368]{0:T(1024)(128)(4,1)} %bitcast.8), calls=%async_computation.3 | async-start | bytes 8388608
  42.9 1.3 %collective-permute-start.6 = (f32[8,768]{1,0:T(8,128)S(1)}, f32[8,768]{1,0:T(8,128)S(1)}, u32[]{:S(2)}, u32[]{:S(2)}) collective-permute-start(f32[8,768]{1,0:T(8,128)S(1)} %shard_map.126.refs_0_), channel_id=1, source_target_pairs={{0,1},{1,0},{2,3},{3,2},{4,5},{5,4},{6,7},{7,6},{8,9},{9,8},{10,11... | collective-permute-start | bytes 73736 | tf_op jit(solution)/shard_map/ppermute | solution.py:26
  44.2 4.5 %collective-permute-start.7 = (bf16[1,8,768]{2,1,0:T(8,128)(2,1)S(1)}, bf16[1,8,768]{2,1,0:T(8,128)(2,1)S(1)}, u32[]{:S(2)}, u32[]{:S(2)}) collective-permute-start(bf16[1,8,768]{2,1,0:T(8,128)(2,1)S(1)} %shard_map.127), channel_id=1, source_target_pairs={{0,9},{1,8},{2,11},{3,10},{4,13},{5,12},{6,15},{7,14},{8,1},{9,0},... | collective-permute-start | bytes 36872 | tf_op jit(solution)/shard_map/ppermute | solution.py:31
  48.7 3.6 %collective-permute-start.8 = (bf16[2,8,768]{2,1,0:T(8,128)(2,1)S(1)}, bf16[2,8,768]{2,1,0:T(8,128)(2,1)S(1)}, u32[]{:S(2)}, u32[]{:S(2)}) collective-permute-start(bf16[2,8,768]{2,1,0:T(8,128)(2,1)S(1)} %pad_maximum_fusion.2), channel_id=1, source_target_pairs={{0,5},{1,4},{2,7},{3,6},{4,1},{5,0},{6,3},{7,2},{8,13},{9,12},{10,... | collective-permute-start | bytes 73736 | tf_op jit(solution)/shard_map/ppermute | solution.py:31
  52.3 7.1 %slice-start.3 = ((s8[18874368]{0:T(1024)(128)(4,1)}), s8[4194304]{0:T(1024)(128)(4,1)S(1)}, s32[]{:S(2)}) async-start(s8[18874368]{0:T(1024)(128)(4,1)} %bitcast.8), calls=%async_computation.4 | async-start | bytes 8388608
  52.3 7.1 %slice-start.4 = ((s8[18874368]{0:T(1024)(128)(4,1)}), s8[2097152]{0:T(1024)(128)(4,1)S(1)}, s32[]{:S(2)}) async-start(s8[18874368]{0:T(1024)(128)(4,1)} %bitcast.8), calls=%async_computation.5 | async-start | bytes 4194304
  52.3 3.6 %collective-permute-start.9 = (bf16[4,8,768]{2,1,0:T(8,128)(2,1)S(1)}, bf16[4,8,768]{2,1,0:T(8,128)(2,1)S(1)}, u32[]{:S(2)}, u32[]{:S(2)}) collective-permute-start(bf16[4,8,768]{2,1,0:T(8,128)(2,1)S(1)} %pad_maximum_fusion.refs_0_), channel_id=1, source_target_pairs={{0,3},{1,2},{2,1},{3,0},{4,7},{5,6},{6,5},{7,4},{8,11},{9,10},{10,... | collective-permute-start | bytes 147464 | tf_op jit(solution)/shard_map/ppermute | solution.py:31
  58.9 2.0 %collective-permute-start.10 = (bf16[8,1536]{1,0:T(8,128)(2,1)S(1)}, bf16[8,1536]{1,0:T(8,128)(2,1)S(1)}, u32[]{:S(2)}, u32[]{:S(2)}) collective-permute-start(bf16[8,1536]{1,0:T(8,128)(2,1)S(1)} %get-tuple-element.54.refs_0_), channel_id=1, source_target_pairs={{0,1},{1,0},{2,3},{3,2},{4,5},{5,4},{6,7},{7,6},{8,9},{9,8},{10,11... | collective-permute-start | bytes 73736 | tf_op jit(solution)/shard_map/ppermute | solution.py:26
  62.3 4.1 %collective-permute-start.11 = (f32[4,3072]{1,0:T(4,128)S(1)}, f32[4,3072]{1,0:T(4,128)S(1)}, u32[]{:S(2)}, u32[]{:S(2)}) collective-permute-start(f32[4,3072]{1,0:T(4,128)S(1)} %get-tuple-element.56), channel_id=1, source_target_pairs={{0,2},{2,0},{4,6},{6,4},{8,10},{10,8},{12,14},{14,12},{1,3},{3,1},... | collective-permute-start | bytes 147464 | tf_op jit(solution)/shard_map/ppermute | solution.py:26
  66.5 3.9 %collective-permute-start.12 = (f32[2,3072]{1,0:T(2,128)S(1)}, f32[2,3072]{1,0:T(2,128)S(1)}, u32[]{:S(2)}, u32[]{:S(2)}) collective-permute-start(f32[2,3072]{1,0:T(2,128)S(1)} %slice.17), channel_id=1, source_target_pairs={{0,4},{2,6},{4,0},{6,2},{8,12},{10,14},{12,8},{14,10},{1,5},{3,7},... | collective-permute-start | bytes 73736 | tf_op jit(solution)/shard_map/ppermute | solution.py:26
  70.4 4.7 %collective-permute-start.13 = (f32[1,3072]{1,0:T(1,128)S(1)}, f32[1,3072]{1,0:T(1,128)S(1)}, u32[]{:S(2)}, u32[]{:S(2)}) collective-permute-start(f32[1,3072]{1,0:T(1,128)S(1)} %slice.19), channel_id=1, source_target_pairs={{0,8},{2,10},{4,12},{6,14},{8,0},{10,2},{12,4},{14,6},{1,9},{3,11}... | collective-permute-start | bytes 36872 | tf_op jit(solution)/shard_map/ppermute | solution.py:26
Sparse Core Ops, SparseCore 0:
  9.5 44.9 all-gather.1

commit v11 on v10

--- a/solution.py
+++ b/solution.py
@@ -302,39 +302,40 @@
     send_ref[...] = total[half:]
 
 
-def ring(devices):
-    if devices > BEAMS:
-        return list(range(BEAMS))
-    return list(range(0, BEAMS, 2)) + list(range(BEAMS - 1, 0, -2))
-
-
-def place_kernel(stride, order, gathered_ref, new_ref, parents_ref, lengths_ref, out_ref, row, sem):
-    position = lax.axis_index("batch")
-    request = lax.rem(position, stride)
+def pick(wanted, near, refs, use):
+    apart = jnp.bitwise_xor(wanted, near)
+    found = jnp.int32(0)
+    for k, offset in enumerate((0, 4, 1, 5)):
+        found = jnp.where(apart == offset, k, found)
+    for k, ref in enumerate(refs):
+        pl.when(found == k)(functools.partial(use, ref))
+
+
+def select_kernel(stride, own_ref, far_ref, side_ref, both_ref, parents_ref, out_ref):
+    position = lax.axis_index("batch")
+    wanted = parents_ref[0, jnp.bitwise_xor(position, 2 * stride)]
+
+    def use(ref):
+        out_ref[...] = ref[...]
+
+    pick(wanted, position // stride, (own_ref, far_ref, side_ref, both_ref), use)
+
+
+def place_kernel(stride, own_ref, far_ref, side_ref, both_ref, sent_ref, new_ref, parents_ref, lengths_ref, out_ref):
+    position = lax.axis_index("batch")
+    beam, request = position // stride, lax.rem(position, stride)
     parent = parents_ref[0, position]
-    place = jnp.int32(0)
-    for k, beam in enumerate(order):
-        place = jnp.where(parent == beam, k, place)
-    place = jnp.where(lax.axis_index("tensor") == 1, BEAMS - 1 - place, place)
-    copy = pltpu.make_async_copy(gathered_ref.at[place], row, sem)
-    copy.start()
-    slots = lax.broadcasted_iota(jnp.int32, row.shape[1:], 0)
-    copy.wait()
-    for kind in range(2):
-        old = row[kind].astype(jnp.float32)
-        new = new_ref[kind : kind + 1, :].astype(jnp.float32)
-        out_ref[kind] = jnp.where(slots == lengths_ref[request], new, old).astype(jnp.bfloat16)
-
-
-def place(stride, order, gathered, new_kv, parents, lengths):
-    return pl.pallas_call(
-        functools.partial(place_kernel, stride, order),
-        out_shape=jax.ShapeDtypeStruct(gathered.shape[1:], gathered.dtype),
-        in_specs=[ANY, VM, SM, SM],
-        out_specs=VM,
-        scratch_shapes=[pltpu.VMEM(gathered.shape[1:], gathered.dtype), pltpu.SemaphoreType.DMA],
-        compiler_params=pltpu.CompilerParams(vmem_limit_bytes=8 * MIB),
-    )(in_hbm(gathered), new_kv, parents, lengths)
+    slots = lax.broadcasted_iota(jnp.int32, out_ref.shape[1:], 0)
+
+    def use(ref):
+        for kind in range(2):
+            old = ref[kind].astype(jnp.float32)
+            new = new_ref[kind : kind + 1, :].astype(jnp.float32)
+            out_ref[kind] = jnp.where(slots == lengths_ref[request], new, old).astype(jnp.bfloat16)
+
+    held = (jnp.bitwise_xor(parent, beam) // 2) % 2 == 0
+    pl.when(held)(lambda: pick(parent, beam, (own_ref, far_ref, side_ref, both_ref), use))
+    pl.when(jnp.logical_not(held))(lambda: use(sent_ref))
 
 
 def body(
@@ -365,6 +366,8 @@
     sources = (queries[0, 0], init_cache[0], memory[0], new_kv[0, 0], residual)
     bit = devices // 2
     other = xor_permute(queries[0, 0], "batch", bit)
+    far_row = xor_permute(init_cache[0], "batch", 4 * stride)
+    side_row = xor_permute(init_cache[0], "batch", stride)
     loaded = fetch([in_hbm(x) for x in sources], queries[0, 0])
     other, (query, cache_row, memory_row, new_row, residual_row) = pin(other, loaded)
     query, far = doubling(jnp.concatenate([query, other]), stride, bit)
@@ -385,7 +388,7 @@
         parents,
         lengths,
         specs=[VM] * 5 + [SM] * 2,
-        hold=(),
+        hold=(side_row,),
     )
     bit = stride
     while True:
@@ -393,7 +396,9 @@
         bit *= 2
         if bit == devices:
             break
-        num, state, pay = call(merge_kernel, state_shapes, num, state, arrived, hold=())
+        num, state, pay = call(merge_kernel, state_shapes, num, state, arrived)
+        if bit == 2 * stride:
+            both_row = xor_permute(pin(far_row, num)[0], "batch", stride)
     if stride == 1:
         partial = finish_project(num, state, arrived, out_row)
     else:
@@ -404,6 +409,15 @@
         attended = stacked.transpose(1, 2, 0, 3).reshape(2 * rows, width)
         partial = call(project_kernel, shape((rows, columns), f32), attended, out_row)
     other = xor_permute(partial, "tensor", 1)
+    rows_held = (cache_row, far_row, side_row, pin(both_row, partial)[0])
+    sent_row = call(
+        functools.partial(select_kernel, stride),
+        shape(cache_row.shape, bf16),
+        *rows_held,
+        parents,
+        specs=[VM] * 4 + [SM],
+    )
+    sent_row = xor_permute(sent_row, "batch", 2 * stride)
     mine = call(add_kernel, pltpu.VMEM((1, rows, columns), bf16), partial, other, residual_row, hold=())
     near, far = doubling(mine, 1, devices, cross=True)
     hidden, activation = call(
@@ -425,18 +439,21 @@
         down_weight,
         before,
     )
-    order = ring(devices)
-    groups = []
-    for r in range(stride):
-        groups.append([(beam * stride + r) * 2 for beam in order])
-        groups.append([(beam * stride + r) * 2 + 1 for beam in reversed(order)])
-    gathered = lax.all_gather(init_cache[0], ("batch", "tensor"), axis_index_groups=groups)
     bit = 1
     while True:
         arrived = xor_permute(send, "batch", bit)
         bit *= 2
         if 2 * bit == devices:
-            cache = place(stride, order, gathered, new_row, parents, lengths)
+            cache = call(
+                functools.partial(place_kernel, stride),
+                shape(cache_row.shape, bf16),
+                *rows_held,
+                sent_row,
+                new_row,
+                parents,
+                lengths,
+                specs=[VM] * 6 + [SM] * 2,
+            )
             arrived, cache = pin(arrived, cache)
         total = keep + arrived
         if bit == devices:

time: 82.7 us -> 71.2 us (0.86)
  between operations: 14.9 us -> 1.47 us
  starting transfers between devices: 19.4 us -> 21.6 us
    ppermute x11 -> x15, starting transfers between devices: 16.4 us -> 20.4 us  [xor_permute(): return lax.ppermute(value, axis, [(i, i ^ bit) for i in range(total)])]
    pallas_call x1 -> x0, Pallas kernels: 2.38 us -> none  [place(): pl.pallas_call(functools.partial(place_kernel, stride, order), out_shape=...]
    pallas_call x7 -> x9, Pallas kernels: 7.75 us -> 9.76 us  [call(): pl.pallas_call(functools.partial(drop, kernel, first, len(hold)), out_sha...]
    ppermute x11 -> x15, waiting for transfers between devices: 23.4 us -> 25.3 us  [xor_permute(): return lax.ppermute(value, axis, [(i, i ^ bit) for i in range(total)])]
    ppermute x3, starting transfers between devices: 2.97 us -> 1.22 us  [cross_permute(): return lax.ppermute(value, ('batch', 'tensor'), pairs)]
    ppermute x3, waiting for transfers between devices: 8.67 us -> 6.92 us  [cross_permute(): return lax.ppermute(value, ('batch', 'tensor'), pairs)]
  transfers between devices with their start and end apart: 15 -> 18, of which waited for: 12 -> 11; matrix products, arithmetic and copies ran while one was open for 0% -> 0% of each run, Pallas kernels for 18% -> 20%
where the time goes in v11:
time: 71.2 us; the launch traced here: 71 us
  waiting for transfers between devices  32.2 us (45%)
  starting transfers between devices  21.6 us (30%)
  Pallas kernels  14.3 us (20%)
  between operations  1.47 us (2%)
  local copies, waits for them, and re-layouts  0.72 us (1%)
    ppermute x15, waiting for transfers between devices, xor_permute(): return lax.ppermute(value, axis, [(i, i ^ bit) for i in range(total)])  25.3 us
    ppermute x15, starting transfers between devices, xor_permute(): return lax.ppermute(value, axis, [(i, i ^ bit) for i in range(total)])  20.4 us
    pallas_call x9, Pallas kernels, call(): pl.pallas_call(functools.partial(drop, kernel, first, len(hold)), out_sha...  9.76 us
    ppermute x3, waiting for transfers between devices, cross_permute(): return lax.ppermute(value, ('batch', 'tensor'), pairs)  6.92 us
    pallas_call x2, Pallas kernels, fetch(): pl.pallas_call(functools.partial(fetch_kernel, count), out_shape=[pltpu.V...  3.71 us
  transfers between devices with their start and end apart: 18, of which 11 were waited for; matrix products, arithmetic and copies ran while one was open for 0% of the time, Pallas kernels for 20%

profile of v11, /device:TPU:0, one launch (start us, length us, event | category | flops | bytes accessed | tf_op | source)
XLA Modules:
  0.0 71.0 jit_solution(12095776753690245807)
XLA Ops:
  0.6 4.1 %collective-permute-start = (bf16[2,1536]{1,0:T(2,128)(2,1)}, bf16[2,1536]{1,0:T(2,128)(2,1)S(1)}, u32[]{:S(2)}, u32[]{:S(2)}) collective-permute-start(bf16[2,1536]{1,0:T(2,128)(2,1)} %bitcast.14), channel_id=1, source_target_pairs={{0,8},{2,10},{4,12},{6,14},{8,0},{10,2},{12,4},{14,6},{1,9},{3,11}... | collective-permute-start | bytes 18440 | tf_op jit(solution)/shard_map/ppermute | solution.py:26
  4.7 1.5 %collective-permute-start.3 = (bf16[2,64,1536]{2,1,0:T(8,128)(2,1)}, bf16[2,64,1536]{2,1,0:T(8,128)(2,1)S(1)}, u32[]{:S(2)}, u32[]{:S(2)}) collective-permute-start(bf16[2,64,1536]{2,1,0:T(8,128)(2,1)} %bitcast.11), channel_id=1, source_target_pairs={{0,2},{2,0},{4,6},{6,4},{8,10},{10,8},{12,14},{14,12},{1,3},{3,1},... | collective-permute-start | bytes 1179656 | tf_op jit(solution)/shard_map/ppermute | solution.py:26
  6.2 1.3 %shard_map.121 = (bf16[2,1536]{1,0:T(2,128)(2,1)S(1)}, bf16[2,64,1536]{2,1,0:T(8,128)(2,1)S(1)}, bf16[2,64,1536]{2,1,0:T(8,128)(2,1)S(1)}, bf16[2,1536]{1,0:T(2,128)(2,1)S(1)}, bf16[1,8,768]{2,1,0:T(8,128)(2,1)S(1)}) custom-call(bf16[2,1536]{1,0:T(2,128)(2,1)} %bitcast.15, bf16[2,64,1536]{2,1,0:T(8,128)(2,1)} %bitcast.12, bf16[2,64,1536]{2,1,0:T(8,128)(2,1)} %bitcast.10, ...), custom_call_target="tpu_custom_call" | custom-call | bytes 2097152 | tf_op jit(solution)/shard_map/pallas_call | solution.py:94
  7.6 2.4 %collective-permute-start.1 = (bf16[4,1536]{1,0:T(4,128)(2,1)S(1)}, bf16[4,1536]{1,0:T(4,128)(2,1)S(1)}, u32[]{:S(2)}, u32[]{:S(2)}) collective-permute-start(bf16[4,1536]{1,0:T(4,128)(2,1)S(1)} %pad_maximum_fusion.3), channel_id=1, source_target_pairs={{0,4},{2,6},{4,0},{6,2},{8,12},{10,14},{12,8},{14,10},{1,5},{3,7},... | collective-permute-start | bytes 36872 | tf_op jit(solution)/shard_map/ppermute | solution.py:26
  10.0 1.7 %collective-permute-done.1 = bf16[4,1536]{1,0:T(4,128)(2,1)S(1)} collective-permute-done((bf16[4,1536]{1,0:T(4,128)(2,1)S(1)}, bf16[4,1536]{1,0:T(4,128)(2,1)S(1)}, u32[]{:S(2)}, u32[]{:S(2)}) %collective-permute-start.1) | collective-permute-done | bytes 12320 | tf_op jit(solution)/shard_map/ppermute | solution.py:26
  11.7 1.0 %collective-permute-start.2 = (bf16[8,1536]{1,0:T(8,128)(2,1)S(1)}, bf16[8,1536]{1,0:T(8,128)(2,1)S(1)}, u32[]{:S(2)}, u32[]{:S(2)}) collective-permute-start(bf16[8,1536]{1,0:T(8,128)(2,1)S(1)} %pad_maximum_fusion.1.refs_1_.refs_0_), channel_id=1, source_target_pairs={{0,2},{2,0},{4,6},{6,4},{8,10},{10,8},{12,14},{14,12},{1,3},{3,1},... | collective-permute-start | bytes 73736 | tf_op jit(solution)/shard_map/ppermute | solution.py:26
  12.7 2.1 %collective-permute-start.14 = (bf16[2,64,1536]{2,1,0:T(8,128)(2,1)}, bf16[2,64,1536]{2,1,0:T(8,128)(2,1)S(1)}, u32[]{:S(2)}, u32[]{:S(2)}) collective-permute-start(bf16[2,64,1536]{2,1,0:T(8,128)(2,1)} %bitcast.13), channel_id=1, source_target_pairs={{0,8},{2,10},{4,12},{6,14},{8,0},{10,2},{12,4},{14,6},{1,9},{3,11}... | collective-permute-start | bytes 1179656 | tf_op jit(solution)/shard_map/ppermute | solution.py:26
  15.5 2.4 %shard_map.122.weight_ref = bf16[2,1536,768]{2,1,0:T(8,128)(2,1)S(1)} custom-call(bf16[2,1536,768]{2,1,0:T(8,128)(2,1)} %refs_0_.1, bf16[8,1536]{1,0:T(8,128)(2,1)S(1)} %pad_maximum_fusion.1.refs_1_.refs_0_), custom_call_target="tpu_custom_call" | custom-call | bytes 2097152 | tf_op jit(solution)/shard_map/pallas_call | solution.py:94
  17.9 0.6 copy-done.1
  18.6 1.3 %shard_map.123 = (f32[16,1536]{1,0:T(8,128)S(1)}, f32[16,256]{1,0:T(8,128)S(1)}, bf16[16,1664]{1,0:T(8,128)(2,1)S(1)}) custom-call(bf16[8,1536]{1,0:T(8,128)(2,1)S(1)} %pad_maximum_fusion.1.refs_1_.refs_0_, bf16[8,1536]{1,0:T(8,128)(2,1)S(1)} %collective-permute-done.2.refs_1_, bf16[2,64,1536]{2,1,0:T(8,128)(2,1)S(1)} %get-tuple-element.41.refs_2_.refs_0_, ...), custom_call_target="tpu_custom_call" | custom-call | flops 1000000000 | tf_op jit(solution)/shard_map/pallas_call | solution.py:55
  19.9 0.6 collective-permute-start.4
  20.5 3.6 %collective-permute-done.4.refs_2_ = bf16[16,1664]{1,0:T(8,128)(2,1)S(1)} collective-permute-done((bf16[16,1664]{1,0:T(8,128)(2,1)S(1)}, bf16[16,1664]{1,0:T(8,128)(2,1)S(1)}, u32[]{:S(2)}, u32[]{:S(2)}) %collective-permute-start.4) | collective-permute-done | bytes 53280 | tf_op jit(solution)/shard_map/ppermute | solution.py:26
  24.4 1.6 %collective-permute-start.5 = (bf16[16,1664]{1,0:T(8,128)(2,1)S(1)}, bf16[16,1664]{1,0:T(8,128)(2,1)S(1)}, u32[]{:S(2)}, u32[]{:S(2)}) collective-permute-start(bf16[16,1664]{1,0:T(8,128)(2,1)S(1)} %get-tuple-element.49), channel_id=1, source_target_pairs={{0,4},{2,6},{4,0},{6,2},{8,12},{10,14},{12,8},{14,10},{1,5},{3,7},... | collective-permute-start | bytes 159752 | tf_op jit(solution)/shard_map/ppermute | solution.py:26
  26.0 6.0 %collective-permute-done.5.refs_2_ = bf16[16,1664]{1,0:T(8,128)(2,1)S(1)} collective-permute-done((bf16[16,1664]{1,0:T(8,128)(2,1)S(1)}, bf16[16,1664]{1,0:T(8,128)(2,1)S(1)}, u32[]{:S(2)}, u32[]{:S(2)}) %collective-permute-start.5) | collective-permute-done | bytes 53280 | tf_op jit(solution)/shard_map/ppermute | solution.py:26
  32.3 1.1 %collective-permute-start.6 = (bf16[16,1664]{1,0:T(8,128)(2,1)S(1)}, bf16[16,1664]{1,0:T(8,128)(2,1)S(1)}, u32[]{:S(2)}, u32[]{:S(2)}) collective-permute-start(bf16[16,1664]{1,0:T(8,128)(2,1)S(1)} %get-tuple-element.52), channel_id=1, source_target_pairs={{0,8},{2,10},{4,12},{6,14},{8,0},{10,2},{12,4},{14,6},{1,9},{3,11}... | collective-permute-start | bytes 159752 | tf_op jit(solution)/shard_map/ppermute | solution.py:26
  34.0 4.0 %collective-permute-done.6.pay_ref = bf16[16,1664]{1,0:T(8,128)(2,1)S(1)} collective-permute-done((bf16[16,1664]{1,0:T(8,128)(2,1)S(1)}, bf16[16,1664]{1,0:T(8,128)(2,1)S(1)}, u32[]{:S(2)}, u32[]{:S(2)}) %collective-permute-start.6) | collective-permute-done | bytes 53280 | tf_op jit(solution)/shard_map/ppermute | solution.py:26
  38.0 0.8 %shard_map.126.refs_0_ = f32[8,768]{1,0:T(8,128)S(1)} custom-call(f32[16,1536]{1,0:T(8,128)S(1)} %get-tuple-element.50.num_ref, f32[16,256]{1,0:T(8,128)S(1)} %get-tuple-element.51.state_ref, bf16[16,1664]{1,0:T(8,128)(2,1)S(1)} %collective-permute-done.6.pay_ref, bf16[2,1536,768]{2,1,0:T(8,128)(2,1)S(1)} %shard_map.122.weight_ref), custom_call_target="tpu_custom_call" | custom-call | flops 2000000000 | tf_op jit(solution)/shard_map/pallas_call | solution.py:251
  38.9 1.2 %collective-permute-done.7.refs_1_ = f32[8,768]{1,0:T(8,128)S(1)} collective-permute-done((f32[8,768]{1,0:T(8,128)S(1)}, f32[8,768]{1,0:T(8,128)S(1)}, u32[]{:S(2)}, u32[]{:S(2)}) %collective-permute-start.7) | collective-permute-done | bytes 24608 | tf_op jit(solution)/shard_map/ppermute | solution.py:26
  40.5 3.8 %collective-permute-done.8 = bf16[1,8,768]{2,1,0:T(8,128)(2,1)S(1)} collective-permute-done((bf16[1,8,768]{2,1,0:T(8,128)(2,1)S(1)}, bf16[1,8,768]{2,1,0:T(8,128)(2,1)S(1)}, u32[]{:S(2)}, u32[]{:S(2)}) %collective-permute-start.8) | collective-permute-done | bytes 12320 | tf_op jit(solution)/shard_map/ppermute | solution.py:31
  45.0 2.4 %collective-permute-start.16 = (bf16[2,64,1536]{2,1,0:T(8,128)(2,1)S(1)}, bf16[2,64,1536]{2,1,0:T(8,128)(2,1)S(1)}, u32[]{:S(2)}, u32[]{:S(2)}) collective-permute-start(bf16[2,64,1536]{2,1,0:T(8,128)(2,1)S(1)} %shard_map.131), channel_id=1, source_target_pairs={{0,4},{2,6},{4,0},{6,2},{8,12},{10,14},{12,8},{14,10},{1,5},{3,7},... | collective-permute-start | bytes 1179656 | tf_op jit(solution)/shard_map/ppermute | solution.py:26
  47.5 0.7 collective-permute-start.10
  48.2 3.1 %collective-permute-done.10.refs_1_ = bf16[4,8,768]{2,1,0:T(8,128)(2,1)S(1)} collective-permute-done((bf16[4,8,768]{2,1,0:T(8,128)(2,1)S(1)}, bf16[4,8,768]{2,1,0:T(8,128)(2,1)S(1)}, u32[]{:S(2)}, u32[]{:S(2)}) %collective-permute-start.10) | collective-permute-done | bytes 49184 | tf_op jit(solution)/shard_map/ppermute | solution.py:31
  51.3 3.0 %shard_map.128 = (bf16[8,768]{1,0:T(8,128)(2,1)}, bf16[8,1536]{1,0:T(8,128)(2,1)S(1)}) custom-call(bf16[4,8,768]{2,1,0:T(8,128)(2,1)S(1)} %pad_maximum_fusion.refs_0_, bf16[4,8,768]{2,1,0:T(8,128)(2,1)S(1)} %collective-permute-done.10.refs_1_, bf16[6144,1536]{1,0:T(8,128)(2,1)S(1)} %copy-done), custom_call_target="tpu_custom_call" | custom-call | flops 1000000000 | tf_op jit(solution)/shard_map/pallas_call | solution.py:55
  54.8 1.4 %shard_map.129.refs_2_ = f32[8,3072]{1,0:T(8,128)S(1)} custom-call(bf16[8,1536]{1,0:T(8,128)(2,1)S(1)} %get-tuple-element.56.refs_0_, bf16[3072,3072]{1,0:T(8,128)(2,1)S(1)} %bitcast.9), custom_call_target="tpu_custom_call" | custom-call | flops 1000000000 | tf_op jit(solution)/shard_map/pallas_call | solution.py:55
  56.2 1.4 %shard_map.130 = (f32[4,3072]{1,0:T(4,128)S(1)}, f32[4,3072]{1,0:T(4,128)S(1)}) custom-call(bf16[8,1536]{1,0:T(8,128)(2,1)S(1)} %collective-permute-done.11.refs_0_, bf16[3072,3072]{1,0:T(8,128)(2,1)S(1)} %bitcast.9, f32[8,3072]{1,0:T(8,128)S(1)} %shard_map.129.refs_2_), custom_call_target="tpu_custom_call" | custom-call | flops 1000000000 | tf_op jit(solution)/shard_map/pallas_call | solution.py:55
  57.6 0.9 %collective-permute-start.12 = (f32[4,3072]{1,0:T(4,128)S(1)}, f32[4,3072]{1,0:T(4,128)S(1)}, u32[]{:S(2)}, u32[]{:S(2)}) collective-permute-start(f32[4,3072]{1,0:T(4,128)S(1)} %get-tuple-element.58), channel_id=1, source_target_pairs={{0,2},{2,0},{4,6},{6,4},{8,10},{10,8},{12,14},{14,12},{1,3},{3,1},... | collective-permute-start | bytes 147464 | tf_op jit(solution)/shard_map/ppermute | solution.py:26
  58.6 3.2 %collective-permute-done.12 = f32[4,3072]{1,0:T(4,128)S(1)} collective-permute-done((f32[4,3072]{1,0:T(4,128)S(1)}, f32[4,3072]{1,0:T(4,128)S(1)}, u32[]{:S(2)}, u32[]{:S(2)}) %collective-permute-start.12) | collective-permute-done | bytes 49184 | tf_op jit(solution)/shard_map/ppermute | solution.py:26
  62.1 1.4 %shard_map.132 = bf16[2,64,1536]{2,1,0:T(8,128)(2,1)} custom-call(bf16[2,64,1536]{2,1,0:T(8,128)(2,1)S(1)} %get-tuple-element.41.refs_2_.refs_0_, bf16[2,64,1536]{2,1,0:T(8,128)(2,1)S(1)} %collective-permute-done.14.refs_1_, bf16[2,64,1536]{2,1,0:T(8,128)(2,1)S(1)} %collective-permute-done.3.refs_7_.refs_2_, ...), custom_call_target="tpu_custom_call" | custom-call | flops 1000000000 | tf_op jit(solution)/shard_map/pallas_call | solution.py:55
  63.5 2.2 %collective-permute-done.13 = f32[2,3072]{1,0:T(2,128)S(1)} collective-permute-done((f32[2,3072]{1,0:T(2,128)S(1)}, f32[2,3072]{1,0:T(2,128)S(1)}, u32[]{:S(2)}, u32[]{:S(2)}) %collective-permute-start.13) | collective-permute-done | bytes 24608 | tf_op jit(solution)/shard_map/ppermute | solution.py:26
  65.7 1.2 %collective-permute-start.17 = (f32[1,3072]{1,0:T(1,128)S(1)}, f32[1,3072]{1,0:T(1,128)S(1)}, u32[]{:S(2)}, u32[]{:S(2)}) collective-permute-start(f32[1,3072]{1,0:T(1,128)S(1)} %slice.19), channel_id=1, source_target_pairs={{0,8},{2,10},{4,12},{6,14},{8,0},{10,2},{12,4},{14,6},{1,9},{3,11}... | collective-permute-start | bytes 36872 | tf_op jit(solution)/shard_map/ppermute | solution.py:26
  66.9 3.5 %collective-permute-done.17 = f32[1,3072]{1,0:T(1,128)S(1)} collective-permute-done((f32[1,3072]{1,0:T(1,128)S(1)}, f32[1,3072]{1,0:T(1,128)S(1)}, u32[]{:S(2)}, u32[]{:S(2)}) %collective-permute-start.17) | collective-permute-done | bytes 12320 | tf_op jit(solution)/shard_map/ppermute | solution.py:26
  70.4 0.6 fusion.1
  (42 shorter events, 3.4 us)
Async XLA Ops:
  0.6 50.6 %copy-start = (bf16[6144,1536]{1,0:T(8,128)(2,1)S(1)}, bf16[6144,1536]{1,0:T(8,128)(2,1)}, u32[]{:S(2)}) copy-start(bf16[6144,1536]{1,0:T(8,128)(2,1)} %refs_2_.1) | copy-start | bytes 56623108
  0.6 6.9 %collective-permute-start = (bf16[2,1536]{1,0:T(2,128)(2,1)}, bf16[2,1536]{1,0:T(2,128)(2,1)S(1)}, u32[]{:S(2)}, u32[]{:S(2)}) collective-permute-start(bf16[2,1536]{1,0:T(2,128)(2,1)} %bitcast.14), channel_id=1, source_target_pairs={{0,8},{2,10},{4,12},{6,14},{8,0},{10,2},{12,4},{14,6},{1,9},{3,11}... | collective-permute-start | bytes 18440 | tf_op jit(solution)/shard_map/ppermute | solution.py:26
  4.7 13.2 %collective-permute-start.3 = (bf16[2,64,1536]{2,1,0:T(8,128)(2,1)}, bf16[2,64,1536]{2,1,0:T(8,128)(2,1)S(1)}, u32[]{:S(2)}, u32[]{:S(2)}) collective-permute-start(bf16[2,64,1536]{2,1,0:T(8,128)(2,1)} %bitcast.11), channel_id=1, source_target_pairs={{0,2},{2,0},{4,6},{6,4},{8,10},{10,8},{12,14},{14,12},{1,3},{3,1},... | collective-permute-start | bytes 1179656 | tf_op jit(solution)/shard_map/ppermute | solution.py:26
  7.6 4.1 %collective-permute-start.1 = (bf16[4,1536]{1,0:T(4,128)(2,1)S(1)}, bf16[4,1536]{1,0:T(4,128)(2,1)S(1)}, u32[]{:S(2)}, u32[]{:S(2)}) collective-permute-start(bf16[4,1536]{1,0:T(4,128)(2,1)S(1)} %pad_maximum_fusion.3), channel_id=1, source_target_pairs={{0,4},{2,6},{4,0},{6,2},{8,12},{10,14},{12,8},{14,10},{1,5},{3,7},... | collective-permute-start | bytes 36872 | tf_op jit(solution)/shard_map/ppermute | solution.py:26
  11.7 6.2 %collective-permute-start.2 = (bf16[8,1536]{1,0:T(8,128)(2,1)S(1)}, bf16[8,1536]{1,0:T(8,128)(2,1)S(1)}, u32[]{:S(2)}, u32[]{:S(2)}) collective-permute-start(bf16[8,1536]{1,0:T(8,128)(2,1)S(1)} %pad_maximum_fusion.1.refs_1_.refs_0_), channel_id=1, source_target_pairs={{0,2},{2,0},{4,6},{6,4},{8,10},{10,8},{12,14},{14,12},{1,3},{3,1},... | collective-permute-start | bytes 73736 | tf_op jit(solution)/shard_map/ppermute | solution.py:26
  12.7 20.7 %collective-permute-start.14 = (bf16[2,64,1536]{2,1,0:T(8,128)(2,1)}, bf16[2,64,1536]{2,1,0:T(8,128)(2,1)S(1)}, u32[]{:S(2)}, u32[]{:S(2)}) collective-permute-start(bf16[2,64,1536]{2,1,0:T(8,128)(2,1)} %bitcast.13), channel_id=1, source_target_pairs={{0,8},{2,10},{4,12},{6,14},{8,0},{10,2},{12,4},{14,6},{1,9},{3,11}... | collective-permute-start | bytes 1179656 | tf_op jit(solution)/shard_map/ppermute | solution.py:26
  17.9 0.7 copy-start.1
  19.9 4.2 %collective-permute-start.4 = (bf16[16,1664]{1,0:T(8,128)(2,1)S(1)}, bf16[16,1664]{1,0:T(8,128)(2,1)S(1)}, u32[]{:S(2)}, u32[]{:S(2)}) collective-permute-start(bf16[16,1664]{1,0:T(8,128)(2,1)S(1)} %get-tuple-element.46), channel_id=1, source_target_pairs={{0,2},{2,0},{4,6},{6,4},{8,10},{10,8},{12,14},{14,12},{1,3},{3,1},... | collective-permute-start | bytes 159752 | tf_op jit(solution)/shard_map/ppermute | solution.py:26
  24.4 30.4 %slice-start = ((s8[18874368]{0:T(1024)(128)(4,1)}), s8[4194304]{0:T(1024)(128)(4,1)S(1)}, s32[]{:S(2)}) async-start(s8[18874368]{0:T(1024)(128)(4,1)} %bitcast.8), calls=%async_computation | async-start | bytes 8388608
  24.4 7.6 %collective-permute-start.5 = (bf16[16,1664]{1,0:T(8,128)(2,1)S(1)}, bf16[16,1664]{1,0:T(8,128)(2,1)S(1)}, u32[]{:S(2)}, u32[]{:S(2)}) collective-permute-start(bf16[16,1664]{1,0:T(8,128)(2,1)S(1)} %get-tuple-element.49), channel_id=1, source_target_pairs={{0,4},{2,6},{4,0},{6,2},{8,12},{10,14},{12,8},{14,10},{1,5},{3,7},... | collective-permute-start | bytes 159752 | tf_op jit(solution)/shard_map/ppermute | solution.py:26
  32.3 5.7 %collective-permute-start.6 = (bf16[16,1664]{1,0:T(8,128)(2,1)S(1)}, bf16[16,1664]{1,0:T(8,128)(2,1)S(1)}, u32[]{:S(2)}, u32[]{:S(2)}) collective-permute-start(bf16[16,1664]{1,0:T(8,128)(2,1)S(1)} %get-tuple-element.52), channel_id=1, source_target_pairs={{0,8},{2,10},{4,12},{6,14},{8,0},{10,2},{12,4},{14,6},{1,9},{3,11}... | collective-permute-start | bytes 159752 | tf_op jit(solution)/shard_map/ppermute | solution.py:26
  33.4 11.0 %collective-permute-start.15 = (bf16[2,64,1536]{2,1,0:T(8,128)(2,1)S(1)}, bf16[2,64,1536]{2,1,0:T(8,128)(2,1)S(1)}, u32[]{:S(2)}, u32[]{:S(2)}) collective-permute-start(bf16[2,64,1536]{2,1,0:T(8,128)(2,1)S(1)} %collective-permute-done.14.refs_1_), channel_id=1, source_target_pairs={{0,2},{2,0},{4,6},{6,4},{8,10},{10,8},{12,14},{14,12},{1,3},{3,1},... | collective-permute-start | bytes 1179656 | tf_op jit(solution)/shard_map/ppermute | solution.py:26
  38.0 16.8 %slice-start.1 = ((s8[18874368]{0:T(1024)(128)(4,1)}), s8[4194304]{0:T(1024)(128)(4,1)S(1)}, s32[]{:S(2)}) async-start(s8[18874368]{0:T(1024)(128)(4,1)} %bitcast.8), calls=%async_computation.1 | async-start | bytes 8388608
  38.8 1.3 %collective-permute-start.7 = (f32[8,768]{1,0:T(8,128)S(1)}, f32[8,768]{1,0:T(8,128)S(1)}, u32[]{:S(2)}, u32[]{:S(2)}) collective-permute-start(f32[8,768]{1,0:T(8,128)S(1)} %shard_map.126.refs_0_), channel_id=1, source_target_pairs={{0,1},{1,0},{2,3},{3,2},{4,5},{5,4},{6,7},{7,6},{8,9},{9,8},{10,11... | collective-permute-start | bytes 73736 | tf_op jit(solution)/shard_map/ppermute | solution.py:26
  40.1 4.1 %collective-permute-start.8 = (bf16[1,8,768]{2,1,0:T(8,128)(2,1)S(1)}, bf16[1,8,768]{2,1,0:T(8,128)(2,1)S(1)}, u32[]{:S(2)}, u32[]{:S(2)}) collective-permute-start(bf16[1,8,768]{2,1,0:T(8,128)(2,1)S(1)} %shard_map.127), channel_id=1, source_target_pairs={{0,9},{1,8},{2,11},{3,10},{4,13},{5,12},{6,15},{7,14},{8,1},{9,0},... | collective-permute-start | bytes 36872 | tf_op jit(solution)/shard_map/ppermute | solution.py:31
  44.2 10.5 %slice-start.2 = ((s8[18874368]{0:T(1024)(128)(4,1)}), s8[4194304]{0:T(1024)(128)(4,1)S(1)}, s32[]{:S(2)}) async-start(s8[18874368]{0:T(1024)(128)(4,1)} %bitcast.8), calls=%async_computation.2 | async-start | bytes 8388608
  44.2 3.3 %collective-permute-start.9 = (bf16[2,8,768]{2,1,0:T(8,128)(2,1)S(1)}, bf16[2,8,768]{2,1,0:T(8,128)(2,1)S(1)}, u32[]{:S(2)}, u32[]{:S(2)}) collective-permute-start(bf16[2,8,768]{2,1,0:T(8,128)(2,1)S(1)} %pad_maximum_fusion.2), channel_id=1, source_target_pairs={{0,5},{1,4},{2,7},{3,6},{4,1},{5,0},{6,3},{7,2},{8,13},{9,12},{10,... | collective-permute-start | bytes 73736 | tf_op jit(solution)/shard_map/ppermute | solution.py:31
  45.0 17.1 %collective-permute-start.16 = (bf16[2,64,1536]{2,1,0:T(8,128)(2,1)S(1)}, bf16[2,64,1536]{2,1,0:T(8,128)(2,1)S(1)}, u32[]{:S(2)}, u32[]{:S(2)}) collective-permute-start(bf16[2,64,1536]{2,1,0:T(8,128)(2,1)S(1)} %shard_map.131), channel_id=1, source_target_pairs={{0,4},{2,6},{4,0},{6,2},{8,12},{10,14},{12,8},{14,10},{1,5},{3,7},... | collective-permute-start | bytes 1179656 | tf_op jit(solution)/shard_map/ppermute | solution.py:26
  47.5 7.3 %slice-start.3 = ((s8[18874368]{0:T(1024)(128)(4,1)}), s8[4194304]{0:T(1024)(128)(4,1)S(1)}, s32[]{:S(2)}) async-start(s8[18874368]{0:T(1024)(128)(4,1)} %bitcast.8), calls=%async_computation.3 | async-start | bytes 8388608
  47.5 7.3 %slice-start.4 = ((s8[18874368]{0:T(1024)(128)(4,1)}), s8[2097152]{0:T(1024)(128)(4,1)S(1)}, s32[]{:S(2)}) async-start(s8[18874368]{0:T(1024)(128)(4,1)} %bitcast.8), calls=%async_computation.4 | async-start | bytes 4194304
  47.5 3.8 %collective-permute-start.10 = (bf16[4,8,768]{2,1,0:T(8,128)(2,1)S(1)}, bf16[4,8,768]{2,1,0:T(8,128)(2,1)S(1)}, u32[]{:S(2)}, u32[]{:S(2)}) collective-permute-start(bf16[4,8,768]{2,1,0:T(8,128)(2,1)S(1)} %pad_maximum_fusion.refs_0_), channel_id=1, source_target_pairs={{0,3},{1,2},{2,1},{3,0},{4,7},{5,6},{6,5},{7,4},{8,11},{9,10},{10,... | collective-permute-start | bytes 147464 | tf_op jit(solution)/shard_map/ppermute | solution.py:31
  54.3 7.8 %copy-start.2 = (s32[1,8]{1,0:T(1,128)S(1)}, s32[1,8]{1,0:T(1,128)}, u32[]{:S(2)}) copy-start(s32[1,8]{1,0:T(1,128)} %refs_6_.2) | copy-start | bytes 100
  54.3 1.9 %collective-permute-start.11 = (bf16[8,1536]{1,0:T(8,128)(2,1)S(1)}, bf16[8,1536]{1,0:T(8,128)(2,1)S(1)}, u32[]{:S(2)}, u32[]{:S(2)}) collective-permute-start(bf16[8,1536]{1,0:T(8,128)(2,1)S(1)} %get-tuple-element.56.refs_0_), channel_id=1, source_target_pairs={{0,1},{1,0},{2,3},{3,2},{4,5},{5,4},{6,7},{7,6},{8,9},{9,8},{10,11... | collective-permute-start | bytes 73736 | tf_op jit(solution)/shard_map/ppermute | solution.py:26
  57.6 4.1 %collective-permute-start.12 = (f32[4,3072]{1,0:T(4,128)S(1)}, f32[4,3072]{1,0:T(4,128)S(1)}, u32[]{:S(2)}, u32[]{:S(2)}) collective-permute-start(f32[4,3072]{1,0:T(4,128)S(1)} %get-tuple-element.58), channel_id=1, source_target_pairs={{0,2},{2,0},{4,6},{6,4},{8,10},{10,8},{12,14},{14,12},{1,3},{3,1},... | collective-permute-start | bytes 147464 | tf_op jit(solution)/shard_map/ppermute | solution.py:26
  61.8 3.9 %collective-permute-start.13 = (f32[2,3072]{1,0:T(2,128)S(1)}, f32[2,3072]{1,0:T(2,128)S(1)}, u32[]{:S(2)}, u32[]{:S(2)}) collective-permute-start(f32[2,3072]{1,0:T(2,128)S(1)} %slice.17), channel_id=1, source_target_pairs={{0,4},{2,6},{4,0},{6,2},{8,12},{10,14},{12,8},{14,10},{1,5},{3,7},... | collective-permute-start | bytes 73736 | tf_op jit(solution)/shard_map/ppermute | solution.py:26
  65.7 4.7 %collective-permute-start.17 = (f32[1,3072]{1,0:T(1,128)S(1)}, f32[1,3072]{1,0:T(1,128)S(1)}, u32[]{:S(2)}, u32[]{:S(2)}) collective-permute-start(f32[1,3072]{1,0:T(1,128)S(1)} %slice.19), channel_id=1, source_target_pairs={{0,8},{2,10},{4,12},{6,14},{8,0},{10,2},{12,4},{14,6},{1,9},{3,11}... | collective-permute-start | bytes 36872 | tf_op jit(solution)/shard_map/ppermute | solution.py:26

commit v12 on v11

--- a/solution.py
+++ b/solution.py
@@ -396,7 +396,8 @@
         bit *= 2
         if bit == devices:
             break
-        num, state, pay = call(merge_kernel, state_shapes, num, state, arrived)
+        hold = (far_row,) if bit == 4 * stride else ()
+        num, state, pay = call(merge_kernel, state_shapes, num, state, arrived, hold=hold)
         if bit == 2 * stride:
             both_row = xor_permute(pin(far_row, num)[0], "batch", stride)
     if stride == 1:

time: 71.2 us -> 69.3 us (0.973)
  starting transfers between devices: 21.6 us -> 17.5 us
  waiting for transfers between devices: 32.2 us -> 34.5 us
    ppermute x15, starting transfers between devices: 20.4 us -> 17.1 us  [xor_permute(): return lax.ppermute(value, axis, [(i, i ^ bit) for i in range(total)])]
    ppermute x3, waiting for transfers between devices: 6.92 us -> 8.38 us  [cross_permute(): return lax.ppermute(value, ('batch', 'tensor'), pairs)]
    ppermute x3, starting transfers between devices: 1.22 us -> 0.33 us  [cross_permute(): return lax.ppermute(value, ('batch', 'tensor'), pairs)]
    ppermute x15, waiting for transfers between devices: 25.3 us -> 26.1 us  [xor_permute(): return lax.ppermute(value, axis, [(i, i ^ bit) for i in range(total)])]
  transfers between devices with their start and end apart: 18 -> 18, of which waited for: 11 -> 13; matrix products, arithmetic and copies ran while one was open for 0% -> 0% of each run, Pallas kernels for 20% -> 20%
where the time goes in v12:
time: 69.3 us; the launch traced here: 69.2 us
  waiting for transfers between devices  34.5 us (50%)
  starting transfers between devices  17.5 us (25%)
  Pallas kernels  14.3 us (21%)
  between operations  1.48 us (2%)
  local copies, waits for them, and re-layouts  0.72 us (1%)
  other arithmetic  0.7 us (1%)
    ppermute x15, waiting for transfers between devices, xor_permute(): return lax.ppermute(value, axis, [(i, i ^ bit) for i in range(total)])  26.1 us
    ppermute x15, starting transfers between devices, xor_permute(): return lax.ppermute(value, axis, [(i, i ^ bit) for i in range(total)])  17.1 us
    pallas_call x9, Pallas kernels, call(): pl.pallas_call(functools.partial(drop, kernel, first, len(hold)), out_sha...  9.74 us
    ppermute x3, waiting for transfers between devices, cross_permute(): return lax.ppermute(value, ('batch', 'tensor'), pairs)  8.38 us
    pallas_call x2, Pallas kernels, fetch(): pl.pallas_call(functools.partial(fetch_kernel, count), out_shape=[pltpu.V...  3.71 us
  transfers between devices with their start and end apart: 18, of which 13 were waited for; matrix products, arithmetic and copies ran while one was open for 0% of the time, Pallas kernels for 20%

profile of v12, /device:TPU:0, one launch (start us, length us, event | category | flops | bytes accessed | tf_op | source)
XLA Modules:
  0.0 69.2 jit_solution(3285237850646203101)
XLA Ops:
  0.6 4.1 %collective-permute-start = (bf16[2,1536]{1,0:T(2,128)(2,1)}, bf16[2,1536]{1,0:T(2,128)(2,1)S(1)}, u32[]{:S(2)}, u32[]{:S(2)}) collective-permute-start(bf16[2,1536]{1,0:T(2,128)(2,1)} %bitcast.14), channel_id=1, source_target_pairs={{0,8},{2,10},{4,12},{6,14},{8,0},{10,2},{12,4},{14,6},{1,9},{3,11}... | collective-permute-start | bytes 18440 | tf_op jit(solution)/shard_map/ppermute | solution.py:26
  4.7 1.5 %collective-permute-start.3 = (bf16[2,64,1536]{2,1,0:T(8,128)(2,1)}, bf16[2,64,1536]{2,1,0:T(8,128)(2,1)S(1)}, u32[]{:S(2)}, u32[]{:S(2)}) collective-permute-start(bf16[2,64,1536]{2,1,0:T(8,128)(2,1)} %bitcast.11), channel_id=1, source_target_pairs={{0,2},{2,0},{4,6},{6,4},{8,10},{10,8},{12,14},{14,12},{1,3},{3,1},... | collective-permute-start | bytes 1179656 | tf_op jit(solution)/shard_map/ppermute | solution.py:26
  6.2 1.3 %shard_map.121 = (bf16[2,1536]{1,0:T(2,128)(2,1)S(1)}, bf16[2,64,1536]{2,1,0:T(8,128)(2,1)S(1)}, bf16[2,64,1536]{2,1,0:T(8,128)(2,1)S(1)}, bf16[2,1536]{1,0:T(2,128)(2,1)S(1)}, bf16[1,8,768]{2,1,0:T(8,128)(2,1)S(1)}) custom-call(bf16[2,1536]{1,0:T(2,128)(2,1)} %bitcast.15, bf16[2,64,1536]{2,1,0:T(8,128)(2,1)} %bitcast.12, bf16[2,64,1536]{2,1,0:T(8,128)(2,1)} %bitcast.10, ...), custom_call_target="tpu_custom_call" | custom-call | bytes 2097152 | tf_op jit(solution)/shard_map/pallas_call | solution.py:94
  7.6 2.4 %collective-permute-start.1 = (bf16[4,1536]{1,0:T(4,128)(2,1)S(1)}, bf16[4,1536]{1,0:T(4,128)(2,1)S(1)}, u32[]{:S(2)}, u32[]{:S(2)}) collective-permute-start(bf16[4,1536]{1,0:T(4,128)(2,1)S(1)} %pad_maximum_fusion.3), channel_id=1, source_target_pairs={{0,4},{2,6},{4,0},{6,2},{8,12},{10,14},{12,8},{14,10},{1,5},{3,7},... | collective-permute-start | bytes 36872 | tf_op jit(solution)/shard_map/ppermute | solution.py:26
  10.0 1.2 %collective-permute-start.6 = (bf16[2,64,1536]{2,1,0:T(8,128)(2,1)}, bf16[2,64,1536]{2,1,0:T(8,128)(2,1)S(1)}, u32[]{:S(2)}, u32[]{:S(2)}) collective-permute-start(bf16[2,64,1536]{2,1,0:T(8,128)(2,1)} %bitcast.13), channel_id=1, source_target_pairs={{0,8},{2,10},{4,12},{6,14},{8,0},{10,2},{12,4},{14,6},{1,9},{3,11}... | collective-permute-start | bytes 1179656 | tf_op jit(solution)/shard_map/ppermute | solution.py:26
  11.1 0.5 collective-permute-done.1
  11.7 1.0 %collective-permute-start.2 = (bf16[8,1536]{1,0:T(8,128)(2,1)S(1)}, bf16[8,1536]{1,0:T(8,128)(2,1)S(1)}, u32[]{:S(2)}, u32[]{:S(2)}) collective-permute-start(bf16[8,1536]{1,0:T(8,128)(2,1)S(1)} %pad_maximum_fusion.1.refs_1_.refs_0_), channel_id=1, source_target_pairs={{0,2},{2,0},{4,6},{6,4},{8,10},{10,8},{12,14},{14,12},{1,3},{3,1},... | collective-permute-start | bytes 73736 | tf_op jit(solution)/shard_map/ppermute | solution.py:26
  13.4 2.4 %shard_map.122.weight_ref = bf16[2,1536,768]{2,1,0:T(8,128)(2,1)S(1)} custom-call(bf16[2,1536,768]{2,1,0:T(8,128)(2,1)} %refs_0_.1, bf16[8,1536]{1,0:T(8,128)(2,1)S(1)} %pad_maximum_fusion.1.refs_1_.refs_0_), custom_call_target="tpu_custom_call" | custom-call | bytes 2097152 | tf_op jit(solution)/shard_map/pallas_call | solution.py:94
  16.1 0.7 copy-done.1
  16.7 1.3 %shard_map.123 = (f32[16,1536]{1,0:T(8,128)S(1)}, f32[16,256]{1,0:T(8,128)S(1)}, bf16[16,1664]{1,0:T(8,128)(2,1)S(1)}) custom-call(bf16[8,1536]{1,0:T(8,128)(2,1)S(1)} %pad_maximum_fusion.1.refs_1_.refs_0_, bf16[8,1536]{1,0:T(8,128)(2,1)S(1)} %collective-permute-done.2.refs_1_, bf16[2,64,1536]{2,1,0:T(8,128)(2,1)S(1)} %get-tuple-element.41.refs_2_.refs_0_, ...), custom_call_target="tpu_custom_call" | custom-call | flops 1000000000 | tf_op jit(solution)/shard_map/pallas_call | solution.py:55
  18.0 1.6 %collective-permute-start.4 = (bf16[16,1664]{1,0:T(8,128)(2,1)S(1)}, bf16[16,1664]{1,0:T(8,128)(2,1)S(1)}, u32[]{:S(2)}, u32[]{:S(2)}) collective-permute-start(bf16[16,1664]{1,0:T(8,128)(2,1)S(1)} %get-tuple-element.46), channel_id=1, source_target_pairs={{0,2},{2,0},{4,6},{6,4},{8,10},{10,8},{12,14},{14,12},{1,3},{3,1},... | collective-permute-start | bytes 159752 | tf_op jit(solution)/shard_map/ppermute | solution.py:26
  19.6 2.6 %collective-permute-done.4.refs_2_ = bf16[16,1664]{1,0:T(8,128)(2,1)S(1)} collective-permute-done((bf16[16,1664]{1,0:T(8,128)(2,1)S(1)}, bf16[16,1664]{1,0:T(8,128)(2,1)S(1)}, u32[]{:S(2)}, u32[]{:S(2)}) %collective-permute-start.4) | collective-permute-done | bytes 53280 | tf_op jit(solution)/shard_map/ppermute | solution.py:26
  22.5 1.8 %collective-permute-start.5 = (bf16[16,1664]{1,0:T(8,128)(2,1)S(1)}, bf16[16,1664]{1,0:T(8,128)(2,1)S(1)}, u32[]{:S(2)}, u32[]{:S(2)}) collective-permute-start(bf16[16,1664]{1,0:T(8,128)(2,1)S(1)} %get-tuple-element.49), channel_id=1, source_target_pairs={{0,4},{2,6},{4,0},{6,2},{8,12},{10,14},{12,8},{14,10},{1,5},{3,7},... | collective-permute-start | bytes 159752 | tf_op jit(solution)/shard_map/ppermute | solution.py:26
  24.3 5.3 %collective-permute-done.6.refs_3_.refs_1_ = bf16[2,64,1536]{2,1,0:T(8,128)(2,1)S(1)} collective-permute-done((bf16[2,64,1536]{2,1,0:T(8,128)(2,1)}, bf16[2,64,1536]{2,1,0:T(8,128)(2,1)S(1)}, u32[]{:S(2)}, u32[]{:S(2)}) %collective-permute-start.6) | collective-permute-done | bytes 393248 | tf_op jit(solution)/shard_map/ppermute | solution.py:26
  29.6 1.0 %collective-permute-done.5.refs_2_ = bf16[16,1664]{1,0:T(8,128)(2,1)S(1)} collective-permute-done((bf16[16,1664]{1,0:T(8,128)(2,1)S(1)}, bf16[16,1664]{1,0:T(8,128)(2,1)S(1)}, u32[]{:S(2)}, u32[]{:S(2)}) %collective-permute-start.5) | collective-permute-done | bytes 53280 | tf_op jit(solution)/shard_map/ppermute | solution.py:26
  31.0 0.5 collective-permute-start.15
  31.5 4.6 %collective-permute-done.7.pay_ref = bf16[16,1664]{1,0:T(8,128)(2,1)S(1)} collective-permute-done((bf16[16,1664]{1,0:T(8,128)(2,1)S(1)}, bf16[16,1664]{1,0:T(8,128)(2,1)S(1)}, u32[]{:S(2)}, u32[]{:S(2)}) %collective-permute-start.7) | collective-permute-done | bytes 53280 | tf_op jit(solution)/shard_map/ppermute | solution.py:26
  36.1 0.8 %shard_map.126.refs_0_ = f32[8,768]{1,0:T(8,128)S(1)} custom-call(f32[16,1536]{1,0:T(8,128)S(1)} %get-tuple-element.50.num_ref, f32[16,256]{1,0:T(8,128)S(1)} %get-tuple-element.51.state_ref, bf16[16,1664]{1,0:T(8,128)(2,1)S(1)} %collective-permute-done.7.pay_ref, bf16[2,1536,768]{2,1,0:T(8,128)(2,1)S(1)} %shard_map.122.weight_ref), custom_call_target="tpu_custom_call" | custom-call | flops 2000000000 | tf_op jit(solution)/shard_map/pallas_call | solution.py:251
  37.1 1.2 %collective-permute-done.8.refs_1_ = f32[8,768]{1,0:T(8,128)S(1)} collective-permute-done((f32[8,768]{1,0:T(8,128)S(1)}, f32[8,768]{1,0:T(8,128)S(1)}, u32[]{:S(2)}, u32[]{:S(2)}) %collective-permute-start.8) | collective-permute-done | bytes 24608 | tf_op jit(solution)/shard_map/ppermute | solution.py:26
  38.4 4.0 %collective-permute-done.9 = bf16[1,8,768]{2,1,0:T(8,128)(2,1)S(1)} collective-permute-done((bf16[1,8,768]{2,1,0:T(8,128)(2,1)S(1)}, bf16[1,8,768]{2,1,0:T(8,128)(2,1)S(1)}, u32[]{:S(2)}, u32[]{:S(2)}) %collective-permute-start.9) | collective-permute-done | bytes 12320 | tf_op jit(solution)/shard_map/ppermute | solution.py:31
  42.4 0.6 shard_map.131
  43.0 1.8 %collective-permute-start.16 = (bf16[2,64,1536]{2,1,0:T(8,128)(2,1)S(1)}, bf16[2,64,1536]{2,1,0:T(8,128)(2,1)S(1)}, u32[]{:S(2)}, u32[]{:S(2)}) collective-permute-start(bf16[2,64,1536]{2,1,0:T(8,128)(2,1)S(1)} %shard_map.131), channel_id=1, source_target_pairs={{0,4},{2,6},{4,0},{6,2},{8,12},{10,14},{12,8},{14,10},{1,5},{3,7},... | collective-permute-start | bytes 1179656 | tf_op jit(solution)/shard_map/ppermute | solution.py:26
  44.8 0.8 %collective-permute-done.10 = bf16[2,8,768]{2,1,0:T(8,128)(2,1)S(1)} collective-permute-done((bf16[2,8,768]{2,1,0:T(8,128)(2,1)S(1)}, bf16[2,8,768]{2,1,0:T(8,128)(2,1)S(1)}, u32[]{:S(2)}, u32[]{:S(2)}) %collective-permute-start.10) | collective-permute-done | bytes 24608 | tf_op jit(solution)/shard_map/ppermute | solution.py:31
  45.9 3.5 %collective-permute-done.11.refs_1_ = bf16[4,8,768]{2,1,0:T(8,128)(2,1)S(1)} collective-permute-done((bf16[4,8,768]{2,1,0:T(8,128)(2,1)S(1)}, bf16[4,8,768]{2,1,0:T(8,128)(2,1)S(1)}, u32[]{:S(2)}, u32[]{:S(2)}) %collective-permute-start.11) | collective-permute-done | bytes 49184 | tf_op jit(solution)/shard_map/ppermute | solution.py:31
  49.5 3.0 %shard_map.128 = (bf16[8,768]{1,0:T(8,128)(2,1)}, bf16[8,1536]{1,0:T(8,128)(2,1)S(1)}) custom-call(bf16[4,8,768]{2,1,0:T(8,128)(2,1)S(1)} %pad_maximum_fusion.refs_0_, bf16[4,8,768]{2,1,0:T(8,128)(2,1)S(1)} %collective-permute-done.11.refs_1_, bf16[6144,1536]{1,0:T(8,128)(2,1)S(1)} %copy-done), custom_call_target="tpu_custom_call" | custom-call | flops 1000000000 | tf_op jit(solution)/shard_map/pallas_call | solution.py:55
  52.9 1.4 %shard_map.129.refs_2_ = f32[8,3072]{1,0:T(8,128)S(1)} custom-call(bf16[8,1536]{1,0:T(8,128)(2,1)S(1)} %get-tuple-element.56.refs_0_, bf16[3072,3072]{1,0:T(8,128)(2,1)S(1)} %bitcast.9), custom_call_target="tpu_custom_call" | custom-call | flops 1000000000 | tf_op jit(solution)/shard_map/pallas_call | solution.py:55
  54.4 1.4 %shard_map.130 = (f32[4,3072]{1,0:T(4,128)S(1)}, f32[4,3072]{1,0:T(4,128)S(1)}) custom-call(bf16[8,1536]{1,0:T(8,128)(2,1)S(1)} %collective-permute-done.12.refs_0_, bf16[3072,3072]{1,0:T(8,128)(2,1)S(1)} %bitcast.9, f32[8,3072]{1,0:T(8,128)S(1)} %shard_map.129.refs_2_), custom_call_target="tpu_custom_call" | custom-call | flops 1000000000 | tf_op jit(solution)/shard_map/pallas_call | solution.py:55
  56.3 3.6 %collective-permute-done.13 = f32[4,3072]{1,0:T(4,128)S(1)} collective-permute-done((f32[4,3072]{1,0:T(4,128)S(1)}, f32[4,3072]{1,0:T(4,128)S(1)}, u32[]{:S(2)}, u32[]{:S(2)}) %collective-permute-start.13) | collective-permute-done | bytes 49184 | tf_op jit(solution)/shard_map/ppermute | solution.py:26
  60.1 1.4 %shard_map.132 = bf16[2,64,1536]{2,1,0:T(8,128)(2,1)} custom-call(bf16[2,64,1536]{2,1,0:T(8,128)(2,1)S(1)} %get-tuple-element.41.refs_2_.refs_0_, bf16[2,64,1536]{2,1,0:T(8,128)(2,1)S(1)} %collective-permute-done.6.refs_3_.refs_1_, bf16[2,64,1536]{2,1,0:T(8,128)(2,1)S(1)} %collective-permute-done.3.refs_7_.refs_2_, ...), custom_call_target="tpu_custom_call" | custom-call | flops 1000000000 | tf_op jit(solution)/shard_map/pallas_call | solution.py:55
  61.5 2.4 %collective-permute-done.14 = f32[2,3072]{1,0:T(2,128)S(1)} collective-permute-done((f32[2,3072]{1,0:T(2,128)S(1)}, f32[2,3072]{1,0:T(2,128)S(1)}, u32[]{:S(2)}, u32[]{:S(2)}) %collective-permute-start.14) | collective-permute-done | bytes 24608 | tf_op jit(solution)/shard_map/ppermute | solution.py:26
  64.0 4.5 %collective-permute-done.17 = f32[1,3072]{1,0:T(1,128)S(1)} collective-permute-done((f32[1,3072]{1,0:T(1,128)S(1)}, f32[1,3072]{1,0:T(1,128)S(1)}, u32[]{:S(2)}, u32[]{:S(2)}) %collective-permute-start.17) | collective-permute-done | bytes 12320 | tf_op jit(solution)/shard_map/ppermute | solution.py:26
  68.5 0.6 fusion.1
  (42 shorter events, 2.6 us)
Async XLA Ops:
  0.6 48.8 %copy-start = (bf16[6144,1536]{1,0:T(8,128)(2,1)S(1)}, bf16[6144,1536]{1,0:T(8,128)(2,1)}, u32[]{:S(2)}) copy-start(bf16[6144,1536]{1,0:T(8,128)(2,1)} %refs_2_.1) | copy-start | bytes 56623108
  0.6 6.9 %collective-permute-start = (bf16[2,1536]{1,0:T(2,128)(2,1)}, bf16[2,1536]{1,0:T(2,128)(2,1)S(1)}, u32[]{:S(2)}, u32[]{:S(2)}) collective-permute-start(bf16[2,1536]{1,0:T(2,128)(2,1)} %bitcast.14), channel_id=1, source_target_pairs={{0,8},{2,10},{4,12},{6,14},{8,0},{10,2},{12,4},{14,6},{1,9},{3,11}... | collective-permute-start | bytes 18440 | tf_op jit(solution)/shard_map/ppermute | solution.py:26
  4.7 11.3 %collective-permute-start.3 = (bf16[2,64,1536]{2,1,0:T(8,128)(2,1)}, bf16[2,64,1536]{2,1,0:T(8,128)(2,1)S(1)}, u32[]{:S(2)}, u32[]{:S(2)}) collective-permute-start(bf16[2,64,1536]{2,1,0:T(8,128)(2,1)} %bitcast.11), channel_id=1, source_target_pairs={{0,2},{2,0},{4,6},{6,4},{8,10},{10,8},{12,14},{14,12},{1,3},{3,1},... | collective-permute-start | bytes 1179656 | tf_op jit(solution)/shard_map/ppermute | solution.py:26
  7.6 4.1 %collective-permute-start.1 = (bf16[4,1536]{1,0:T(4,128)(2,1)S(1)}, bf16[4,1536]{1,0:T(4,128)(2,1)S(1)}, u32[]{:S(2)}, u32[]{:S(2)}) collective-permute-start(bf16[4,1536]{1,0:T(4,128)(2,1)S(1)} %pad_maximum_fusion.3), channel_id=1, source_target_pairs={{0,4},{2,6},{4,0},{6,2},{8,12},{10,14},{12,8},{14,10},{1,5},{3,7},... | collective-permute-start | bytes 36872 | tf_op jit(solution)/shard_map/ppermute | solution.py:26
  10.0 19.6 %collective-permute-start.6 = (bf16[2,64,1536]{2,1,0:T(8,128)(2,1)}, bf16[2,64,1536]{2,1,0:T(8,128)(2,1)S(1)}, u32[]{:S(2)}, u32[]{:S(2)}) collective-permute-start(bf16[2,64,1536]{2,1,0:T(8,128)(2,1)} %bitcast.13), channel_id=1, source_target_pairs={{0,8},{2,10},{4,12},{6,14},{8,0},{10,2},{12,4},{14,6},{1,9},{3,11}... | collective-permute-start | bytes 1179656 | tf_op jit(solution)/shard_map/ppermute | solution.py:26
  11.7 4.4 %collective-permute-start.2 = (bf16[8,1536]{1,0:T(8,128)(2,1)S(1)}, bf16[8,1536]{1,0:T(8,128)(2,1)S(1)}, u32[]{:S(2)}, u32[]{:S(2)}) collective-permute-start(bf16[8,1536]{1,0:T(8,128)(2,1)S(1)} %pad_maximum_fusion.1.refs_1_.refs_0_), channel_id=1, source_target_pairs={{0,2},{2,0},{4,6},{6,4},{8,10},{10,8},{12,14},{14,12},{1,3},{3,1},... | collective-permute-start | bytes 73736 | tf_op jit(solution)/shard_map/ppermute | solution.py:26
  16.1 0.7 copy-start.1
  18.0 4.2 %collective-permute-start.4 = (bf16[16,1664]{1,0:T(8,128)(2,1)S(1)}, bf16[16,1664]{1,0:T(8,128)(2,1)S(1)}, u32[]{:S(2)}, u32[]{:S(2)}) collective-permute-start(bf16[16,1664]{1,0:T(8,128)(2,1)S(1)} %get-tuple-element.46), channel_id=1, source_target_pairs={{0,2},{2,0},{4,6},{6,4},{8,10},{10,8},{12,14},{14,12},{1,3},{3,1},... | collective-permute-start | bytes 159752 | tf_op jit(solution)/shard_map/ppermute | solution.py:26
  22.5 30.4 %slice-start = ((s8[18874368]{0:T(1024)(128)(4,1)}), s8[4194304]{0:T(1024)(128)(4,1)S(1)}, s32[]{:S(2)}) async-start(s8[18874368]{0:T(1024)(128)(4,1)} %bitcast.8), calls=%async_computation | async-start | bytes 8388608
  22.5 8.1 %collective-permute-start.5 = (bf16[16,1664]{1,0:T(8,128)(2,1)S(1)}, bf16[16,1664]{1,0:T(8,128)(2,1)S(1)}, u32[]{:S(2)}, u32[]{:S(2)}) collective-permute-start(bf16[16,1664]{1,0:T(8,128)(2,1)S(1)} %get-tuple-element.49), channel_id=1, source_target_pairs={{0,4},{2,6},{4,0},{6,2},{8,12},{10,14},{12,8},{14,10},{1,5},{3,7},... | collective-permute-start | bytes 159752 | tf_op jit(solution)/shard_map/ppermute | solution.py:26
  30.9 5.2 %collective-permute-start.7 = (bf16[16,1664]{1,0:T(8,128)(2,1)S(1)}, bf16[16,1664]{1,0:T(8,128)(2,1)S(1)}, u32[]{:S(2)}, u32[]{:S(2)}) collective-permute-start(bf16[16,1664]{1,0:T(8,128)(2,1)S(1)} %get-tuple-element.52), channel_id=1, source_target_pairs={{0,8},{2,10},{4,12},{6,14},{8,0},{10,2},{12,4},{14,6},{1,9},{3,11}... | collective-permute-start | bytes 159752 | tf_op jit(solution)/shard_map/ppermute | solution.py:26
  31.0 11.4 %collective-permute-start.15 = (bf16[2,64,1536]{2,1,0:T(8,128)(2,1)S(1)}, bf16[2,64,1536]{2,1,0:T(8,128)(2,1)S(1)}, u32[]{:S(2)}, u32[]{:S(2)}) collective-permute-start(bf16[2,64,1536]{2,1,0:T(8,128)(2,1)S(1)} %collective-permute-done.6.refs_3_.refs_1_), channel_id=1, source_target_pairs={{0,2},{2,0},{4,6},{6,4},{8,10},{10,8},{12,14},{14,12},{1,3},{3,1},... | collective-permute-start | bytes 1179656 | tf_op jit(solution)/shard_map/ppermute | solution.py:26
  36.1 16.8 %slice-start.1 = ((s8[18874368]{0:T(1024)(128)(4,1)}), s8[4194304]{0:T(1024)(128)(4,1)S(1)}, s32[]{:S(2)}) async-start(s8[18874368]{0:T(1024)(128)(4,1)} %bitcast.8), calls=%async_computation.1 | async-start | bytes 8388608
  37.0 1.3 %collective-permute-start.8 = (f32[8,768]{1,0:T(8,128)S(1)}, f32[8,768]{1,0:T(8,128)S(1)}, u32[]{:S(2)}, u32[]{:S(2)}) collective-permute-start(f32[8,768]{1,0:T(8,128)S(1)} %shard_map.126.refs_0_), channel_id=1, source_target_pairs={{0,1},{1,0},{2,3},{3,2},{4,5},{5,4},{6,7},{7,6},{8,9},{9,8},{10,11... | collective-permute-start | bytes 73736 | tf_op jit(solution)/shard_map/ppermute | solution.py:26
  38.3 4.1 %collective-permute-start.9 = (bf16[1,8,768]{2,1,0:T(8,128)(2,1)S(1)}, bf16[1,8,768]{2,1,0:T(8,128)(2,1)S(1)}, u32[]{:S(2)}, u32[]{:S(2)}) collective-permute-start(bf16[1,8,768]{2,1,0:T(8,128)(2,1)S(1)} %shard_map.127), channel_id=1, source_target_pairs={{0,9},{1,8},{2,11},{3,10},{4,13},{5,12},{6,15},{7,14},{8,1},{9,0},... | collective-permute-start | bytes 36872 | tf_op jit(solution)/shard_map/ppermute | solution.py:31
  42.4 10.5 %slice-start.2 = ((s8[18874368]{0:T(1024)(128)(4,1)}), s8[4194304]{0:T(1024)(128)(4,1)S(1)}, s32[]{:S(2)}) async-start(s8[18874368]{0:T(1024)(128)(4,1)} %bitcast.8), calls=%async_computation.2 | async-start | bytes 8388608
  42.4 3.3 %collective-permute-start.10 = (bf16[2,8,768]{2,1,0:T(8,128)(2,1)S(1)}, bf16[2,8,768]{2,1,0:T(8,128)(2,1)S(1)}, u32[]{:S(2)}, u32[]{:S(2)}) collective-permute-start(bf16[2,8,768]{2,1,0:T(8,128)(2,1)S(1)} %pad_maximum_fusion.2), channel_id=1, source_target_pairs={{0,5},{1,4},{2,7},{3,6},{4,1},{5,0},{6,3},{7,2},{8,13},{9,12},{10,... | collective-permute-start | bytes 73736 | tf_op jit(solution)/shard_map/ppermute | solution.py:31
  43.0 17.1 %collective-permute-start.16 = (bf16[2,64,1536]{2,1,0:T(8,128)(2,1)S(1)}, bf16[2,64,1536]{2,1,0:T(8,128)(2,1)S(1)}, u32[]{:S(2)}, u32[]{:S(2)}) collective-permute-start(bf16[2,64,1536]{2,1,0:T(8,128)(2,1)S(1)} %shard_map.131), channel_id=1, source_target_pairs={{0,4},{2,6},{4,0},{6,2},{8,12},{10,14},{12,8},{14,10},{1,5},{3,7},... | collective-permute-start | bytes 1179656 | tf_op jit(solution)/shard_map/ppermute | solution.py:26
  45.6 7.3 %slice-start.3 = ((s8[18874368]{0:T(1024)(128)(4,1)}), s8[4194304]{0:T(1024)(128)(4,1)S(1)}, s32[]{:S(2)}) async-start(s8[18874368]{0:T(1024)(128)(4,1)} %bitcast.8), calls=%async_computation.3 | async-start | bytes 8388608
  45.7 7.3 %slice-start.4 = ((s8[18874368]{0:T(1024)(128)(4,1)}), s8[2097152]{0:T(1024)(128)(4,1)S(1)}, s32[]{:S(2)}) async-start(s8[18874368]{0:T(1024)(128)(4,1)} %bitcast.8), calls=%async_computation.4 | async-start | bytes 4194304
  45.7 3.8 %collective-permute-start.11 = (bf16[4,8,768]{2,1,0:T(8,128)(2,1)S(1)}, bf16[4,8,768]{2,1,0:T(8,128)(2,1)S(1)}, u32[]{:S(2)}, u32[]{:S(2)}) collective-permute-start(bf16[4,8,768]{2,1,0:T(8,128)(2,1)S(1)} %pad_maximum_fusion.refs_0_), channel_id=1, source_target_pairs={{0,3},{1,2},{2,1},{3,0},{4,7},{5,6},{6,5},{7,4},{8,11},{9,10},{10,... | collective-permute-start | bytes 147464 | tf_op jit(solution)/shard_map/ppermute | solution.py:31
  52.5 7.6 %copy-start.2 = (s32[1,8]{1,0:T(1,128)S(1)}, s32[1,8]{1,0:T(1,128)}, u32[]{:S(2)}) copy-start(s32[1,8]{1,0:T(1,128)} %refs_6_.2) | copy-start | bytes 100
  52.5 1.9 %collective-permute-start.12 = (bf16[8,1536]{1,0:T(8,128)(2,1)S(1)}, bf16[8,1536]{1,0:T(8,128)(2,1)S(1)}, u32[]{:S(2)}, u32[]{:S(2)}) collective-permute-start(bf16[8,1536]{1,0:T(8,128)(2,1)S(1)} %get-tuple-element.56.refs_0_), channel_id=1, source_target_pairs={{0,1},{1,0},{2,3},{3,2},{4,5},{5,4},{6,7},{7,6},{8,9},{9,8},{10,11... | collective-permute-start | bytes 73736 | tf_op jit(solution)/shard_map/ppermute | solution.py:26
  55.8 4.1 %collective-permute-start.13 = (f32[4,3072]{1,0:T(4,128)S(1)}, f32[4,3072]{1,0:T(4,128)S(1)}, u32[]{:S(2)}, u32[]{:S(2)}) collective-permute-start(f32[4,3072]{1,0:T(4,128)S(1)} %get-tuple-element.58), channel_id=1, source_target_pairs={{0,2},{2,0},{4,6},{6,4},{8,10},{10,8},{12,14},{14,12},{1,3},{3,1},... | collective-permute-start | bytes 147464 | tf_op jit(solution)/shard_map/ppermute | solution.py:26
  59.9 3.9 %collective-permute-start.14 = (f32[2,3072]{1,0:T(2,128)S(1)}, f32[2,3072]{1,0:T(2,128)S(1)}, u32[]{:S(2)}, u32[]{:S(2)}) collective-permute-start(f32[2,3072]{1,0:T(2,128)S(1)} %slice.17), channel_id=1, source_target_pairs={{0,4},{2,6},{4,0},{6,2},{8,12},{10,14},{12,8},{14,10},{1,5},{3,7},... | collective-permute-start | bytes 73736 | tf_op jit(solution)/shard_map/ppermute | solution.py:26
  63.9 4.7 %collective-permute-start.17 = (f32[1,3072]{1,0:T(1,128)S(1)}, f32[1,3072]{1,0:T(1,128)S(1)}, u32[]{:S(2)}, u32[]{:S(2)}) collective-permute-start(f32[1,3072]{1,0:T(1,128)S(1)} %slice.19), channel_id=1, source_target_pairs={{0,8},{2,10},{4,12},{6,14},{8,0},{10,2},{12,4},{14,6},{1,9},{3,11}... | collective-permute-start | bytes 36872 | tf_op jit(solution)/shard_map/ppermute | solution.py:26

commit v13 on v12

--- a/solution.py
+++ b/solution.py
@@ -396,7 +396,7 @@
         bit *= 2
         if bit == devices:
             break
-        hold = (far_row,) if bit == 4 * stride else ()
+        hold = (far_row,) if bit == 2 * stride else ()
         num, state, pay = call(merge_kernel, state_shapes, num, state, arrived, hold=hold)
         if bit == 2 * stride:
             both_row = xor_permute(pin(far_row, num)[0], "batch", stride)

time: 69.3 us -> 72.6 us (1.048)
  waiting for transfers between devices: 34.5 us -> 39.4 us
  starting transfers between devices: 17.5 us -> 15.8 us
    ppermute x15, waiting for transfers between devices: 26.1 us -> 31 us  [xor_permute(): return lax.ppermute(value, axis, [(i, i ^ bit) for i in range(total)])]
    ppermute x15, starting transfers between devices: 17.1 us -> 15.5 us  [xor_permute(): return lax.ppermute(value, axis, [(i, i ^ bit) for i in range(total)])]
  transfers between devices with their start and end apart: 18 -> 18, of which waited for: 13 -> 12; matrix products, arithmetic and copies ran while one was open for 0% -> 0% of each run, Pallas kernels for 20% -> 19%
where the time goes in v13:
time: 72.6 us; the launch traced here: 72.4 us
  waiting for transfers between devices  39.4 us (54%)
  starting transfers between devices  15.8 us (22%)
  Pallas kernels  14.3 us (20%)
  between operations  1.49 us (2%)
    ppermute x15, waiting for transfers between devices, xor_permute(): return lax.ppermute(value, axis, [(i, i ^ bit) for i in range(total)])  31 us
    ppermute x15, starting transfers between devices, xor_permute(): return lax.ppermute(value, axis, [(i, i ^ bit) for i in range(total)])  15.5 us
    pallas_call x9, Pallas kernels, call(): pl.pallas_call(functools.partial(drop, kernel, first, len(hold)), out_sha...  9.74 us
    ppermute x3, waiting for transfers between devices, cross_permute(): return lax.ppermute(value, ('batch', 'tensor'), pairs)  8.38 us
    pallas_call x2, Pallas kernels, fetch(): pl.pallas_call(functools.partial(fetch_kernel, count), out_shape=[pltpu.V...  3.71 us
  transfers between devices with their start and end apart: 18, of which 12 were waited for; matrix products, arithmetic and copies ran while one was open for 0% of the time, Pallas kernels for 19%

profile of v13, /device:TPU:0, one launch (start us, length us, event | category | flops | bytes accessed | tf_op | source)
XLA Modules:
  0.0 72.4 jit_solution(7403387660214440783)
XLA Ops:
  0.6 4.1 %collective-permute-start = (bf16[2,1536]{1,0:T(2,128)(2,1)}, bf16[2,1536]{1,0:T(2,128)(2,1)S(1)}, u32[]{:S(2)}, u32[]{:S(2)}) collective-permute-start(bf16[2,1536]{1,0:T(2,128)(2,1)} %bitcast.14), channel_id=1, source_target_pairs={{0,8},{2,10},{4,12},{6,14},{8,0},{10,2},{12,4},{14,6},{1,9},{3,11}... | collective-permute-start | bytes 18440 | tf_op jit(solution)/shard_map/ppermute | solution.py:26
  4.7 1.5 %collective-permute-start.3 = (bf16[2,64,1536]{2,1,0:T(8,128)(2,1)}, bf16[2,64,1536]{2,1,0:T(8,128)(2,1)S(1)}, u32[]{:S(2)}, u32[]{:S(2)}) collective-permute-start(bf16[2,64,1536]{2,1,0:T(8,128)(2,1)} %bitcast.11), channel_id=1, source_target_pairs={{0,2},{2,0},{4,6},{6,4},{8,10},{10,8},{12,14},{14,12},{1,3},{3,1},... | collective-permute-start | bytes 1179656 | tf_op jit(solution)/shard_map/ppermute | solution.py:26
  6.2 1.3 %shard_map.121 = (bf16[2,1536]{1,0:T(2,128)(2,1)S(1)}, bf16[2,64,1536]{2,1,0:T(8,128)(2,1)S(1)}, bf16[2,64,1536]{2,1,0:T(8,128)(2,1)S(1)}, bf16[2,1536]{1,0:T(2,128)(2,1)S(1)}, bf16[1,8,768]{2,1,0:T(8,128)(2,1)S(1)}) custom-call(bf16[2,1536]{1,0:T(2,128)(2,1)} %bitcast.15, bf16[2,64,1536]{2,1,0:T(8,128)(2,1)} %bitcast.12, bf16[2,64,1536]{2,1,0:T(8,128)(2,1)} %bitcast.10, ...), custom_call_target="tpu_custom_call" | custom-call | bytes 2097152 | tf_op jit(solution)/shard_map/pallas_call | solution.py:94
  7.6 2.4 %collective-permute-start.1 = (bf16[4,1536]{1,0:T(4,128)(2,1)S(1)}, bf16[4,1536]{1,0:T(4,128)(2,1)S(1)}, u32[]{:S(2)}, u32[]{:S(2)}) collective-permute-start(bf16[4,1536]{1,0:T(4,128)(2,1)S(1)} %pad_maximum_fusion.3), channel_id=1, source_target_pairs={{0,4},{2,6},{4,0},{6,2},{8,12},{10,14},{12,8},{14,10},{1,5},{3,7},... | collective-permute-start | bytes 36872 | tf_op jit(solution)/shard_map/ppermute | solution.py:26
  10.0 1.2 %collective-permute-start.5 = (bf16[2,64,1536]{2,1,0:T(8,128)(2,1)}, bf16[2,64,1536]{2,1,0:T(8,128)(2,1)S(1)}, u32[]{:S(2)}, u32[]{:S(2)}) collective-permute-start(bf16[2,64,1536]{2,1,0:T(8,128)(2,1)} %bitcast.13), channel_id=1, source_target_pairs={{0,8},{2,10},{4,12},{6,14},{8,0},{10,2},{12,4},{14,6},{1,9},{3,11}... | collective-permute-start | bytes 1179656 | tf_op jit(solution)/shard_map/ppermute | solution.py:26
  11.1 0.5 collective-permute-done.1
  11.7 1.0 %collective-permute-start.2 = (bf16[8,1536]{1,0:T(8,128)(2,1)S(1)}, bf16[8,1536]{1,0:T(8,128)(2,1)S(1)}, u32[]{:S(2)}, u32[]{:S(2)}) collective-permute-start(bf16[8,1536]{1,0:T(8,128)(2,1)S(1)} %pad_maximum_fusion.1.refs_1_.refs_0_), channel_id=1, source_target_pairs={{0,2},{2,0},{4,6},{6,4},{8,10},{10,8},{12,14},{14,12},{1,3},{3,1},... | collective-permute-start | bytes 73736 | tf_op jit(solution)/shard_map/ppermute | solution.py:26
  13.4 2.4 %shard_map.122.weight_ref = bf16[2,1536,768]{2,1,0:T(8,128)(2,1)S(1)} custom-call(bf16[2,1536,768]{2,1,0:T(8,128)(2,1)} %refs_0_.1, bf16[8,1536]{1,0:T(8,128)(2,1)S(1)} %pad_maximum_fusion.1.refs_1_.refs_0_), custom_call_target="tpu_custom_call" | custom-call | bytes 2097152 | tf_op jit(solution)/shard_map/pallas_call | solution.py:94
  16.1 0.7 copy-done.1
  16.7 1.3 %shard_map.123 = (f32[16,1536]{1,0:T(8,128)S(1)}, f32[16,256]{1,0:T(8,128)S(1)}, bf16[16,1664]{1,0:T(8,128)(2,1)S(1)}) custom-call(bf16[8,1536]{1,0:T(8,128)(2,1)S(1)} %pad_maximum_fusion.1.refs_1_.refs_0_, bf16[8,1536]{1,0:T(8,128)(2,1)S(1)} %collective-permute-done.2.refs_1_, bf16[2,64,1536]{2,1,0:T(8,128)(2,1)S(1)} %get-tuple-element.41.refs_2_.refs_0_, ...), custom_call_target="tpu_custom_call" | custom-call | flops 1000000000 | tf_op jit(solution)/shard_map/pallas_call | solution.py:55
  18.0 1.6 %collective-permute-start.4 = (bf16[16,1664]{1,0:T(8,128)(2,1)S(1)}, bf16[16,1664]{1,0:T(8,128)(2,1)S(1)}, u32[]{:S(2)}, u32[]{:S(2)}) collective-permute-start(bf16[16,1664]{1,0:T(8,128)(2,1)S(1)} %get-tuple-element.46), channel_id=1, source_target_pairs={{0,2},{2,0},{4,6},{6,4},{8,10},{10,8},{12,14},{14,12},{1,3},{3,1},... | collective-permute-start | bytes 159752 | tf_op jit(solution)/shard_map/ppermute | solution.py:26
  19.6 9.9 %collective-permute-done.5.refs_3_.refs_1_ = bf16[2,64,1536]{2,1,0:T(8,128)(2,1)S(1)} collective-permute-done((bf16[2,64,1536]{2,1,0:T(8,128)(2,1)}, bf16[2,64,1536]{2,1,0:T(8,128)(2,1)S(1)}, u32[]{:S(2)}, u32[]{:S(2)}) %collective-permute-start.5) | collective-permute-done | bytes 393248 | tf_op jit(solution)/shard_map/ppermute | solution.py:26
  29.9 4.1 %collective-permute-done.6.refs_2_ = bf16[16,1664]{1,0:T(8,128)(2,1)S(1)} collective-permute-done((bf16[16,1664]{1,0:T(8,128)(2,1)S(1)}, bf16[16,1664]{1,0:T(8,128)(2,1)S(1)}, u32[]{:S(2)}, u32[]{:S(2)}) %collective-permute-start.6) | collective-permute-done | bytes 53280 | tf_op jit(solution)/shard_map/ppermute | solution.py:26
  34.4 0.5 collective-permute-start.15
  34.9 4.5 %collective-permute-done.7.pay_ref = bf16[16,1664]{1,0:T(8,128)(2,1)S(1)} collective-permute-done((bf16[16,1664]{1,0:T(8,128)(2,1)S(1)}, bf16[16,1664]{1,0:T(8,128)(2,1)S(1)}, u32[]{:S(2)}, u32[]{:S(2)}) %collective-permute-start.7) | collective-permute-done | bytes 53280 | tf_op jit(solution)/shard_map/ppermute | solution.py:26
  39.4 0.8 %shard_map.126.refs_0_ = f32[8,768]{1,0:T(8,128)S(1)} custom-call(f32[16,1536]{1,0:T(8,128)S(1)} %get-tuple-element.50.num_ref, f32[16,256]{1,0:T(8,128)S(1)} %get-tuple-element.51.state_ref, bf16[16,1664]{1,0:T(8,128)(2,1)S(1)} %collective-permute-done.7.pay_ref, bf16[2,1536,768]{2,1,0:T(8,128)(2,1)S(1)} %shard_map.122.weight_ref), custom_call_target="tpu_custom_call" | custom-call | flops 2000000000 | tf_op jit(solution)/shard_map/pallas_call | solution.py:251
  40.3 1.2 %collective-permute-done.8.refs_1_ = f32[8,768]{1,0:T(8,128)S(1)} collective-permute-done((f32[8,768]{1,0:T(8,128)S(1)}, f32[8,768]{1,0:T(8,128)S(1)}, u32[]{:S(2)}, u32[]{:S(2)}) %collective-permute-start.8) | collective-permute-done | bytes 24608 | tf_op jit(solution)/shard_map/ppermute | solution.py:26
  41.6 4.0 %collective-permute-done.9 = bf16[1,8,768]{2,1,0:T(8,128)(2,1)S(1)} collective-permute-done((bf16[1,8,768]{2,1,0:T(8,128)(2,1)S(1)}, bf16[1,8,768]{2,1,0:T(8,128)(2,1)S(1)}, u32[]{:S(2)}, u32[]{:S(2)}) %collective-permute-start.9) | collective-permute-done | bytes 12320 | tf_op jit(solution)/shard_map/ppermute | solution.py:31
  45.7 0.6 shard_map.131
  46.3 1.8 %collective-permute-start.16 = (bf16[2,64,1536]{2,1,0:T(8,128)(2,1)S(1)}, bf16[2,64,1536]{2,1,0:T(8,128)(2,1)S(1)}, u32[]{:S(2)}, u32[]{:S(2)}) collective-permute-start(bf16[2,64,1536]{2,1,0:T(8,128)(2,1)S(1)} %shard_map.131), channel_id=1, source_target_pairs={{0,4},{2,6},{4,0},{6,2},{8,12},{10,14},{12,8},{14,10},{1,5},{3,7},... | collective-permute-start | bytes 1179656 | tf_op jit(solution)/shard_map/ppermute | solution.py:26
  48.1 0.8 %collective-permute-done.10 = bf16[2,8,768]{2,1,0:T(8,128)(2,1)S(1)} collective-permute-done((bf16[2,8,768]{2,1,0:T(8,128)(2,1)S(1)}, bf16[2,8,768]{2,1,0:T(8,128)(2,1)S(1)}, u32[]{:S(2)}, u32[]{:S(2)}) %collective-permute-start.10) | collective-permute-done | bytes 24608 | tf_op jit(solution)/shard_map/ppermute | solution.py:31
  49.2 3.5 %collective-permute-done.11.refs_1_ = bf16[4,8,768]{2,1,0:T(8,128)(2,1)S(1)} collective-permute-done((bf16[4,8,768]{2,1,0:T(8,128)(2,1)S(1)}, bf16[4,8,768]{2,1,0:T(8,128)(2,1)S(1)}, u32[]{:S(2)}, u32[]{:S(2)}) %collective-permute-start.11) | collective-permute-done | bytes 49184 | tf_op jit(solution)/shard_map/ppermute | solution.py:31
  52.7 3.0 %shard_map.128 = (bf16[8,768]{1,0:T(8,128)(2,1)}, bf16[8,1536]{1,0:T(8,128)(2,1)S(1)}) custom-call(bf16[4,8,768]{2,1,0:T(8,128)(2,1)S(1)} %pad_maximum_fusion.refs_0_, bf16[4,8,768]{2,1,0:T(8,128)(2,1)S(1)} %collective-permute-done.11.refs_1_, bf16[6144,1536]{1,0:T(8,128)(2,1)S(1)} %copy-done), custom_call_target="tpu_custom_call" | custom-call | flops 1000000000 | tf_op jit(solution)/shard_map/pallas_call | solution.py:55
  55.8 0.4 collective-permute-start.12
  56.2 1.4 %shard_map.129.refs_2_ = f32[8,3072]{1,0:T(8,128)S(1)} custom-call(bf16[8,1536]{1,0:T(8,128)(2,1)S(1)} %get-tuple-element.56.refs_0_, bf16[3072,3072]{1,0:T(8,128)(2,1)S(1)} %bitcast.9), custom_call_target="tpu_custom_call" | custom-call | flops 1000000000 | tf_op jit(solution)/shard_map/pallas_call | solution.py:55
  57.6 1.4 %shard_map.130 = (f32[4,3072]{1,0:T(4,128)S(1)}, f32[4,3072]{1,0:T(4,128)S(1)}) custom-call(bf16[8,1536]{1,0:T(8,128)(2,1)S(1)} %collective-permute-done.12.refs_0_, bf16[3072,3072]{1,0:T(8,128)(2,1)S(1)} %bitcast.9, f32[8,3072]{1,0:T(8,128)S(1)} %shard_map.129.refs_2_), custom_call_target="tpu_custom_call" | custom-call | flops 1000000000 | tf_op jit(solution)/shard_map/pallas_call | solution.py:55
  59.1 0.5 collective-permute-start.13
  59.6 3.6 %collective-permute-done.13 = f32[4,3072]{1,0:T(4,128)S(1)} collective-permute-done((f32[4,3072]{1,0:T(4,128)S(1)}, f32[4,3072]{1,0:T(4,128)S(1)}, u32[]{:S(2)}, u32[]{:S(2)}) %collective-permute-start.13) | collective-permute-done | bytes 49184 | tf_op jit(solution)/shard_map/ppermute | solution.py:26
  63.3 1.4 %shard_map.132 = bf16[2,64,1536]{2,1,0:T(8,128)(2,1)} custom-call(bf16[2,64,1536]{2,1,0:T(8,128)(2,1)S(1)} %get-tuple-element.41.refs_2_.refs_0_, bf16[2,64,1536]{2,1,0:T(8,128)(2,1)S(1)} %collective-permute-done.5.refs_3_.refs_1_, bf16[2,64,1536]{2,1,0:T(8,128)(2,1)S(1)} %collective-permute-done.3.refs_7_.refs_2_, ...), custom_call_target="tpu_custom_call" | custom-call | flops 1000000000 | tf_op jit(solution)/shard_map/pallas_call | solution.py:55
  64.7 2.4 %collective-permute-done.14 = f32[2,3072]{1,0:T(2,128)S(1)} collective-permute-done((f32[2,3072]{1,0:T(2,128)S(1)}, f32[2,3072]{1,0:T(2,128)S(1)}, u32[]{:S(2)}, u32[]{:S(2)}) %collective-permute-start.14) | collective-permute-done | bytes 24608 | tf_op jit(solution)/shard_map/ppermute | solution.py:26
  67.3 4.5 %collective-permute-done.17 = f32[1,3072]{1,0:T(1,128)S(1)} collective-permute-done((f32[1,3072]{1,0:T(1,128)S(1)}, f32[1,3072]{1,0:T(1,128)S(1)}, u32[]{:S(2)}, u32[]{:S(2)}) %collective-permute-start.17) | collective-permute-done | bytes 12320 | tf_op jit(solution)/shard_map/ppermute | solution.py:26
  71.8 0.6 fusion.1
  (42 shorter events, 1.9 us)
Async XLA Ops:
  0.6 52.1 %copy-start = (bf16[6144,1536]{1,0:T(8,128)(2,1)S(1)}, bf16[6144,1536]{1,0:T(8,128)(2,1)}, u32[]{:S(2)}) copy-start(bf16[6144,1536]{1,0:T(8,128)(2,1)} %refs_2_.1) | copy-start | bytes 56623108
  0.6 6.9 %collective-permute-start = (bf16[2,1536]{1,0:T(2,128)(2,1)}, bf16[2,1536]{1,0:T(2,128)(2,1)S(1)}, u32[]{:S(2)}, u32[]{:S(2)}) collective-permute-start(bf16[2,1536]{1,0:T(2,128)(2,1)} %bitcast.14), channel_id=1, source_target_pairs={{0,8},{2,10},{4,12},{6,14},{8,0},{10,2},{12,4},{14,6},{1,9},{3,11}... | collective-permute-start | bytes 18440 | tf_op jit(solution)/shard_map/ppermute | solution.py:26
  4.7 11.3 %collective-permute-start.3 = (bf16[2,64,1536]{2,1,0:T(8,128)(2,1)}, bf16[2,64,1536]{2,1,0:T(8,128)(2,1)S(1)}, u32[]{:S(2)}, u32[]{:S(2)}) collective-permute-start(bf16[2,64,1536]{2,1,0:T(8,128)(2,1)} %bitcast.11), channel_id=1, source_target_pairs={{0,2},{2,0},{4,6},{6,4},{8,10},{10,8},{12,14},{14,12},{1,3},{3,1},... | collective-permute-start | bytes 1179656 | tf_op jit(solution)/shard_map/ppermute | solution.py:26
  7.6 4.1 %collective-permute-start.1 = (bf16[4,1536]{1,0:T(4,128)(2,1)S(1)}, bf16[4,1536]{1,0:T(4,128)(2,1)S(1)}, u32[]{:S(2)}, u32[]{:S(2)}) collective-permute-start(bf16[4,1536]{1,0:T(4,128)(2,1)S(1)} %pad_maximum_fusion.3), channel_id=1, source_target_pairs={{0,4},{2,6},{4,0},{6,2},{8,12},{10,14},{12,8},{14,10},{1,5},{3,7},... | collective-permute-start | bytes 36872 | tf_op jit(solution)/shard_map/ppermute | solution.py:26
  10.0 19.5 %collective-permute-start.5 = (bf16[2,64,1536]{2,1,0:T(8,128)(2,1)}, bf16[2,64,1536]{2,1,0:T(8,128)(2,1)S(1)}, u32[]{:S(2)}, u32[]{:S(2)}) collective-permute-start(bf16[2,64,1536]{2,1,0:T(8,128)(2,1)} %bitcast.13), channel_id=1, source_target_pairs={{0,8},{2,10},{4,12},{6,14},{8,0},{10,2},{12,4},{14,6},{1,9},{3,11}... | collective-permute-start | bytes 1179656 | tf_op jit(solution)/shard_map/ppermute | solution.py:26
  11.7 4.4 %collective-permute-start.2 = (bf16[8,1536]{1,0:T(8,128)(2,1)S(1)}, bf16[8,1536]{1,0:T(8,128)(2,1)S(1)}, u32[]{:S(2)}, u32[]{:S(2)}) collective-permute-start(bf16[8,1536]{1,0:T(8,128)(2,1)S(1)} %pad_maximum_fusion.1.refs_1_.refs_0_), channel_id=1, source_target_pairs={{0,2},{2,0},{4,6},{6,4},{8,10},{10,8},{12,14},{14,12},{1,3},{3,1},... | collective-permute-start | bytes 73736 | tf_op jit(solution)/shard_map/ppermute | solution.py:26
  16.1 0.7 copy-start.1
  18.0 11.5 %collective-permute-start.4 = (bf16[16,1664]{1,0:T(8,128)(2,1)S(1)}, bf16[16,1664]{1,0:T(8,128)(2,1)S(1)}, u32[]{:S(2)}, u32[]{:S(2)}) collective-permute-start(bf16[16,1664]{1,0:T(8,128)(2,1)S(1)} %get-tuple-element.46), channel_id=1, source_target_pairs={{0,2},{2,0},{4,6},{6,4},{8,10},{10,8},{12,14},{14,12},{1,3},{3,1},... | collective-permute-start | bytes 159752 | tf_op jit(solution)/shard_map/ppermute | solution.py:26
  29.8 26.4 %slice-start = ((s8[18874368]{0:T(1024)(128)(4,1)}), s8[4194304]{0:T(1024)(128)(4,1)S(1)}, s32[]{:S(2)}) async-start(s8[18874368]{0:T(1024)(128)(4,1)} %bitcast.8), calls=%async_computation | async-start | bytes 8388608
  29.8 4.2 %collective-permute-start.6 = (bf16[16,1664]{1,0:T(8,128)(2,1)S(1)}, bf16[16,1664]{1,0:T(8,128)(2,1)S(1)}, u32[]{:S(2)}, u32[]{:S(2)}) collective-permute-start(bf16[16,1664]{1,0:T(8,128)(2,1)S(1)} %get-tuple-element.49), channel_id=1, source_target_pairs={{0,4},{2,6},{4,0},{6,2},{8,12},{10,14},{12,8},{14,10},{1,5},{3,7},... | collective-permute-start | bytes 159752 | tf_op jit(solution)/shard_map/ppermute | solution.py:26
  34.3 5.1 %collective-permute-start.7 = (bf16[16,1664]{1,0:T(8,128)(2,1)S(1)}, bf16[16,1664]{1,0:T(8,128)(2,1)S(1)}, u32[]{:S(2)}, u32[]{:S(2)}) collective-permute-start(bf16[16,1664]{1,0:T(8,128)(2,1)S(1)} %get-tuple-element.52), channel_id=1, source_target_pairs={{0,8},{2,10},{4,12},{6,14},{8,0},{10,2},{12,4},{14,6},{1,9},{3,11}... | collective-permute-start | bytes 159752 | tf_op jit(solution)/shard_map/ppermute | solution.py:26
  34.4 11.3 %collective-permute-start.15 = (bf16[2,64,1536]{2,1,0:T(8,128)(2,1)S(1)}, bf16[2,64,1536]{2,1,0:T(8,128)(2,1)S(1)}, u32[]{:S(2)}, u32[]{:S(2)}) collective-permute-start(bf16[2,64,1536]{2,1,0:T(8,128)(2,1)S(1)} %collective-permute-done.5.refs_3_.refs_1_), channel_id=1, source_target_pairs={{0,2},{2,0},{4,6},{6,4},{8,10},{10,8},{12,14},{14,12},{1,3},{3,1},... | collective-permute-start | bytes 1179656 | tf_op jit(solution)/shard_map/ppermute | solution.py:26
  39.4 16.8 %slice-start.1 = ((s8[18874368]{0:T(1024)(128)(4,1)}), s8[4194304]{0:T(1024)(128)(4,1)S(1)}, s32[]{:S(2)}) async-start(s8[18874368]{0:T(1024)(128)(4,1)} %bitcast.8), calls=%async_computation.1 | async-start | bytes 8388608
  40.2 1.3 %collective-permute-start.8 = (f32[8,768]{1,0:T(8,128)S(1)}, f32[8,768]{1,0:T(8,128)S(1)}, u32[]{:S(2)}, u32[]{:S(2)}) collective-permute-start(f32[8,768]{1,0:T(8,128)S(1)} %shard_map.126.refs_0_), channel_id=1, source_target_pairs={{0,1},{1,0},{2,3},{3,2},{4,5},{5,4},{6,7},{7,6},{8,9},{9,8},{10,11... | collective-permute-start | bytes 73736 | tf_op jit(solution)/shard_map/ppermute | solution.py:26
  41.6 4.1 %collective-permute-start.9 = (bf16[1,8,768]{2,1,0:T(8,128)(2,1)S(1)}, bf16[1,8,768]{2,1,0:T(8,128)(2,1)S(1)}, u32[]{:S(2)}, u32[]{:S(2)}) collective-permute-start(bf16[1,8,768]{2,1,0:T(8,128)(2,1)S(1)} %shard_map.127), channel_id=1, source_target_pairs={{0,9},{1,8},{2,11},{3,10},{4,13},{5,12},{6,15},{7,14},{8,1},{9,0},... | collective-permute-start | bytes 36872 | tf_op jit(solution)/shard_map/ppermute | solution.py:31
  45.6 10.5 %slice-start.2 = ((s8[18874368]{0:T(1024)(128)(4,1)}), s8[4194304]{0:T(1024)(128)(4,1)S(1)}, s32[]{:S(2)}) async-start(s8[18874368]{0:T(1024)(128)(4,1)} %bitcast.8), calls=%async_computation.2 | async-start | bytes 8388608
  45.6 3.3 %collective-permute-start.10 = (bf16[2,8,768]{2,1,0:T(8,128)(2,1)S(1)}, bf16[2,8,768]{2,1,0:T(8,128)(2,1)S(1)}, u32[]{:S(2)}, u32[]{:S(2)}) collective-permute-start(bf16[2,8,768]{2,1,0:T(8,128)(2,1)S(1)} %pad_maximum_fusion.2), channel_id=1, source_target_pairs={{0,5},{1,4},{2,7},{3,6},{4,1},{5,0},{6,3},{7,2},{8,13},{9,12},{10,... | collective-permute-start | bytes 73736 | tf_op jit(solution)/shard_map/ppermute | solution.py:31
  46.3 17.1 %collective-permute-start.16 = (bf16[2,64,1536]{2,1,0:T(8,128)(2,1)S(1)}, bf16[2,64,1536]{2,1,0:T(8,128)(2,1)S(1)}, u32[]{:S(2)}, u32[]{:S(2)}) collective-permute-start(bf16[2,64,1536]{2,1,0:T(8,128)(2,1)S(1)} %shard_map.131), channel_id=1, source_target_pairs={{0,4},{2,6},{4,0},{6,2},{8,12},{10,14},{12,8},{14,10},{1,5},{3,7},... | collective-permute-start | bytes 1179656 | tf_op jit(solution)/shard_map/ppermute | solution.py:26
  48.9 7.3 %slice-start.3 = ((s8[18874368]{0:T(1024)(128)(4,1)}), s8[4194304]{0:T(1024)(128)(4,1)S(1)}, s32[]{:S(2)}) async-start(s8[18874368]{0:T(1024)(128)(4,1)} %bitcast.8), calls=%async_computation.3 | async-start | bytes 8388608
  48.9 7.3 %slice-start.4 = ((s8[18874368]{0:T(1024)(128)(4,1)}), s8[2097152]{0:T(1024)(128)(4,1)S(1)}, s32[]{:S(2)}) async-start(s8[18874368]{0:T(1024)(128)(4,1)} %bitcast.8), calls=%async_computation.4 | async-start | bytes 4194304
  48.9 3.8 %collective-permute-start.11 = (bf16[4,8,768]{2,1,0:T(8,128)(2,1)S(1)}, bf16[4,8,768]{2,1,0:T(8,128)(2,1)S(1)}, u32[]{:S(2)}, u32[]{:S(2)}) collective-permute-start(bf16[4,8,768]{2,1,0:T(8,128)(2,1)S(1)} %pad_maximum_fusion.refs_0_), channel_id=1, source_target_pairs={{0,3},{1,2},{2,1},{3,0},{4,7},{5,6},{6,5},{7,4},{8,11},{9,10},{10,... | collective-permute-start | bytes 147464 | tf_op jit(solution)/shard_map/ppermute | solution.py:31
  55.8 7.6 %copy-start.2 = (s32[1,8]{1,0:T(1,128)S(1)}, s32[1,8]{1,0:T(1,128)}, u32[]{:S(2)}) copy-start(s32[1,8]{1,0:T(1,128)} %refs_6_.2) | copy-start | bytes 100
  55.8 1.9 %collective-permute-start.12 = (bf16[8,1536]{1,0:T(8,128)(2,1)S(1)}, bf16[8,1536]{1,0:T(8,128)(2,1)S(1)}, u32[]{:S(2)}, u32[]{:S(2)}) collective-permute-start(bf16[8,1536]{1,0:T(8,128)(2,1)S(1)} %get-tuple-element.56.refs_0_), channel_id=1, source_target_pairs={{0,1},{1,0},{2,3},{3,2},{4,5},{5,4},{6,7},{7,6},{8,9},{9,8},{10,11... | collective-permute-start | bytes 73736 | tf_op jit(solution)/shard_map/ppermute | solution.py:26
  59.1 4.1 %collective-permute-start.13 = (f32[4,3072]{1,0:T(4,128)S(1)}, f32[4,3072]{1,0:T(4,128)S(1)}, u32[]{:S(2)}, u32[]{:S(2)}) collective-permute-start(f32[4,3072]{1,0:T(4,128)S(1)} %get-tuple-element.58), channel_id=1, source_target_pairs={{0,2},{2,0},{4,6},{6,4},{8,10},{10,8},{12,14},{14,12},{1,3},{3,1},... | collective-permute-start | bytes 147464 | tf_op jit(solution)/shard_map/ppermute | solution.py:26
  63.2 3.9 %collective-permute-start.14 = (f32[2,3072]{1,0:T(2,128)S(1)}, f32[2,3072]{1,0:T(2,128)S(1)}, u32[]{:S(2)}, u32[]{:S(2)}) collective-permute-start(f32[2,3072]{1,0:T(2,128)S(1)} %slice.17), channel_id=1, source_target_pairs={{0,4},{2,6},{4,0},{6,2},{8,12},{10,14},{12,8},{14,10},{1,5},{3,7},... | collective-permute-start | bytes 73736 | tf_op jit(solution)/shard_map/ppermute | solution.py:26
  67.2 4.7 %collective-permute-start.17 = (f32[1,3072]{1,0:T(1,128)S(1)}, f32[1,3072]{1,0:T(1,128)S(1)}, u32[]{:S(2)}, u32[]{:S(2)}) collective-permute-start(f32[1,3072]{1,0:T(1,128)S(1)} %slice.19), channel_id=1, source_target_pairs={{0,8},{2,10},{4,12},{6,14},{8,0},{10,2},{12,4},{14,6},{1,9},{3,11}... | collective-permute-start | bytes 36872 | tf_op jit(solution)/shard_map/ppermute | solution.py:26
